TPU v7x, 32 devices: a whole 2x2x4 slice. The times are simulated.
32 devices in a mesh: rep: 8 (over y, x, core), exp: 4 (over z).
Axes of the slice: x: 2, y: 2, z: 4, core: 2. Of those that a mesh axis runs over, the one named last changes fastest.
Arguments:
- activations: bfloat16 [8192, 3072], P('rep', 'exp'), may hold values from -6 to 6
- kv_grad: bfloat16 [8192, 1024], P('rep'), may hold values from -0.1875 to 0.1875
- errors: bfloat16 [8, 3072, 1024], P('rep', 'exp'), may hold values from -6 to 6
- right_factor: float32 [1024, 64], replicated, may hold values from -6 to 6
- hidden: bfloat16 [8, 512, 768], P('rep', 'exp'), may hold values from -6 to 6
- out_grad: bfloat16 [8, 512, 2048], P('rep', 'exp'), may hold values from -0.25 to 0.25
- moment_one: float32 [8, 768, 2048], P('rep', 'exp'), may hold values from -4 to 4
- moment_two: float32 [8, 768, 2048], P('rep', 'exp'), may hold values from 0.05 to 1
Outputs:
- new_error: bfloat16 [8, 3072, 1024], P('rep', 'exp')
- new_right: float32 [1024, 64], replicated
- new_moment_one: float32 [8, 768, 2048], P('rep', 'exp')
- new_moment_two: float32 [8, 768, 2048], P('rep', 'exp')
- update: bfloat16 [8, 768, 2048], P('rep', 'exp')
All inputs are finite; a program needn't handle non-finite values.
Results may differ from a plain program's by a relative error of at most 0.006.
Values may be sent and summed in bfloat16 or wider, within the bound.
No kernel may reach another device: no remote copies, remote signals or barrier semaphores. Data moves between devices by JAX's collectives and lax.ppermute only.
A program may use at most 64 MiB of HBM per device.

v0:
```python
import jax
import jax.numpy as jnp
from jax import lax
from jax.sharding import PartitionSpec as P

HIGHEST = lax.Precision.HIGHEST
beta_one = 0.9
beta_two = 0.99
correction_one = 1.0 - 0.9**10
correction_two = 1.0 - 0.99**10
epsilon = 1e-08


def apply_inverse(lower, matrix):
    return lax.linalg.triangular_solve(lower, matrix, left_side=False, lower=True, transpose_a=True)


def body(activations, kv_grad, errors, right_factor, hidden, out_grad, moment_one, moment_two):
    replicas = lax.axis_size("rep")
    contract_rows = (((0,), (0,)), ((), ()))
    merged = lax.dot_general(
        activations, kv_grad, contract_rows, preferred_element_type=jnp.float32
    )
    merged = merged + errors[0].astype(jnp.float32)
    local_left = jnp.dot(merged, right_factor, precision=HIGHEST)
    left_factor = lax.psum(local_left, "rep")
    local_gram = jnp.dot(left_factor.T, left_factor, precision=HIGHEST)
    gram_matrix = lax.psum(local_gram, "exp")
    lower_factor = jnp.linalg.cholesky(gram_matrix)
    basis_left = apply_inverse(lower_factor, left_factor)
    local_right = lax.dot_general(merged, basis_left, contract_rows, precision=HIGHEST)
    new_right = lax.psum(local_right, ("rep", "exp")) / replicas
    approx = jnp.dot(basis_left, new_right.T, precision=HIGHEST)
    new_error = (merged - approx).astype(jnp.bfloat16)[None]
    hidden_rows = hidden[0]
    grad_rows = out_grad[0]
    expert_grad = lax.psum_scatter(
        lax.dot_general(
            hidden_rows, grad_rows, contract_rows, preferred_element_type=jnp.float32
        ).astype(jnp.bfloat16),
        "exp",
        scatter_dimension=0,
        tiled=True,
    ).astype(jnp.float32)
    first_new = beta_one * moment_one[0] + (1.0 - beta_one) * expert_grad
    second_new = beta_two * moment_two[0] + (1.0 - beta_two) * expert_grad * expert_grad
    step_dir = first_new / correction_one / (jnp.sqrt(second_new / correction_two) + epsilon)
    return (
        new_error,
        new_right,
        first_new[None],
        second_new[None],
        step_dir.astype(jnp.bfloat16)[None],
    )


def solution(mesh):
    placed = (
        P("rep", "exp"),
        P("rep", None),
        P("rep", "exp", None),
        P(),
        P("rep", "exp", None),
        P("rep", "exp", None),
        P("rep", "exp", None),
        P("rep", "exp", None),
    )
    return jax.shard_map(
        body,
        mesh=mesh,
        in_specs=placed,
        out_specs=(
            P("rep", "exp", None),
            P(),
            P("rep", "exp", None),
            P("rep", "exp", None),
            P("rep", "exp", None),
        ),
        check_vma=False,
    )
```

profile of v0, /device:TPU:0, one launch (start us, length us, event | category | flops | bytes accessed | tf_op | source)
XLA Modules:
  0.0 297.4 jit_solution(15798921127597682742)
XLA Ops:
  8.0 0.0 all-reduce.3.cloned.1.call-start
  8.1 1.5 copy-done
  9.6 3.7 %convert_add_fusion = f32[768,1024]{1,0:T(8,128)S(1)} fusion(bf16[1024,768]{1,0:T(8,128)(2,1)} %param.8, bf16[1024,1024]{1,0:T(8,128)(2,1)S(1)} %copy-done, bf16[1,768,1024]{2,1,0:T(8,128)(2,1)} %param.10), kind=kOutput, calls=%fused_computation.1 | convolution fusion | flops 1612185600 | bytes 8388608 | tf_op jit(solution)/shard_map/dot_general | solution.py:21
  13.4 1.7 copy-done.1
  15.0 3.8 %fusion.12 = f32[768,64]{0,1:T(8,128)} fusion(f32[768,1024]{1,0:T(8,128)S(1)} %convert_add_fusion, f32[1024,64]{0,1:T(8,128)S(1)} %copy-done.4), kind=kOutput, calls=%fused_computation.25 | convolution fusion | flops 603979776 | bytes 3604480 | tf_op jit(solution)/shard_map/dot_general | solution.py:25
  18.8 0.0 all-reduce.3.cloned.1.call-update
  18.8 0.0 all-reduce.5.cloned.1.call-start
  18.9 56.1 %all-reduce.3.cloned.1.call-done = f32[768,64]{0,1:T(8,128)} async-done(((f32[768,64]{0,1:T(8,128)}), f32[768,64]{0,1:T(8,128)}) %all-reduce.3.cloned.1.call-update) | async-done | bytes 196624 | tf_op jit(solution)/shard_map/psum | solution.py:26
  75.0 1.3 fusion.13
  76.4 19.0 %psum.22 = f32[64,64]{0,1:T(8,128)S(1)} all-reduce(f32[64,64]{0,1:T(8,128)S(1)} %fusion.13), channel_id=1, replica_groups=mesh['rep'=8,'exp'=4] {'exp'}, use_global_device_ids=true, to_apply=%region_1.0 | all-reduce | flops 4096 | bytes 32768 | tf_op jit(solution)/shard_map/psum | solution.py:28
  95.3 0.1 copy.14
  95.4 5.8 %cholesky.16 = f32[64,64]{1,0:T(8,128)S(1)} custom-call(f32[64,64]{1,0:T(8,128)S(1)} %fusion.11), custom_call_target="Cholesky" | custom-call | tf_op jit(solution)/shard_map/jit(cholesky)/cholesky | solution.py:29
  101.3 0.6 compare_reduce_fusion
  102.0 0.7 fusion.8
  102.6 4.9 %custom-call.6 = f32[1,64,64]{1,2,0:T(8,128)S(1)} custom-call(f32[1,64,64]{2,1,0:T(8,128)S(1)} %fusion.8), custom_call_target="InvertDiagBlocksLowerTriangular" | custom-call | tf_op jit(solution)/shard_map/triangular_solve | solution.py:15
  107.5 1.3 fusion.9
  108.9 4.7 %fusion.14 = f32[1024,64]{0,1:T(8,128)} fusion(f32[768,1024]{1,0:T(8,128)} %copy-done.1, f32[768,64]{0,1:T(8,128)S(1)} %fusion.9), kind=kOutput, calls=%fused_computation.27 | convolution fusion | flops 603979776 | bytes 3604480 | tf_op jit(solution)/shard_map/dot_general | solution.py:31
  113.6 0.2 reduce-scatter.2.cloned.1.call-start
  113.9 2.7 convolution_convert_fusion
  116.6 0.0 reduce-scatter.2.cloned.1.call-update
  116.6 162.3 %all-reduce.5.cloned.1.call-done = f32[1024,64]{0,1:T(8,128)} async-done(((f32[1024,64]{0,1:T(8,128)}), f32[1024,64]{0,1:T(8,128)}) %all-reduce.5.cloned.1.call-update) | async-done | bytes 262160 | tf_op jit(solution)/shard_map/psum | solution.py:32
  278.9 1.0 broadcast_multiply_fusion
  279.9 5.3 %fusion.2 = bf16[1,768,1024]{2,1,0:T(8,128)(2,1)} fusion(f32[768,1024]{1,0:T(8,128)} %copy-done.1, f32[768,64]{0,1:T(8,128)S(1)} %fusion.9, f32[1024,64]{0,1:T(8,128)S(1)} %broadcast_multiply_fusion), kind=kOutput, calls=%fused_computation.8 | convolution fusion | flops 605552640 | bytes 5177344 | tf_op jit(solution)/shard_map/dot_general | solution.py:33
  285.2 4.8 %fusion.5 = (bf16[1,192,2048]{2,1,0:T(8,128)(2,1)}, f32[1,192,2048]{2,1,0:T(8,128)}, f32[1,192,2048]{2,1,0:T(8,128)}) fusion(f32[1,192,2048]{2,1,0:T(8,128)} %param.15, bf16[192,2048]{1,0:T(8,128)(2,1)} %reduce-scatter.2.cloned.1.call-done, f32[1,192,2048]{2,1,0:T(8,128)} %param.14), kind=kLoop, calls=%fused_computation.11 | loop fusion | flops 5111808 | bytes 7864320 | tf_op jit(solution)/shard_map/broadcast_in_dim | solution.py:53
  (14 shorter events, 0.1 us)
Async XLA Ops:
  8.0 1.6 copy-start
  8.0 7.0 %copy-start.4 = (f32[1024,64]{0,1:T(8,128)S(1)}, f32[1024,64]{0,1:T(8,128)}, u32[]{:S(2)}) copy-start(f32[1024,64]{0,1:T(8,128)} %param.11) | copy-start | bytes 786436
  8.0 67.0 %all-reduce.3.cloned.1.call-start = ((), (), s32[]{:S(2)}) async-start(), calls=%async_computation.1 | async-start | bytes 393216 | tf_op jit(solution)/shard_map/psum | solution.py:26
  13.3 1.7 copy-start.1
  18.8 260.1 %all-reduce.5.cloned.1.call-start = ((), (), s32[]{:S(2)}) async-start(), calls=%async_computation.2 | async-start | bytes 524288 | tf_op jit(solution)/shard_map/psum | solution.py:32
  108.8 5.0 %copy-start.3 = (bf16[1,128,2048]{2,1,0:T(8,128)(2,1)S(1)}, bf16[1,128,2048]{2,1,0:T(8,128)(2,1)}, u32[]{:S(2)}) copy-start(bf16[1,128,2048]{2,1,0:T(8,128)(2,1)} %param.13) | copy-start | bytes 1572868
  108.8 5.0 %copy-start.5 = (bf16[1,128,768]{2,1,0:T(8,128)(2,1)S(1)}, bf16[1,128,768]{2,1,0:T(8,128)(2,1)}, u32[]{:S(2)}) copy-start(bf16[1,128,768]{2,1,0:T(8,128)(2,1)} %param.12) | copy-start | bytes 589828
  113.6 171.6 %reduce-scatter.2.cloned.1.call-start = ((), (), s32[]{:S(2)}) async-start(), calls=%async_computation.3 | async-start | bytes 3932160 | tf_op jit(solution)/shard_map/reduce_scatter | solution.py:37
  279.9 5.3 %copy-start.2 = (f32[1024,64]{0,1:T(8,128)}, f32[1024,64]{0,1:T(8,128)S(1)}, u32[]{:S(2)}) copy-start(f32[1024,64]{0,1:T(8,128)S(1)} %broadcast_multiply_fusion) | copy-start | bytes 786436
Sparse Core Ops, SparseCore 0:
  18.9 56.0 all-reduce.2
  113.7 165.1 all-reduce.4
Sparse Core Ops, SparseCore 1:
  116.7 57.3 reduce-scatter.1
where the time goes:
time: 298 us; the launch traced here: 297 us
  waiting for transfers between devices  219 us (73%)
  matrix products  22.9 us (8%)
  blocking collectives  19 us (6%)
  other arithmetic  17.8 us (6%)
  between operations  15.6 us (5%)
  local copies, waits for them, and re-layouts  3.29 us (1%)
    psum x1, waiting for transfers between devices, body(): new_right = lax.psum(local_right, ('rep', 'exp')) / replicas  162 us
    psum x1, waiting for transfers between devices, body(): left_factor = lax.psum(local_left, 'rep')  56.1 us
    psum x1, blocking collectives, body(): gram_matrix = lax.psum(local_gram, 'exp')  19 us
    another operation x3, other arithmetic, body(): lower_factor = jnp.linalg.cholesky(gram_matrix)  6.52 us
  transfers between devices with their start and end apart: 3, of which 2 were waited for; matrix products, arithmetic and copies ran while one was open for 3% of the time, Pallas kernels for 0%

commit v1 on v0

v1 whole, which is shorter than its diff:
```python
import functools

import jax
import jax.numpy as jnp
from jax import lax
from jax.experimental import pallas as pl
from jax.experimental.pallas import tpu as pltpu
from jax.sharding import PartitionSpec as P

HIGHEST = lax.Precision.HIGHEST
F32 = jnp.float32
BF16 = jnp.bfloat16
beta_one = 0.9
beta_two = 0.99
correction_one = 1.0 - 0.9**10
correction_two = 1.0 - 0.99**10
epsilon = 1e-08

ROWS_FIRST = (((0,), (0,)), ((), ()))
COLS_LAST = (((1,), (1,)), ((), ()))
TILE_R, TILE_C = 16, 128
VMEM_LIMIT = 40 * 1024 * 1024


def params():
    return pltpu.CompilerParams(vmem_limit_bytes=VMEM_LIMIT)


def cost(flops, nbytes):
    return pl.CostEstimate(flops=int(flops), bytes_accessed=int(nbytes), transcendentals=0)


def split_two(x):
    hi = x.astype(BF16)
    return hi, (x - hi.astype(F32)).astype(BF16)


def left_times(left, right_bf16, dims):
    rows = left.shape[0]
    hi, lo = split_two(left)
    both = jnp.concatenate([hi, lo], axis=0)
    out = lax.dot_general(both, right_bf16, dims, preferred_element_type=F32)
    return out[:rows] + out[rows:]


def merge_kernel(acts_ref, kv_ref, err_ref, vt_ref, merged_ref, lt_ref):
    merged = lax.dot_general(acts_ref[...], kv_ref[...], ROWS_FIRST, preferred_element_type=F32)
    merged = merged + err_ref[0].astype(F32)
    merged_ref[...] = merged
    lt_ref[...] = left_times(vt_ref[...], merged.astype(BF16), COLS_LAST)


def merge(acts, kv, err, vt):
    tokens, rows = acts.shape
    cols = kv.shape[1]
    rank = vt.shape[0]
    block = 256
    return pl.pallas_call(
        merge_kernel,
        grid=(rows // block,),
        in_specs=[
            pl.BlockSpec((tokens, block), lambda i: (0, i)),
            pl.BlockSpec((tokens, cols), lambda i: (0, 0)),
            pl.BlockSpec((1, block, cols), lambda i: (0, i, 0)),
            pl.BlockSpec((rank, cols), lambda i: (0, 0)),
        ],
        out_specs=[
            pl.BlockSpec((block, cols), lambda i: (i, 0)),
            pl.BlockSpec((rank, block), lambda i: (0, i)),
        ],
        out_shape=[
            jax.ShapeDtypeStruct((rows, cols), F32),
            jax.ShapeDtypeStruct((rank, rows), F32),
        ],
        compiler_params=params(),
        cost_estimate=cost(2 * tokens * rows * cols, 2 * tokens * (rows + cols) + 6 * rows * cols),
        name="merge",
    )(acts, kv, err, vt)


def right_kernel(parts_ref, merged_ref, lt_ref, gram_ref, chunk_ref):
    parts = [parts_ref[i].astype(F32) for i in range(parts_ref.shape[0])]
    while len(parts) > 1:
        parts = [a + b for a, b in zip(parts[0::2], parts[1::2])]
    lt = parts[0]
    rank = lt.shape[0]
    lt_ref[...] = lt
    gram = lax.dot_general(lt, lt, COLS_LAST, precision=HIGHEST, preferred_element_type=F32)
    gram_ref[...] = jnp.concatenate([gram, jnp.zeros_like(gram)], axis=1)
    product = left_times(lt, merged_ref[...].astype(BF16), (((1,), (0,)), ((), ()))).astype(BF16)
    across = product.shape[1] // TILE_C
    for a in range(rank // TILE_R):
        for b in range(across):
            chunk_ref[a * across + b] = product[
                a * TILE_R : (a + 1) * TILE_R, b * TILE_C : (b + 1) * TILE_C
            ]


def right_product(parts, merged):
    _, rank, rows = parts.shape
    cols = merged.shape[1]
    chunks = rank * cols // (TILE_R * TILE_C)
    return pl.pallas_call(
        right_kernel,
        out_shape=[
            jax.ShapeDtypeStruct((rank, rows), F32),
            jax.ShapeDtypeStruct((rank, 2 * rank), F32),
            jax.ShapeDtypeStruct((chunks, TILE_R, TILE_C), BF16),
        ],
        compiler_params=params(),
        cost_estimate=cost(2 * rows * cols * 128, 4 * rows * cols),
        name="right_product",
    )(parts, merged)


def inverse_kernel(gram_ref, w_ref):
    parts = [gram_ref[i] for i in range(gram_ref.shape[0])]
    while len(parts) > 1:
        parts = [a + b for a, b in zip(parts[0::2], parts[1::2])]
    rank, width = parts[0].shape
    row = lax.broadcasted_iota(jnp.int32, (rank, width), 0)
    col = lax.broadcasted_iota(jnp.int32, (rank, width), 1)
    a = parts[0] + jnp.where(col == row + rank, 1.0, 0.0).astype(F32)
    row_ids = lax.broadcasted_iota(jnp.int32, (rank, 1), 0)
    for k in range(rank):
        pivot_row = a[k : k + 1, :]
        pivot = pivot_row[:, k : k + 1]
        w_ref[k : k + 1, :] = pivot_row[:, rank:] * lax.rsqrt(pivot)
        if k + 1 < rank:
            factor = jnp.where(row_ids > k, a[:, k : k + 1] / pivot, 0.0)
            a = a - factor * pivot_row


def inverse_factor(gram_parts):
    rank = gram_parts.shape[1]
    return pl.pallas_call(
        inverse_kernel,
        out_shape=jax.ShapeDtypeStruct((rank, rank), F32),
        compiler_params=params(),
        cost_estimate=cost(4e9, 1e5),
        name="inverse_factor",
    )(gram_parts)


def finish_kernel(replicas, w_ref, chunk_ref, lt_ref, merged_ref, right_ref, err_ref, nr_ref):
    @pl.when(pl.program_id(0) == 0)
    def _():
        cols = right_ref.shape[1]
        across = cols // TILE_C
        pieces = []
        for a in range(right_ref.shape[0] // TILE_R):
            pieces.append(
                jnp.concatenate([chunk_ref[a * across + b] for b in range(across)], axis=1)
            )
        product = jnp.concatenate(pieces, axis=0)
        new_right = left_times(w_ref[...], product, (((1,), (0,)), ((), ()))) * (1.0 / replicas)
        right_ref[...] = new_right
        nr_ref[...] = new_right.astype(BF16)

    basis = jnp.dot(w_ref[...], lt_ref[...], precision=HIGHEST, preferred_element_type=F32)
    approx = lax.dot_general(basis.astype(BF16), nr_ref[...], ROWS_FIRST, preferred_element_type=F32)
    err_ref[0] = (merged_ref[...] - approx).astype(BF16)


def finish(replicas, w, chunks, lt, merged):
    rank, rows = lt.shape
    cols = merged.shape[1]
    block = 256
    return pl.pallas_call(
        functools.partial(finish_kernel, replicas),
        grid=(rows // block,),
        in_specs=[
            pl.BlockSpec(w.shape, lambda i: (0, 0)),
            pl.BlockSpec(chunks.shape, lambda i: (0, 0, 0)),
            pl.BlockSpec((rank, block), lambda i: (0, i)),
            pl.BlockSpec((block, cols), lambda i: (i, 0)),
        ],
        out_specs=[
            pl.BlockSpec((rank, cols), lambda i: (0, 0)),
            pl.BlockSpec((1, block, cols), lambda i: (0, i, 0)),
        ],
        out_shape=[
            jax.ShapeDtypeStruct((rank, cols), F32),
            jax.ShapeDtypeStruct((1, rows, cols), BF16),
        ],
        scratch_shapes=[pltpu.VMEM((rank, cols), BF16)],
        compiler_params=params(),
        cost_estimate=cost(2 * rows * cols * 128, 6 * rows * cols),
        name="finish",
    )(w, chunks, lt, merged)


def expert_kernel(n_hid, n_grad, *refs):
    hid_refs, grad_refs = refs[:n_hid], refs[n_hid : n_hid + sum(n_grad)]
    one_ref, two_ref, first_ref, second_ref, step_ref = refs[n_hid + sum(n_grad) :]
    grad = None
    at = 0
    for h_ref, count in zip(hid_refs, n_grad):
        rows = grad_refs[at][0]
        if count == 2:
            rows = rows + grad_refs[at + 1][0]
        at += count
        part = jnp.dot(h_ref[...], rows, preferred_element_type=F32).astype(BF16).astype(F32)
        grad = part if grad is None else grad + part
    first_new = beta_one * one_ref[0] + (1.0 - beta_one) * grad
    second_new = beta_two * two_ref[0] + (1.0 - beta_two) * grad * grad
    first_ref[0] = first_new
    second_ref[0] = second_new
    step = first_new / correction_one / (jnp.sqrt(second_new / correction_two) + epsilon)
    step_ref[0] = step.astype(BF16)


def expert_step(hids, grads, moment_one, moment_two):
    _, units, width = moment_one.shape
    block = 512
    n_grad = tuple(len(g) for g in grads)
    flat = [g for group in grads for g in group]
    tokens = flat[0].shape[1]
    wide = pl.BlockSpec((1, units, block), lambda i: (0, 0, i))
    return pl.pallas_call(
        functools.partial(expert_kernel, len(hids), n_grad),
        grid=(width // block,),
        in_specs=[pl.BlockSpec((units, tokens), lambda i: (0, 0))] * len(hids)
        + [pl.BlockSpec((1, tokens, block), lambda i: (0, 0, i))] * len(flat)
        + [wide, wide],
        out_specs=[wide, wide, wide],
        out_shape=[
            jax.ShapeDtypeStruct((1, units, width), F32),
            jax.ShapeDtypeStruct((1, units, width), F32),
            jax.ShapeDtypeStruct((1, units, width), BF16),
        ],
        compiler_params=params(),
        cost_estimate=cost(2 * units * width * tokens * len(hids), 20 * units * width),
        name="expert_step",
    )(*hids, *flat, moment_one, moment_two)


def power_of_two(n):
    return n & (n - 1) == 0


def swap(x, axis, size, mask):
    return lax.ppermute(x, axis, [(i, i ^ mask) for i in range(size)])


def gather_line(x, axis, size):
    right, left = [x], [x]
    for k in range(1, size):
        right.append(lax.ppermute(right[-1], axis, [(i, i + 1) for i in range(k - 1, size - 1)]))
        left.append(lax.ppermute(left[-1], axis, [(i, i - 1) for i in range(1, size - k + 1)]))
    return [(right[k], left[size - k]) for k in range(1, size)]


def body(n_rep, n_exp, activations, kv_grad, errors, right_factor, hidden, out_grad, moment_one, moment_two):
    others = gather_line(out_grad, "exp", n_exp)

    merged, lt = merge(activations, kv_grad, errors, right_factor.T)

    place = lax.axis_index("exp")
    tokens, units = hidden.shape[1], hidden.shape[2] // n_exp
    slabs = hidden[0].T.reshape(n_exp, units, tokens)
    hids = [lax.dynamic_index_in_dim(slabs, place, 0, keepdims=False)]
    for k in range(1, n_exp):
        piece = lax.dynamic_index_in_dim(slabs, lax.rem(place + k, n_exp), 0, keepdims=False)
        hids.append(lax.ppermute(piece, "exp", [(i, (i + k) % n_exp) for i in range(n_exp)]))

    lt = lt + swap(lt, "rep", n_rep, 1)
    bit = 2
    parts = lt.astype(BF16)[None]
    while bit < n_rep:
        if bit > 2:
            total = parts.astype(F32)
            while total.shape[0] > 1:
                total = total[0::2] + total[1::2]
            parts = total.astype(BF16)
        own = parts[0]
        masks = [bit] if 2 * bit >= n_rep else [bit, 2 * bit, 3 * bit]
        parts = jnp.stack([own] + [swap(own, "rep", n_rep, m) for m in masks])
        bit *= 2 * len(masks) if len(masks) == 1 else 4
    lt, gram, chunks = right_product(parts, merged)

    if power_of_two(n_exp):
        gram_parts = jnp.stack([gram] + [swap(gram, "exp", n_exp, m) for m in range(1, n_exp)])
    else:
        gram_parts = lax.psum(gram, "exp")[None]
    w = inverse_factor(gram_parts)

    n_chunks = chunks.shape[0]
    if n_chunks == n_rep * n_exp:
        both = ("rep", "exp")
        shares = lax.all_to_all(chunks, both, 0, 0, tiled=True)
        share = jnp.sum(shares.astype(F32), axis=0).astype(BF16)
        chunks = lax.all_to_all(jnp.broadcast_to(share[None], chunks.shape), both, 0, 0, tiled=True)
    else:
        chunks = lax.psum(chunks.astype(F32), ("rep", "exp")).astype(BF16)

    new_right, new_error = finish(n_rep, w, chunks, lt, merged)
    first_new, second_new, step = expert_step(hids, [(out_grad,)] + others, moment_one, moment_two)
    return new_error, new_right.T, first_new, second_new, step


def solution(mesh):
    placed = (
        P("rep", "exp"),
        P("rep", None),
        P("rep", "exp", None),
        P(),
        P("rep", "exp", None),
        P("rep", "exp", None),
        P("rep", "exp", None),
        P("rep", "exp", None),
    )
    return jax.shard_map(
        functools.partial(body, mesh.shape["rep"], mesh.shape["exp"]),
        mesh=mesh,
        in_specs=placed,
        out_specs=(
            P("rep", "exp", None),
            P(),
            P("rep", "exp", None),
            P("rep", "exp", None),
            P("rep", "exp", None),
        ),
        check_vma=False,
    )
```

time: 298 us -> 79.2 us (0.27)
  waiting for transfers between devices: 219 us -> 7.3 us
  starting transfers between devices: 0.3 us -> 40 us
  matrix products: 22.9 us -> 0 us
  blocking collectives: 19 us -> 0 us
  Pallas kernels: 0 us -> 18.4 us
  other arithmetic: 17.8 us -> 0.78 us
  between operations: 15.6 us -> 0.8 us
  local copies, waits for them, and re-layouts: 3.29 us -> 11.2 us
    psum x2 -> x0, waiting for transfers between devices: 218 us -> none  [the longest x1 162 us: body(): new_right = lax.psum(local_right, ('rep', 'exp')) / replicas]
    ppermute x0 -> x16, starting transfers between devices: none -> 29.7 us  [the longest x3 9.34 us: gather_line(): lax.ppermute(right[-1], axis, [(i, i + 1) for i in range(k - 1, size - 1)])]
    dot_general x6 -> x0, matrix products: 21.6 us -> none  [the longest x1 5.3 us: body(): approx = jnp.dot(basis_left, new_right.T, precision=HIGHEST)]
    psum x1 -> x0, blocking collectives: 19 us -> none  [body(): gram_matrix = lax.psum(local_gram, 'exp')]
    pallas_call x0 -> x5, Pallas kernels: none -> 18.4 us  [the longest x1 5.61 us: expert_step(): pl.pallas_call(functools.partial(expert_kernel, len(hids), n_grad), grid=...]
    another operation x5 -> x2, other arithmetic: 12.1 us -> 0.72 us  [the longest x1 0.67 us: body(): jnp.stack([gram] + [swap(gram, 'exp', n_exp, m) for m in range(1, n_exp)])]
    all_to_all x0 -> x2, starting transfers between devices: none -> 10.2 us  [the longest x1 7.47 us: body(): shares = lax.all_to_all(chunks, both, 0, 0, tiled=True)]
    unnamed x12 -> x17, local copies, waits for them, and re-layouts: 3.22 us -> 9.04 us
  transfers between devices with their start and end apart: 3 -> 18, of which waited for: 2 -> 5; matrix products, arithmetic and copies ran while one was open for 3% -> 6% of each run, Pallas kernels for 0% -> 16%
where the time goes in v1:
time: 79.2 us; the launch traced here: 78.5 us
  starting transfers between devices  40 us (51%)
  Pallas kernels  18.4 us (23%)
  local copies, waits for them, and re-layouts  11.2 us (14%)
  waiting for transfers between devices  7.3 us (9%)
  between operations  0.8 us (1%)
    ppermute x3, starting transfers between devices, gather_line(): lax.ppermute(right[-1], axis, [(i, i + 1) for i in range(k - 1, size - 1)])  9.34 us
    unnamed x17, local copies, waits for them, and re-layouts  9.04 us
    ppermute x3, starting transfers between devices, body(): lax.ppermute(piece, 'exp', [(i, (i + k) % n_exp) for i in range(n_exp)])  8.5 us
    ppermute x7, starting transfers between devices, swap(): return lax.ppermute(x, axis, [(i, i ^ mask) for i in range(size)])  8.01 us
    all_to_all x1, starting transfers between devices, body(): shares = lax.all_to_all(chunks, both, 0, 0, tiled=True)  7.47 us
    pallas_call x1, Pallas kernels, expert_step(): pl.pallas_call(functools.partial(expert_kernel, len(hids), n_grad), grid=...  5.61 us
    pallas_call x1, Pallas kernels, inverse_factor(): pl.pallas_call(inverse_kernel, out_shape=jax.ShapeDtypeStruct((rank, rank...  5.54 us
    ppermute x7, waiting for transfers between devices, swap(): return lax.ppermute(x, axis, [(i, i ^ mask) for i in range(size)])  4.36 us
  transfers between devices with their start and end apart: 18, of which 5 were waited for; matrix products, arithmetic and copies ran while one was open for 6% of the time, Pallas kernels for 16%

profile of v1, /device:TPU:0, one launch (start us, length us, event | category | flops | bytes accessed | tf_op | source)
XLA Modules:
  0.0 78.5 jit_solution(8759169206094787190)
XLA Ops:
  0.6 1.3 %collective-permute-start.11 = (bf16[1,128,2048]{2,1,0:T(8,128)(2,1)}, bf16[1,128,2048]{2,1,0:T(8,128)(2,1)}, u32[]{:S(2)}, u32[]{:S(2)}) collective-permute-start(bf16[1,128,2048]{2,1,0:T(8,128)(2,1)} %refs_4_.1), channel_id=1, source_target_pairs={{1,0},{2,1},{3,2},{5,4},{6,5},{7,6},{9,8},{10,9},{11,10},{13,12},{... | collective-permute-start | bytes 1572872 | tf_op jit(solution)/shard_map/ppermute | solution.py:250
  1.9 6.4 %collective-permute-start.10 = (bf16[1,128,2048]{2,1,0:T(8,128)(2,1)}, bf16[1,128,2048]{2,1,0:T(8,128)(2,1)}, u32[]{:S(2)}, u32[]{:S(2)}) collective-permute-start(bf16[1,128,2048]{2,1,0:T(8,128)(2,1)} %refs_4_.1), channel_id=1, source_target_pairs={{0,1},{1,2},{2,3},{4,5},{5,6},{6,7},{8,9},{9,10},{10,11},{12,13},{... | collective-permute-start | bytes 1572872 | tf_op jit(solution)/shard_map/ppermute | solution.py:249
  8.3 1.6 %copy-done.4 = bf16[1024,1024]{1,0:T(8,128)(2,1)S(1)} copy-done((bf16[1024,1024]{1,0:T(8,128)(2,1)S(1)}, bf16[1024,1024]{1,0:T(8,128)(2,1)}, u32[]{:S(2)}) %copy-start.4) | copy-done | bytes 2097176
  9.9 1.4 %copy-done.5 = bf16[1024,768]{1,0:T(8,128)(2,1)S(1)} copy-done((bf16[1024,768]{1,0:T(8,128)(2,1)S(1)}, bf16[1024,768]{1,0:T(8,128)(2,1)}, u32[]{:S(2)}) %copy-start.5) | copy-done | bytes 1572888
  11.3 1.4 %copy-done.6 = bf16[1,768,1024]{2,1,0:T(8,128)(2,1)S(1)} copy-done((bf16[1,768,1024]{2,1,0:T(8,128)(2,1)S(1)}, bf16[1,768,1024]{2,1,0:T(8,128)(2,1)}, u32[]{:S(2)}) %copy-start.6) | copy-done | bytes 1572888
  13.7 3.1 %merge.1 = (f32[768,1024]{1,0:T(8,128)S(1)}, f32[64,768]{1,0:T(8,128)S(1)}) custom-call(bf16[1024,768]{1,0:T(8,128)(2,1)S(1)} %copy-done.5, bf16[1024,1024]{1,0:T(8,128)(2,1)S(1)} %copy-done.4, bf16[1,768,1024]{2,1,0:T(8,128)(2,1)S(1)} %copy-done.6, f32[64,1024]{1,0:T(8,128)S(1)} %bitcast.24), custom_call_target="tpu_custom_call" | custom-call | flops 1610612736 | bytes 8388608 | tf_op jit(solution)/shard_map/merge/pallas_call | solution.py:58
  19.1 1.5 %collective-permute-start.14 = (bf16[1,128,2048]{2,1,0:T(8,128)(2,1)}, bf16[1,128,2048]{2,1,0:T(8,128)(2,1)}, u32[]{:S(2)}, u32[]{:S(2)}) collective-permute-start(bf16[1,128,2048]{2,1,0:T(8,128)(2,1)} %collective-permute-done.10.refs_5_), channel_id=1, source_target_pairs={{1,2},{2,3},{5,6},{6,7},{9,10},{10,11},{13,14},{14,15},{17,18},{18... | collective-permute-start | bytes 1572872 | tf_op jit(solution)/shard_map/ppermute | solution.py:249
  20.6 2.7 %collective-permute-start.3 = (bf16[64,768]{1,0:T(8,128)(2,1)S(1)}, bf16[64,768]{1,0:T(8,128)(2,1)S(1)}, u32[]{:S(2)}, u32[]{:S(2)}) collective-permute-start(bf16[64,768]{1,0:T(8,128)(2,1)S(1)} %add_convert_fusion), channel_id=1, source_target_pairs={{0,24},{4,28},{8,16},{12,20},{16,8},{20,12},{24,0},{28,4},{1,25},{... | collective-permute-start | bytes 294920 | tf_op jit(solution)/shard_map/ppermute | solution.py:243
  24.2 2.3 %collective-permute-done.3 = bf16[64,768]{1,0:T(8,128)(2,1)S(1)} collective-permute-done((bf16[64,768]{1,0:T(8,128)(2,1)S(1)}, bf16[64,768]{1,0:T(8,128)(2,1)S(1)}, u32[]{:S(2)}, u32[]{:S(2)}) %collective-permute-start.3) | collective-permute-done | bytes 98336 | tf_op jit(solution)/shard_map/ppermute | solution.py:243
  26.4 1.8 %collective-permute-done.2 = bf16[64,768]{1,0:T(8,128)(2,1)S(1)} collective-permute-done((bf16[64,768]{1,0:T(8,128)(2,1)S(1)}, bf16[64,768]{1,0:T(8,128)(2,1)S(1)}, u32[]{:S(2)}, u32[]{:S(2)}) %collective-permute-start.2) | collective-permute-done | bytes 98336 | tf_op jit(solution)/shard_map/ppermute | solution.py:243
  29.8 7.5 %all-to-all-start = ((bf16[32,16,128]{2,1,0:T(8,128)(2,1)}), bf16[32,16,128]{2,1,0:T(8,128)(2,1)S(1)}, u32[]{:S(2)}, u32[]{:S(2)}) async-start(bf16[32,16,128]{2,1,0:T(8,128)(2,1)} %get-tuple-element.18), calls=%async_computation | async-start | bytes 262144 | tf_op jit(solution)/shard_map/all_to_all | solution.py:291
  37.3 1.7 %copy.17 = bf16[1,128,768]{1,2,0:T(8,128)(2,1)} copy(bf16[1,128,768]{2,1,0:T(8,128)(2,1)} %param.12) | data formatting | bytes 393216 | tf_op args[4]
  39.0 3.6 %collective-permute-start.6 = (f32[64,128]{1,0:T(8,128)S(1)}, f32[64,128]{1,0:T(8,128)S(1)}, u32[]{:S(2)}, u32[]{:S(2)}) collective-permute-start(f32[64,128]{1,0:T(8,128)S(1)} %get-tuple-element.17), channel_id=1, source_target_pairs={{0,3},{1,2},{2,1},{3,0},{4,7},{5,6},{6,5},{7,4},{8,11},{9,10},{10,... | collective-permute-start | bytes 98312 | tf_op jit(solution)/shard_map/ppermute | solution.py:243
  43.4 1.3 %collective-permute-start.13 = (bf16[1,128,2048]{2,1,0:T(8,128)(2,1)}, bf16[1,128,2048]{2,1,0:T(8,128)(2,1)}, u32[]{:S(2)}, u32[]{:S(2)}) collective-permute-start(bf16[1,128,2048]{2,1,0:T(8,128)(2,1)} %collective-permute-done.12.refs_8_), channel_id=1, source_target_pairs={{1,0},{5,4},{9,8},{13,12},{17,16},{21,20},{25,24},{29,28}} | collective-permute-start | bytes 1572872 | tf_op jit(solution)/shard_map/ppermute | solution.py:250
  44.7 1.5 %collective-permute-start.15 = (bf16[1,128,2048]{2,1,0:T(8,128)(2,1)}, bf16[1,128,2048]{2,1,0:T(8,128)(2,1)}, u32[]{:S(2)}, u32[]{:S(2)}) collective-permute-start(bf16[1,128,2048]{2,1,0:T(8,128)(2,1)} %collective-permute-done.14.refs_7_), channel_id=1, source_target_pairs={{2,3},{6,7},{10,11},{14,15},{18,19},{22,23},{26,27},{30,31}} | collective-permute-start | bytes 1572872 | tf_op jit(solution)/shard_map/ppermute | solution.py:249
  46.2 1.5 %dynamic-slice_bitcast_fusion = (bf16[192,128]{1,0:T(8,128)(2,1)}, bf16[192,128]{1,0:T(8,128)(2,1)}, bf16[192,128]{1,0:T(8,128)(2,1)}, bf16[192,128]{1,0:T(8,128)(2,1)S(1)}) fusion(bf16[4,192,128]{2,1,0:T(8,128)(2,1)} %bitcast.25, s32[]{:T(128)S(6)} %select_n.16, s32[]{:T(128)S(6)} %select_n.15, s32[]{:T(128)S(6)} %select_n.14, s32[]{:T(128)S(6)} %select_n.13), kind=kLoop, calls=%fused_computation.3 | loop fusion | bytes 393232 | tf_op jit(solution)/shard_map/jit(dynamic_index_in_dim)/squeeze | solution.py:264
  47.7 3.4 %collective-permute-start.7 = (bf16[192,128]{1,0:T(8,128)(2,1)}, bf16[192,128]{1,0:T(8,128)(2,1)}, u32[]{:S(2)}, u32[]{:S(2)}) collective-permute-start(bf16[192,128]{1,0:T(8,128)(2,1)} %get-tuple-element.27), channel_id=1, source_target_pairs={{0,1},{1,2},{2,3},{3,0},{4,5},{5,6},{6,7},{7,4},{8,9},{9,10},{10,1... | collective-permute-start | bytes 147464 | tf_op jit(solution)/shard_map/ppermute | solution.py:265
  51.1 2.2 %collective-permute-start.8 = (bf16[192,128]{1,0:T(8,128)(2,1)}, bf16[192,128]{1,0:T(8,128)(2,1)}, u32[]{:S(2)}, u32[]{:S(2)}) collective-permute-start(bf16[192,128]{1,0:T(8,128)(2,1)} %get-tuple-element.26), channel_id=1, source_target_pairs={{0,2},{1,3},{2,0},{3,1},{4,6},{5,7},{6,4},{7,5},{8,10},{9,11},{10,... | collective-permute-start | bytes 147464 | tf_op jit(solution)/shard_map/ppermute | solution.py:265
  53.4 2.8 %collective-permute-start.9 = (bf16[192,128]{1,0:T(8,128)(2,1)}, bf16[192,128]{1,0:T(8,128)(2,1)}, u32[]{:S(2)}, u32[]{:S(2)}) collective-permute-start(bf16[192,128]{1,0:T(8,128)(2,1)} %get-tuple-element.25), channel_id=1, source_target_pairs={{0,3},{1,0},{2,1},{3,2},{4,7},{5,4},{6,5},{7,6},{8,11},{9,8},{10,9... | collective-permute-start | bytes 147464 | tf_op jit(solution)/shard_map/ppermute | solution.py:265
  57.6 2.8 %all-to-all-start.1 = ((bf16[32,16,128]{2,1,0:T(8,128)(2,1)}), bf16[32,16,128]{2,1,0:T(8,128)(2,1)S(1)}, u32[]{:S(2)}, u32[]{:S(2)}) async-start(bf16[32,16,128]{2,1,0:T(8,128)(2,1)} %broadcast_in_dim.10), calls=%async_computation.1 | async-start | bytes 262144 | tf_op jit(solution)/shard_map/all_to_all | solution.py:293
  61.3 5.5 %inverse_factor.1.w_ref = f32[64,64]{1,0:T(8,128)S(1)} custom-call(f32[4,64,128]{2,1,0:T(8,128)S(1)} %copy-done.3), custom_call_target="tpu_custom_call" | custom-call | flops 4000000000 | bytes 100000 | tf_op jit(solution)/shard_map/inverse_factor/pallas_call | solution.py:136
  66.8 2.0 %all-to-all-done.1.chunk_ref = bf16[32,16,128]{2,1,0:T(8,128)(2,1)S(1)} async-done(((bf16[32,16,128]{2,1,0:T(8,128)(2,1)}), bf16[32,16,128]{2,1,0:T(8,128)(2,1)S(1)}, u32[]{:S(2)}, u32[]{:S(2)}) %all-to-all-start.1) | async-done | bytes 131104 | tf_op jit(solution)/shard_map/all_to_all | solution.py:293
  68.8 3.0 %finish.1 = (f32[64,1024]{1,0:T(8,128)}, bf16[1,768,1024]{2,1,0:T(8,128)(2,1)}) custom-call(f32[64,64]{1,0:T(8,128)S(1)} %inverse_factor.1.w_ref, bf16[32,16,128]{2,1,0:T(8,128)(2,1)S(1)} %all-to-all-done.1.chunk_ref, f32[64,768]{1,0:T(8,128)S(1)} %get-tuple-element.19.lt_ref, f32[768,1024]{1,0:T(8,128)S(1)} %get-tuple-element.16.merged_ref), custom_call_target="tpu_custom_call" | custom-call | flops 201326592 | bytes 4718592 | tf_op jit(solution)/shard_map/finish/pallas_call | solution.py:169
  72.9 5.6 %expert_step.1 = (f32[1,192,2048]{2,1,0:T(8,128)}, f32[1,192,2048]{2,1,0:T(8,128)}, bf16[1,192,2048]{2,1,0:T(8,128)(2,1)}) custom-call(bf16[192,128]{1,0:T(8,128)(2,1)S(1)} %get-tuple-element.28.refs_0_, bf16[192,128]{1,0:T(8,128)(2,1)} %collective-permute-done.7.refs_1_, bf16[192,128]{1,0:T(8,128)(2,1)} %collective-permute-done.8.refs_2_, ...), custom_call_target="tpu_custom_call" | custom-call | flops 402653184 | bytes 7864320 | tf_op jit(solution)/shard_map/expert_step/pallas_call | solution.py:220
  (40 shorter events, 9.8 us)
Async XLA Ops:
  0.6 17.2 %collective-permute-start.11 = (bf16[1,128,2048]{2,1,0:T(8,128)(2,1)}, bf16[1,128,2048]{2,1,0:T(8,128)(2,1)}, u32[]{:S(2)}, u32[]{:S(2)}) collective-permute-start(bf16[1,128,2048]{2,1,0:T(8,128)(2,1)} %refs_4_.1), channel_id=1, source_target_pairs={{1,0},{2,1},{3,2},{5,4},{6,5},{7,6},{9,8},{10,9},{11,10},{13,12},{... | collective-permute-start | bytes 1572872 | tf_op jit(solution)/shard_map/ppermute | solution.py:250
  1.9 17.2 %collective-permute-start.10 = (bf16[1,128,2048]{2,1,0:T(8,128)(2,1)}, bf16[1,128,2048]{2,1,0:T(8,128)(2,1)}, u32[]{:S(2)}, u32[]{:S(2)}) collective-permute-start(bf16[1,128,2048]{2,1,0:T(8,128)(2,1)} %refs_4_.1), channel_id=1, source_target_pairs={{0,1},{1,2},{2,3},{4,5},{5,6},{6,7},{8,9},{9,10},{10,11},{12,13},{... | collective-permute-start | bytes 1572872 | tf_op jit(solution)/shard_map/ppermute | solution.py:249
  8.3 1.6 %copy-start.4 = (bf16[1024,1024]{1,0:T(8,128)(2,1)S(1)}, bf16[1024,1024]{1,0:T(8,128)(2,1)}, u32[]{:S(2)}) copy-start(bf16[1024,1024]{1,0:T(8,128)(2,1)} %kv_ref.1) | copy-start | bytes 6291460
  9.9 1.4 %copy-start.5 = (bf16[1024,768]{1,0:T(8,128)(2,1)S(1)}, bf16[1024,768]{1,0:T(8,128)(2,1)}, u32[]{:S(2)}) copy-start(bf16[1024,768]{1,0:T(8,128)(2,1)} %acts_ref.1) | copy-start | bytes 4718596
  11.3 1.4 %copy-start.6 = (bf16[1,768,1024]{2,1,0:T(8,128)(2,1)S(1)}, bf16[1,768,1024]{2,1,0:T(8,128)(2,1)}, u32[]{:S(2)}) copy-start(bf16[1,768,1024]{2,1,0:T(8,128)(2,1)} %err_ref.1) | copy-start | bytes 4718596
  16.8 3.8 %collective-permute-start = (f32[64,768]{1,0:T(8,128)S(1)}, f32[64,768]{1,0:T(8,128)S(1)}, u32[]{:S(2)}, u32[]{:S(2)}) collective-permute-start(f32[64,768]{1,0:T(8,128)S(1)} %get-tuple-element.15), channel_id=1, source_target_pairs={{0,4},{4,0},{8,12},{12,8},{16,20},{20,16},{24,28},{28,24},{1,5},{5... | collective-permute-start | bytes 589832 | tf_op jit(solution)/shard_map/ppermute | solution.py:243
  17.8 25.6 %collective-permute-start.12 = (bf16[1,128,2048]{2,1,0:T(8,128)(2,1)}, bf16[1,128,2048]{2,1,0:T(8,128)(2,1)}, u32[]{:S(2)}, u32[]{:S(2)}) collective-permute-start(bf16[1,128,2048]{2,1,0:T(8,128)(2,1)} %collective-permute-done.11.refs_10_), channel_id=1, source_target_pairs={{1,0},{2,1},{5,4},{6,5},{9,8},{10,9},{13,12},{14,13},{17,16},{18,1... | collective-permute-start | bytes 1572872 | tf_op jit(solution)/shard_map/ppermute | solution.py:250
  19.1 25.6 %collective-permute-start.14 = (bf16[1,128,2048]{2,1,0:T(8,128)(2,1)}, bf16[1,128,2048]{2,1,0:T(8,128)(2,1)}, u32[]{:S(2)}, u32[]{:S(2)}) collective-permute-start(bf16[1,128,2048]{2,1,0:T(8,128)(2,1)} %collective-permute-done.10.refs_5_), channel_id=1, source_target_pairs={{1,2},{2,3},{5,6},{6,7},{9,10},{10,11},{13,14},{14,15},{17,18},{18... | collective-permute-start | bytes 1572872 | tf_op jit(solution)/shard_map/ppermute | solution.py:249
  20.6 5.8 %collective-permute-start.3 = (bf16[64,768]{1,0:T(8,128)(2,1)S(1)}, bf16[64,768]{1,0:T(8,128)(2,1)S(1)}, u32[]{:S(2)}, u32[]{:S(2)}) collective-permute-start(bf16[64,768]{1,0:T(8,128)(2,1)S(1)} %add_convert_fusion), channel_id=1, source_target_pairs={{0,24},{4,28},{8,16},{12,20},{16,8},{20,12},{24,0},{28,4},{1,25},{... | collective-permute-start | bytes 294920 | tf_op jit(solution)/shard_map/ppermute | solution.py:243
  23.3 5.0 %collective-permute-start.2 = (bf16[64,768]{1,0:T(8,128)(2,1)S(1)}, bf16[64,768]{1,0:T(8,128)(2,1)S(1)}, u32[]{:S(2)}, u32[]{:S(2)}) collective-permute-start(bf16[64,768]{1,0:T(8,128)(2,1)S(1)} %add_convert_fusion), channel_id=1, source_target_pairs={{0,16},{4,20},{8,24},{12,28},{16,0},{20,4},{24,8},{28,12},{1,17},{... | collective-permute-start | bytes 294920 | tf_op jit(solution)/shard_map/ppermute | solution.py:243
  23.8 4.7 %collective-permute-start.1 = (bf16[64,768]{1,0:T(8,128)(2,1)S(1)}, bf16[64,768]{1,0:T(8,128)(2,1)S(1)}, u32[]{:S(2)}, u32[]{:S(2)}) collective-permute-start(bf16[64,768]{1,0:T(8,128)(2,1)S(1)} %add_convert_fusion), channel_id=1, source_target_pairs={{0,8},{4,12},{8,0},{12,4},{16,24},{20,28},{24,16},{28,20},{1,9},{5... | collective-permute-start | bytes 294920 | tf_op jit(solution)/shard_map/ppermute | solution.py:243
  29.8 27.1 %all-to-all-start = ((bf16[32,16,128]{2,1,0:T(8,128)(2,1)}), bf16[32,16,128]{2,1,0:T(8,128)(2,1)S(1)}, u32[]{:S(2)}, u32[]{:S(2)}) async-start(bf16[32,16,128]{2,1,0:T(8,128)(2,1)} %get-tuple-element.18), calls=%async_computation | async-start | bytes 262144 | tf_op jit(solution)/shard_map/all_to_all | solution.py:291
  39.0 8.7 %collective-permute-start.6 = (f32[64,128]{1,0:T(8,128)S(1)}, f32[64,128]{1,0:T(8,128)S(1)}, u32[]{:S(2)}, u32[]{:S(2)}) collective-permute-start(f32[64,128]{1,0:T(8,128)S(1)} %get-tuple-element.17), channel_id=1, source_target_pairs={{0,3},{1,2},{2,1},{3,0},{4,7},{5,6},{6,5},{7,4},{8,11},{9,10},{10,... | collective-permute-start | bytes 98312 | tf_op jit(solution)/shard_map/ppermute | solution.py:243
  42.6 8.5 %collective-permute-start.5 = (f32[64,128]{1,0:T(8,128)S(1)}, f32[64,128]{1,0:T(8,128)S(1)}, u32[]{:S(2)}, u32[]{:S(2)}) collective-permute-start(f32[64,128]{1,0:T(8,128)S(1)} %get-tuple-element.17), channel_id=1, source_target_pairs={{0,2},{1,3},{2,0},{3,1},{4,6},{5,7},{6,4},{7,5},{8,10},{9,11},{10,... | collective-permute-start | bytes 98312 | tf_op jit(solution)/shard_map/ppermute | solution.py:243
  42.6 10.7 %collective-permute-start.4 = (f32[64,128]{1,0:T(8,128)S(1)}, f32[64,128]{1,0:T(8,128)S(1)}, u32[]{:S(2)}, u32[]{:S(2)}) collective-permute-start(f32[64,128]{1,0:T(8,128)S(1)} %get-tuple-element.17), channel_id=1, source_target_pairs={{0,1},{1,0},{2,3},{3,2},{4,5},{5,4},{6,7},{7,6},{8,9},{9,8},{10,11... | collective-permute-start | bytes 98312 | tf_op jit(solution)/shard_map/ppermute | solution.py:243
  43.4 28.4 %collective-permute-start.13 = (bf16[1,128,2048]{2,1,0:T(8,128)(2,1)}, bf16[1,128,2048]{2,1,0:T(8,128)(2,1)}, u32[]{:S(2)}, u32[]{:S(2)}) collective-permute-start(bf16[1,128,2048]{2,1,0:T(8,128)(2,1)} %collective-permute-done.12.refs_8_), channel_id=1, source_target_pairs={{1,0},{5,4},{9,8},{13,12},{17,16},{21,20},{25,24},{29,28}} | collective-permute-start | bytes 1572872 | tf_op jit(solution)/shard_map/ppermute | solution.py:250
  44.7 27.1 %collective-permute-start.15 = (bf16[1,128,2048]{2,1,0:T(8,128)(2,1)}, bf16[1,128,2048]{2,1,0:T(8,128)(2,1)}, u32[]{:S(2)}, u32[]{:S(2)}) collective-permute-start(bf16[1,128,2048]{2,1,0:T(8,128)(2,1)} %collective-permute-done.14.refs_7_), channel_id=1, source_target_pairs={{2,3},{6,7},{10,11},{14,15},{18,19},{22,23},{26,27},{30,31}} | collective-permute-start | bytes 1572872 | tf_op jit(solution)/shard_map/ppermute | solution.py:249
  47.7 24.1 %collective-permute-start.7 = (bf16[192,128]{1,0:T(8,128)(2,1)}, bf16[192,128]{1,0:T(8,128)(2,1)}, u32[]{:S(2)}, u32[]{:S(2)}) collective-permute-start(bf16[192,128]{1,0:T(8,128)(2,1)} %get-tuple-element.27), channel_id=1, source_target_pairs={{0,1},{1,2},{2,3},{3,0},{4,5},{5,6},{6,7},{7,4},{8,9},{9,10},{10,1... | collective-permute-start | bytes 147464 | tf_op jit(solution)/shard_map/ppermute | solution.py:265
  51.1 20.7 %collective-permute-start.8 = (bf16[192,128]{1,0:T(8,128)(2,1)}, bf16[192,128]{1,0:T(8,128)(2,1)}, u32[]{:S(2)}, u32[]{:S(2)}) collective-permute-start(bf16[192,128]{1,0:T(8,128)(2,1)} %get-tuple-element.26), channel_id=1, source_target_pairs={{0,2},{1,3},{2,0},{3,1},{4,6},{5,7},{6,4},{7,5},{8,10},{9,11},{10,... | collective-permute-start | bytes 147464 | tf_op jit(solution)/shard_map/ppermute | solution.py:265
  53.4 18.5 %collective-permute-start.9 = (bf16[192,128]{1,0:T(8,128)(2,1)}, bf16[192,128]{1,0:T(8,128)(2,1)}, u32[]{:S(2)}, u32[]{:S(2)}) collective-permute-start(bf16[192,128]{1,0:T(8,128)(2,1)} %get-tuple-element.25), channel_id=1, source_target_pairs={{0,3},{1,0},{2,1},{3,2},{4,7},{5,4},{6,5},{7,6},{8,11},{9,8},{10,9... | collective-permute-start | bytes 147464 | tf_op jit(solution)/shard_map/ppermute | solution.py:265
  57.6 11.2 %all-to-all-start.1 = ((bf16[32,16,128]{2,1,0:T(8,128)(2,1)}), bf16[32,16,128]{2,1,0:T(8,128)(2,1)S(1)}, u32[]{:S(2)}, u32[]{:S(2)}) async-start(bf16[32,16,128]{2,1,0:T(8,128)(2,1)} %broadcast_in_dim.10), calls=%async_computation.1 | async-start | bytes 262144 | tf_op jit(solution)/shard_map/all_to_all | solution.py:293
  68.8 3.1 %copy-start = (f32[1,192,2048]{2,1,0:T(8,128)S(1)}, f32[1,192,2048]{2,1,0:T(8,128)}, u32[]{:S(2)}) copy-start(f32[1,192,2048]{2,1,0:T(8,128)} %refs_11_.1) | copy-start | bytes 4718596
  68.8 3.1 %copy-start.1 = (f32[1,192,2048]{2,1,0:T(8,128)S(1)}, f32[1,192,2048]{2,1,0:T(8,128)}, u32[]{:S(2)}) copy-start(f32[1,192,2048]{2,1,0:T(8,128)} %refs_12_.1) | copy-start | bytes 4718596
  71.9 1.0 %copy-start.2 = (bf16[1,128,2048]{2,1,0:T(8,128)(2,1)S(1)}, bf16[1,128,2048]{2,1,0:T(8,128)(2,1)}, u32[]{:S(2)}) copy-start(bf16[1,128,2048]{2,1,0:T(8,128)(2,1)} %refs_4_.1) | copy-start | bytes 1572868
  (2 other events, 1.9 us)

commit v2 on v1

v2 whole, which is shorter than its diff:
```python
import functools

import jax
import jax.numpy as jnp
from jax import lax
from jax.experimental import pallas as pl
from jax.experimental.pallas import tpu as pltpu
from jax.sharding import PartitionSpec as P

HIGHEST = lax.Precision.HIGHEST
F32 = jnp.float32
BF16 = jnp.bfloat16
beta_one = 0.9
beta_two = 0.99
correction_one = 1.0 - 0.9**10
correction_two = 1.0 - 0.99**10
epsilon = 1e-08

ROWS_FIRST = (((0,), (0,)), ((), ()))
COLS_LAST = (((1,), (1,)), ((), ()))
TILE_R, TILE_C = 16, 128
VMEM_LIMIT = 40 * 1024 * 1024


def params():
    return pltpu.CompilerParams(vmem_limit_bytes=VMEM_LIMIT)


def cost(flops, nbytes):
    return pl.CostEstimate(flops=int(flops), bytes_accessed=int(nbytes), transcendentals=0)


def split_two(x):
    hi = x.astype(BF16)
    return hi, (x - hi.astype(F32)).astype(BF16)


def left_times(left, right_bf16, dims):
    rows = left.shape[0]
    hi, lo = split_two(left)
    both = jnp.concatenate([hi, lo], axis=0)
    out = lax.dot_general(both, right_bf16, dims, preferred_element_type=F32)
    return out[:rows] + out[rows:]


def merge_kernel(acts_ref, kv_ref, err_ref, vt_ref, merged_ref, lt_ref):
    merged = lax.dot_general(acts_ref[...], kv_ref[...], ROWS_FIRST, preferred_element_type=F32)
    merged = merged + err_ref[0].astype(F32)
    merged_ref[...] = merged
    lt_ref[...] = left_times(vt_ref[...], merged.astype(BF16), COLS_LAST)


def merge(acts, kv, err, vt):
    tokens, rows = acts.shape
    cols = kv.shape[1]
    rank = vt.shape[0]
    block = 256
    return pl.pallas_call(
        merge_kernel,
        grid=(rows // block,),
        in_specs=[
            pl.BlockSpec((tokens, block), lambda i: (0, i)),
            pl.BlockSpec((tokens, cols), lambda i: (0, 0)),
            pl.BlockSpec((1, block, cols), lambda i: (0, i, 0)),
            pl.BlockSpec((rank, cols), lambda i: (0, 0)),
        ],
        out_specs=[
            pl.BlockSpec((block, cols), lambda i: (i, 0)),
            pl.BlockSpec((rank, block), lambda i: (0, i)),
        ],
        out_shape=[
            jax.ShapeDtypeStruct((rows, cols), F32),
            jax.ShapeDtypeStruct((rank, rows), F32),
        ],
        compiler_params=params(),
        cost_estimate=cost(2 * tokens * rows * cols, 2 * tokens * (rows + cols) + 6 * rows * cols),
        name="merge",
    )(*[pltpu.with_memory_space_constraint(x, pltpu.HBM) for x in (acts, kv, err, vt)])


def slab_kernel(hidden_ref, slab_ref):
    slab_ref[...] = hidden_ref[0].T.reshape(slab_ref.shape)


def unit_slabs(hidden, parts):
    _, tokens, units = hidden.shape
    return pl.pallas_call(
        slab_kernel,
        out_shape=jax.ShapeDtypeStruct((parts, units // parts, tokens), BF16),
        compiler_params=params(),
        cost_estimate=cost(0, 4 * tokens * units),
        name="unit_slabs",
    )(hidden)


def right_kernel(n_parts, n_exp, *refs):
    part_refs, merged_ref, slab_ref = refs[:n_parts], refs[n_parts], refs[n_parts + 1]
    lt_ref, gram_ref, chunk_ref = refs[n_parts + 2 : n_parts + 5]
    load_refs = refs[n_parts + 5 :]
    parts = [ref[...].astype(F32) for ref in part_refs]
    while len(parts) > 1:
        parts = [a + b for a, b in zip(parts[0::2], parts[1::2])]
    lt = parts[0]
    rank = lt.shape[0]
    lt_ref[...] = lt
    product = left_times(lt, merged_ref[...].astype(BF16), (((1,), (0,)), ((), ()))).astype(BF16)
    across = product.shape[1] // TILE_C
    for a in range(rank // TILE_R):
        for b in range(across):
            chunk_ref[a * across + b] = product[
                a * TILE_R : (a + 1) * TILE_R, b * TILE_C : (b + 1) * TILE_C
            ]
    gram = lax.dot_general(lt, lt, COLS_LAST, precision=HIGHEST, preferred_element_type=F32)
    half = rank // 2
    packed = jnp.concatenate([gram[:half], gram[half:]], axis=1)
    high = packed.astype(BF16)
    rest = packed - high.astype(F32)
    middle = rest.astype(BF16)
    low = (rest - middle.astype(F32)).astype(BF16)
    gram_ref[...] = high.astype(F32) + middle.astype(F32) + low.astype(F32)
    place = lax.axis_index("exp")
    units = slab_ref.shape[1]
    for k in range(n_exp):
        load_ref = load_refs[k]
        load_ref[0:units] = slab_ref[lax.rem(place + k, n_exp)]
        if k:
            load_ref[units : units + half] = high
            load_ref[units + half : units + 2 * half] = middle
            load_ref[units + 2 * half : units + 3 * half] = low


def right_product(parts, merged, slabs):
    rank, rows = parts[0].shape
    cols = merged.shape[1]
    chunks = rank * cols // (TILE_R * TILE_C)
    n_exp, units, tokens = slabs.shape
    assert tokens == 2 * rank
    load = jax.ShapeDtypeStruct((units + 3 * (rank // 2), tokens), BF16)
    out = pl.pallas_call(
        functools.partial(right_kernel, len(parts), n_exp),
        out_shape=[
            jax.ShapeDtypeStruct((rank, rows), F32),
            jax.ShapeDtypeStruct((rank // 2, 2 * rank), F32),
            jax.ShapeDtypeStruct((chunks, TILE_R, TILE_C), BF16),
        ]
        + [jax.ShapeDtypeStruct((units, tokens), BF16)]
        + [load] * (n_exp - 1),
        compiler_params=params(),
        cost_estimate=cost(2 * rows * cols * 128, 4 * rows * cols),
        name="right_product",
    )(*parts, merged, slabs)
    return out[0], out[1], out[2], out[3:]


def inverse_kernel(n_exp, *refs):
    gram_ref, load_refs = refs[0], refs[1:n_exp]
    lt_ref, w_ref, basis_ref, parts_ref = refs[n_exp:]
    rank = lt_ref.shape[0]
    half = rank // 2
    parts_ref[0] = gram_ref[...]
    for k in range(1, n_exp):
        terms = load_refs[k - 1][load_refs[k - 1].shape[0] - 3 * half :].astype(F32)
        parts_ref[k] = terms[:half] + terms[half : 2 * half] + terms[2 * half :]
    place = lax.axis_index("exp")
    packed = None
    for j in range(n_exp):
        part = parts_ref[lax.rem(place + n_exp - j, n_exp)]
        packed = part if packed is None else packed + part
    gram = jnp.concatenate([packed[:, :rank], packed[:, rank:]], axis=0)
    row = lax.broadcasted_iota(jnp.int32, (rank, rank), 0)
    col = lax.broadcasted_iota(jnp.int32, (rank, rank), 1)
    a = jnp.concatenate([gram, jnp.where(row == col, 1.0, 0.0).astype(F32)], axis=1)
    row_ids = lax.broadcasted_iota(jnp.int32, (rank, 1), 0)
    for k in range(rank):
        pivot_row = a[k : k + 1, :]
        pivot = pivot_row[:, k : k + 1]
        w_ref[k : k + 1, :] = pivot_row[:, rank:] * lax.rsqrt(pivot)
        if k + 1 < rank:
            factor = jnp.where(row_ids > k, a[:, k : k + 1] / pivot, 0.0)
            a = a - factor * pivot_row
    basis = jnp.dot(w_ref[...], lt_ref[...], precision=HIGHEST, preferred_element_type=F32)
    basis_ref[...] = basis.T.astype(BF16)


def inverse_factor(gram, loads, lt):
    rank, rows = lt.shape
    n_exp = len(loads) + 1
    return pl.pallas_call(
        functools.partial(inverse_kernel, n_exp),
        out_shape=[
            jax.ShapeDtypeStruct((rank, rank), F32),
            jax.ShapeDtypeStruct((rows, rank), BF16),
        ],
        scratch_shapes=[pltpu.VMEM((n_exp, rank // 2, 2 * rank), F32)],
        compiler_params=params(),
        cost_estimate=cost(4e9, 1e5),
        name="inverse_factor",
    )(gram, *loads, lt)


def finish_kernel(replicas, w_ref, chunk_ref, basis_ref, merged_ref, right_hbm, err_hbm, right_ref, err_ref, sems):
    rank, cols = right_ref.shape
    across = cols // TILE_C
    pieces = []
    for a in range(rank // TILE_R):
        pieces.append(jnp.concatenate([chunk_ref[a * across + b] for b in range(across)], axis=1))
    product = jnp.concatenate(pieces, axis=0)
    new_right = left_times(w_ref[...], product, (((1,), (0,)), ((), ()))) * (1.0 / replicas)
    right_ref[...] = new_right
    copies = [pltpu.make_async_copy(right_ref, right_hbm, sems.at[0])]
    copies[0].start()
    rounded = new_right.astype(BF16)
    rows, block = err_ref.shape[0], 128
    for i in range(rows // block):
        here = slice(i * block, (i + 1) * block)
        approx = jnp.dot(basis_ref[here, :], rounded, preferred_element_type=F32)
        err_ref[here, :] = (merged_ref[here, :] - approx).astype(BF16)
        copies.append(
            pltpu.make_async_copy(err_ref.at[here, :], err_hbm.at[0, here, :], sems.at[i + 1])
        )
        copies[-1].start()
    for copy in copies:
        copy.wait()


def finish(replicas, w, chunks, basis, merged):
    rows, rank = basis.shape
    cols = merged.shape[1]
    return pl.pallas_call(
        functools.partial(finish_kernel, replicas),
        out_specs=[pl.BlockSpec(memory_space=pltpu.HBM)] * 2,
        out_shape=[
            jax.ShapeDtypeStruct((rank, cols), F32),
            jax.ShapeDtypeStruct((1, rows, cols), BF16),
        ],
        scratch_shapes=[
            pltpu.VMEM((rank, cols), F32),
            pltpu.VMEM((rows, cols), BF16),
            pltpu.SemaphoreType.DMA((rows // 128 + 1,)),
        ],
        compiler_params=params(),
        cost_estimate=cost(2 * rows * cols * 128, 6 * rows * cols),
        name="finish",
    )(w, chunks, basis, merged)


def expert_kernel(n_exp, *refs):
    hid_refs, grad_refs = refs[:n_exp], refs[n_exp : 2 * n_exp]
    one_ref, two_ref, first_ref, second_ref, step_ref = refs[2 * n_exp :]
    units = one_ref.shape[1]
    hid = jnp.concatenate([ref[0:units, :] for ref in hid_refs], axis=1)
    rows = jnp.concatenate([ref[0] for ref in grad_refs], axis=0)
    grad = jnp.dot(hid, rows, preferred_element_type=F32)
    first_new = beta_one * one_ref[0] + (1.0 - beta_one) * grad
    second_new = beta_two * two_ref[0] + (1.0 - beta_two) * grad * grad
    first_ref[0] = first_new
    second_ref[0] = second_new
    scaled = second_new * (1.0 / correction_two)
    bottom = scaled * lax.rsqrt(scaled) + epsilon
    step = first_new * (1.0 / correction_one) * pl.reciprocal(bottom, approx=True)
    step_ref[0] = step.astype(BF16)


def expert_step(hids, grads, moment_one, moment_two):
    _, units, width = moment_one.shape
    block = 512
    n_exp = len(hids)
    tokens = grads[0].shape[1]
    wide = pl.BlockSpec((1, units, block), lambda i: (0, 0, i))
    return pl.pallas_call(
        functools.partial(expert_kernel, n_exp),
        grid=(width // block,),
        in_specs=[pl.BlockSpec(h.shape, lambda i: (0, 0)) for h in hids]
        + [pl.BlockSpec((1, tokens, block), lambda i: (0, 0, i))] * n_exp
        + [wide, wide],
        out_specs=[wide, wide, wide],
        out_shape=[
            jax.ShapeDtypeStruct((1, units, width), F32),
            jax.ShapeDtypeStruct((1, units, width), F32),
            jax.ShapeDtypeStruct((1, units, width), BF16),
        ],
        compiler_params=params(),
        cost_estimate=cost(2 * units * width * tokens * n_exp, 20 * units * width),
        name="expert_step",
    )(*hids, pltpu.with_memory_space_constraint(grads[0], pltpu.HBM), *grads[1:], moment_one, moment_two)


def swap(x, axis, size, mask):
    return lax.ppermute(x, axis, [(i, i ^ mask) for i in range(size)])


def shift(x, size, k):
    return lax.ppermute(x, "exp", [(i, (i + k) % size) for i in range(size)])


def after(x, y):
    return lax.optimization_barrier((x, y))[0]


def body(n_rep, n_exp, activations, kv_grad, errors, right_factor, hidden, out_grad, moment_one, moment_two):
    grads = {0: out_grad}
    if n_exp > 1:
        grads[1] = shift(out_grad, n_exp, 1)
    merged, lt = merge(activations, kv_grad, errors, right_factor.T)
    if n_exp > 2:
        grads[n_exp - 1] = shift(after(out_grad, lt), n_exp, -1)

    lt = (lt + swap(lt, "rep", n_rep, 1)).astype(BF16)
    slabs = unit_slabs(after(hidden, lt), n_exp)
    bit = 2
    parts = [lt]
    while bit < n_rep:
        while len(parts) > 1:
            parts = [a.astype(F32) + b.astype(F32) for a, b in zip(parts[0::2], parts[1::2])]
        own = parts[0].astype(BF16)
        masks = [bit] if 2 * bit >= n_rep else [bit, 2 * bit, 3 * bit]
        parts = [own] + [swap(own, "rep", n_rep, m) for m in masks]
        bit *= len(parts)
    lt, gram, chunks, loads = right_product(parts, merged, slabs)

    left, right = 1, n_exp - 1
    while right - left > 1:
        if left <= n_exp - right:
            grads[left + 1] = shift(after(grads[left], chunks), n_exp, 1)
            left += 1
        else:
            grads[right - 1] = shift(after(grads[right], chunks), n_exp, -1)
            right -= 1

    loads = [loads[0]] + [shift(loads[k], n_exp, k) for k in range(1, n_exp)]
    w, basis = inverse_factor(gram, loads[1:], lt)

    n_chunks = chunks.shape[0]
    if n_chunks == n_rep * n_exp:
        both = ("rep", "exp")
        shares = lax.all_to_all(chunks, both, 0, 0, tiled=True)
        share = jnp.sum(shares.astype(F32), axis=0).astype(BF16)
        chunks = lax.all_to_all(jnp.broadcast_to(share[None], chunks.shape), both, 0, 0, tiled=True)
    else:
        chunks = lax.psum(chunks.astype(F32), ("rep", "exp")).astype(BF16)

    new_right, new_error = finish(n_rep, w, chunks, basis, merged)
    first_new, second_new, step = expert_step(
        loads, [grads[k] for k in range(n_exp)], moment_one, moment_two
    )
    return new_error, new_right.T, first_new, second_new, step


def solution(mesh):
    placed = (
        P("rep", "exp"),
        P("rep", None),
        P("rep", "exp", None),
        P(),
        P("rep", "exp", None),
        P("rep", "exp", None),
        P("rep", "exp", None),
        P("rep", "exp", None),
    )
    return jax.shard_map(
        functools.partial(body, mesh.shape["rep"], mesh.shape["exp"]),
        mesh=mesh,
        in_specs=placed,
        out_specs=(
            P("rep", "exp", None),
            P(),
            P("rep", "exp", None),
            P("rep", "exp", None),
            P("rep", "exp", None),
        ),
        check_vma=False,
    )
```

time: 79.2 us -> 79.8 us (level)
  waiting for transfers between devices: 7.3 us -> 26.5 us
  starting transfers between devices: 40 us -> 23.3 us
  local copies, waits for them, and re-layouts: 11.2 us -> 9.55 us
    ppermute x9 -> x6, waiting for transfers between devices: 0.99 us -> 21.6 us  [shift(): return lax.ppermute(x, 'exp', [(i, (i + k) % size) for i in range(size)])]
    ppermute x9 -> x6, starting transfers between devices: 21.7 us -> 10.7 us  [shift(): return lax.ppermute(x, 'exp', [(i, (i + k) % size) for i in range(size)])]
    ppermute x7 -> x4, starting transfers between devices: 8.01 us -> 4.07 us  [swap(): return lax.ppermute(x, axis, [(i, i ^ mask) for i in range(size)])]
    all_to_all x1, starting transfers between devices: 7.47 us -> 4.87 us  [body(): shares = lax.all_to_all(chunks, both, 0, 0, tiled=True)]
    pallas_call x1, Pallas kernels: 3.06 us -> 5.24 us  [merge(): pl.pallas_call(merge_kernel, grid=(rows // block,), in_specs=[pl.BlockSpe...]
    all_to_all x1, waiting for transfers between devices: 1.96 us -> 0.01 us  [body(): lax.all_to_all(jnp.broadcast_to(share[None], chunks.shape), both, 0, 0, t...]
    pallas_call x4 -> x5, Pallas kernels: 15.4 us -> 13.8 us  [the longest x1 5.81 us: inverse_factor(): pl.pallas_call(functools.partial(inverse_kernel, n_exp), out_shape=[jax.S...]
    squeeze x1 -> x0, local copies, waits for them, and re-layouts: 1.52 us -> none  [body(): lax.dynamic_index_in_dim(slabs, lax.rem(place + k, n_exp), 0, keepdims=Fa...]
  transfers between devices with their start and end apart: 18 -> 12, of which waited for: 5 -> 6; matrix products, arithmetic and copies ran while one was open for 6% -> 1% of each run, Pallas kernels for 16% -> 11%
where the time goes in v2:
time: 79.8 us; the launch traced here: 79.2 us
  waiting for transfers between devices  26.5 us (33%)
  starting transfers between devices  23.3 us (29%)
  Pallas kernels  19.1 us (24%)
  local copies, waits for them, and re-layouts  9.55 us (12%)
    ppermute x6, waiting for transfers between devices, shift(): return lax.ppermute(x, 'exp', [(i, (i + k) % size) for i in range(size)])  21.6 us
    ppermute x6, starting transfers between devices, shift(): return lax.ppermute(x, 'exp', [(i, (i + k) % size) for i in range(size)])  10.7 us
    unnamed x34, local copies, waits for them, and re-layouts  8.88 us
    pallas_call x1, Pallas kernels, inverse_factor(): pl.pallas_call(functools.partial(inverse_kernel, n_exp), out_shape=[jax.S...  5.81 us
    pallas_call x1, Pallas kernels, merge(): pl.pallas_call(merge_kernel, grid=(rows // block,), in_specs=[pl.BlockSpe...  5.24 us
    pallas_call x1, Pallas kernels, expert_step(): pl.pallas_call(functools.partial(expert_kernel, n_exp), grid=(width // bl...  5.03 us
    all_to_all x1, starting transfers between devices, body(): shares = lax.all_to_all(chunks, both, 0, 0, tiled=True)  4.87 us
    ppermute x4, waiting for transfers between devices, swap(): return lax.ppermute(x, axis, [(i, i ^ mask) for i in range(size)])  4.33 us
  transfers between devices with their start and end apart: 12, of which 6 were waited for; matrix products, arithmetic and copies ran while one was open for 1% of the time, Pallas kernels for 11%

profile of v2, /device:TPU:0, one launch (start us, length us, event | category | flops | bytes accessed | tf_op | source)
XLA Modules:
  0.0 79.2 jit_solution(354802237668748633)
XLA Ops:
  0.6 5.2 %merge.1 = (f32[768,1024]{1,0:T(8,128)S(1)}, f32[64,768]{1,0:T(8,128)S(1)}) custom-call(bf16[1024,768]{1,0:T(8,128)(2,1)} %acts_ref.1, bf16[1024,1024]{1,0:T(8,128)(2,1)} %kv_ref.1, bf16[1,768,1024]{2,1,0:T(8,128)(2,1)} %err_ref.1, f32[64,1024]{1,0:T(8,128)} %bitcast.2), custom_call_target="tpu_custom_call" | custom-call | flops 1610612736 | bytes 8388608 | tf_op jit(solution)/shard_map/merge/pallas_call | solution.py:58
  6.4 2.6 %collective-permute-start.7 = (bf16[1,128,2048]{2,1,0:T(8,128)(2,1)}, bf16[1,128,2048]{2,1,0:T(8,128)(2,1)}, u32[]{:S(2)}, u32[]{:S(2)}) collective-permute-start(bf16[1,128,2048]{2,1,0:T(8,128)(2,1)} %refs_4_.1), channel_id=1, source_target_pairs={{0,1},{1,2},{2,3},{3,0},{4,5},{5,6},{6,7},{7,4},{8,9},{9,10},{10,1... | collective-permute-start | bytes 1572872 | tf_op jit(solution)/shard_map/ppermute | solution.py:293
  9.1 2.5 %collective-permute-start.3 = (bf16[64,768]{1,0:T(8,128)(2,1)S(1)}, bf16[64,768]{1,0:T(8,128)(2,1)S(1)}, u32[]{:S(2)}, u32[]{:S(2)}) collective-permute-start(bf16[64,768]{1,0:T(8,128)(2,1)S(1)} %add_convert_fusion.refs_0_), channel_id=1, source_target_pairs={{0,24},{4,28},{8,16},{12,20},{16,8},{20,12},{24,0},{28,4},{1,25},{... | collective-permute-start | bytes 294920 | tf_op jit(solution)/shard_map/ppermute | solution.py:289
  12.7 2.3 %collective-permute-done.3.refs_3_ = bf16[64,768]{1,0:T(8,128)(2,1)S(1)} collective-permute-done((bf16[64,768]{1,0:T(8,128)(2,1)S(1)}, bf16[64,768]{1,0:T(8,128)(2,1)S(1)}, u32[]{:S(2)}, u32[]{:S(2)}) %collective-permute-start.3) | collective-permute-done | bytes 98336 | tf_op jit(solution)/shard_map/ppermute | solution.py:289
  15.0 2.0 %collective-permute-done.2.refs_2_ = bf16[64,768]{1,0:T(8,128)(2,1)S(1)} collective-permute-done((bf16[64,768]{1,0:T(8,128)(2,1)S(1)}, bf16[64,768]{1,0:T(8,128)(2,1)S(1)}, u32[]{:S(2)}, u32[]{:S(2)}) %collective-permute-start.2) | collective-permute-done | bytes 98336 | tf_op jit(solution)/shard_map/ppermute | solution.py:289
  17.1 1.3 %right_product.1 = (f32[64,768]{1,0:T(8,128)S(1)}, f32[32,128]{1,0:T(8,128)S(1)}, bf16[32,16,128]{2,1,0:T(8,128)(2,1)}, bf16[192,128]{1,0:T(8,128)(2,1)S(1)}, bf...) custom-call(bf16[64,768]{1,0:T(8,128)(2,1)S(1)} %add_convert_fusion.refs_0_, ...), custom_call_target="tpu_custom_call" | custom-call | flops 201326592 | bytes 3145728 | tf_op jit(solution)/shard_map/right_product/pallas_call | solution.py:139
  19.0 0.7 copy-done.13
  20.3 4.9 %all-to-all-start = ((bf16[32,16,128]{2,1,0:T(8,128)(2,1)}), bf16[32,16,128]{2,1,0:T(8,128)(2,1)S(1)}, u32[]{:S(2)}, u32[]{:S(2)}) async-start(bf16[32,16,128]{2,1,0:T(8,128)(2,1)} %get-tuple-element.33), calls=%async_computation | async-start | bytes 262144 | tf_op jit(solution)/shard_map/all_to_all | solution.py:336
  25.2 3.7 %collective-permute-start.9 = (bf16[1,128,2048]{2,1,0:T(8,128)(2,1)}, bf16[1,128,2048]{2,1,0:T(8,128)(2,1)}, u32[]{:S(2)}, u32[]{:S(2)}) collective-permute-start(bf16[1,128,2048]{2,1,0:T(8,128)(2,1)} %refs_4_.1), channel_id=1, source_target_pairs={{0,3},{1,0},{2,1},{3,2},{4,7},{5,4},{6,5},{7,6},{8,11},{9,8},{10,9... | collective-permute-start | bytes 1572872 | tf_op jit(solution)/shard_map/ppermute | solution.py:293
  29.0 4.2 %collective-permute-start.5 = (bf16[288,128]{1,0:T(8,128)(2,1)}, bf16[288,128]{1,0:T(8,128)(2,1)S(1)}, u32[]{:S(2)}, u32[]{:S(2)}) collective-permute-start(bf16[288,128]{1,0:T(8,128)(2,1)} %get-tuple-element.29), channel_id=1, source_target_pairs={{0,2},{1,3},{2,0},{3,1},{4,6},{5,7},{6,4},{7,5},{8,10},{9,11},{10,... | collective-permute-start | bytes 221192 | tf_op jit(solution)/shard_map/ppermute | solution.py:293
  33.8 0.7 broadcast_in_dim.2
  34.5 3.7 %all-to-all-start.1 = ((bf16[32,16,128]{2,1,0:T(8,128)(2,1)}), bf16[32,16,128]{2,1,0:T(8,128)(2,1)S(1)}, u32[]{:S(2)}, u32[]{:S(2)}) async-start(bf16[32,16,128]{2,1,0:T(8,128)(2,1)} %broadcast_in_dim.2), calls=%async_computation.1 | async-start | bytes 262144 | tf_op jit(solution)/shard_map/all_to_all | solution.py:338
  38.2 18.4 %collective-permute-done.4.refs_1_ = bf16[288,128]{1,0:T(8,128)(2,1)S(1)} collective-permute-done((bf16[288,128]{1,0:T(8,128)(2,1)}, bf16[288,128]{1,0:T(8,128)(2,1)S(1)}, u32[]{:S(2)}, u32[]{:S(2)}) %collective-permute-start.4) | collective-permute-done | bytes 73760 | tf_op jit(solution)/shard_map/ppermute | solution.py:293
  56.6 3.2 %collective-permute-done.5.refs_2_ = bf16[288,128]{1,0:T(8,128)(2,1)S(1)} collective-permute-done((bf16[288,128]{1,0:T(8,128)(2,1)}, bf16[288,128]{1,0:T(8,128)(2,1)S(1)}, u32[]{:S(2)}, u32[]{:S(2)}) %collective-permute-start.5) | collective-permute-done | bytes 73760 | tf_op jit(solution)/shard_map/ppermute | solution.py:293
  60.4 0.6 copy-done.6
  61.0 0.9 %copy-done.4 = bf16[288,128]{1,0:T(8,128)(2,1)S(1)} copy-done((bf16[288,128]{1,0:T(8,128)(2,1)S(1)}, bf16[288,128]{1,0:T(8,128)(2,1)}, u32[]{:S(2)}) %copy-start.4) | copy-done | bytes 73752
  61.9 0.9 %copy-done.7 = bf16[288,128]{1,0:T(8,128)(2,1)S(1)} copy-done((bf16[288,128]{1,0:T(8,128)(2,1)S(1)}, bf16[288,128]{1,0:T(8,128)(2,1)}, u32[]{:S(2)}) %copy-start.7) | copy-done | bytes 73752
  62.8 0.9 %copy-done.14 = f32[64,768]{1,0:T(8,128)S(1)} copy-done((f32[64,768]{1,0:T(8,128)S(1)}, f32[64,768]{1,0:T(8,128)}, u32[]{:S(2)}) %copy-start.14) | copy-done | bytes 196632
  63.7 0.7 copy-done.16
  64.5 5.8 %inverse_factor.1 = (f32[64,64]{1,0:T(8,128)S(1)}, bf16[768,64]{1,0:T(8,128)(2,1)S(1)}) custom-call(f32[32,128]{1,0:T(8,128)S(1)} %copy-done.16, bf16[288,128]{1,0:T(8,128)(2,1)S(1)} %collective-permute-done.4.refs_1_, bf16[288,128]{1,0:T(8,128)(2,1)S(1)} %copy-done.4, bf16[288,128]{1,0:T(8,128)(2,1)S(1)} %copy-done.7, f32[64,768]{1,0:T(8,128)S(1)} %copy-done.14), custom_call_target="tpu_custom_call" | custom-call | flops 4000000000 | bytes 100000 | tf_op jit(solution)/shard_map/inverse_factor/pallas_call | solution.py:188
  70.9 0.8 copy-done.12
  71.7 1.6 %finish.1 = (f32[64,1024]{1,0:T(8,128)}, bf16[1,768,1024]{2,1,0:T(8,128)(2,1)}) custom-call(f32[64,64]{1,0:T(8,128)S(1)} %copy-done.12, bf16[32,16,128]{2,1,0:T(8,128)(2,1)S(1)} %all-to-all-done.1.chunk_ref, bf16[768,64]{1,0:T(8,128)(2,1)S(1)} %get-tuple-element.34.basis_ref, f32[768,1024]{1,0:T(8,128)S(1)} %get-tuple-element.25.refs_4_.merged_ref), custom_call_target="tpu_custom_call" | custom-call | flops 201326592 | bytes 4718592 | tf_op jit(solution)/shard_map/finish/pallas_call | solution.py:229
  73.5 0.7 copy-done.1
  74.2 5.0 %expert_step.1 = (f32[1,192,2048]{2,1,0:T(8,128)}, f32[1,192,2048]{2,1,0:T(8,128)}, bf16[1,192,2048]{2,1,0:T(8,128)(2,1)}) custom-call(bf16[192,128]{1,0:T(8,128)(2,1)S(1)} %copy-done.10, bf16[288,128]{1,0:T(8,128)(2,1)S(1)} %collective-permute-done.4.refs_1_, bf16[288,128]{1,0:T(8,128)(2,1)S(1)} %copy-done.5, bf16[288,128]{1,0:T(8,128)(2,1)S(1)} %copy-done.8, ...), custom_call_target="tpu_custom_call" | custom-call | flops 402653184 | bytes 7864320 | tf_op jit(solution)/shard_map/expert_step/pallas_call | solution.py:270
  (43 shorter events, 5.3 us)
Async XLA Ops:
  0.6 12.0 %copy-start.2 = (bf16[1,128,768]{2,1,0:T(8,128)(2,1)S(1)}, bf16[1,128,768]{2,1,0:T(8,128)(2,1)}, u32[]{:S(2)}) copy-start(bf16[1,128,768]{2,1,0:T(8,128)(2,1)} %hidden_ref) | copy-start | bytes 589828
  5.9 3.2 %collective-permute-start = (f32[64,768]{1,0:T(8,128)S(1)}, f32[64,768]{1,0:T(8,128)S(1)}, u32[]{:S(2)}, u32[]{:S(2)}) collective-permute-start(f32[64,768]{1,0:T(8,128)S(1)} %get-tuple-element.24), channel_id=1, source_target_pairs={{0,4},{4,0},{8,12},{12,8},{16,20},{20,16},{24,28},{28,24},{1,5},{5... | collective-permute-start | bytes 589832 | tf_op jit(solution)/shard_map/ppermute | solution.py:289
  6.4 22.4 %collective-permute-start.7 = (bf16[1,128,2048]{2,1,0:T(8,128)(2,1)}, bf16[1,128,2048]{2,1,0:T(8,128)(2,1)}, u32[]{:S(2)}, u32[]{:S(2)}) collective-permute-start(bf16[1,128,2048]{2,1,0:T(8,128)(2,1)} %refs_4_.1), channel_id=1, source_target_pairs={{0,1},{1,2},{2,3},{3,0},{4,5},{5,6},{6,7},{7,4},{8,9},{9,10},{10,1... | collective-permute-start | bytes 1572872 | tf_op jit(solution)/shard_map/ppermute | solution.py:293
  9.1 5.9 %collective-permute-start.3 = (bf16[64,768]{1,0:T(8,128)(2,1)S(1)}, bf16[64,768]{1,0:T(8,128)(2,1)S(1)}, u32[]{:S(2)}, u32[]{:S(2)}) collective-permute-start(bf16[64,768]{1,0:T(8,128)(2,1)S(1)} %add_convert_fusion.refs_0_), channel_id=1, source_target_pairs={{0,24},{4,28},{8,16},{12,20},{16,8},{20,12},{24,0},{28,4},{1,25},{... | collective-permute-start | bytes 294920 | tf_op jit(solution)/shard_map/ppermute | solution.py:289
  11.6 5.4 %collective-permute-start.2 = (bf16[64,768]{1,0:T(8,128)(2,1)S(1)}, bf16[64,768]{1,0:T(8,128)(2,1)S(1)}, u32[]{:S(2)}, u32[]{:S(2)}) collective-permute-start(bf16[64,768]{1,0:T(8,128)(2,1)S(1)} %add_convert_fusion.refs_0_), channel_id=1, source_target_pairs={{0,16},{4,20},{8,24},{12,28},{16,0},{20,4},{24,8},{28,12},{1,17},{... | collective-permute-start | bytes 294920 | tf_op jit(solution)/shard_map/ppermute | solution.py:289
  12.1 5.0 %collective-permute-start.1 = (bf16[64,768]{1,0:T(8,128)(2,1)S(1)}, bf16[64,768]{1,0:T(8,128)(2,1)S(1)}, u32[]{:S(2)}, u32[]{:S(2)}) collective-permute-start(bf16[64,768]{1,0:T(8,128)(2,1)S(1)} %add_convert_fusion.refs_0_), channel_id=1, source_target_pairs={{0,8},{4,12},{8,0},{12,4},{16,24},{20,28},{24,16},{28,20},{1,9},{5... | collective-permute-start | bytes 294920 | tf_op jit(solution)/shard_map/ppermute | solution.py:289
  19.0 0.7 copy-start.13
  20.3 13.5 %all-to-all-start = ((bf16[32,16,128]{2,1,0:T(8,128)(2,1)}), bf16[32,16,128]{2,1,0:T(8,128)(2,1)S(1)}, u32[]{:S(2)}, u32[]{:S(2)}) async-start(bf16[32,16,128]{2,1,0:T(8,128)(2,1)} %get-tuple-element.33), calls=%async_computation | async-start | bytes 262144 | tf_op jit(solution)/shard_map/all_to_all | solution.py:336
  25.2 48.1 %collective-permute-start.9 = (bf16[1,128,2048]{2,1,0:T(8,128)(2,1)}, bf16[1,128,2048]{2,1,0:T(8,128)(2,1)}, u32[]{:S(2)}, u32[]{:S(2)}) collective-permute-start(bf16[1,128,2048]{2,1,0:T(8,128)(2,1)} %refs_4_.1), channel_id=1, source_target_pairs={{0,3},{1,0},{2,1},{3,2},{4,7},{5,4},{6,5},{7,6},{8,11},{9,8},{10,9... | collective-permute-start | bytes 1572872 | tf_op jit(solution)/shard_map/ppermute | solution.py:293
  28.8 44.4 %collective-permute-start.8 = (bf16[1,128,2048]{2,1,0:T(8,128)(2,1)}, bf16[1,128,2048]{2,1,0:T(8,128)(2,1)}, u32[]{:S(2)}, u32[]{:S(2)}) collective-permute-start(bf16[1,128,2048]{2,1,0:T(8,128)(2,1)} %collective-permute-done.7.refs_5_), channel_id=1, source_target_pairs={{0,1},{1,2},{2,3},{3,0},{4,5},{5,6},{6,7},{7,4},{8,9},{9,10},{10,1... | collective-permute-start | bytes 1572872 | tf_op jit(solution)/shard_map/ppermute | solution.py:293
  28.8 27.8 %collective-permute-start.4 = (bf16[288,128]{1,0:T(8,128)(2,1)}, bf16[288,128]{1,0:T(8,128)(2,1)S(1)}, u32[]{:S(2)}, u32[]{:S(2)}) collective-permute-start(bf16[288,128]{1,0:T(8,128)(2,1)} %get-tuple-element.28), channel_id=1, source_target_pairs={{0,1},{1,2},{2,3},{3,0},{4,5},{5,6},{6,7},{7,4},{8,9},{9,10},{10,1... | collective-permute-start | bytes 221192 | tf_op jit(solution)/shard_map/ppermute | solution.py:293
  29.0 30.8 %collective-permute-start.5 = (bf16[288,128]{1,0:T(8,128)(2,1)}, bf16[288,128]{1,0:T(8,128)(2,1)S(1)}, u32[]{:S(2)}, u32[]{:S(2)}) collective-permute-start(bf16[288,128]{1,0:T(8,128)(2,1)} %get-tuple-element.29), channel_id=1, source_target_pairs={{0,2},{1,3},{2,0},{3,1},{4,6},{5,7},{6,4},{7,5},{8,10},{9,11},{10,... | collective-permute-start | bytes 221192 | tf_op jit(solution)/shard_map/ppermute | solution.py:293
  33.2 27.2 %collective-permute-start.6 = (bf16[288,128]{1,0:T(8,128)(2,1)}, bf16[288,128]{1,0:T(8,128)(2,1)S(1)}, u32[]{:S(2)}, u32[]{:S(2)}) collective-permute-start(bf16[288,128]{1,0:T(8,128)(2,1)} %get-tuple-element.30), channel_id=1, source_target_pairs={{0,3},{1,0},{2,1},{3,2},{4,7},{5,4},{6,5},{7,6},{8,11},{9,8},{10,9... | collective-permute-start | bytes 221192 | tf_op jit(solution)/shard_map/ppermute | solution.py:293
  34.5 36.4 %all-to-all-start.1 = ((bf16[32,16,128]{2,1,0:T(8,128)(2,1)}), bf16[32,16,128]{2,1,0:T(8,128)(2,1)S(1)}, u32[]{:S(2)}, u32[]{:S(2)}) async-start(bf16[32,16,128]{2,1,0:T(8,128)(2,1)} %broadcast_in_dim.2), calls=%async_computation.1 | async-start | bytes 262144 | tf_op jit(solution)/shard_map/all_to_all | solution.py:338
  61.0 0.9 %copy-start.4 = (bf16[288,128]{1,0:T(8,128)(2,1)S(1)}, bf16[288,128]{1,0:T(8,128)(2,1)}, u32[]{:S(2)}) copy-start(bf16[288,128]{1,0:T(8,128)(2,1)} %copy-done.3) | copy-start | bytes 221188
  61.9 0.9 %copy-start.7 = (bf16[288,128]{1,0:T(8,128)(2,1)S(1)}, bf16[288,128]{1,0:T(8,128)(2,1)}, u32[]{:S(2)}) copy-start(bf16[288,128]{1,0:T(8,128)(2,1)} %copy-done.6) | copy-start | bytes 221188
  62.8 0.9 %copy-start.14 = (f32[64,768]{1,0:T(8,128)S(1)}, f32[64,768]{1,0:T(8,128)}, u32[]{:S(2)}) copy-start(f32[64,768]{1,0:T(8,128)} %copy-done.13) | copy-start | bytes 589828
  63.7 0.7 copy-start.16
  70.9 0.8 copy-start.12
  71.7 1.9 %copy-start = (f32[1,192,2048]{2,1,0:T(8,128)S(1)}, f32[1,192,2048]{2,1,0:T(8,128)}, u32[]{:S(2)}) copy-start(f32[1,192,2048]{2,1,0:T(8,128)} %refs_8_.1) | copy-start | bytes 4718596
  71.7 2.5 %copy-start.1 = (f32[1,192,2048]{2,1,0:T(8,128)S(1)}, f32[1,192,2048]{2,1,0:T(8,128)}, u32[]{:S(2)}) copy-start(f32[1,192,2048]{2,1,0:T(8,128)} %refs_9_.1) | copy-start | bytes 4718596
  71.7 2.5 %copy-start.5 = (bf16[288,128]{1,0:T(8,128)(2,1)S(1)}, bf16[288,128]{1,0:T(8,128)(2,1)}, u32[]{:S(2)}) copy-start(bf16[288,128]{1,0:T(8,128)(2,1)} %copy-done.3) | copy-start | bytes 221188
  71.7 2.5 %copy-start.8 = (bf16[288,128]{1,0:T(8,128)(2,1)S(1)}, bf16[288,128]{1,0:T(8,128)(2,1)}, u32[]{:S(2)}) copy-start(bf16[288,128]{1,0:T(8,128)(2,1)} %copy-done.6) | copy-start | bytes 221188
  71.7 2.5 %copy-start.10 = (bf16[192,128]{1,0:T(8,128)(2,1)S(1)}, bf16[192,128]{1,0:T(8,128)(2,1)}, u32[]{:S(2)}) copy-start(bf16[192,128]{1,0:T(8,128)(2,1)} %copy-done.9) | copy-start | bytes 147460
  (5 other events, 3.1 us)

commit v3 on v2

v3 whole, which is shorter than its diff:
```python
import functools

import jax
import jax.numpy as jnp
from jax import lax
from jax.experimental import pallas as pl
from jax.experimental.pallas import tpu as pltpu
from jax.sharding import PartitionSpec as P

HIGHEST = lax.Precision.HIGHEST
F32 = jnp.float32
BF16 = jnp.bfloat16
beta_one = 0.9
beta_two = 0.99
correction_one = 1.0 - 0.9**10
correction_two = 1.0 - 0.99**10
epsilon = 1e-08

ROWS_FIRST = (((0,), (0,)), ((), ()))
COLS_LAST = (((1,), (1,)), ((), ()))
TILE_R, TILE_C = 16, 128
HBM = pl.BlockSpec(memory_space=pltpu.HBM)
VMEM = pl.BlockSpec(memory_space=pltpu.VMEM)


def params(mebibytes):
    return pltpu.CompilerParams(vmem_limit_bytes=mebibytes * 1024 * 1024)


def in_hbm(*arrays):
    return [pltpu.with_memory_space_constraint(x, pltpu.HBM) for x in arrays]


def cost(flops, nbytes):
    return pl.CostEstimate(flops=int(flops), bytes_accessed=int(nbytes), transcendentals=0)


def split_two(x):
    hi = x.astype(BF16)
    return hi, (x - hi.astype(F32)).astype(BF16)


def left_times(left, right_bf16, dims):
    rows = left.shape[0]
    hi, lo = split_two(left)
    both = jnp.concatenate([hi, lo], axis=0)
    out = lax.dot_general(both, right_bf16, dims, preferred_element_type=F32)
    return out[:rows] + out[rows:]


def merge_kernel(block, acts_hbm, kv_hbm, err_hbm, vt_hbm, merged_ref, lt_ref, acts, kv, err, vt, sems):
    tokens, rows = acts.shape
    half = tokens // 2
    count = rows // block

    def acts_copy(i):
        here = slice(i * block, (i + 1) * block)
        return pltpu.make_async_copy(acts_hbm.at[:, here], acts.at[:, here], sems.at[3 + i])

    def err_copy(i):
        here = slice(i * block, (i + 1) * block)
        return pltpu.make_async_copy(err_hbm.at[0, here, :], err.at[here, :], sems.at[3 + count + i])

    def kv_copy(i):
        here = slice(i * half, (i + 1) * half)
        return pltpu.make_async_copy(kv_hbm.at[here, :], kv.at[here, :], sems.at[i])

    vt_copy = pltpu.make_async_copy(vt_hbm, vt, sems.at[2])
    acts_copy(0).start()
    kv_copy(0).start()
    kv_copy(1).start()
    err_copy(0).start()
    vt_copy.start()
    for i in range(count):
        here = slice(i * block, (i + 1) * block)
        acts_copy(i).wait()
        if i == 0:
            kv_copy(0).wait()
            for later in range(1, count):
                acts_copy(later).start()
                err_copy(later).start()
            merged = lax.dot_general(
                acts[:half, here], kv[:half, :], ROWS_FIRST, preferred_element_type=F32
            )
            kv_copy(1).wait()
            merged = merged + lax.dot_general(
                acts[half:, here], kv[half:, :], ROWS_FIRST, preferred_element_type=F32
            )
        else:
            merged = lax.dot_general(acts[:, here], kv[...], ROWS_FIRST, preferred_element_type=F32)
        err_copy(i).wait()
        merged = merged + err[here, :].astype(F32)
        merged_ref[here, :] = merged
        if i == 0:
            vt_copy.wait()
        lt_ref[:, here] = left_times(vt[...], merged.astype(BF16), COLS_LAST)


def merge(acts, kv, err, vt):
    tokens, rows = acts.shape
    cols = kv.shape[1]
    rank = vt.shape[0]
    block = 256
    return pl.pallas_call(
        functools.partial(merge_kernel, block),
        in_specs=[HBM] * 4,
        out_specs=[VMEM] * 2,
        out_shape=[
            jax.ShapeDtypeStruct((rows, cols), F32),
            jax.ShapeDtypeStruct((rank, rows), F32),
        ],
        scratch_shapes=[
            pltpu.VMEM((tokens, rows), BF16),
            pltpu.VMEM((tokens, cols), BF16),
            pltpu.VMEM((rows, cols), BF16),
            pltpu.VMEM((rank, cols), F32),
            pltpu.SemaphoreType.DMA((3 + 2 * (rows // block),)),
        ],
        compiler_params=params(24),
        cost_estimate=cost(2 * tokens * rows * cols, 2 * tokens * (rows + cols) + 6 * rows * cols),
        name="merge",
    )(*in_hbm(acts, kv, err, vt))


def slab_kernel(hidden_ref, slab_ref):
    slab_ref[...] = hidden_ref[0].T.reshape(slab_ref.shape)


def unit_slabs(hidden, parts):
    _, tokens, units = hidden.shape
    return pl.pallas_call(
        slab_kernel,
        out_shape=jax.ShapeDtypeStruct((parts, units // parts, tokens), BF16),
        compiler_params=params(8),
        cost_estimate=cost(0, 4 * tokens * units),
        name="unit_slabs",
    )(hidden)


def right_kernel(n_parts, *refs):
    part_refs, merged_ref = refs[:n_parts], refs[n_parts]
    lt_ref, gram_ref, chunk_ref = refs[n_parts + 1 :]
    parts = [ref[...].astype(F32) for ref in part_refs]
    while len(parts) > 1:
        parts = [a + b for a, b in zip(parts[0::2], parts[1::2])]
    lt = parts[0]
    rank = lt.shape[0]
    lt_ref[...] = lt
    product = left_times(lt, merged_ref[...].astype(BF16), (((1,), (0,)), ((), ()))).astype(BF16)
    across = product.shape[1] // TILE_C
    for a in range(rank // TILE_R):
        for b in range(across):
            chunk_ref[a * across + b] = product[
                a * TILE_R : (a + 1) * TILE_R, b * TILE_C : (b + 1) * TILE_C
            ]
    gram = lax.dot_general(lt, lt, COLS_LAST, precision=HIGHEST, preferred_element_type=F32)
    half = rank // 2
    packed = jnp.concatenate([gram[:half], gram[half:]], axis=1)
    high = packed.astype(BF16)
    rest = packed - high.astype(F32)
    middle = rest.astype(BF16)
    low = (rest - middle.astype(F32)).astype(BF16)
    gram_ref[0:half] = high
    gram_ref[half : 2 * half] = middle
    gram_ref[2 * half : 3 * half] = low


def right_product(parts, merged):
    rank, rows = parts[0].shape
    cols = merged.shape[1]
    chunks = rank * cols // (TILE_R * TILE_C)
    return pl.pallas_call(
        functools.partial(right_kernel, len(parts)),
        out_shape=[
            jax.ShapeDtypeStruct((rank, rows), F32),
            jax.ShapeDtypeStruct((3 * (rank // 2), 2 * rank), BF16),
            jax.ShapeDtypeStruct((chunks, TILE_R, TILE_C), BF16),
        ],
        compiler_params=params(16),
        cost_estimate=cost(2 * rows * cols * 128, 4 * rows * cols),
        name="right_product",
    )(*parts, merged)


def load_kernel(share_ref, gram_ref, load_ref):
    total = share_ref[0].astype(F32)
    for i in range(1, share_ref.shape[0]):
        total = total + share_ref[i].astype(F32)
    terms, rows = gram_ref.shape[0], load_ref.shape[1] - gram_ref.shape[0]
    if rows > total.shape[0]:
        total = jnp.concatenate([total, jnp.zeros((rows - total.shape[0], TILE_C), F32)], axis=0)
    total = total.astype(BF16)
    for k in range(load_ref.shape[0]):
        load_ref[k, 0:terms] = gram_ref[...]
        load_ref[k, terms : terms + rows] = total


def line_load(shares, gram, n_exp):
    rows = -(-shares.shape[1] // TILE_R) * TILE_R
    return pl.pallas_call(
        load_kernel,
        out_shape=jax.ShapeDtypeStruct((n_exp, gram.shape[0] + rows, TILE_C), BF16),
        compiler_params=params(8),
        cost_estimate=cost(0, 1e6),
        name="line_load",
    )(shares, gram)


def spread_kernel(terms, load_ref, chunk_ref):
    rows = chunk_ref.shape[1]
    total = load_ref[0, terms:].astype(F32)
    for j in range(1, load_ref.shape[0]):
        total = total + load_ref[j, terms:].astype(F32)
    total = total[:rows].astype(BF16)
    for i in range(chunk_ref.shape[0]):
        chunk_ref[i] = total


def spread(loads, terms, n_rep, rows):
    return pl.pallas_call(
        functools.partial(spread_kernel, terms),
        out_shape=jax.ShapeDtypeStruct((n_rep, rows, TILE_C), BF16),
        compiler_params=params(8),
        cost_estimate=cost(0, 1e6),
        name="spread",
    )(loads)


def inverse_kernel(load_ref, lt_ref, w_ref, basis_ref, wide_ref):
    rank = lt_ref.shape[0]
    half = rank // 2
    packed = None
    for j in range(load_ref.shape[0]):
        terms = load_ref[j, 0 : 3 * half].astype(F32)
        part = terms[:half] + terms[half : 2 * half] + terms[2 * half :]
        packed = part if packed is None else packed + part
    gram = jnp.concatenate([packed[:, :rank], packed[:, rank:]], axis=0)
    row = lax.broadcasted_iota(jnp.int32, (rank, rank), 0)
    col = lax.broadcasted_iota(jnp.int32, (rank, rank), 1)
    a = jnp.concatenate([gram, jnp.where(row == col, 1.0, 0.0).astype(F32)], axis=1)
    group = 4
    for k in range(0, rank, group):
        cols = [jnp.broadcast_to(a[:, k + j : k + j + 1], a.shape) for j in range(group)]
        rows = [a[k + j : k + j + 1, :] for j in range(group)]
        for j in range(group):
            pivot = cols[j][k + j : k + j + 1, :]
            wide_ref[k + j : k + j + 1, :] = rows[j] * lax.rsqrt(pivot)
            factor = cols[j] * (1.0 / pivot)
            for m in range(j + 1, group):
                cols[m] = cols[m] - factor * cols[m][k + j : k + j + 1, :]
                rows[m] = rows[m] - factor[k + m : k + m + 1, :] * rows[j]
            a = a - factor * rows[j]
    w = wide_ref[:, rank:]
    w_ref[...] = w
    basis = jnp.dot(w, lt_ref[...], precision=HIGHEST, preferred_element_type=F32)
    basis_ref[...] = basis.T.astype(BF16)


def inverse_factor(loads, lt):
    rank, rows = lt.shape
    return pl.pallas_call(
        inverse_kernel,
        out_shape=[
            jax.ShapeDtypeStruct((rank, rank), F32),
            jax.ShapeDtypeStruct((rows, rank), BF16),
        ],
        scratch_shapes=[pltpu.VMEM((rank, 2 * rank), F32)],
        compiler_params=params(8),
        cost_estimate=cost(4e9, 1e5),
        name="inverse_factor",
    )(loads, lt)


def finish_kernel(replicas, w_ref, chunk_ref, basis_ref, merged_ref, right_hbm, err_hbm, right_ref, err_ref, sems):
    rank, cols = right_ref.shape
    across = cols // TILE_C
    pieces = []
    for a in range(rank // TILE_R):
        pieces.append(jnp.concatenate([chunk_ref[a * across + b] for b in range(across)], axis=1))
    product = jnp.concatenate(pieces, axis=0)
    new_right = left_times(w_ref[...], product, (((1,), (0,)), ((), ()))) * (1.0 / replicas)
    right_ref[...] = new_right
    copies = [pltpu.make_async_copy(right_ref, right_hbm, sems.at[0])]
    copies[0].start()
    rounded = new_right.astype(BF16)
    rows, block = err_ref.shape[0], 128
    for i in range(rows // block):
        here = slice(i * block, (i + 1) * block)
        approx = jnp.dot(basis_ref[here, :], rounded, preferred_element_type=F32)
        err_ref[here, :] = (merged_ref[here, :] - approx).astype(BF16)
        copies.append(
            pltpu.make_async_copy(err_ref.at[here, :], err_hbm.at[0, here, :], sems.at[i + 1])
        )
        copies[-1].start()
    for copy in copies:
        copy.wait()


def finish(replicas, w, chunks, basis, merged):
    rows, rank = basis.shape
    cols = merged.shape[1]
    return pl.pallas_call(
        functools.partial(finish_kernel, replicas),
        out_specs=[HBM] * 2,
        out_shape=[
            jax.ShapeDtypeStruct((rank, cols), F32),
            jax.ShapeDtypeStruct((1, rows, cols), BF16),
        ],
        scratch_shapes=[
            pltpu.VMEM((rank, cols), F32),
            pltpu.VMEM((rows, cols), BF16),
            pltpu.SemaphoreType.DMA((rows // 128 + 1,)),
        ],
        compiler_params=params(16),
        cost_estimate=cost(2 * rows * cols * 128, 6 * rows * cols),
        name="finish",
    )(w, chunks, basis, merged)


def expert_kernel(n_exp, chunk, *refs):
    slab_ref, grad_refs = refs[0], refs[1 : n_exp + 1]
    one_hbm, two_hbm, first_hbm, second_hbm, step_hbm = refs[n_exp + 1 : n_exp + 6]
    rows, one, two, first, second, step, in_sems, out_sems = refs[n_exp + 6 :]
    units, width = one.shape
    tokens = grad_refs[0].shape[1]
    place = lax.axis_index("exp")

    def loads(c):
        here = slice(c * chunk, (c + 1) * chunk)
        pairs = [
            (grad_refs[k].at[0, :, here], rows.at[k * tokens : (k + 1) * tokens, here])
            for k in range(n_exp)
        ]
        pairs += [(one_hbm.at[0, :, here], one.at[:, here]), (two_hbm.at[0, :, here], two.at[:, here])]
        return [pltpu.make_async_copy(a, b, in_sems.at[c, i]) for i, (a, b) in enumerate(pairs)]

    def stores(c):
        here = slice(c * chunk, (c + 1) * chunk)
        pairs = [(first, first_hbm), (second, second_hbm), (step, step_hbm)]
        return [
            pltpu.make_async_copy(a.at[:, here], b.at[0, :, here], out_sems.at[c, i])
            for i, (a, b) in enumerate(pairs)
        ]

    count = width // chunk
    for c in range(count):
        for copy in loads(c):
            copy.start()
    hid = jnp.concatenate(
        [slab_ref[lax.rem(place + n_exp - k, n_exp)] for k in range(n_exp)], axis=1
    )
    for c in range(count):
        here = slice(c * chunk, (c + 1) * chunk)
        for copy in loads(c):
            copy.wait()
        grad = jnp.dot(hid, rows[:, here], preferred_element_type=F32)
        first_new = beta_one * one[:, here] + (1.0 - beta_one) * grad
        second_new = beta_two * two[:, here] + (1.0 - beta_two) * grad * grad
        first[:, here] = first_new
        second[:, here] = second_new
        scaled = second_new * (1.0 / correction_two)
        bottom = scaled * lax.rsqrt(scaled) + epsilon
        step[:, here] = (
            first_new * (1.0 / correction_one) * pl.reciprocal(bottom, approx=True)
        ).astype(BF16)
        for copy in stores(c):
            copy.start()
    for c in range(count):
        for copy in stores(c):
            copy.wait()


def expert_step(slabs, grads, moment_one, moment_two):
    _, units, width = moment_one.shape
    chunk = 256
    n_exp = len(grads)
    tokens = grads[0].shape[1]
    return pl.pallas_call(
        functools.partial(expert_kernel, n_exp, chunk),
        in_specs=[VMEM, HBM] + [pl.BlockSpec(memory_space=pl.ANY)] * (n_exp - 1) + [HBM] * 2,
        out_specs=[HBM] * 3,
        out_shape=[
            jax.ShapeDtypeStruct((1, units, width), F32),
            jax.ShapeDtypeStruct((1, units, width), F32),
            jax.ShapeDtypeStruct((1, units, width), BF16),
        ],
        scratch_shapes=[
            pltpu.VMEM((n_exp * tokens, width), BF16),
            pltpu.VMEM((units, width), F32),
            pltpu.VMEM((units, width), F32),
            pltpu.VMEM((units, width), F32),
            pltpu.VMEM((units, width), F32),
            pltpu.VMEM((units, width), BF16),
            pltpu.SemaphoreType.DMA((width // chunk, n_exp + 2)),
            pltpu.SemaphoreType.DMA((width // chunk, 3)),
        ],
        compiler_params=params(24),
        cost_estimate=cost(2 * units * width * tokens * n_exp, 20 * units * width),
        name="expert_step",
    )(slabs, *in_hbm(grads[0]), *grads[1:], *in_hbm(moment_one, moment_two))


def swap(x, axis, size, mask):
    return lax.ppermute(x, axis, [(i, i ^ mask) for i in range(size)])


def shift(x, size, k):
    return lax.ppermute(x, "exp", [(i, (i + k) % size) for i in range(size)])


def after(x, y):
    return lax.optimization_barrier((x, y))[0]


def body(n_rep, n_exp, activations, kv_grad, errors, right_factor, hidden, out_grad, moment_one, moment_two):
    grads = [out_grad, shift(out_grad, n_exp, 1)]
    merged, lt = merge(activations, kv_grad, errors, right_factor.T)

    lt = (lt + swap(lt, "rep", n_rep, 1)).astype(BF16)
    bit = 2
    parts = [lt]
    while bit < n_rep:
        while len(parts) > 1:
            parts = [a.astype(F32) + b.astype(F32) for a, b in zip(parts[0::2], parts[1::2])]
        own = parts[0].astype(BF16)
        masks = [bit] if 2 * bit >= n_rep else [bit, 2 * bit, 3 * bit]
        parts = [own] + [swap(own, "rep", n_rep, m) for m in masks]
        bit *= len(parts)

    grads.append(shift(after(grads[1], parts[1]), n_exp, 1))
    lt, gram, chunks = right_product(parts, merged)

    slabs = unit_slabs(after(hidden, chunks), n_exp)
    slabs = lax.all_to_all(slabs, "exp", 0, 0, tiled=True)

    rows = chunks.shape[0] * TILE_R // n_rep
    shares = lax.all_to_all(chunks.reshape(n_rep, rows, TILE_C), "rep", 0, 0, tiled=True)
    load = line_load(shares, gram, n_exp)
    loads = lax.all_to_all(load, "exp", 0, 0, tiled=True)
    share = spread(loads, gram.shape[0], n_rep, rows)
    for k in range(3, n_exp):
        grads.append(shift(after(grads[-1], share), n_exp, 1))
    back = lax.all_to_all(share, "rep", 0, 0, tiled=True).reshape(chunks.shape)
    w, basis = inverse_factor(loads, lt)

    new_right, new_error = finish(n_rep, w, back, basis, merged)
    first_new, second_new, step = expert_step(slabs, grads, moment_one, moment_two)
    return new_error, new_right.T, first_new, second_new, step


def solution(mesh):
    placed = (
        P("rep", "exp"),
        P("rep", None),
        P("rep", "exp", None),
        P(),
        P("rep", "exp", None),
        P("rep", "exp", None),
        P("rep", "exp", None),
        P("rep", "exp", None),
    )
    return jax.shard_map(
        functools.partial(body, mesh.shape["rep"], mesh.shape["exp"]),
        mesh=mesh,
        in_specs=placed,
        out_specs=(
            P("rep", "exp", None),
            P(),
            P("rep", "exp", None),
            P("rep", "exp", None),
            P("rep", "exp", None),
        ),
        check_vma=False,
    )
```

time: 79.8 us -> 81.1 us (1.016)
  blocking collectives: 0 us -> 19.8 us
  starting transfers between devices: 23.3 us -> 16.1 us
  local copies, waits for them, and re-layouts: 9.55 us -> 3.57 us
  waiting for transfers between devices: 26.5 us -> 23 us
  Pallas kernels: 19.1 us -> 17.4 us
    all_to_all x0 -> x2, blocking collectives: none -> 19.8 us  [the longest x1 11.6 us: body(): loads = lax.all_to_all(load, 'exp', 0, 0, tiled=True)]
    ppermute x6 -> x3, waiting for transfers between devices: 21.6 us -> 9.59 us  [shift(): return lax.ppermute(x, 'exp', [(i, (i + k) % size) for i in range(size)])]
    ppermute x6 -> x3, starting transfers between devices: 10.7 us -> 3.15 us  [shift(): return lax.ppermute(x, 'exp', [(i, (i + k) % size) for i in range(size)])]
    unnamed x34 -> x16, local copies, waits for them, and re-layouts: 8.88 us -> 3.57 us
    all_to_all x2, waiting for transfers between devices: 0.56 us -> 5.35 us  [the longest x1 3.75 us: body(): back = lax.all_to_all(share, 'rep', 0, 0, tiled=True).reshape(chunks.shape)]
    ppermute x4, waiting for transfers between devices: 4.33 us -> 8.02 us  [swap(): return lax.ppermute(x, axis, [(i, i ^ mask) for i in range(size)])]
    pallas_call x5 -> x7, Pallas kernels: 19 us -> 16.6 us  [the longest x1 5.51 us: merge(): pl.pallas_call(functools.partial(merge_kernel, block), in_specs=[HBM] * 4...]
    ppermute x4, starting transfers between devices: 4.07 us -> 5.04 us  [swap(): return lax.ppermute(x, axis, [(i, i ^ mask) for i in range(size)])]
  transfers between devices with their start and end apart: 12 -> 9, of which waited for: 6 -> 6; matrix products, arithmetic and copies ran while one was open for 1% -> 0% of each run, Pallas kernels for 11% -> 9%
where the time goes in v3:
time: 81.1 us; the launch traced here: 80.6 us
  waiting for transfers between devices  23 us (28%)
  blocking collectives  19.8 us (24%)
  Pallas kernels  17.4 us (21%)
  starting transfers between devices  16.1 us (20%)
  local copies, waits for them, and re-layouts  3.57 us (4%)
    all_to_all x1, blocking collectives, body(): loads = lax.all_to_all(load, 'exp', 0, 0, tiled=True)  11.6 us
    ppermute x3, waiting for transfers between devices, shift(): return lax.ppermute(x, 'exp', [(i, (i + k) % size) for i in range(size)])  9.59 us
    all_to_all x1, blocking collectives, body(): lax.all_to_all(chunks.reshape(n_rep, rows, TILE_C), 'rep', 0, 0, tiled=True)  8.29 us
    ppermute x4, waiting for transfers between devices, swap(): return lax.ppermute(x, axis, [(i, i ^ mask) for i in range(size)])  8.02 us
    pallas_call x1, Pallas kernels, merge(): pl.pallas_call(functools.partial(merge_kernel, block), in_specs=[HBM] * 4...  5.51 us
    ppermute x4, starting transfers between devices, swap(): return lax.ppermute(x, axis, [(i, i ^ mask) for i in range(size)])  5.04 us
    pallas_call x1, Pallas kernels, expert_step(): pl.pallas_call(functools.partial(expert_kernel, n_exp, chunk), in_specs=[...  5 us
    all_to_all x1, starting transfers between devices, body(): slabs = lax.all_to_all(slabs, 'exp', 0, 0, tiled=True)  4.58 us
  transfers between devices with their start and end apart: 9, of which 6 were waited for; matrix products, arithmetic and copies ran while one was open for 0% of the time, Pallas kernels for 9%

profile of v3, /device:TPU:0, one launch (start us, length us, event | category | flops | bytes accessed | tf_op | source)
XLA Modules:
  0.0 80.6 jit_solution(15437479681243681672)
XLA Ops:
  0.6 5.5 %merge.1 = (f32[768,1024]{1,0:T(8,128)S(1)}, f32[64,768]{1,0:T(8,128)S(1)}) custom-call(bf16[1024,768]{1,0:T(8,128)(2,1)} %acts_hbm.1, bf16[1024,1024]{1,0:T(8,128)(2,1)} %kv_hbm.1, bf16[1,768,1024]{2,1,0:T(8,128)(2,1)} %err_hbm.1, f32[64,1024]{1,0:T(8,128)} %bitcast.6), custom_call_target="tpu_custom_call" | custom-call | flops 1610612736 | bytes 8388608 | tf_op jit(solution)/shard_map/merge/pallas_call | solution.py:104
  6.7 2.6 %collective-permute-start.4 = (bf16[1,128,2048]{2,1,0:T(8,128)(2,1)S(1)}, bf16[1,128,2048]{2,1,0:T(8,128)(2,1)S(1)}, u32[]{:S(2)}, u32[]{:S(2)}) collective-permute-start(bf16[1,128,2048]{2,1,0:T(8,128)(2,1)S(1)} %copy-done.7), channel_id=1, source_target_pairs={{0,1},{1,2},{2,3},{3,0},{4,5},{5,6},{6,7},{7,4},{8,9},{9,10},{10,1... | collective-permute-start | bytes 1572872 | tf_op jit(solution)/shard_map/ppermute | solution.py:408
  9.3 1.6 %collective-permute-start.1 = (bf16[64,768]{1,0:T(8,128)(2,1)S(1)}, bf16[64,768]{1,0:T(8,128)(2,1)S(1)}, u32[]{:S(2)}, u32[]{:S(2)}) collective-permute-start(bf16[64,768]{1,0:T(8,128)(2,1)S(1)} %add_convert_fusion.refs_0_), channel_id=1, source_target_pairs={{0,8},{4,12},{8,0},{12,4},{16,24},{20,28},{24,16},{28,20},{1,9},{5... | collective-permute-start | bytes 294920 | tf_op jit(solution)/shard_map/ppermute | solution.py:404
  10.9 3.4 %collective-permute-done.1.refs_1_ = bf16[64,768]{1,0:T(8,128)(2,1)S(1)} collective-permute-done((bf16[64,768]{1,0:T(8,128)(2,1)S(1)}, bf16[64,768]{1,0:T(8,128)(2,1)S(1)}, u32[]{:S(2)}, u32[]{:S(2)}) %collective-permute-start.1) | collective-permute-done | bytes 98336 | tf_op jit(solution)/shard_map/ppermute | solution.py:404
  14.3 9.6 %collective-permute-done.4.refs_2_ = bf16[1,128,2048]{2,1,0:T(8,128)(2,1)S(1)} collective-permute-done((bf16[1,128,2048]{2,1,0:T(8,128)(2,1)S(1)}, bf16[1,128,2048]{2,1,0:T(8,128)(2,1)S(1)}, u32[]{:S(2)}, u32[]{:S(2)}) %collective-permute-start.4) | collective-permute-done | bytes 524320 | tf_op jit(solution)/shard_map/ppermute | solution.py:408
  23.9 2.5 %collective-permute-start.3 = (bf16[64,768]{1,0:T(8,128)(2,1)S(1)}, bf16[64,768]{1,0:T(8,128)(2,1)S(1)}, u32[]{:S(2)}, u32[]{:S(2)}) collective-permute-start(bf16[64,768]{1,0:T(8,128)(2,1)S(1)} %add_convert_fusion.refs_0_), channel_id=1, source_target_pairs={{0,24},{4,28},{8,16},{12,20},{16,8},{20,12},{24,0},{28,4},{1,25},{... | collective-permute-start | bytes 294920 | tf_op jit(solution)/shard_map/ppermute | solution.py:404
  26.8 2.7 %collective-permute-done.3.refs_3_ = bf16[64,768]{1,0:T(8,128)(2,1)S(1)} collective-permute-done((bf16[64,768]{1,0:T(8,128)(2,1)S(1)}, bf16[64,768]{1,0:T(8,128)(2,1)S(1)}, u32[]{:S(2)}, u32[]{:S(2)}) %collective-permute-start.3) | collective-permute-done | bytes 98336 | tf_op jit(solution)/shard_map/ppermute | solution.py:404
  29.5 2.0 %collective-permute-done.2.refs_2_ = bf16[64,768]{1,0:T(8,128)(2,1)S(1)} collective-permute-done((bf16[64,768]{1,0:T(8,128)(2,1)S(1)}, bf16[64,768]{1,0:T(8,128)(2,1)S(1)}, u32[]{:S(2)}, u32[]{:S(2)}) %collective-permute-start.2) | collective-permute-done | bytes 98336 | tf_op jit(solution)/shard_map/ppermute | solution.py:404
  31.5 0.6 right_product.1
  32.1 8.3 %all_to_all.20.share_ref = bf16[8,64,128]{2,1,0:T(8,128)(2,1)S(1)} all-to-all(bf16[8,64,128]{2,1,0:T(8,128)(2,1)S(1)} %bitcast.5), channel_id=1, replica_groups=mesh['rep'=8,'exp'=4] {'rep'}, dimensions={0} | all-to-all | bytes 262144 | tf_op jit(solution)/shard_map/all_to_all | solution.py:437
  40.5 11.6 %all_to_all.21.load_ref = bf16[4,160,128]{2,1,0:T(8,128)(2,1)S(1)} all-to-all(bf16[4,160,128]{2,1,0:T(8,128)(2,1)S(1)} %line_load.1), channel_id=1, replica_groups=mesh['rep'=8,'exp'=4] {'exp'}, dimensions={0} | all-to-all | bytes 327680 | tf_op jit(solution)/shard_map/all_to_all | solution.py:439
  52.0 0.7 spread.1
  53.2 3.4 %all-to-all-start.2 = ((bf16[8,64,128]{2,1,0:T(8,128)(2,1)}), bf16[8,64,128]{2,1,0:T(8,128)(2,1)S(1)}, u32[]{:S(2)}, u32[]{:S(2)}) async-start(bf16[8,64,128]{2,1,0:T(8,128)(2,1)} %spread.1), calls=%async_computation.2 | async-start | bytes 262144 | tf_op jit(solution)/shard_map/all_to_all | solution.py:443
  56.6 0.9 %copy-done.4 = bf16[1,128,768]{2,1,0:T(8,128)(2,1)S(1)} copy-done((bf16[1,128,768]{2,1,0:T(8,128)(2,1)S(1)}, bf16[1,128,768]{2,1,0:T(8,128)(2,1)}, u32[]{:S(2)}) %copy-start.4) | copy-done | bytes 196632
  57.5 0.8 unit_slabs.1
  58.3 3.8 %all-to-all-done.2 = bf16[8,64,128]{2,1,0:T(8,128)(2,1)S(1)} async-done(((bf16[8,64,128]{2,1,0:T(8,128)(2,1)}), bf16[8,64,128]{2,1,0:T(8,128)(2,1)S(1)}, u32[]{:S(2)}, u32[]{:S(2)}) %all-to-all-start.2) | async-done | bytes 131104 | tf_op jit(solution)/shard_map/all_to_all | solution.py:443
  62.0 0.7 copy-done.2
  62.7 4.6 %all-to-all-start.3 = ((bf16[4,192,128]{2,1,0:T(8,128)(2,1)}), bf16[4,192,128]{2,1,0:T(8,128)(2,1)S(1)}, u32[]{:S(2)}, u32[]{:S(2)}) async-start(bf16[4,192,128]{2,1,0:T(8,128)(2,1)} %unit_slabs.1), calls=%async_computation.3 | async-start | bytes 393216 | tf_op jit(solution)/shard_map/all_to_all | solution.py:434
  67.3 0.9 %copy-done.6 = f32[64,768]{1,0:T(8,128)S(1)} copy-done((f32[64,768]{1,0:T(8,128)S(1)}, f32[64,768]{1,0:T(8,128)}, u32[]{:S(2)}) %copy-start.6) | copy-done | bytes 196632
  68.2 3.2 %inverse_factor.1 = (f32[64,64]{1,0:T(8,128)S(1)}, bf16[768,64]{1,0:T(8,128)(2,1)S(1)}) custom-call(bf16[4,160,128]{2,1,0:T(8,128)(2,1)S(1)} %all_to_all.21.load_ref, f32[64,768]{1,0:T(8,128)S(1)} %copy-done.6), custom_call_target="tpu_custom_call" | custom-call | flops 4000000000 | bytes 100000 | tf_op jit(solution)/shard_map/inverse_factor/pallas_call | solution.py:261
  71.4 1.6 %finish.1 = (f32[64,1024]{1,0:T(8,128)}, bf16[1,768,1024]{2,1,0:T(8,128)(2,1)}) custom-call(f32[64,64]{1,0:T(8,128)S(1)} %get-tuple-element.25.w_ref, bf16[32,16,128]{2,1,0:T(8,128)(2,1)S(1)} %bitcast.4, bf16[768,64]{1,0:T(8,128)(2,1)S(1)} %get-tuple-element.26.basis_ref, f32[768,1024]{1,0:T(8,128)S(1)} %get-tuple-element.21.refs_4_.merged_ref), custom_call_target="tpu_custom_call" | custom-call | flops 201326592 | bytes 4718592 | tf_op jit(solution)/shard_map/finish/pallas_call | solution.py:302
  73.0 1.6 %all-to-all-done.3.refs_0_ = bf16[4,192,128]{2,1,0:T(8,128)(2,1)S(1)} async-done(((bf16[4,192,128]{2,1,0:T(8,128)(2,1)}), bf16[4,192,128]{2,1,0:T(8,128)(2,1)S(1)}, u32[]{:S(2)}, u32[]{:S(2)}) %all-to-all-start.3) | async-done | bytes 196640 | tf_op jit(solution)/shard_map/all_to_all | solution.py:434
  74.6 1.0 %copy-done.1 = bf16[1,128,2048]{2,1,0:T(8,128)(2,1)S(1)} copy-done((bf16[1,128,2048]{2,1,0:T(8,128)(2,1)S(1)}, bf16[1,128,2048]{2,1,0:T(8,128)(2,1)}, u32[]{:S(2)}) %copy-start.1) | copy-done | bytes 524312
  75.6 5.0 %expert_step.1 = (f32[1,192,2048]{2,1,0:T(8,128)}, f32[1,192,2048]{2,1,0:T(8,128)}, bf16[1,192,2048]{2,1,0:T(8,128)(2,1)}) custom-call(bf16[4,192,128]{2,1,0:T(8,128)(2,1)S(1)} %all-to-all-done.3.refs_0_, bf16[1,128,2048]{2,1,0:T(8,128)(2,1)} %refs_1_.1, bf16[1,128,2048]{2,1,0:T(8,128)(2,1)S(1)} %copy-done.1, ...), custom_call_target="tpu_custom_call" | custom-call | flops 402653184 | bytes 7864320 | tf_op jit(solution)/shard_map/expert_step/pallas_call | solution.py:378
  (21 shorter events, 1.6 us)
Async XLA Ops:
  0.6 6.0 %copy-start.7 = (bf16[1,128,2048]{2,1,0:T(8,128)(2,1)S(1)}, bf16[1,128,2048]{2,1,0:T(8,128)(2,1)}, u32[]{:S(2)}) copy-start(bf16[1,128,2048]{2,1,0:T(8,128)(2,1)} %refs_1_.1) | copy-start | bytes 1572868
  6.2 3.2 %collective-permute-start = (f32[64,768]{1,0:T(8,128)S(1)}, f32[64,768]{1,0:T(8,128)S(1)}, u32[]{:S(2)}, u32[]{:S(2)}) collective-permute-start(f32[64,768]{1,0:T(8,128)S(1)} %get-tuple-element.20), channel_id=1, source_target_pairs={{0,4},{4,0},{8,12},{12,8},{16,20},{20,16},{24,28},{28,24},{1,5},{5... | collective-permute-start | bytes 589832 | tf_op jit(solution)/shard_map/ppermute | solution.py:404
  6.7 17.2 %collective-permute-start.4 = (bf16[1,128,2048]{2,1,0:T(8,128)(2,1)S(1)}, bf16[1,128,2048]{2,1,0:T(8,128)(2,1)S(1)}, u32[]{:S(2)}, u32[]{:S(2)}) collective-permute-start(bf16[1,128,2048]{2,1,0:T(8,128)(2,1)S(1)} %copy-done.7), channel_id=1, source_target_pairs={{0,1},{1,2},{2,3},{3,0},{4,5},{5,6},{6,7},{7,4},{8,9},{9,10},{10,1... | collective-permute-start | bytes 1572872 | tf_op jit(solution)/shard_map/ppermute | solution.py:408
  9.3 4.9 %collective-permute-start.1 = (bf16[64,768]{1,0:T(8,128)(2,1)S(1)}, bf16[64,768]{1,0:T(8,128)(2,1)S(1)}, u32[]{:S(2)}, u32[]{:S(2)}) collective-permute-start(bf16[64,768]{1,0:T(8,128)(2,1)S(1)} %add_convert_fusion.refs_0_), channel_id=1, source_target_pairs={{0,8},{4,12},{8,0},{12,4},{16,24},{20,28},{24,16},{28,20},{1,9},{5... | collective-permute-start | bytes 294920 | tf_op jit(solution)/shard_map/ppermute | solution.py:404
  23.9 8.3 %copy-start = (bf16[1,128,2048]{2,1,0:T(8,128)(2,1)}, bf16[1,128,2048]{2,1,0:T(8,128)(2,1)S(1)}, u32[]{:S(2)}) copy-start(bf16[1,128,2048]{2,1,0:T(8,128)(2,1)S(1)} %collective-permute-done.4.refs_2_) | copy-start | bytes 1572868
  23.9 28.8 %collective-permute-start.5 = (bf16[1,128,2048]{2,1,0:T(8,128)(2,1)S(1)}, bf16[1,128,2048]{2,1,0:T(8,128)(2,1)}, u32[]{:S(2)}, u32[]{:S(2)}) collective-permute-start(bf16[1,128,2048]{2,1,0:T(8,128)(2,1)S(1)} %collective-permute-done.4.refs_2_), channel_id=1, source_target_pairs={{0,1},{1,2},{2,3},{3,0},{4,5},{5,6},{6,7},{7,4},{8,9},{9,10},{10,1... | collective-permute-start | bytes 1572872 | tf_op jit(solution)/shard_map/ppermute | solution.py:408
  23.9 5.6 %collective-permute-start.3 = (bf16[64,768]{1,0:T(8,128)(2,1)S(1)}, bf16[64,768]{1,0:T(8,128)(2,1)S(1)}, u32[]{:S(2)}, u32[]{:S(2)}) collective-permute-start(bf16[64,768]{1,0:T(8,128)(2,1)S(1)} %add_convert_fusion.refs_0_), channel_id=1, source_target_pairs={{0,24},{4,28},{8,16},{12,20},{16,8},{20,12},{24,0},{28,4},{1,25},{... | collective-permute-start | bytes 294920 | tf_op jit(solution)/shard_map/ppermute | solution.py:404
  26.3 5.2 %collective-permute-start.2 = (bf16[64,768]{1,0:T(8,128)(2,1)S(1)}, bf16[64,768]{1,0:T(8,128)(2,1)S(1)}, u32[]{:S(2)}, u32[]{:S(2)}) collective-permute-start(bf16[64,768]{1,0:T(8,128)(2,1)S(1)} %add_convert_fusion.refs_0_), channel_id=1, source_target_pairs={{0,16},{4,20},{8,24},{12,28},{16,0},{20,4},{24,8},{28,12},{1,17},{... | collective-permute-start | bytes 294920 | tf_op jit(solution)/shard_map/ppermute | solution.py:404
  32.1 20.6 %copy-start.5 = (f32[64,768]{1,0:T(8,128)}, f32[64,768]{1,0:T(8,128)S(1)}, u32[]{:S(2)}) copy-start(f32[64,768]{1,0:T(8,128)S(1)} %get-tuple-element.24.lt_ref) | copy-start | bytes 589828
  52.7 21.9 %collective-permute-start.6 = (bf16[1,128,2048]{2,1,0:T(8,128)(2,1)}, bf16[1,128,2048]{2,1,0:T(8,128)(2,1)}, u32[]{:S(2)}, u32[]{:S(2)}) collective-permute-start(bf16[1,128,2048]{2,1,0:T(8,128)(2,1)} %collective-permute-done.5.refs_3_), channel_id=1, source_target_pairs={{0,1},{1,2},{2,3},{3,0},{4,5},{5,6},{6,7},{7,4},{8,9},{9,10},{10,1... | collective-permute-start | bytes 1572872 | tf_op jit(solution)/shard_map/ppermute | solution.py:408
  53.2 8.8 %all-to-all-start.2 = ((bf16[8,64,128]{2,1,0:T(8,128)(2,1)}), bf16[8,64,128]{2,1,0:T(8,128)(2,1)S(1)}, u32[]{:S(2)}, u32[]{:S(2)}) async-start(bf16[8,64,128]{2,1,0:T(8,128)(2,1)} %spread.1), calls=%async_computation.2 | async-start | bytes 262144 | tf_op jit(solution)/shard_map/all_to_all | solution.py:443
  56.6 0.9 %copy-start.4 = (bf16[1,128,768]{2,1,0:T(8,128)(2,1)S(1)}, bf16[1,128,768]{2,1,0:T(8,128)(2,1)}, u32[]{:S(2)}) copy-start(bf16[1,128,768]{2,1,0:T(8,128)(2,1)} %hidden_ref) | copy-start | bytes 589828
  62.0 0.7 copy-start.2
  62.7 11.9 %all-to-all-start.3 = ((bf16[4,192,128]{2,1,0:T(8,128)(2,1)}), bf16[4,192,128]{2,1,0:T(8,128)(2,1)S(1)}, u32[]{:S(2)}, u32[]{:S(2)}) async-start(bf16[4,192,128]{2,1,0:T(8,128)(2,1)} %unit_slabs.1), calls=%async_computation.3 | async-start | bytes 393216 | tf_op jit(solution)/shard_map/all_to_all | solution.py:434
  67.3 0.9 %copy-start.6 = (f32[64,768]{1,0:T(8,128)S(1)}, f32[64,768]{1,0:T(8,128)}, u32[]{:S(2)}) copy-start(f32[64,768]{1,0:T(8,128)} %copy-done.5) | copy-start | bytes 589828
  68.2 3.2 %copy-start.3 = (bf16[8,64,128]{2,1,0:T(8,128)(2,1)S(1)}, bf16[8,64,128]{2,1,0:T(8,128)(2,1)}, u32[]{:S(2)}) copy-start(bf16[8,64,128]{2,1,0:T(8,128)(2,1)} %copy-done.2) | copy-start | bytes 393220
  74.6 1.0 %copy-start.1 = (bf16[1,128,2048]{2,1,0:T(8,128)(2,1)S(1)}, bf16[1,128,2048]{2,1,0:T(8,128)(2,1)}, u32[]{:S(2)}) copy-start(bf16[1,128,2048]{2,1,0:T(8,128)(2,1)} %copy-done) | copy-start | bytes 1572868

commit v4 on v3

v4 whole, which is shorter than its diff:
```python
import functools

import jax
import jax.numpy as jnp
from jax import lax
from jax.experimental import pallas as pl
from jax.experimental.pallas import tpu as pltpu
from jax.sharding import PartitionSpec as P

HIGHEST = lax.Precision.HIGHEST
F32 = jnp.float32
BF16 = jnp.bfloat16
beta_one = 0.9
beta_two = 0.99
correction_one = 1.0 - 0.9**10
correction_two = 1.0 - 0.99**10
epsilon = 1e-08

ROWS_FIRST = (((0,), (0,)), ((), ()))
COLS_LAST = (((1,), (1,)), ((), ()))
TILE_R, TILE_C = 16, 128
HBM = pl.BlockSpec(memory_space=pltpu.HBM)
ANY = pl.BlockSpec(memory_space=pl.ANY)
VMEM = pl.BlockSpec(memory_space=pltpu.VMEM)


def params(mebibytes):
    return pltpu.CompilerParams(vmem_limit_bytes=mebibytes * 1024 * 1024)


def in_hbm(*arrays):
    return [pltpu.with_memory_space_constraint(x, pltpu.HBM) for x in arrays]


SMALL = pl.CostEstimate(flops=1000, bytes_accessed=1000, transcendentals=0)


def split_two(x):
    hi = x.astype(BF16)
    return hi, (x - hi.astype(F32)).astype(BF16)


def left_times(left, right_bf16, dims):
    rows = left.shape[0]
    hi, lo = split_two(left)
    both = jnp.concatenate([hi, lo], axis=0)
    out = lax.dot_general(both, right_bf16, dims, preferred_element_type=F32)
    return out[:rows] + out[rows:]


def merge_kernel(block, acts_hbm, kv_hbm, err_hbm, vt_hbm, merged_ref, lt_ref, acts, kv, err, vt, sems):
    tokens, rows = acts.shape
    part = tokens // 4
    half = tokens // 2
    count = rows // block

    def acts_copy(i):
        here = slice(i * block, (i + 1) * block)
        return pltpu.make_async_copy(acts_hbm.at[:, here], acts.at[:, here], sems.at[5 + i])

    def err_copy(i):
        here = slice(i * block, (i + 1) * block)
        return pltpu.make_async_copy(err_hbm.at[0, here, :], err.at[here, :], sems.at[5 + count + i])

    def kv_copy(i):
        here = slice(i * part, (i + 1) * part)
        return pltpu.make_async_copy(kv_hbm.at[here, :], kv.at[here, :], sems.at[i])

    vt_copy = pltpu.make_async_copy(vt_hbm, vt, sems.at[4])
    acts_copy(0).start()
    for i in range(4):
        kv_copy(i).start()
    err_copy(0).start()
    vt_copy.start()
    for i in range(count):
        here = slice(i * block, (i + 1) * block)
        acts_copy(i).wait()
        if i == 0:
            kv_copy(0).wait()
            kv_copy(1).wait()
            for later in range(1, count):
                acts_copy(later).start()
                err_copy(later).start()
            merged = lax.dot_general(
                acts[:half, here], kv[:half, :], ROWS_FIRST, preferred_element_type=F32
            )
            kv_copy(2).wait()
            kv_copy(3).wait()
            merged = merged + lax.dot_general(
                acts[half:, here], kv[half:, :], ROWS_FIRST, preferred_element_type=F32
            )
        else:
            merged = lax.dot_general(acts[:, here], kv[...], ROWS_FIRST, preferred_element_type=F32)
        err_copy(i).wait()
        merged = merged + err[here, :].astype(F32)
        merged_ref[here, :] = merged
        if i == 0:
            vt_copy.wait()
            both = jnp.concatenate(split_two(vt[...]), axis=0)
        left = lax.dot_general(merged.astype(BF16), both, COLS_LAST, preferred_element_type=F32).T
        lt_ref[:, here] = left[: left.shape[0] // 2] + left[left.shape[0] // 2 :]


def merge(acts, kv, err, vt):
    tokens, rows = acts.shape
    cols = kv.shape[1]
    rank = vt.shape[0]
    block = 256
    return pl.pallas_call(
        functools.partial(merge_kernel, block),
        in_specs=[HBM] * 4,
        out_specs=[VMEM] * 2,
        out_shape=[
            jax.ShapeDtypeStruct((rows, cols), F32),
            jax.ShapeDtypeStruct((rank, rows), F32),
        ],
        scratch_shapes=[
            pltpu.VMEM((tokens, rows), BF16),
            pltpu.VMEM((tokens, cols), BF16),
            pltpu.VMEM((rows, cols), BF16),
            pltpu.VMEM((rank, cols), F32),
            pltpu.SemaphoreType.DMA((5 + 2 * (rows // block),)),
        ],
        compiler_params=params(24),
        cost_estimate=SMALL,
        name="merge",
    )(*in_hbm(acts, kv, err, vt))


def slab_kernel(hidden_ref, slab_ref):
    slab_ref[...] = hidden_ref[0].T.reshape(slab_ref.shape)


def unit_slabs(hidden, parts):
    _, tokens, units = hidden.shape
    return pl.pallas_call(
        slab_kernel,
        out_shape=jax.ShapeDtypeStruct((parts, units // parts, tokens), BF16),
        compiler_params=params(8),
        cost_estimate=SMALL,
        name="unit_slabs",
    )(hidden)


def right_kernel(n_parts, n_exp, *refs):
    part_refs, merged_ref, slab_ref = refs[:n_parts], refs[n_parts], refs[n_parts + 1]
    lt_hbm, own_hbm, chunk_ref = refs[n_parts + 2 : n_parts + 5]
    load_refs = refs[n_parts + 5 : n_parts + 4 + n_exp]
    lt_ref, own_ref, sems = refs[n_parts + 4 + n_exp :]
    parts = [ref[...].astype(F32) for ref in part_refs]
    while len(parts) > 1:
        parts = [a + b for a, b in zip(parts[0::2], parts[1::2])]
    lt = parts[0]
    rank = lt.shape[0]
    lt_ref[...] = lt
    lt_copy = pltpu.make_async_copy(lt_ref, lt_hbm, sems.at[0])
    lt_copy.start()
    gram = lax.dot_general(lt, lt, COLS_LAST, precision=HIGHEST, preferred_element_type=F32)
    half = rank // 2
    packed = jnp.concatenate([gram[:half], gram[half:]], axis=1)
    high = packed.astype(BF16)
    rest = packed - high.astype(F32)
    middle = rest.astype(BF16)
    low = (rest - middle.astype(F32)).astype(BF16)
    place = lax.axis_index("exp")
    units = slab_ref.shape[1]
    for k, load_ref in enumerate((own_ref,) + tuple(load_refs)):
        load_ref[0:units] = slab_ref[lax.rem(place + k, n_exp)]
        load_ref[units : units + half] = high
        load_ref[units + half : units + 2 * half] = middle
        load_ref[units + 2 * half : units + 3 * half] = low
    own_copy = pltpu.make_async_copy(own_ref, own_hbm, sems.at[1])
    own_copy.start()
    product = left_times(lt, merged_ref[...].astype(BF16), (((1,), (0,)), ((), ()))).astype(BF16)
    across = product.shape[1] // TILE_C
    for a in range(rank // TILE_R):
        for b in range(across):
            chunk_ref[a * across + b] = product[
                a * TILE_R : (a + 1) * TILE_R, b * TILE_C : (b + 1) * TILE_C
            ]
    lt_copy.wait()
    own_copy.wait()


def right_product(parts, merged, slabs):
    rank, rows = parts[0].shape
    cols = merged.shape[1]
    chunks = rank * cols // (TILE_R * TILE_C)
    n_exp, units, tokens = slabs.shape
    assert tokens == 2 * rank
    load = (units + 3 * (rank // 2), tokens)
    out = pl.pallas_call(
        functools.partial(right_kernel, len(parts), n_exp),
        out_specs=[HBM, HBM] + [VMEM] * n_exp,
        out_shape=[
            pltpu.HBM((rank, rows), F32),
            pltpu.HBM(load, BF16),
            jax.ShapeDtypeStruct((chunks, TILE_R, TILE_C), BF16),
        ]
        + [jax.ShapeDtypeStruct(load, BF16)] * (n_exp - 1),
        scratch_shapes=[
            pltpu.VMEM((rank, rows), F32),
            pltpu.VMEM(load, BF16),
            pltpu.SemaphoreType.DMA((2,)),
        ],
        compiler_params=params(16),
        cost_estimate=SMALL,
        name="right_product",
    )(*parts, merged, slabs)
    return out[0], out[2], [out[1]] + list(out[3:])


def fold_kernel(share_ref, out_ref):
    total = share_ref[0].astype(F32)
    for i in range(1, share_ref.shape[0]):
        total = total + share_ref[i].astype(F32)
    total = total.astype(BF16)
    for i in range(out_ref.shape[0]):
        out_ref[i] = total


def fold(shares):
    return pl.pallas_call(
        fold_kernel,
        out_shape=jax.ShapeDtypeStruct(shares.shape, BF16),
        compiler_params=params(4),
        cost_estimate=SMALL,
        name="fold",
    )(shares)


def inverse_kernel(n_exp, *refs):
    load_hbms, lt_hbm = refs[:n_exp], refs[n_exp]
    w_ref, basis_ref, terms_ref, lt_ref, wide_ref, sems = refs[n_exp + 1 :]
    rank = lt_ref.shape[0]
    half = rank // 2
    units = load_hbms[0].shape[0] - 3 * half
    copies = [
        pltpu.make_async_copy(load_hbms[k].at[units : units + 3 * half], terms_ref.at[k], sems.at[k])
        for k in range(n_exp)
    ]
    lt_copy = pltpu.make_async_copy(lt_hbm, lt_ref, sems.at[n_exp])
    for copy in copies:
        copy.start()
    lt_copy.start()
    for copy in copies:
        copy.wait()
    place = lax.axis_index("exp")
    packed = None
    for j in range(n_exp):
        terms = terms_ref[lax.rem(place + n_exp - j, n_exp)].astype(F32)
        part = terms[:half] + terms[half : 2 * half] + terms[2 * half :]
        packed = part if packed is None else packed + part
    gram = jnp.concatenate([packed[:, :rank], packed[:, rank:]], axis=0)
    row = lax.broadcasted_iota(jnp.int32, (rank, rank), 0)
    col = lax.broadcasted_iota(jnp.int32, (rank, rank), 1)
    a = jnp.concatenate([gram, jnp.where(row == col, 1.0, 0.0).astype(F32)], axis=1)
    group = 4
    for k in range(0, rank, group):
        cols = [jnp.broadcast_to(a[:, k + j : k + j + 1], a.shape) for j in range(group)]
        rows = [a[k + j : k + j + 1, :] for j in range(group)]
        for j in range(group):
            pivot = cols[j][k + j : k + j + 1, :]
            wide_ref[k + j : k + j + 1, :] = rows[j] * lax.rsqrt(pivot)
            factor = cols[j] * (1.0 / pivot)
            for m in range(j + 1, group):
                cols[m] = cols[m] - factor * cols[m][k + j : k + j + 1, :]
                rows[m] = rows[m] - factor[k + m : k + m + 1, :] * rows[j]
            a = a - factor * rows[j]
    w = wide_ref[:, rank:]
    w_ref[...] = w
    lt_copy.wait()
    basis = jnp.dot(w, lt_ref[...], precision=HIGHEST, preferred_element_type=F32)
    basis_ref[...] = basis.T.astype(BF16)


def inverse_factor(loads, lt):
    rank, rows = lt.shape
    n_exp = len(loads)
    return pl.pallas_call(
        functools.partial(inverse_kernel, n_exp),
        in_specs=[HBM] + [ANY] * (n_exp - 1) + [HBM],
        out_shape=[
            jax.ShapeDtypeStruct((rank, rank), F32),
            jax.ShapeDtypeStruct((rows, rank), BF16),
        ],
        scratch_shapes=[
            pltpu.VMEM((n_exp, 3 * (rank // 2), 2 * rank), BF16),
            pltpu.VMEM((rank, rows), F32),
            pltpu.VMEM((rank, 2 * rank), F32),
            pltpu.SemaphoreType.DMA((n_exp + 1,)),
        ],
        compiler_params=params(8),
        cost_estimate=SMALL,
        name="inverse_factor",
    )(*in_hbm(loads[0]), *loads[1:], *in_hbm(lt))


def finish_kernel(replicas, w_ref, chunk_ref, basis_ref, merged_ref, right_hbm, err_hbm, right_ref, err_ref, sems):
    rank, cols = right_ref.shape
    across = cols // TILE_C
    pieces = []
    for a in range(rank // TILE_R):
        pieces.append(jnp.concatenate([chunk_ref[a * across + b] for b in range(across)], axis=1))
    product = jnp.concatenate(pieces, axis=0)
    new_right = left_times(w_ref[...], product, (((1,), (0,)), ((), ()))) * (1.0 / replicas)
    right_ref[...] = new_right
    copies = [pltpu.make_async_copy(right_ref, right_hbm, sems.at[0])]
    copies[0].start()
    rounded = new_right.astype(BF16)
    rows, block = err_ref.shape[0], 128
    for i in range(rows // block):
        here = slice(i * block, (i + 1) * block)
        approx = jnp.dot(basis_ref[here, :], rounded, preferred_element_type=F32)
        err_ref[here, :] = (merged_ref[here, :] - approx).astype(BF16)
        copies.append(
            pltpu.make_async_copy(err_ref.at[here, :], err_hbm.at[0, here, :], sems.at[i + 1])
        )
        copies[-1].start()
    for copy in copies:
        copy.wait()


def finish(replicas, w, chunks, basis, merged):
    rows, rank = basis.shape
    cols = merged.shape[1]
    return pl.pallas_call(
        functools.partial(finish_kernel, replicas),
        out_specs=[HBM] * 2,
        out_shape=[
            jax.ShapeDtypeStruct((rank, cols), F32),
            jax.ShapeDtypeStruct((1, rows, cols), BF16),
        ],
        scratch_shapes=[
            pltpu.VMEM((rank, cols), F32),
            pltpu.VMEM((rows, cols), BF16),
            pltpu.SemaphoreType.DMA((rows // 128 + 1,)),
        ],
        compiler_params=params(16),
        cost_estimate=SMALL,
        name="finish",
    )(w, chunks, basis, merged)


def expert_kernel(n_exp, chunk, *refs):
    load_hbms, grad_hbms = refs[:n_exp], refs[n_exp : 2 * n_exp]
    one_hbm, two_hbm, first_hbm, second_hbm, step_hbm = refs[2 * n_exp : 2 * n_exp + 5]
    hid, rows, one, two, first, second, step, in_sems, out_sems = refs[2 * n_exp + 5 :]
    units, width = one.shape
    tokens = grad_hbms[0].shape[1]
    count = width // chunk

    slabs = [
        pltpu.make_async_copy(load_hbms[k].at[0:units], hid.at[k], in_sems.at[count, k])
        for k in range(n_exp)
    ]

    def loads(c):
        here = slice(c * chunk, (c + 1) * chunk)
        pairs = [
            (grad_hbms[k].at[0, :, here], rows.at[k * tokens : (k + 1) * tokens, here])
            for k in range(n_exp)
        ]
        pairs += [(one_hbm.at[0, :, here], one.at[:, here]), (two_hbm.at[0, :, here], two.at[:, here])]
        return [pltpu.make_async_copy(a, b, in_sems.at[c, i]) for i, (a, b) in enumerate(pairs)]

    def stores(c):
        here = slice(c * chunk, (c + 1) * chunk)
        pairs = [(first, first_hbm), (second, second_hbm), (step, step_hbm)]
        return [
            pltpu.make_async_copy(a.at[:, here], b.at[0, :, here], out_sems.at[c, i])
            for i, (a, b) in enumerate(pairs)
        ]

    for copy in slabs:
        copy.start()
    for c in range(count):
        for copy in loads(c):
            copy.start()
    for copy in slabs:
        copy.wait()
    left = jnp.concatenate([hid[k] for k in range(n_exp)], axis=1)
    for c in range(count):
        here = slice(c * chunk, (c + 1) * chunk)
        for copy in loads(c):
            copy.wait()
        grad = jnp.dot(left, rows[:, here], preferred_element_type=F32)
        first_new = beta_one * one[:, here] + (1.0 - beta_one) * grad
        second_new = beta_two * two[:, here] + (1.0 - beta_two) * grad * grad
        first[:, here] = first_new
        second[:, here] = second_new
        scaled = second_new * (1.0 / correction_two)
        bottom = scaled * lax.rsqrt(scaled) + epsilon
        step[:, here] = (
            first_new * (1.0 / correction_one) * pl.reciprocal(bottom, approx=True)
        ).astype(BF16)
        for copy in stores(c):
            copy.start()
    for c in range(count):
        for copy in stores(c):
            copy.wait()


def expert_step(slabs, grads, moment_one, moment_two):
    _, units, width = moment_one.shape
    chunk = 512
    n_exp = len(grads)
    tokens = grads[0].shape[1]
    return pl.pallas_call(
        functools.partial(expert_kernel, n_exp, chunk),
        in_specs=([HBM] + [ANY] * (n_exp - 1)) * 2 + [HBM] * 2,
        out_specs=[HBM] * 3,
        out_shape=[
            jax.ShapeDtypeStruct((1, units, width), F32),
            jax.ShapeDtypeStruct((1, units, width), F32),
            jax.ShapeDtypeStruct((1, units, width), BF16),
        ],
        scratch_shapes=[
            pltpu.VMEM((n_exp, units, tokens), BF16),
            pltpu.VMEM((n_exp * tokens, width), BF16),
            pltpu.VMEM((units, width), F32),
            pltpu.VMEM((units, width), F32),
            pltpu.VMEM((units, width), F32),
            pltpu.VMEM((units, width), F32),
            pltpu.VMEM((units, width), BF16),
            pltpu.SemaphoreType.DMA((width // chunk + 1, n_exp + 2)),
            pltpu.SemaphoreType.DMA((width // chunk, 3)),
        ],
        compiler_params=params(24),
        cost_estimate=SMALL,
        name="expert_step",
    )(
        *in_hbm(slabs[0]), *slabs[1:], *in_hbm(grads[0]), *grads[1:], *in_hbm(moment_one, moment_two)
    )


def swap(x, axis, size, mask):
    return lax.ppermute(x, axis, [(i, i ^ mask) for i in range(size)])


def shift(x, size, k):
    return lax.ppermute(x, "exp", [(i, (i + k) % size) for i in range(size)])


def after(x, y):
    return lax.optimization_barrier((x, y))[0]


def body(n_rep, n_exp, activations, kv_grad, errors, right_factor, hidden, out_grad, moment_one, moment_two):
    grads = {0: out_grad, 1: shift(out_grad, n_exp, 1)}
    merged, lt = merge(activations, kv_grad, errors, right_factor.T)

    lt = (lt + swap(lt, "rep", n_rep, 1)).astype(BF16)
    slabs = unit_slabs(after(hidden, lt), n_exp)
    if n_exp > 2:
        grads[n_exp - 1] = shift(after(out_grad, slabs), n_exp, -1)
    bit = 2
    parts = [lt]
    while bit < n_rep:
        while len(parts) > 1:
            parts = [a.astype(F32) + b.astype(F32) for a, b in zip(parts[0::2], parts[1::2])]
        own = parts[0].astype(BF16)
        masks = [bit] if 2 * bit >= n_rep else [bit, 2 * bit, 3 * bit]
        parts = [own] + [swap(own, "rep", n_rep, m) for m in masks]
        bit *= len(parts)
    lt, chunks, loads = right_product(parts, merged, slabs)

    loads = [loads[0]] + [shift(loads[k], n_exp, k) for k in range(1, n_exp)]
    w, basis = inverse_factor(loads, lt)

    if chunks.shape[0] == n_rep * n_exp:
        both = ("rep", "exp")
        share = fold(lax.all_to_all(chunks, both, 0, 0, tiled=True))
        chunks = lax.all_to_all(share, both, 0, 0, tiled=True)
    else:
        share = chunks
        chunks = lax.psum(chunks.astype(F32), ("rep", "exp")).astype(BF16)

    left, right = 1, n_exp - 1
    while right - left > 1:
        if left <= n_exp - right:
            grads[left + 1] = shift(after(grads[left], share), n_exp, 1)
            left += 1
        else:
            grads[right - 1] = shift(after(grads[right], share), n_exp, -1)
            right -= 1

    new_right, new_error = finish(n_rep, w, chunks, basis, merged)
    first_new, second_new, step = expert_step(
        loads, [grads[k] for k in range(n_exp)], moment_one, moment_two
    )
    return new_error, new_right.T, first_new, second_new, step


def solution(mesh):
    placed = (
        P("rep", "exp"),
        P("rep", None),
        P("rep", "exp", None),
        P(),
        P("rep", "exp", None),
        P("rep", "exp", None),
        P("rep", "exp", None),
        P("rep", "exp", None),
    )
    return jax.shard_map(
        functools.partial(body, mesh.shape["rep"], mesh.shape["exp"]),
        mesh=mesh,
        in_specs=placed,
        out_specs=(
            P("rep", "exp", None),
            P(),
            P("rep", "exp", None),
            P("rep", "exp", None),
            P("rep", "exp", None),
        ),
        check_vma=False,
    )
```

time: 81.1 us -> 73.9 us (0.911)
  blocking collectives: 19.8 us -> 0 us
  starting transfers between devices: 16.1 us -> 25.5 us
  waiting for transfers between devices: 23 us -> 26.4 us
  local copies, waits for them, and re-layouts: 3.57 us -> 2.23 us
  Pallas kernels: 17.4 us -> 18.7 us
    all_to_all x2 -> x0, blocking collectives: 19.8 us -> none  [the longest x1 11.6 us: body(): loads = lax.all_to_all(load, 'exp', 0, 0, tiled=True)]
    ppermute x3 -> x6, starting transfers between devices: 3.15 us -> 12 us  [shift(): return lax.ppermute(x, 'exp', [(i, (i + k) % size) for i in range(size)])]
    ppermute x3 -> x6, waiting for transfers between devices: 9.59 us -> 17.1 us  [shift(): return lax.ppermute(x, 'exp', [(i, (i + k) % size) for i in range(size)])]
    ppermute x4, waiting for transfers between devices: 8.02 us -> 4.33 us  [swap(): return lax.ppermute(x, axis, [(i, i ^ mask) for i in range(size)])]
    pallas_call x5 -> x4, Pallas kernels: 9.52 us -> 11.2 us  [the longest x1 4.6 us: expert_step(): pl.pallas_call(functools.partial(expert_kernel, n_exp, chunk), in_specs=(...]
    all_to_all x2, starting transfers between devices: 7.96 us -> 9.49 us  [the longest x1 4.86 us: body(): share = fold(lax.all_to_all(chunks, both, 0, 0, tiled=True))]
    unnamed x16 -> x8, local copies, waits for them, and re-layouts: 3.57 us -> 2.23 us
    ppermute x4, starting transfers between devices: 5.04 us -> 4.08 us  [swap(): return lax.ppermute(x, axis, [(i, i ^ mask) for i in range(size)])]
  transfers between devices with their start and end apart: 9 -> 12, of which waited for: 6 -> 6; matrix products, arithmetic and copies ran while one was open for 0% -> 0% of each run, Pallas kernels for 9% -> 11%
where the time goes in v4:
time: 73.9 us; the launch traced here: 73.7 us
  waiting for transfers between devices  26.4 us (36%)
  starting transfers between devices  25.5 us (35%)
  Pallas kernels  18.7 us (25%)
  local copies, waits for them, and re-layouts  2.23 us (3%)
  between operations  0.74 us (1%)
    ppermute x6, waiting for transfers between devices, shift(): return lax.ppermute(x, 'exp', [(i, (i + k) % size) for i in range(size)])  17.1 us
    ppermute x6, starting transfers between devices, shift(): return lax.ppermute(x, 'exp', [(i, (i + k) % size) for i in range(size)])  12 us
    pallas_call x1, Pallas kernels, merge(): pl.pallas_call(functools.partial(merge_kernel, block), in_specs=[HBM] * 4...  5.87 us
    all_to_all x1, waiting for transfers between devices, body(): share = fold(lax.all_to_all(chunks, both, 0, 0, tiled=True))  4.95 us
    all_to_all x1, starting transfers between devices, body(): share = fold(lax.all_to_all(chunks, both, 0, 0, tiled=True))  4.86 us
    all_to_all x1, starting transfers between devices, body(): chunks = lax.all_to_all(share, both, 0, 0, tiled=True)  4.62 us
    pallas_call x1, Pallas kernels, expert_step(): pl.pallas_call(functools.partial(expert_kernel, n_exp, chunk), in_specs=(...  4.6 us
    ppermute x4, waiting for transfers between devices, swap(): return lax.ppermute(x, axis, [(i, i ^ mask) for i in range(size)])  4.33 us
  transfers between devices with their start and end apart: 12, of which 6 were waited for; matrix products, arithmetic and copies ran while one was open for 0% of the time, Pallas kernels for 11%

profile of v4, /device:TPU:0, one launch (start us, length us, event | category | flops | bytes accessed | tf_op | source)
XLA Modules:
  0.0 73.7 jit_solution(11432672570530416805)
XLA Ops:
  0.6 5.9 %merge.1 = (f32[768,1024]{1,0:T(8,128)S(1)}, f32[64,768]{1,0:T(8,128)S(1)}) custom-call(bf16[1024,768]{1,0:T(8,128)(2,1)} %acts_hbm.1, bf16[1024,1024]{1,0:T(8,128)(2,1)} %kv_hbm.1, bf16[1,768,1024]{2,1,0:T(8,128)(2,1)} %err_hbm.1, f32[64,1024]{1,0:T(8,128)} %bitcast.2), custom_call_target="tpu_custom_call" | custom-call | flops 1000 | bytes 1000 | tf_op jit(solution)/shard_map/merge/pallas_call | solution.py:109
  6.5 0.5 collective-permute-start
  7.0 2.6 %collective-permute-start.7 = (bf16[1,128,2048]{2,1,0:T(8,128)(2,1)}, bf16[1,128,2048]{2,1,0:T(8,128)(2,1)}, u32[]{:S(2)}, u32[]{:S(2)}) collective-permute-start(bf16[1,128,2048]{2,1,0:T(8,128)(2,1)} %refs_4_.1), channel_id=1, source_target_pairs={{0,1},{1,2},{2,3},{3,0},{4,5},{5,6},{6,7},{7,4},{8,9},{9,10},{10,1... | collective-permute-start | bytes 1572872 | tf_op jit(solution)/shard_map/ppermute | solution.py:442
  9.7 2.5 %collective-permute-start.3 = (bf16[64,768]{1,0:T(8,128)(2,1)S(1)}, bf16[64,768]{1,0:T(8,128)(2,1)S(1)}, u32[]{:S(2)}, u32[]{:S(2)}) collective-permute-start(bf16[64,768]{1,0:T(8,128)(2,1)S(1)} %add_convert_fusion.refs_0_), channel_id=1, source_target_pairs={{0,24},{4,28},{8,16},{12,20},{16,8},{20,12},{24,0},{28,4},{1,25},{... | collective-permute-start | bytes 294920 | tf_op jit(solution)/shard_map/ppermute | solution.py:438
  12.7 0.5 collective-permute-start.1
  13.4 2.3 %collective-permute-done.3.refs_3_ = bf16[64,768]{1,0:T(8,128)(2,1)S(1)} collective-permute-done((bf16[64,768]{1,0:T(8,128)(2,1)S(1)}, bf16[64,768]{1,0:T(8,128)(2,1)S(1)}, u32[]{:S(2)}, u32[]{:S(2)}) %collective-permute-start.3) | collective-permute-done | bytes 98336 | tf_op jit(solution)/shard_map/ppermute | solution.py:438
  15.6 2.0 %collective-permute-done.2.refs_2_ = bf16[64,768]{1,0:T(8,128)(2,1)S(1)} collective-permute-done((bf16[64,768]{1,0:T(8,128)(2,1)S(1)}, bf16[64,768]{1,0:T(8,128)(2,1)S(1)}, u32[]{:S(2)}, u32[]{:S(2)}) %collective-permute-start.2) | collective-permute-done | bytes 98336 | tf_op jit(solution)/shard_map/ppermute | solution.py:438
  17.7 1.9 %right_product.1 = (f32[64,768]{1,0:T(8,128)}, bf16[288,128]{1,0:T(8,128)(2,1)}, bf16[32,16,128]{2,1,0:T(8,128)(2,1)}, bf16[288,128]{1,0:T(8,128)(2,1)}, bf16[28...) custom-call(bf16[64,768]{1,0:T(8,128)(2,1)S(1)} %add_convert_fusion.refs_0_, ...), custom_call_target="tpu_custom_call" | custom-call | flops 1000 | bytes 1000 | tf_op jit(solution)/shard_map/right_product/pallas_call | solution.py:192
  19.6 0.6 copy-done.3
  20.2 4.9 %all-to-all-start = ((bf16[32,16,128]{2,1,0:T(8,128)(2,1)}), bf16[32,16,128]{2,1,0:T(8,128)(2,1)S(1)}, u32[]{:S(2)}, u32[]{:S(2)}) async-start(bf16[32,16,128]{2,1,0:T(8,128)(2,1)} %get-tuple-element.32), calls=%async_computation | async-start | bytes 262144 | tf_op jit(solution)/shard_map/all_to_all | solution.py:473
  25.1 3.7 %collective-permute-start.9 = (bf16[1,128,2048]{2,1,0:T(8,128)(2,1)}, bf16[1,128,2048]{2,1,0:T(8,128)(2,1)}, u32[]{:S(2)}, u32[]{:S(2)}) collective-permute-start(bf16[1,128,2048]{2,1,0:T(8,128)(2,1)} %refs_4_.1), channel_id=1, source_target_pairs={{0,3},{1,0},{2,1},{3,2},{4,7},{5,4},{6,5},{7,6},{8,11},{9,8},{10,9... | collective-permute-start | bytes 1572872 | tf_op jit(solution)/shard_map/ppermute | solution.py:442
  28.8 4.9 %all-to-all-done.share_ref = bf16[32,16,128]{2,1,0:T(8,128)(2,1)S(1)} async-done(((bf16[32,16,128]{2,1,0:T(8,128)(2,1)}), bf16[32,16,128]{2,1,0:T(8,128)(2,1)S(1)}, u32[]{:S(2)}, u32[]{:S(2)}) %all-to-all-start) | async-done | bytes 131104 | tf_op jit(solution)/shard_map/all_to_all | solution.py:473
  33.7 0.7 fold.1
  34.4 4.6 %all-to-all-start.1 = ((bf16[32,16,128]{2,1,0:T(8,128)(2,1)}), bf16[32,16,128]{2,1,0:T(8,128)(2,1)S(1)}, u32[]{:S(2)}, u32[]{:S(2)}) async-start(bf16[32,16,128]{2,1,0:T(8,128)(2,1)} %fold.1), calls=%async_computation.1 | async-start | bytes 262144 | tf_op jit(solution)/shard_map/all_to_all | solution.py:474
  39.1 1.8 %collective-permute-start.4 = (bf16[288,128]{1,0:T(8,128)(2,1)}, bf16[288,128]{1,0:T(8,128)(2,1)S(1)}, u32[]{:S(2)}, u32[]{:S(2)}) collective-permute-start(bf16[288,128]{1,0:T(8,128)(2,1)} %get-tuple-element.27), channel_id=1, source_target_pairs={{0,1},{1,2},{2,3},{3,0},{4,5},{5,6},{6,7},{7,4},{8,9},{9,10},{10,1... | collective-permute-start | bytes 221192 | tf_op jit(solution)/shard_map/ppermute | solution.py:442
  40.9 2.4 %collective-permute-start.5 = (bf16[288,128]{1,0:T(8,128)(2,1)}, bf16[288,128]{1,0:T(8,128)(2,1)S(1)}, u32[]{:S(2)}, u32[]{:S(2)}) collective-permute-start(bf16[288,128]{1,0:T(8,128)(2,1)} %get-tuple-element.28), channel_id=1, source_target_pairs={{0,2},{1,3},{2,0},{3,1},{4,6},{5,7},{6,4},{7,5},{8,10},{9,11},{10,... | collective-permute-start | bytes 221192 | tf_op jit(solution)/shard_map/ppermute | solution.py:442
  43.3 1.4 %collective-permute-start.6 = (bf16[288,128]{1,0:T(8,128)(2,1)}, bf16[288,128]{1,0:T(8,128)(2,1)S(1)}, u32[]{:S(2)}, u32[]{:S(2)}) collective-permute-start(bf16[288,128]{1,0:T(8,128)(2,1)} %copy-done.3), channel_id=1, source_target_pairs={{0,3},{1,0},{2,1},{3,2},{4,7},{5,4},{6,5},{7,6},{8,11},{9,8},{10,9... | collective-permute-start | bytes 221192 | tf_op jit(solution)/shard_map/ppermute | solution.py:442
  44.7 13.9 %collective-permute-done.4.refs_1_ = bf16[288,128]{1,0:T(8,128)(2,1)S(1)} collective-permute-done((bf16[288,128]{1,0:T(8,128)(2,1)}, bf16[288,128]{1,0:T(8,128)(2,1)S(1)}, u32[]{:S(2)}, u32[]{:S(2)}) %collective-permute-start.4) | collective-permute-done | bytes 73760 | tf_op jit(solution)/shard_map/ppermute | solution.py:442
  58.6 3.2 %collective-permute-done.5.refs_2_ = bf16[288,128]{1,0:T(8,128)(2,1)S(1)} collective-permute-done((bf16[288,128]{1,0:T(8,128)(2,1)}, bf16[288,128]{1,0:T(8,128)(2,1)S(1)}, u32[]{:S(2)}, u32[]{:S(2)}) %collective-permute-start.5) | collective-permute-done | bytes 73760 | tf_op jit(solution)/shard_map/ppermute | solution.py:442
  61.9 4.0 %inverse_factor.1 = (f32[64,64]{1,0:T(8,128)S(1)}, bf16[768,64]{1,0:T(8,128)(2,1)S(1)}) custom-call(bf16[288,128]{1,0:T(8,128)(2,1)} %get-tuple-element.26.refs_0_, bf16[288,128]{1,0:T(8,128)(2,1)S(1)} %collective-permute-done.4.refs_1_, bf16[288,128]{1,0:T(8,128)(2,1)S(1)} %collective-permute-done.5.refs_2_, ...), custom_call_target="tpu_custom_call" | custom-call | flops 1000 | bytes 1000 | tf_op jit(solution)/shard_map/inverse_factor/pallas_call | solution.py:280
  65.9 0.7 copy-done.1
  66.5 0.9 %copy-done.2 = bf16[768,64]{1,0:T(8,128)(2,1)S(1)} copy-done((bf16[768,64]{1,0:T(8,128)(2,1)S(1)}, bf16[768,64]{1,0:T(8,128)(2,1)}, u32[]{:S(2)}) %copy-start.2) | copy-done | bytes 98328
  67.5 1.6 %finish.1 = (f32[64,1024]{1,0:T(8,128)}, bf16[1,768,1024]{2,1,0:T(8,128)(2,1)}) custom-call(f32[64,64]{1,0:T(8,128)S(1)} %get-tuple-element.31.w_ref, bf16[32,16,128]{2,1,0:T(8,128)(2,1)S(1)} %all-to-all-done.1.chunk_ref, bf16[768,64]{1,0:T(8,128)(2,1)S(1)} %copy-done.2, f32[768,1024]{1,0:T(8,128)S(1)} %get-tuple-element.24.refs_4_.merged_ref), custom_call_target="tpu_custom_call" | custom-call | flops 1000 | bytes 1000 | tf_op jit(solution)/shard_map/finish/pallas_call | solution.py:327
  69.1 4.6 %expert_step.1 = (f32[1,192,2048]{2,1,0:T(8,128)}, f32[1,192,2048]{2,1,0:T(8,128)}, bf16[1,192,2048]{2,1,0:T(8,128)(2,1)}) custom-call(bf16[288,128]{1,0:T(8,128)(2,1)} %get-tuple-element.26.refs_0_, bf16[288,128]{1,0:T(8,128)(2,1)S(1)} %collective-permute-done.4.refs_1_, bf16[288,128]{1,0:T(8,128)(2,1)S(1)} %collective-permute-done.5.refs_2_, ...), custom_call_target="tpu_custom_call" | custom-call | flops 1000 | bytes 1000 | tf_op jit(solution)/shard_map/expert_step/pallas_call | solution.py:409
  (16 shorter events, 0.7 us)
Async XLA Ops:
  0.6 12.6 %copy-start = (bf16[1,128,768]{2,1,0:T(8,128)(2,1)S(1)}, bf16[1,128,768]{2,1,0:T(8,128)(2,1)}, u32[]{:S(2)}) copy-start(bf16[1,128,768]{2,1,0:T(8,128)(2,1)} %hidden_ref) | copy-start | bytes 589828
  6.5 3.2 %collective-permute-start = (f32[64,768]{1,0:T(8,128)S(1)}, f32[64,768]{1,0:T(8,128)S(1)}, u32[]{:S(2)}, u32[]{:S(2)}) collective-permute-start(f32[64,768]{1,0:T(8,128)S(1)} %get-tuple-element.23), channel_id=1, source_target_pairs={{0,4},{4,0},{8,12},{12,8},{16,20},{20,16},{24,28},{28,24},{1,5},{5... | collective-permute-start | bytes 589832 | tf_op jit(solution)/shard_map/ppermute | solution.py:438
  7.0 27.4 %collective-permute-start.7 = (bf16[1,128,2048]{2,1,0:T(8,128)(2,1)}, bf16[1,128,2048]{2,1,0:T(8,128)(2,1)}, u32[]{:S(2)}, u32[]{:S(2)}) collective-permute-start(bf16[1,128,2048]{2,1,0:T(8,128)(2,1)} %refs_4_.1), channel_id=1, source_target_pairs={{0,1},{1,2},{2,3},{3,0},{4,5},{5,6},{6,7},{7,4},{8,9},{9,10},{10,1... | collective-permute-start | bytes 1572872 | tf_op jit(solution)/shard_map/ppermute | solution.py:442
  9.7 5.9 %collective-permute-start.3 = (bf16[64,768]{1,0:T(8,128)(2,1)S(1)}, bf16[64,768]{1,0:T(8,128)(2,1)S(1)}, u32[]{:S(2)}, u32[]{:S(2)}) collective-permute-start(bf16[64,768]{1,0:T(8,128)(2,1)S(1)} %add_convert_fusion.refs_0_), channel_id=1, source_target_pairs={{0,24},{4,28},{8,16},{12,20},{16,8},{20,12},{24,0},{28,4},{1,25},{... | collective-permute-start | bytes 294920 | tf_op jit(solution)/shard_map/ppermute | solution.py:438
  12.2 5.4 %collective-permute-start.2 = (bf16[64,768]{1,0:T(8,128)(2,1)S(1)}, bf16[64,768]{1,0:T(8,128)(2,1)S(1)}, u32[]{:S(2)}, u32[]{:S(2)}) collective-permute-start(bf16[64,768]{1,0:T(8,128)(2,1)S(1)} %add_convert_fusion.refs_0_), channel_id=1, source_target_pairs={{0,16},{4,20},{8,24},{12,28},{16,0},{20,4},{24,8},{28,12},{1,17},{... | collective-permute-start | bytes 294920 | tf_op jit(solution)/shard_map/ppermute | solution.py:438
  12.7 5.0 %collective-permute-start.1 = (bf16[64,768]{1,0:T(8,128)(2,1)S(1)}, bf16[64,768]{1,0:T(8,128)(2,1)S(1)}, u32[]{:S(2)}, u32[]{:S(2)}) collective-permute-start(bf16[64,768]{1,0:T(8,128)(2,1)S(1)} %add_convert_fusion.refs_0_), channel_id=1, source_target_pairs={{0,8},{4,12},{8,0},{12,4},{16,24},{20,28},{24,16},{28,20},{1,9},{5... | collective-permute-start | bytes 294920 | tf_op jit(solution)/shard_map/ppermute | solution.py:438
  19.6 0.6 copy-start.3
  20.2 13.5 %all-to-all-start = ((bf16[32,16,128]{2,1,0:T(8,128)(2,1)}), bf16[32,16,128]{2,1,0:T(8,128)(2,1)S(1)}, u32[]{:S(2)}, u32[]{:S(2)}) async-start(bf16[32,16,128]{2,1,0:T(8,128)(2,1)} %get-tuple-element.32), calls=%async_computation | async-start | bytes 262144 | tf_op jit(solution)/shard_map/all_to_all | solution.py:473
  25.1 43.9 %collective-permute-start.9 = (bf16[1,128,2048]{2,1,0:T(8,128)(2,1)}, bf16[1,128,2048]{2,1,0:T(8,128)(2,1)}, u32[]{:S(2)}, u32[]{:S(2)}) collective-permute-start(bf16[1,128,2048]{2,1,0:T(8,128)(2,1)} %refs_4_.1), channel_id=1, source_target_pairs={{0,3},{1,0},{2,1},{3,2},{4,7},{5,4},{6,5},{7,6},{8,11},{9,8},{10,9... | collective-permute-start | bytes 1572872 | tf_op jit(solution)/shard_map/ppermute | solution.py:442
  34.4 34.6 %collective-permute-start.8 = (bf16[1,128,2048]{2,1,0:T(8,128)(2,1)}, bf16[1,128,2048]{2,1,0:T(8,128)(2,1)}, u32[]{:S(2)}, u32[]{:S(2)}) collective-permute-start(bf16[1,128,2048]{2,1,0:T(8,128)(2,1)} %collective-permute-done.7.refs_5_), channel_id=1, source_target_pairs={{0,1},{1,2},{2,3},{3,0},{4,5},{5,6},{6,7},{7,4},{8,9},{9,10},{10,1... | collective-permute-start | bytes 1572872 | tf_op jit(solution)/shard_map/ppermute | solution.py:442
  34.4 32.1 %all-to-all-start.1 = ((bf16[32,16,128]{2,1,0:T(8,128)(2,1)}), bf16[32,16,128]{2,1,0:T(8,128)(2,1)S(1)}, u32[]{:S(2)}, u32[]{:S(2)}) async-start(bf16[32,16,128]{2,1,0:T(8,128)(2,1)} %fold.1), calls=%async_computation.1 | async-start | bytes 262144 | tf_op jit(solution)/shard_map/all_to_all | solution.py:474
  39.1 19.6 %collective-permute-start.4 = (bf16[288,128]{1,0:T(8,128)(2,1)}, bf16[288,128]{1,0:T(8,128)(2,1)S(1)}, u32[]{:S(2)}, u32[]{:S(2)}) collective-permute-start(bf16[288,128]{1,0:T(8,128)(2,1)} %get-tuple-element.27), channel_id=1, source_target_pairs={{0,1},{1,2},{2,3},{3,0},{4,5},{5,6},{6,7},{7,4},{8,9},{9,10},{10,1... | collective-permute-start | bytes 221192 | tf_op jit(solution)/shard_map/ppermute | solution.py:442
  40.9 21.0 %collective-permute-start.5 = (bf16[288,128]{1,0:T(8,128)(2,1)}, bf16[288,128]{1,0:T(8,128)(2,1)S(1)}, u32[]{:S(2)}, u32[]{:S(2)}) collective-permute-start(bf16[288,128]{1,0:T(8,128)(2,1)} %get-tuple-element.28), channel_id=1, source_target_pairs={{0,2},{1,3},{2,0},{3,1},{4,6},{5,7},{6,4},{7,5},{8,10},{9,11},{10,... | collective-permute-start | bytes 221192 | tf_op jit(solution)/shard_map/ppermute | solution.py:442
  43.3 18.5 %collective-permute-start.6 = (bf16[288,128]{1,0:T(8,128)(2,1)}, bf16[288,128]{1,0:T(8,128)(2,1)S(1)}, u32[]{:S(2)}, u32[]{:S(2)}) collective-permute-start(bf16[288,128]{1,0:T(8,128)(2,1)} %copy-done.3), channel_id=1, source_target_pairs={{0,3},{1,0},{2,1},{3,2},{4,7},{5,4},{6,5},{7,6},{8,11},{9,8},{10,9... | collective-permute-start | bytes 221192 | tf_op jit(solution)/shard_map/ppermute | solution.py:442
  65.9 0.7 copy-start.1
  66.5 0.9 %copy-start.2 = (bf16[768,64]{1,0:T(8,128)(2,1)S(1)}, bf16[768,64]{1,0:T(8,128)(2,1)}, u32[]{:S(2)}) copy-start(bf16[768,64]{1,0:T(8,128)(2,1)} %copy-done.1) | copy-start | bytes 294916

commit v5 on v4

--- a/solution.py
+++ b/solution.py
@@ -48,57 +48,11 @@
     return out[:rows] + out[rows:]
 
 
-def merge_kernel(block, acts_hbm, kv_hbm, err_hbm, vt_hbm, merged_ref, lt_ref, acts, kv, err, vt, sems):
-    tokens, rows = acts.shape
-    part = tokens // 4
-    half = tokens // 2
-    count = rows // block
-
-    def acts_copy(i):
-        here = slice(i * block, (i + 1) * block)
-        return pltpu.make_async_copy(acts_hbm.at[:, here], acts.at[:, here], sems.at[5 + i])
-
-    def err_copy(i):
-        here = slice(i * block, (i + 1) * block)
-        return pltpu.make_async_copy(err_hbm.at[0, here, :], err.at[here, :], sems.at[5 + count + i])
-
-    def kv_copy(i):
-        here = slice(i * part, (i + 1) * part)
-        return pltpu.make_async_copy(kv_hbm.at[here, :], kv.at[here, :], sems.at[i])
-
-    vt_copy = pltpu.make_async_copy(vt_hbm, vt, sems.at[4])
-    acts_copy(0).start()
-    for i in range(4):
-        kv_copy(i).start()
-    err_copy(0).start()
-    vt_copy.start()
-    for i in range(count):
-        here = slice(i * block, (i + 1) * block)
-        acts_copy(i).wait()
-        if i == 0:
-            kv_copy(0).wait()
-            kv_copy(1).wait()
-            for later in range(1, count):
-                acts_copy(later).start()
-                err_copy(later).start()
-            merged = lax.dot_general(
-                acts[:half, here], kv[:half, :], ROWS_FIRST, preferred_element_type=F32
-            )
-            kv_copy(2).wait()
-            kv_copy(3).wait()
-            merged = merged + lax.dot_general(
-                acts[half:, here], kv[half:, :], ROWS_FIRST, preferred_element_type=F32
-            )
-        else:
-            merged = lax.dot_general(acts[:, here], kv[...], ROWS_FIRST, preferred_element_type=F32)
-        err_copy(i).wait()
-        merged = merged + err[here, :].astype(F32)
-        merged_ref[here, :] = merged
-        if i == 0:
-            vt_copy.wait()
-            both = jnp.concatenate(split_two(vt[...]), axis=0)
-        left = lax.dot_general(merged.astype(BF16), both, COLS_LAST, preferred_element_type=F32).T
-        lt_ref[:, here] = left[: left.shape[0] // 2] + left[left.shape[0] // 2 :]
+def merge_kernel(acts_ref, kv_ref, err_ref, vt_ref, merged_ref, lt_ref):
+    merged = lax.dot_general(acts_ref[...], kv_ref[...], ROWS_FIRST, preferred_element_type=F32)
+    merged = merged + err_ref[0].astype(F32)
+    merged_ref[...] = merged
+    lt_ref[...] = left_times(vt_ref[...], merged.astype(BF16), COLS_LAST)
 
 
 def merge(acts, kv, err, vt):
@@ -107,54 +61,66 @@
     rank = vt.shape[0]
     block = 256
     return pl.pallas_call(
-        functools.partial(merge_kernel, block),
-        in_specs=[HBM] * 4,
-        out_specs=[VMEM] * 2,
+        merge_kernel,
+        grid=(rows // block,),
+        in_specs=[
+            pl.BlockSpec((tokens, block), lambda i: (0, i)),
+            pl.BlockSpec((tokens, cols), lambda i: (0, 0)),
+            pl.BlockSpec((1, block, cols), lambda i: (0, i, 0)),
+            pl.BlockSpec((rank, cols), lambda i: (0, 0)),
+        ],
+        out_specs=[
+            pl.BlockSpec((block, cols), lambda i: (i, 0)),
+            pl.BlockSpec((rank, block), lambda i: (0, i)),
+        ],
         out_shape=[
             jax.ShapeDtypeStruct((rows, cols), F32),
             jax.ShapeDtypeStruct((rank, rows), F32),
         ],
-        scratch_shapes=[
-            pltpu.VMEM((tokens, rows), BF16),
-            pltpu.VMEM((tokens, cols), BF16),
-            pltpu.VMEM((rows, cols), BF16),
-            pltpu.VMEM((rank, cols), F32),
-            pltpu.SemaphoreType.DMA((5 + 2 * (rows // block),)),
-        ],
         compiler_params=params(24),
         cost_estimate=SMALL,
         name="merge",
-    )(*in_hbm(acts, kv, err, vt))
-
-
-def slab_kernel(hidden_ref, slab_ref):
-    slab_ref[...] = hidden_ref[0].T.reshape(slab_ref.shape)
-
-
-def unit_slabs(hidden, parts):
+    )(*[pltpu.with_memory_space_constraint(x, pltpu.HBM) for x in (acts, kv, err, vt)])
+
+
+def slab_kernel(hidden_ref, own_ref, *refs):
+    send_refs, all_ref = refs[:-1], refs[-1]
+    n_exp = all_ref.shape[0]
+    all_ref[...] = hidden_ref[0].T.reshape(all_ref.shape)
+    place = lax.axis_index("exp")
+    for k, ref in enumerate((own_ref,) + tuple(send_refs)):
+        ref[...] = all_ref[lax.rem(place + k, n_exp)]
+
+
+def unit_slabs(hidden, n_exp):
     _, tokens, units = hidden.shape
+    slab = (units // n_exp, tokens)
     return pl.pallas_call(
         slab_kernel,
-        out_shape=jax.ShapeDtypeStruct((parts, units // parts, tokens), BF16),
+        out_shape=[jax.ShapeDtypeStruct(slab, BF16)] * n_exp,
+        scratch_shapes=[pltpu.VMEM((n_exp,) + slab, BF16)],
         compiler_params=params(8),
         cost_estimate=SMALL,
         name="unit_slabs",
     )(hidden)
 
 
-def right_kernel(n_parts, n_exp, *refs):
-    part_refs, merged_ref, slab_ref = refs[:n_parts], refs[n_parts], refs[n_parts + 1]
-    lt_hbm, own_hbm, chunk_ref = refs[n_parts + 2 : n_parts + 5]
-    load_refs = refs[n_parts + 5 : n_parts + 4 + n_exp]
-    lt_ref, own_ref, sems = refs[n_parts + 4 + n_exp :]
+def right_kernel(n_parts, *refs):
+    part_refs, merged_ref = refs[:n_parts], refs[n_parts]
+    lt_ref, gram_ref, chunk_ref = refs[n_parts + 1 :]
     parts = [ref[...].astype(F32) for ref in part_refs]
     while len(parts) > 1:
         parts = [a + b for a, b in zip(parts[0::2], parts[1::2])]
     lt = parts[0]
     rank = lt.shape[0]
     lt_ref[...] = lt
-    lt_copy = pltpu.make_async_copy(lt_ref, lt_hbm, sems.at[0])
-    lt_copy.start()
+    product = left_times(lt, merged_ref[...].astype(BF16), (((1,), (0,)), ((), ()))).astype(BF16)
+    across = product.shape[1] // TILE_C
+    for a in range(rank // TILE_R):
+        for b in range(across):
+            chunk_ref[a * across + b] = product[
+                a * TILE_R : (a + 1) * TILE_R, b * TILE_C : (b + 1) * TILE_C
+            ]
     gram = lax.dot_general(lt, lt, COLS_LAST, precision=HIGHEST, preferred_element_type=F32)
     half = rank // 2
     packed = jnp.concatenate([gram[:half], gram[half:]], axis=1)
@@ -162,52 +128,26 @@
     rest = packed - high.astype(F32)
     middle = rest.astype(BF16)
     low = (rest - middle.astype(F32)).astype(BF16)
-    place = lax.axis_index("exp")
-    units = slab_ref.shape[1]
-    for k, load_ref in enumerate((own_ref,) + tuple(load_refs)):
-        load_ref[0:units] = slab_ref[lax.rem(place + k, n_exp)]
-        load_ref[units : units + half] = high
-        load_ref[units + half : units + 2 * half] = middle
-        load_ref[units + 2 * half : units + 3 * half] = low
-    own_copy = pltpu.make_async_copy(own_ref, own_hbm, sems.at[1])
-    own_copy.start()
-    product = left_times(lt, merged_ref[...].astype(BF16), (((1,), (0,)), ((), ()))).astype(BF16)
-    across = product.shape[1] // TILE_C
-    for a in range(rank // TILE_R):
-        for b in range(across):
-            chunk_ref[a * across + b] = product[
-                a * TILE_R : (a + 1) * TILE_R, b * TILE_C : (b + 1) * TILE_C
-            ]
-    lt_copy.wait()
-    own_copy.wait()
-
-
-def right_product(parts, merged, slabs):
+    gram_ref[0:half] = high
+    gram_ref[half : 2 * half] = middle
+    gram_ref[2 * half : 3 * half] = low
+
+
+def right_product(parts, merged):
     rank, rows = parts[0].shape
     cols = merged.shape[1]
     chunks = rank * cols // (TILE_R * TILE_C)
-    n_exp, units, tokens = slabs.shape
-    assert tokens == 2 * rank
-    load = (units + 3 * (rank // 2), tokens)
-    out = pl.pallas_call(
-        functools.partial(right_kernel, len(parts), n_exp),
-        out_specs=[HBM, HBM] + [VMEM] * n_exp,
+    return pl.pallas_call(
+        functools.partial(right_kernel, len(parts)),
         out_shape=[
-            pltpu.HBM((rank, rows), F32),
-            pltpu.HBM(load, BF16),
+            jax.ShapeDtypeStruct((rank, rows), F32),
+            jax.ShapeDtypeStruct((3 * (rank // 2), 2 * rank), BF16),
             jax.ShapeDtypeStruct((chunks, TILE_R, TILE_C), BF16),
-        ]
-        + [jax.ShapeDtypeStruct(load, BF16)] * (n_exp - 1),
-        scratch_shapes=[
-            pltpu.VMEM((rank, rows), F32),
-            pltpu.VMEM(load, BF16),
-            pltpu.SemaphoreType.DMA((2,)),
         ],
         compiler_params=params(16),
         cost_estimate=SMALL,
         name="right_product",
-    )(*parts, merged, slabs)
-    return out[0], out[2], [out[1]] + list(out[3:])
+    )(*parts, merged)
 
 
 def fold_kernel(share_ref, out_ref):
@@ -234,9 +174,8 @@
     w_ref, basis_ref, terms_ref, lt_ref, wide_ref, sems = refs[n_exp + 1 :]
     rank = lt_ref.shape[0]
     half = rank // 2
-    units = load_hbms[0].shape[0] - 3 * half
     copies = [
-        pltpu.make_async_copy(load_hbms[k].at[units : units + 3 * half], terms_ref.at[k], sems.at[k])
+        pltpu.make_async_copy(load_hbms[k], terms_ref.at[k], sems.at[k])
         for k in range(n_exp)
     ]
     lt_copy = pltpu.make_async_copy(lt_hbm, lt_ref, sems.at[n_exp])
@@ -279,7 +218,7 @@
     n_exp = len(loads)
     return pl.pallas_call(
         functools.partial(inverse_kernel, n_exp),
-        in_specs=[HBM] + [ANY] * (n_exp - 1) + [HBM],
+        in_specs=[ANY] * (n_exp + 1),
         out_shape=[
             jax.ShapeDtypeStruct((rank, rank), F32),
             jax.ShapeDtypeStruct((rows, rank), BF16),
@@ -293,22 +232,30 @@
         compiler_params=params(8),
         cost_estimate=SMALL,
         name="inverse_factor",
-    )(*in_hbm(loads[0]), *loads[1:], *in_hbm(lt))
-
-
-def finish_kernel(replicas, w_ref, chunk_ref, basis_ref, merged_ref, right_hbm, err_hbm, right_ref, err_ref, sems):
+    )(*loads, lt)
+
+
+def finish_kernel(
+    replicas, w_any, chunk_ref, basis_any, merged_ref, right_hbm, err_hbm, w_ref, basis_ref, right_ref, err_ref, sems
+):
     rank, cols = right_ref.shape
+    rows, block = err_ref.shape[0], 128
+    w_copy = pltpu.make_async_copy(w_any, w_ref, sems.at[rows // block + 1])
+    w_copy.start()
+    basis_copy = pltpu.make_async_copy(basis_any, basis_ref, sems.at[rows // block + 2])
+    basis_copy.start()
     across = cols // TILE_C
     pieces = []
     for a in range(rank // TILE_R):
         pieces.append(jnp.concatenate([chunk_ref[a * across + b] for b in range(across)], axis=1))
     product = jnp.concatenate(pieces, axis=0)
+    w_copy.wait()
     new_right = left_times(w_ref[...], product, (((1,), (0,)), ((), ()))) * (1.0 / replicas)
     right_ref[...] = new_right
     copies = [pltpu.make_async_copy(right_ref, right_hbm, sems.at[0])]
     copies[0].start()
     rounded = new_right.astype(BF16)
-    rows, block = err_ref.shape[0], 128
+    basis_copy.wait()
     for i in range(rows // block):
         here = slice(i * block, (i + 1) * block)
         approx = jnp.dot(basis_ref[here, :], rounded, preferred_element_type=F32)
@@ -326,15 +273,18 @@
     cols = merged.shape[1]
     return pl.pallas_call(
         functools.partial(finish_kernel, replicas),
+        in_specs=[ANY, VMEM, ANY, VMEM],
         out_specs=[HBM] * 2,
         out_shape=[
             jax.ShapeDtypeStruct((rank, cols), F32),
             jax.ShapeDtypeStruct((1, rows, cols), BF16),
         ],
         scratch_shapes=[
+            pltpu.VMEM((rank, rank), F32),
+            pltpu.VMEM((rows, rank), BF16),
             pltpu.VMEM((rank, cols), F32),
             pltpu.VMEM((rows, cols), BF16),
-            pltpu.SemaphoreType.DMA((rows // 128 + 1,)),
+            pltpu.SemaphoreType.DMA((rows // 128 + 3,)),
         ],
         compiler_params=params(16),
         cost_estimate=SMALL,
@@ -351,7 +301,7 @@
     count = width // chunk
 
     slabs = [
-        pltpu.make_async_copy(load_hbms[k].at[0:units], hid.at[k], in_sems.at[count, k])
+        pltpu.make_async_copy(load_hbms[k], hid.at[k], in_sems.at[count, k])
         for k in range(n_exp)
     ]
 
@@ -408,7 +358,7 @@
     tokens = grads[0].shape[1]
     return pl.pallas_call(
         functools.partial(expert_kernel, n_exp, chunk),
-        in_specs=([HBM] + [ANY] * (n_exp - 1)) * 2 + [HBM] * 2,
+        in_specs=[ANY] * n_exp + [HBM] + [ANY] * (n_exp - 1) + [HBM] * 2,
         out_specs=[HBM] * 3,
         out_shape=[
             jax.ShapeDtypeStruct((1, units, width), F32),
@@ -430,7 +380,7 @@
         cost_estimate=SMALL,
         name="expert_step",
     )(
-        *in_hbm(slabs[0]), *slabs[1:], *in_hbm(grads[0]), *grads[1:], *in_hbm(moment_one, moment_two)
+        *slabs, *in_hbm(grads[0]), *grads[1:], *in_hbm(moment_one, moment_two)
     )
 
 
@@ -448,12 +398,12 @@
 
 def body(n_rep, n_exp, activations, kv_grad, errors, right_factor, hidden, out_grad, moment_one, moment_two):
     grads = {0: out_grad, 1: shift(out_grad, n_exp, 1)}
+    if n_exp > 2:
+        grads[n_exp - 1] = shift(out_grad, n_exp, -1)
     merged, lt = merge(activations, kv_grad, errors, right_factor.T)
 
     lt = (lt + swap(lt, "rep", n_rep, 1)).astype(BF16)
     slabs = unit_slabs(after(hidden, lt), n_exp)
-    if n_exp > 2:
-        grads[n_exp - 1] = shift(after(out_grad, slabs), n_exp, -1)
     bit = 2
     parts = [lt]
     while bit < n_rep:
@@ -463,18 +413,21 @@
         masks = [bit] if 2 * bit >= n_rep else [bit, 2 * bit, 3 * bit]
         parts = [own] + [swap(own, "rep", n_rep, m) for m in masks]
         bit *= len(parts)
-    lt, chunks, loads = right_product(parts, merged, slabs)
-
-    loads = [loads[0]] + [shift(loads[k], n_exp, k) for k in range(1, n_exp)]
-    w, basis = inverse_factor(loads, lt)
+    lt, gram, chunks = right_product(parts, merged)
+
+    slabs = [slabs[0]] + [shift(after(slabs[k], gram), n_exp, k) for k in range(1, n_exp)]
+    grams = [gram] + [shift(gram, n_exp, k) for k in range(1, n_exp)]
 
     if chunks.shape[0] == n_rep * n_exp:
         both = ("rep", "exp")
-        share = fold(lax.all_to_all(chunks, both, 0, 0, tiled=True))
+        shares = lax.all_to_all(chunks, both, 0, 0, tiled=True)
+        shares, grams, grads = lax.optimization_barrier((shares, grams, grads))
+        share = fold(shares)
         chunks = lax.all_to_all(share, both, 0, 0, tiled=True)
     else:
         share = chunks
         chunks = lax.psum(chunks.astype(F32), ("rep", "exp")).astype(BF16)
+    w, basis = inverse_factor(grams, lt)
 
     left, right = 1, n_exp - 1
     while right - left > 1:
@@ -487,7 +440,7 @@
 
     new_right, new_error = finish(n_rep, w, chunks, basis, merged)
     first_new, second_new, step = expert_step(
-        loads, [grads[k] for k in range(n_exp)], moment_one, moment_two
+        slabs, [grads[k] for k in range(n_exp)], moment_one, moment_two
     )
     return new_error, new_right.T, first_new, second_new, step
 

time: 73.9 us -> 69.9 us (0.946)
  waiting for transfers between devices: 26.4 us -> 16.7 us
  local copies, waits for them, and re-layouts: 2.23 us -> 7.03 us
  starting transfers between devices: 25.5 us -> 27.6 us
  Pallas kernels: 18.7 us -> 17.3 us
    ppermute x6 -> x9, waiting for transfers between devices: 17.1 us -> 11.1 us  [shift(): return lax.ppermute(x, 'exp', [(i, (i + k) % size) for i in range(size)])]
    all_to_all x1, waiting for transfers between devices: 4.95 us -> 0.01 us  [body(): shares = lax.all_to_all(chunks, both, 0, 0, tiled=True)]
    unnamed x8 -> x24, local copies, waits for them, and re-layouts: 2.23 us -> 7.03 us
    ppermute x6 -> x9, starting transfers between devices: 12 us -> 14.9 us  [shift(): return lax.ppermute(x, 'exp', [(i, (i + k) % size) for i in range(size)])]
    all_to_all x1, starting transfers between devices: 4.86 us -> 3.24 us  [body(): shares = lax.all_to_all(chunks, both, 0, 0, tiled=True)]
    pallas_call x6, Pallas kernels: 18 us -> 16.7 us  [the longest x1 5.22 us: merge(): pl.pallas_call(merge_kernel, grid=(rows // block,), in_specs=[pl.BlockSpe...]
    all_to_all x1, waiting for transfers between devices: 0.01 us -> 1.22 us  [body(): chunks = lax.all_to_all(share, both, 0, 0, tiled=True)]
  transfers between devices with their start and end apart: 12 -> 15, of which waited for: 6 -> 7; matrix products, arithmetic and copies ran while one was open for 0% -> 0% of each run, Pallas kernels for 11% -> 10%
where the time goes in v5:
time: 69.9 us; the launch traced here: 69.4 us
  starting transfers between devices  27.6 us (39%)
  Pallas kernels  17.3 us (25%)
  waiting for transfers between devices  16.7 us (24%)
  local copies, waits for them, and re-layouts  7.03 us (10%)
  between operations  0.72 us (1%)
    ppermute x9, starting transfers between devices, shift(): return lax.ppermute(x, 'exp', [(i, (i + k) % size) for i in range(size)])  14.9 us
    ppermute x9, waiting for transfers between devices, shift(): return lax.ppermute(x, 'exp', [(i, (i + k) % size) for i in range(size)])  11.1 us
    unnamed x24, local copies, waits for them, and re-layouts  7.03 us
    all_to_all x1, starting transfers between devices, body(): chunks = lax.all_to_all(share, both, 0, 0, tiled=True)  5.35 us
    pallas_call x1, Pallas kernels, merge(): pl.pallas_call(merge_kernel, grid=(rows // block,), in_specs=[pl.BlockSpe...  5.22 us
    pallas_call x1, Pallas kernels, expert_step(): pl.pallas_call(functools.partial(expert_kernel, n_exp, chunk), in_specs=[...  4.51 us
    ppermute x4, waiting for transfers between devices, swap(): return lax.ppermute(x, axis, [(i, i ^ mask) for i in range(size)])  4.36 us
    ppermute x4, starting transfers between devices, swap(): return lax.ppermute(x, axis, [(i, i ^ mask) for i in range(size)])  4.07 us
  transfers between devices with their start and end apart: 15, of which 7 were waited for; matrix products, arithmetic and copies ran while one was open for 0% of the time, Pallas kernels for 10%

profile of v5, /device:TPU:0, one launch (start us, length us, event | category | flops | bytes accessed | tf_op | source)
XLA Modules:
  0.0 69.4 jit_solution(672123161729845031)
XLA Ops:
  0.6 5.2 %merge.1 = (f32[768,1024]{1,0:T(8,128)S(1)}, f32[64,768]{1,0:T(8,128)S(1)}) custom-call(bf16[1024,768]{1,0:T(8,128)(2,1)} %acts_ref.1, bf16[1024,1024]{1,0:T(8,128)(2,1)} %kv_ref.1, bf16[1,768,1024]{2,1,0:T(8,128)(2,1)} %err_ref.1, f32[64,1024]{1,0:T(8,128)} %bitcast.2), custom_call_target="tpu_custom_call" | custom-call | flops 1000 | bytes 1000 | tf_op jit(solution)/shard_map/merge/pallas_call | solution.py:63
  6.4 2.6 %collective-permute-start.7 = (bf16[1,128,2048]{2,1,0:T(8,128)(2,1)}, bf16[1,128,2048]{2,1,0:T(8,128)(2,1)}, u32[]{:S(2)}, u32[]{:S(2)}) collective-permute-start(bf16[1,128,2048]{2,1,0:T(8,128)(2,1)} %refs_4_), channel_id=1, source_target_pairs={{0,1},{1,2},{2,3},{3,0},{4,5},{5,6},{6,7},{7,4},{8,9},{9,10},{10,1... | collective-permute-start | bytes 1572872 | tf_op jit(solution)/shard_map/ppermute | solution.py:392
  9.0 2.1 %collective-permute-start.8 = (bf16[1,128,2048]{2,1,0:T(8,128)(2,1)}, bf16[1,128,2048]{2,1,0:T(8,128)(2,1)}, u32[]{:S(2)}, u32[]{:S(2)}) collective-permute-start(bf16[1,128,2048]{2,1,0:T(8,128)(2,1)} %refs_4_), channel_id=1, source_target_pairs={{0,3},{1,0},{2,1},{3,2},{4,7},{5,4},{6,5},{7,6},{8,11},{9,8},{10,9... | collective-permute-start | bytes 1572872 | tf_op jit(solution)/shard_map/ppermute | solution.py:392
  11.2 2.6 %collective-permute-start.3 = (bf16[64,768]{1,0:T(8,128)(2,1)S(1)}, bf16[64,768]{1,0:T(8,128)(2,1)S(1)}, u32[]{:S(2)}, u32[]{:S(2)}) collective-permute-start(bf16[64,768]{1,0:T(8,128)(2,1)S(1)} %add_convert_fusion.refs_0_), channel_id=1, source_target_pairs={{0,24},{4,28},{8,16},{12,20},{16,8},{20,12},{24,0},{28,4},{1,25},{... | collective-permute-start | bytes 294920 | tf_op jit(solution)/shard_map/ppermute | solution.py:388
  14.7 2.3 %collective-permute-done.3.refs_3_ = bf16[64,768]{1,0:T(8,128)(2,1)S(1)} collective-permute-done((bf16[64,768]{1,0:T(8,128)(2,1)S(1)}, bf16[64,768]{1,0:T(8,128)(2,1)S(1)}, u32[]{:S(2)}, u32[]{:S(2)}) %collective-permute-start.3) | collective-permute-done | bytes 98336 | tf_op jit(solution)/shard_map/ppermute | solution.py:388
  17.0 2.0 %collective-permute-done.2.refs_2_ = bf16[64,768]{1,0:T(8,128)(2,1)S(1)} collective-permute-done((bf16[64,768]{1,0:T(8,128)(2,1)S(1)}, bf16[64,768]{1,0:T(8,128)(2,1)S(1)}, u32[]{:S(2)}, u32[]{:S(2)}) %collective-permute-start.2) | collective-permute-done | bytes 98336 | tf_op jit(solution)/shard_map/ppermute | solution.py:388
  21.0 3.2 %all-to-all-start = ((bf16[32,16,128]{2,1,0:T(8,128)(2,1)}), bf16[32,16,128]{2,1,0:T(8,128)(2,1)S(1)}, u32[]{:S(2)}, u32[]{:S(2)}) async-start(bf16[32,16,128]{2,1,0:T(8,128)(2,1)} %copy-done.3), calls=%async_computation | async-start | bytes 262144 | tf_op jit(solution)/shard_map/all_to_all | solution.py:423
  24.3 3.7 %collective-permute-start.6 = (bf16[96,128]{1,0:T(8,128)(2,1)S(1)}, bf16[96,128]{1,0:T(8,128)(2,1)S(1)}, u32[]{:S(2)}, u32[]{:S(2)}) collective-permute-start(bf16[96,128]{1,0:T(8,128)(2,1)S(1)} %get-tuple-element.38.refs_0_), channel_id=1, source_target_pairs={{0,3},{1,0},{2,1},{3,2},{4,7},{5,4},{6,5},{7,6},{8,11},{9,8},{10,9... | collective-permute-start | bytes 73736 | tf_op jit(solution)/shard_map/ppermute | solution.py:392
  28.0 1.1 %collective-permute-start.4 = (bf16[96,128]{1,0:T(8,128)(2,1)S(1)}, bf16[96,128]{1,0:T(8,128)(2,1)S(1)}, u32[]{:S(2)}, u32[]{:S(2)}) collective-permute-start(bf16[96,128]{1,0:T(8,128)(2,1)S(1)} %get-tuple-element.38.refs_0_), channel_id=1, source_target_pairs={{0,1},{1,2},{2,3},{3,0},{4,5},{5,6},{6,7},{7,4},{8,9},{9,10},{10,1... | collective-permute-start | bytes 73736 | tf_op jit(solution)/shard_map/ppermute | solution.py:392
  29.0 7.3 %collective-permute-done.6.refs_3_ = bf16[96,128]{1,0:T(8,128)(2,1)S(1)} collective-permute-done((bf16[96,128]{1,0:T(8,128)(2,1)S(1)}, bf16[96,128]{1,0:T(8,128)(2,1)S(1)}, u32[]{:S(2)}, u32[]{:S(2)}) %collective-permute-start.6) | collective-permute-done | bytes 24608 | tf_op jit(solution)/shard_map/ppermute | solution.py:392
  36.9 3.0 %collective-permute-done.5.refs_2_ = bf16[96,128]{1,0:T(8,128)(2,1)S(1)} collective-permute-done((bf16[96,128]{1,0:T(8,128)(2,1)S(1)}, bf16[96,128]{1,0:T(8,128)(2,1)S(1)}, u32[]{:S(2)}, u32[]{:S(2)}) %collective-permute-start.5) | collective-permute-done | bytes 24608 | tf_op jit(solution)/shard_map/ppermute | solution.py:392
  42.6 5.4 %all-to-all-start.1 = ((bf16[32,16,128]{2,1,0:T(8,128)(2,1)}), bf16[32,16,128]{2,1,0:T(8,128)(2,1)S(1)}, u32[]{:S(2)}, u32[]{:S(2)}) async-start(bf16[32,16,128]{2,1,0:T(8,128)(2,1)} %fold.1), calls=%async_computation.1 | async-start | bytes 262144 | tf_op jit(solution)/shard_map/all_to_all | solution.py:426
  48.0 0.8 %unit_slabs.1 = (bf16[192,128]{1,0:T(8,128)(2,1)S(1)}, bf16[192,128]{1,0:T(8,128)(2,1)}, bf16[192,128]{1,0:T(8,128)(2,1)}, bf16[192,128]{1,0:T(8,128)(2,1)}) custom-call(bf16[1,128,768]{2,1,0:T(8,128)(2,1)S(1)} %copy-done), custom_call_target="tpu_custom_call" | custom-call | flops 1000 | bytes 1000 | tf_op jit(solution)/shard_map/unit_slabs/pallas_call | solution.py:98
  48.7 3.6 %collective-permute-start.11 = (bf16[192,128]{1,0:T(8,128)(2,1)}, bf16[192,128]{1,0:T(8,128)(2,1)}, u32[]{:S(2)}, u32[]{:S(2)}) collective-permute-start(bf16[192,128]{1,0:T(8,128)(2,1)} %get-tuple-element.55), channel_id=1, source_target_pairs={{0,3},{1,0},{2,1},{3,2},{4,7},{5,4},{6,5},{7,6},{8,11},{9,8},{10,9... | collective-permute-start | bytes 147464 | tf_op jit(solution)/shard_map/ppermute | solution.py:392
  52.4 1.1 %collective-permute-start.9 = (bf16[192,128]{1,0:T(8,128)(2,1)}, bf16[192,128]{1,0:T(8,128)(2,1)}, u32[]{:S(2)}, u32[]{:S(2)}) collective-permute-start(bf16[192,128]{1,0:T(8,128)(2,1)} %get-tuple-element.51), channel_id=1, source_target_pairs={{0,1},{1,2},{2,3},{3,0},{4,5},{5,6},{6,7},{7,4},{8,9},{9,10},{10,1... | collective-permute-start | bytes 147464 | tf_op jit(solution)/shard_map/ppermute | solution.py:392
  53.4 0.9 %copy-done.2 = f32[64,768]{1,0:T(8,128)S(1)} copy-done((f32[64,768]{1,0:T(8,128)S(1)}, f32[64,768]{1,0:T(8,128)}, u32[]{:S(2)}) %copy-start.2) | copy-done | bytes 196632
  54.4 0.7 %copy-done.5 = bf16[96,128]{1,0:T(8,128)(2,1)S(1)} copy-done((bf16[96,128]{1,0:T(8,128)(2,1)S(1)}, bf16[96,128]{1,0:T(8,128)(2,1)}, u32[]{:S(2)}) %copy-start.5) | copy-done | bytes 24600
  55.1 0.7 %copy-done.7 = bf16[96,128]{1,0:T(8,128)(2,1)S(1)} copy-done((bf16[96,128]{1,0:T(8,128)(2,1)S(1)}, bf16[96,128]{1,0:T(8,128)(2,1)}, u32[]{:S(2)}) %copy-start.7) | copy-done | bytes 24600
  55.8 0.7 %copy-done.9 = bf16[96,128]{1,0:T(8,128)(2,1)S(1)} copy-done((bf16[96,128]{1,0:T(8,128)(2,1)S(1)}, bf16[96,128]{1,0:T(8,128)(2,1)}, u32[]{:S(2)}) %copy-start.9) | copy-done | bytes 24600
  57.3 3.6 %inverse_factor.1 = (f32[64,64]{1,0:T(8,128)S(1)}, bf16[768,64]{1,0:T(8,128)(2,1)S(1)}) custom-call(bf16[96,128]{1,0:T(8,128)(2,1)S(1)} %copy-done.5, bf16[96,128]{1,0:T(8,128)(2,1)S(1)} %copy-done.11, bf16[96,128]{1,0:T(8,128)(2,1)S(1)} %copy-done.9, bf16[96,128]{1,0:T(8,128)(2,1)S(1)} %copy-done.7, f32[64,768]{1,0:T(8,128)S(1)} %copy-done.2), custom_call_target="tpu_custom_call" | custom-call | flops 1000 | bytes 1000 | tf_op jit(solution)/shard_map/inverse_factor/pallas_call | solution.py:219
  60.9 1.2 %all-to-all-done.1.chunk_ref = bf16[32,16,128]{2,1,0:T(8,128)(2,1)S(1)} async-done(((bf16[32,16,128]{2,1,0:T(8,128)(2,1)}), bf16[32,16,128]{2,1,0:T(8,128)(2,1)S(1)}, u32[]{:S(2)}, u32[]{:S(2)}) %all-to-all-start.1) | async-done | bytes 131104 | tf_op jit(solution)/shard_map/all_to_all | solution.py:426
  62.2 1.9 %finish.1 = (f32[64,1024]{1,0:T(8,128)}, bf16[1,768,1024]{2,1,0:T(8,128)(2,1)}) custom-call(f32[64,64]{1,0:T(8,128)S(1)} %get-tuple-element.43.w_any, bf16[32,16,128]{2,1,0:T(8,128)(2,1)S(1)} %all-to-all-done.1.chunk_ref, bf16[768,64]{1,0:T(8,128)(2,1)S(1)} %get-tuple-element.45.basis_any, f32[768,1024]{1,0:T(8,128)S(1)} %get-tuple-element.35.refs_4_.merged_ref), custom_call_target="tpu_custom_call" | custom-call | flops 1000 | bytes 1000 | tf_op jit(solution)/shard_map/finish/pallas_call | solution.py:274
  64.1 0.8 %collective-permute-done.10.refs_2_ = bf16[192,128]{1,0:T(8,128)(2,1)} collective-permute-done((bf16[192,128]{1,0:T(8,128)(2,1)}, bf16[192,128]{1,0:T(8,128)(2,1)}, u32[]{:S(2)}, u32[]{:S(2)}) %collective-permute-start.10) | collective-permute-done | bytes 49184 | tf_op jit(solution)/shard_map/ppermute | solution.py:392
  64.9 4.5 %expert_step.1 = (f32[1,192,2048]{2,1,0:T(8,128)}, f32[1,192,2048]{2,1,0:T(8,128)}, bf16[1,192,2048]{2,1,0:T(8,128)(2,1)}) custom-call(bf16[192,128]{1,0:T(8,128)(2,1)S(1)} %get-tuple-element.49.refs_0_, bf16[192,128]{1,0:T(8,128)(2,1)} %collective-permute-done.9.refs_1_, bf16[192,128]{1,0:T(8,128)(2,1)} %collective-permute-done.10.refs_2_, ...), custom_call_target="tpu_custom_call" | custom-call | flops 1000 | bytes 1000 | tf_op jit(solution)/shard_map/expert_step/pallas_call | solution.py:359
  (38 shorter events, 7.5 us)
Async XLA Ops:
  5.9 5.3 %collective-permute-start = (f32[64,768]{1,0:T(8,128)S(1)}, f32[64,768]{1,0:T(8,128)S(1)}, u32[]{:S(2)}, u32[]{:S(2)}) collective-permute-start(f32[64,768]{1,0:T(8,128)S(1)} %get-tuple-element.34), channel_id=1, source_target_pairs={{0,4},{4,0},{8,12},{12,8},{16,20},{20,16},{24,28},{28,24},{1,5},{5... | collective-permute-start | bytes 589832 | tf_op jit(solution)/shard_map/ppermute | solution.py:388
  6.4 34.8 %collective-permute-start.7 = (bf16[1,128,2048]{2,1,0:T(8,128)(2,1)}, bf16[1,128,2048]{2,1,0:T(8,128)(2,1)}, u32[]{:S(2)}, u32[]{:S(2)}) collective-permute-start(bf16[1,128,2048]{2,1,0:T(8,128)(2,1)} %refs_4_), channel_id=1, source_target_pairs={{0,1},{1,2},{2,3},{3,0},{4,5},{5,6},{6,7},{7,4},{8,9},{9,10},{10,1... | collective-permute-start | bytes 1572872 | tf_op jit(solution)/shard_map/ppermute | solution.py:392
  9.0 32.1 %collective-permute-start.8 = (bf16[1,128,2048]{2,1,0:T(8,128)(2,1)}, bf16[1,128,2048]{2,1,0:T(8,128)(2,1)}, u32[]{:S(2)}, u32[]{:S(2)}) collective-permute-start(bf16[1,128,2048]{2,1,0:T(8,128)(2,1)} %refs_4_), channel_id=1, source_target_pairs={{0,3},{1,0},{2,1},{3,2},{4,7},{5,4},{6,5},{7,6},{8,11},{9,8},{10,9... | collective-permute-start | bytes 1572872 | tf_op jit(solution)/shard_map/ppermute | solution.py:392
  11.2 5.8 %collective-permute-start.3 = (bf16[64,768]{1,0:T(8,128)(2,1)S(1)}, bf16[64,768]{1,0:T(8,128)(2,1)S(1)}, u32[]{:S(2)}, u32[]{:S(2)}) collective-permute-start(bf16[64,768]{1,0:T(8,128)(2,1)S(1)} %add_convert_fusion.refs_0_), channel_id=1, source_target_pairs={{0,24},{4,28},{8,16},{12,20},{16,8},{20,12},{24,0},{28,4},{1,25},{... | collective-permute-start | bytes 294920 | tf_op jit(solution)/shard_map/ppermute | solution.py:388
  13.8 5.2 %collective-permute-start.2 = (bf16[64,768]{1,0:T(8,128)(2,1)S(1)}, bf16[64,768]{1,0:T(8,128)(2,1)S(1)}, u32[]{:S(2)}, u32[]{:S(2)}) collective-permute-start(bf16[64,768]{1,0:T(8,128)(2,1)S(1)} %add_convert_fusion.refs_0_), channel_id=1, source_target_pairs={{0,16},{4,20},{8,24},{12,28},{16,0},{20,4},{24,8},{28,12},{1,17},{... | collective-permute-start | bytes 294920 | tf_op jit(solution)/shard_map/ppermute | solution.py:388
  14.3 4.8 %collective-permute-start.1 = (bf16[64,768]{1,0:T(8,128)(2,1)S(1)}, bf16[64,768]{1,0:T(8,128)(2,1)S(1)}, u32[]{:S(2)}, u32[]{:S(2)}) collective-permute-start(bf16[64,768]{1,0:T(8,128)(2,1)S(1)} %add_convert_fusion.refs_0_), channel_id=1, source_target_pairs={{0,8},{4,12},{8,0},{12,4},{16,24},{20,28},{24,16},{28,20},{1,9},{5... | collective-permute-start | bytes 294920 | tf_op jit(solution)/shard_map/ppermute | solution.py:388
  19.1 28.9 %copy-start = (bf16[1,128,768]{2,1,0:T(8,128)(2,1)S(1)}, bf16[1,128,768]{2,1,0:T(8,128)(2,1)}, u32[]{:S(2)}) copy-start(bf16[1,128,768]{2,1,0:T(8,128)(2,1)} %hidden_ref) | copy-start | bytes 589828
  19.7 0.7 copy-start.1
  20.4 0.7 copy-start.3
  21.0 21.5 %copy-start.4 = (bf16[96,128]{1,0:T(8,128)(2,1)}, bf16[96,128]{1,0:T(8,128)(2,1)S(1)}, u32[]{:S(2)}) copy-start(bf16[96,128]{1,0:T(8,128)(2,1)S(1)} %get-tuple-element.38.refs_0_) | copy-start | bytes 73732
  21.0 20.1 %all-to-all-start = ((bf16[32,16,128]{2,1,0:T(8,128)(2,1)}), bf16[32,16,128]{2,1,0:T(8,128)(2,1)S(1)}, u32[]{:S(2)}, u32[]{:S(2)}) async-start(bf16[32,16,128]{2,1,0:T(8,128)(2,1)} %copy-done.3), calls=%async_computation | async-start | bytes 262144 | tf_op jit(solution)/shard_map/all_to_all | solution.py:423
  24.3 12.1 %collective-permute-start.6 = (bf16[96,128]{1,0:T(8,128)(2,1)S(1)}, bf16[96,128]{1,0:T(8,128)(2,1)S(1)}, u32[]{:S(2)}, u32[]{:S(2)}) collective-permute-start(bf16[96,128]{1,0:T(8,128)(2,1)S(1)} %get-tuple-element.38.refs_0_), channel_id=1, source_target_pairs={{0,3},{1,0},{2,1},{3,2},{4,7},{5,4},{6,5},{7,6},{8,11},{9,8},{10,9... | collective-permute-start | bytes 73736 | tf_op jit(solution)/shard_map/ppermute | solution.py:392
  28.0 12.0 %collective-permute-start.5 = (bf16[96,128]{1,0:T(8,128)(2,1)S(1)}, bf16[96,128]{1,0:T(8,128)(2,1)S(1)}, u32[]{:S(2)}, u32[]{:S(2)}) collective-permute-start(bf16[96,128]{1,0:T(8,128)(2,1)S(1)} %get-tuple-element.38.refs_0_), channel_id=1, source_target_pairs={{0,2},{1,3},{2,0},{3,1},{4,6},{5,7},{6,4},{7,5},{8,10},{9,11},{10,... | collective-permute-start | bytes 73736 | tf_op jit(solution)/shard_map/ppermute | solution.py:392
  28.0 12.6 %collective-permute-start.4 = (bf16[96,128]{1,0:T(8,128)(2,1)S(1)}, bf16[96,128]{1,0:T(8,128)(2,1)S(1)}, u32[]{:S(2)}, u32[]{:S(2)}) collective-permute-start(bf16[96,128]{1,0:T(8,128)(2,1)S(1)} %get-tuple-element.38.refs_0_), channel_id=1, source_target_pairs={{0,1},{1,2},{2,3},{3,0},{4,5},{5,6},{6,7},{7,4},{8,9},{9,10},{10,1... | collective-permute-start | bytes 73736 | tf_op jit(solution)/shard_map/ppermute | solution.py:392
  41.9 23.0 %collective-permute-start.12 = (bf16[1,128,2048]{2,1,0:T(8,128)(2,1)}, bf16[1,128,2048]{2,1,0:T(8,128)(2,1)}, u32[]{:S(2)}, u32[]{:S(2)}) collective-permute-start(bf16[1,128,2048]{2,1,0:T(8,128)(2,1)} %collective-permute-done.7.refs_5_), channel_id=1, source_target_pairs={{0,1},{1,2},{2,3},{3,0},{4,5},{5,6},{6,7},{7,4},{8,9},{9,10},{10,1... | collective-permute-start | bytes 1572872 | tf_op jit(solution)/shard_map/ppermute | solution.py:392
  42.6 19.6 %all-to-all-start.1 = ((bf16[32,16,128]{2,1,0:T(8,128)(2,1)}), bf16[32,16,128]{2,1,0:T(8,128)(2,1)S(1)}, u32[]{:S(2)}, u32[]{:S(2)}) async-start(bf16[32,16,128]{2,1,0:T(8,128)(2,1)} %fold.1), calls=%async_computation.1 | async-start | bytes 262144 | tf_op jit(solution)/shard_map/all_to_all | solution.py:426
  48.7 15.3 %collective-permute-start.11 = (bf16[192,128]{1,0:T(8,128)(2,1)}, bf16[192,128]{1,0:T(8,128)(2,1)}, u32[]{:S(2)}, u32[]{:S(2)}) collective-permute-start(bf16[192,128]{1,0:T(8,128)(2,1)} %get-tuple-element.55), channel_id=1, source_target_pairs={{0,3},{1,0},{2,1},{3,2},{4,7},{5,4},{6,5},{7,6},{8,11},{9,8},{10,9... | collective-permute-start | bytes 147464 | tf_op jit(solution)/shard_map/ppermute | solution.py:392
  52.4 12.5 %collective-permute-start.10 = (bf16[192,128]{1,0:T(8,128)(2,1)}, bf16[192,128]{1,0:T(8,128)(2,1)}, u32[]{:S(2)}, u32[]{:S(2)}) collective-permute-start(bf16[192,128]{1,0:T(8,128)(2,1)} %get-tuple-element.53), channel_id=1, source_target_pairs={{0,2},{1,3},{2,0},{3,1},{4,6},{5,7},{6,4},{7,5},{8,10},{9,11},{10,... | collective-permute-start | bytes 147464 | tf_op jit(solution)/shard_map/ppermute | solution.py:392
  52.4 12.5 %collective-permute-start.9 = (bf16[192,128]{1,0:T(8,128)(2,1)}, bf16[192,128]{1,0:T(8,128)(2,1)}, u32[]{:S(2)}, u32[]{:S(2)}) collective-permute-start(bf16[192,128]{1,0:T(8,128)(2,1)} %get-tuple-element.51), channel_id=1, source_target_pairs={{0,1},{1,2},{2,3},{3,0},{4,5},{5,6},{6,7},{7,4},{8,9},{9,10},{10,1... | collective-permute-start | bytes 147464 | tf_op jit(solution)/shard_map/ppermute | solution.py:392
  53.4 0.9 %copy-start.2 = (f32[64,768]{1,0:T(8,128)S(1)}, f32[64,768]{1,0:T(8,128)}, u32[]{:S(2)}) copy-start(f32[64,768]{1,0:T(8,128)} %copy-done.1) | copy-start | bytes 589828
  54.4 0.7 %copy-start.5 = (bf16[96,128]{1,0:T(8,128)(2,1)S(1)}, bf16[96,128]{1,0:T(8,128)(2,1)}, u32[]{:S(2)}) copy-start(bf16[96,128]{1,0:T(8,128)(2,1)} %copy-done.4) | copy-start | bytes 73732
  55.1 0.7 %copy-start.7 = (bf16[96,128]{1,0:T(8,128)(2,1)S(1)}, bf16[96,128]{1,0:T(8,128)(2,1)}, u32[]{:S(2)}) copy-start(bf16[96,128]{1,0:T(8,128)(2,1)} %copy-done.6) | copy-start | bytes 73732
  55.8 0.7 %copy-start.9 = (bf16[96,128]{1,0:T(8,128)(2,1)S(1)}, bf16[96,128]{1,0:T(8,128)(2,1)}, u32[]{:S(2)}) copy-start(bf16[96,128]{1,0:T(8,128)(2,1)} %copy-done.8) | copy-start | bytes 73732
  56.6 0.7 %copy-start.11 = (bf16[96,128]{1,0:T(8,128)(2,1)S(1)}, bf16[96,128]{1,0:T(8,128)(2,1)}, u32[]{:S(2)}) copy-start(bf16[96,128]{1,0:T(8,128)(2,1)} %copy-done.10) | copy-start | bytes 73732
  (3 other events, 1.8 us)

commit v6 on v5

--- a/solution.py
+++ b/solution.py
@@ -107,20 +107,22 @@
 
 def right_kernel(n_parts, *refs):
     part_refs, merged_ref = refs[:n_parts], refs[n_parts]
-    lt_ref, gram_ref, chunk_ref = refs[n_parts + 1 :]
+    lt_ref, gram_ref, keep_ref, send_ref, all_ref = refs[n_parts + 1 :]
     parts = [ref[...].astype(F32) for ref in part_refs]
     while len(parts) > 1:
         parts = [a + b for a, b in zip(parts[0::2], parts[1::2])]
     lt = parts[0]
     rank = lt.shape[0]
     lt_ref[...] = lt
-    product = left_times(lt, merged_ref[...].astype(BF16), (((1,), (0,)), ((), ()))).astype(BF16)
+    product = left_times(lt, merged_ref[...].astype(BF16), (((1,), (0,)), ((), ())))
     across = product.shape[1] // TILE_C
     for a in range(rank // TILE_R):
         for b in range(across):
-            chunk_ref[a * across + b] = product[
+            at = (a * across + b) * TILE_R
+            all_ref[at : at + TILE_R, :] = product[
                 a * TILE_R : (a + 1) * TILE_R, b * TILE_C : (b + 1) * TILE_C
             ]
+    cut(0, all_ref, keep_ref, send_ref)
     gram = lax.dot_general(lt, lt, COLS_LAST, precision=HIGHEST, preferred_element_type=F32)
     half = rank // 2
     packed = jnp.concatenate([gram[:half], gram[half:]], axis=1)
@@ -133,40 +135,117 @@
     gram_ref[2 * half : 3 * half] = low
 
 
+def my_bit(bit):
+    return lax.rem(lax.axis_index("rep") // (1 << bit), 2)
+
+
+def rows_of(which, count):
+    return pl.ds(pl.multiple_of(which * count, count), count)
+
+
+def cut(bit, all_ref, keep_ref, send_ref):
+    half = keep_ref.shape[0]
+    mine = my_bit(bit)
+    keep_ref[...] = all_ref[rows_of(mine, half), :]
+    send_ref[...] = all_ref[rows_of(1 - mine, half), :].astype(BF16)
+
+
 def right_product(parts, merged):
     rank, rows = parts[0].shape
     cols = merged.shape[1]
-    chunks = rank * cols // (TILE_R * TILE_C)
+    tall = rank * cols // TILE_C
     return pl.pallas_call(
         functools.partial(right_kernel, len(parts)),
         out_shape=[
             jax.ShapeDtypeStruct((rank, rows), F32),
             jax.ShapeDtypeStruct((3 * (rank // 2), 2 * rank), BF16),
-            jax.ShapeDtypeStruct((chunks, TILE_R, TILE_C), BF16),
-        ],
+            jax.ShapeDtypeStruct((tall // 2, TILE_C), F32),
+            jax.ShapeDtypeStruct((tall // 2, TILE_C), BF16),
+        ],
+        scratch_shapes=[pltpu.VMEM((tall, TILE_C), F32)],
         compiler_params=params(16),
         cost_estimate=SMALL,
         name="right_product",
     )(*parts, merged)
 
 
-def fold_kernel(share_ref, out_ref):
-    total = share_ref[0].astype(F32)
-    for i in range(1, share_ref.shape[0]):
-        total = total + share_ref[i].astype(F32)
-    total = total.astype(BF16)
-    for i in range(out_ref.shape[0]):
-        out_ref[i] = total
-
-
-def fold(shares):
-    return pl.pallas_call(
-        fold_kernel,
-        out_shape=jax.ShapeDtypeStruct(shares.shape, BF16),
+def halve_kernel(bit, keep_ref, got_ref, next_ref, send_ref, all_ref):
+    all_ref[...] = keep_ref[...] + got_ref[...].astype(F32)
+    cut(bit, all_ref, next_ref, send_ref)
+
+
+def halve(bit, keep, got):
+    rows = keep.shape[0]
+    return pl.pallas_call(
+        functools.partial(halve_kernel, bit),
+        out_shape=[
+            jax.ShapeDtypeStruct((rows // 2, TILE_C), F32),
+            jax.ShapeDtypeStruct((rows // 2, TILE_C), BF16),
+        ],
+        scratch_shapes=[pltpu.VMEM((rows, TILE_C), F32)],
         compiler_params=params(4),
         cost_estimate=SMALL,
-        name="fold",
-    )(shares)
+        name="halve",
+    )(keep, got)
+
+
+def load_kernel(keep_ref, got_ref, gram_ref, load_ref):
+    terms = gram_ref.shape[0]
+    load_ref[0:terms] = gram_ref[...]
+    load_ref[terms:] = (keep_ref[...] + got_ref[...].astype(F32)).astype(BF16)
+
+
+def line_load(keep, got, gram):
+    return pl.pallas_call(
+        load_kernel,
+        out_shape=jax.ShapeDtypeStruct((gram.shape[0] + keep.shape[0], TILE_C), BF16),
+        compiler_params=params(4),
+        cost_estimate=SMALL,
+        name="line_load",
+    )(keep, got, gram)
+
+
+def line_kernel(terms, *refs):
+    load_refs, out_ref, parts_ref = refs[:-2], refs[-2], refs[-1]
+    n_exp = len(load_refs)
+    for k in range(n_exp):
+        parts_ref[k] = load_refs[k][terms:].astype(F32)
+    place = lax.axis_index("exp")
+    total = None
+    for j in range(n_exp):
+        part = parts_ref[lax.rem(place + n_exp - j, n_exp)]
+        total = part if total is None else total + part
+    out_ref[...] = total.astype(BF16)
+
+
+def line_sum(loads, terms):
+    rows = loads[0].shape[0] - terms
+    return pl.pallas_call(
+        functools.partial(line_kernel, terms),
+        out_shape=jax.ShapeDtypeStruct((rows, TILE_C), BF16),
+        scratch_shapes=[pltpu.VMEM((len(loads), rows, TILE_C), F32)],
+        compiler_params=params(4),
+        cost_estimate=SMALL,
+        name="line_sum",
+    )(*loads)
+
+
+def double_kernel(bit, own_ref, got_ref, out_ref):
+    half = own_ref.shape[0]
+    mine = my_bit(bit)
+    out_ref[rows_of(mine, half), :] = own_ref[...]
+    out_ref[rows_of(1 - mine, half), :] = got_ref[...]
+
+
+def double(bit, own, got):
+    rows = own.shape[0]
+    return pl.pallas_call(
+        functools.partial(double_kernel, bit),
+        out_shape=jax.ShapeDtypeStruct((2 * rows, TILE_C), BF16),
+        compiler_params=params(4),
+        cost_estimate=SMALL,
+        name="double",
+    )(own, got)
 
 
 def inverse_kernel(n_exp, *refs):
@@ -175,7 +254,7 @@
     rank = lt_ref.shape[0]
     half = rank // 2
     copies = [
-        pltpu.make_async_copy(load_hbms[k], terms_ref.at[k], sems.at[k])
+        pltpu.make_async_copy(load_hbms[k].at[0 : 3 * half], terms_ref.at[k], sems.at[k])
         for k in range(n_exp)
     ]
     lt_copy = pltpu.make_async_copy(lt_hbm, lt_ref, sems.at[n_exp])
@@ -236,26 +315,22 @@
 
 
 def finish_kernel(
-    replicas, w_any, chunk_ref, basis_any, merged_ref, right_hbm, err_hbm, w_ref, basis_ref, right_ref, err_ref, sems
+    replicas, w_ref, own_ref, got_ref, basis_ref, merged_ref, right_hbm, err_hbm, all_ref, right_ref, err_ref, sems
 ):
     rank, cols = right_ref.shape
     rows, block = err_ref.shape[0], 128
-    w_copy = pltpu.make_async_copy(w_any, w_ref, sems.at[rows // block + 1])
-    w_copy.start()
-    basis_copy = pltpu.make_async_copy(basis_any, basis_ref, sems.at[rows // block + 2])
-    basis_copy.start()
+    double_kernel(0, own_ref, got_ref, all_ref)
     across = cols // TILE_C
     pieces = []
     for a in range(rank // TILE_R):
-        pieces.append(jnp.concatenate([chunk_ref[a * across + b] for b in range(across)], axis=1))
+        at = [(a * across + b) * TILE_R for b in range(across)]
+        pieces.append(jnp.concatenate([all_ref[i : i + TILE_R, :] for i in at], axis=1))
     product = jnp.concatenate(pieces, axis=0)
-    w_copy.wait()
     new_right = left_times(w_ref[...], product, (((1,), (0,)), ((), ()))) * (1.0 / replicas)
     right_ref[...] = new_right
     copies = [pltpu.make_async_copy(right_ref, right_hbm, sems.at[0])]
     copies[0].start()
     rounded = new_right.astype(BF16)
-    basis_copy.wait()
     for i in range(rows // block):
         here = slice(i * block, (i + 1) * block)
         approx = jnp.dot(basis_ref[here, :], rounded, preferred_element_type=F32)
@@ -268,28 +343,27 @@
         copy.wait()
 
 
-def finish(replicas, w, chunks, basis, merged):
+def finish(replicas, w, own, got, basis, merged):
     rows, rank = basis.shape
     cols = merged.shape[1]
     return pl.pallas_call(
         functools.partial(finish_kernel, replicas),
-        in_specs=[ANY, VMEM, ANY, VMEM],
+        in_specs=[VMEM] * 5,
         out_specs=[HBM] * 2,
         out_shape=[
             jax.ShapeDtypeStruct((rank, cols), F32),
             jax.ShapeDtypeStruct((1, rows, cols), BF16),
         ],
         scratch_shapes=[
-            pltpu.VMEM((rank, rank), F32),
-            pltpu.VMEM((rows, rank), BF16),
+            pltpu.VMEM((2 * own.shape[0], TILE_C), BF16),
             pltpu.VMEM((rank, cols), F32),
             pltpu.VMEM((rows, cols), BF16),
-            pltpu.SemaphoreType.DMA((rows // 128 + 3,)),
+            pltpu.SemaphoreType.DMA((rows // 128 + 1,)),
         ],
         compiler_params=params(16),
         cost_estimate=SMALL,
         name="finish",
-    )(w, chunks, basis, merged)
+    )(w, own, got, basis, merged)
 
 
 def expert_kernel(n_exp, chunk, *refs):
@@ -413,21 +487,20 @@
         masks = [bit] if 2 * bit >= n_rep else [bit, 2 * bit, 3 * bit]
         parts = [own] + [swap(own, "rep", n_rep, m) for m in masks]
         bit *= len(parts)
-    lt, gram, chunks = right_product(parts, merged)
-
-    slabs = [slabs[0]] + [shift(after(slabs[k], gram), n_exp, k) for k in range(1, n_exp)]
-    grams = [gram] + [shift(gram, n_exp, k) for k in range(1, n_exp)]
-
-    if chunks.shape[0] == n_rep * n_exp:
-        both = ("rep", "exp")
-        shares = lax.all_to_all(chunks, both, 0, 0, tiled=True)
-        shares, grams, grads = lax.optimization_barrier((shares, grams, grads))
-        share = fold(shares)
-        chunks = lax.all_to_all(share, both, 0, 0, tiled=True)
-    else:
-        share = chunks
-        chunks = lax.psum(chunks.astype(F32), ("rep", "exp")).astype(BF16)
-    w, basis = inverse_factor(grams, lt)
+    parts, grads[1] = lax.optimization_barrier((parts, grads[1]))
+    lt, gram, keep, send = right_product(parts, merged)
+
+    bits = n_rep.bit_length() - 1
+    assert n_rep == 1 << bits and keep.shape[0] >> (bits - 1) >= 8
+    for bit in range(1, bits):
+        keep, send = halve(bit, keep, swap(send, "rep", n_rep, 1 << (bit - 1)))
+    got = swap(send, "rep", n_rep, 1 << (bits - 1))
+    got, grads = lax.optimization_barrier((got, grads))
+
+    load = line_load(keep, got, gram)
+    loads = [load] + [shift(load, n_exp, k) for k in range(1, n_exp)]
+    share = line_sum(loads, gram.shape[0])
+    w, basis = inverse_factor(loads, lt)
 
     left, right = 1, n_exp - 1
     while right - left > 1:
@@ -437,8 +510,11 @@
         else:
             grads[right - 1] = shift(after(grads[right], share), n_exp, -1)
             right -= 1
-
-    new_right, new_error = finish(n_rep, w, chunks, basis, merged)
+    slabs = [slabs[0]] + [shift(after(slabs[k], share), n_exp, k) for k in range(1, n_exp)]
+
+    for bit in range(bits - 1, 0, -1):
+        share = double(bit, share, swap(share, "rep", n_rep, 1 << bit))
+    new_right, new_error = finish(n_rep, w, share, swap(share, "rep", n_rep, 1), basis, merged)
     first_new, second_new, step = expert_step(
         slabs, [grads[k] for k in range(n_exp)], moment_one, moment_two
     )

time: 69.9 us -> 74.8 us (1.070)
  waiting for transfers between devices: 16.7 us -> 24.9 us
  local copies, waits for them, and re-layouts: 7.03 us -> 0.01 us
  starting transfers between devices: 27.6 us -> 33.1 us
  Pallas kernels: 17.3 us -> 15.8 us
    all_to_all x2 -> x0, starting transfers between devices: 8.59 us -> none  [the longest x1 5.35 us: body(): chunks = lax.all_to_all(share, both, 0, 0, tiled=True)]
    ppermute x4 -> x10, waiting for transfers between devices: 4.36 us -> 12.5 us  [swap(): return lax.ppermute(x, axis, [(i, i ^ mask) for i in range(size)])]
    ppermute x9, starting transfers between devices: 14.9 us -> 22.4 us  [shift(): return lax.ppermute(x, 'exp', [(i, (i + k) % size) for i in range(size)])]
    unnamed x24 -> x4, local copies, waits for them, and re-layouts: 7.03 us -> 0.01 us
    ppermute x4 -> x10, starting transfers between devices: 4.07 us -> 10.7 us  [swap(): return lax.ppermute(x, axis, [(i, i ^ mask) for i in range(size)])]
    ppermute x9, waiting for transfers between devices: 11.1 us -> 12.4 us  [shift(): return lax.ppermute(x, 'exp', [(i, (i + k) % size) for i in range(size)])]
    all_to_all x2 -> x0, waiting for transfers between devices: 1.22 us -> none  [the longest x1 1.22 us: body(): chunks = lax.all_to_all(share, both, 0, 0, tiled=True)]
    pallas_call x2 -> x7, Pallas kernels: 2.59 us -> 1.68 us  [the longest x1 1.59 us: finish(): pl.pallas_call(functools.partial(finish_kernel, replicas), in_specs=[VMEM...]
  transfers between devices with their start and end apart: 15 -> 19, of which waited for: 7 -> 13; matrix products, arithmetic and copies ran while one was open for 0% -> 0% of each run, Pallas kernels for 10% -> 8%
where the time goes in v6:
time: 74.8 us; the launch traced here: 74.6 us
  starting transfers between devices  33.1 us (44%)
  waiting for transfers between devices  24.9 us (33%)
  Pallas kernels  15.8 us (21%)
  between operations  0.77 us (1%)
    ppermute x9, starting transfers between devices, shift(): return lax.ppermute(x, 'exp', [(i, (i + k) % size) for i in range(size)])  22.4 us
    ppermute x10, waiting for transfers between devices, swap(): return lax.ppermute(x, axis, [(i, i ^ mask) for i in range(size)])  12.5 us
    ppermute x9, waiting for transfers between devices, shift(): return lax.ppermute(x, 'exp', [(i, (i + k) % size) for i in range(size)])  12.4 us
    ppermute x10, starting transfers between devices, swap(): return lax.ppermute(x, axis, [(i, i ^ mask) for i in range(size)])  10.7 us
    pallas_call x1, Pallas kernels, merge(): pl.pallas_call(merge_kernel, grid=(rows // block,), in_specs=[pl.BlockSpe...  5.26 us
    pallas_call x1, Pallas kernels, expert_step(): pl.pallas_call(functools.partial(expert_kernel, n_exp, chunk), in_specs=[...  4.47 us
    pallas_call x1, Pallas kernels, inverse_factor(): pl.pallas_call(functools.partial(inverse_kernel, n_exp), in_specs=[ANY] *...  3.61 us
    pallas_call x1, Pallas kernels, finish(): pl.pallas_call(functools.partial(finish_kernel, replicas), in_specs=[VMEM...  1.59 us
  transfers between devices with their start and end apart: 19, of which 13 were waited for; matrix products, arithmetic and copies ran while one was open for 0% of the time, Pallas kernels for 8%

profile of v6, /device:TPU:0, one launch (start us, length us, event | category | flops | bytes accessed | tf_op | source)
XLA Modules:
  0.0 74.6 jit_solution(8557747192281921603)
XLA Ops:
  0.6 5.3 %merge.1 = (f32[768,1024]{1,0:T(8,128)S(1)}, f32[64,768]{1,0:T(8,128)S(1)}) custom-call(bf16[1024,768]{1,0:T(8,128)(2,1)} %acts_ref.1, bf16[1024,1024]{1,0:T(8,128)(2,1)} %kv_ref.1, bf16[1,768,1024]{2,1,0:T(8,128)(2,1)} %err_ref.1, f32[64,1024]{1,0:T(8,128)} %bitcast.2), custom_call_target="tpu_custom_call" | custom-call | flops 1000 | bytes 1000 | tf_op jit(solution)/shard_map/merge/pallas_call | solution.py:63
  6.4 2.6 %collective-permute-start.4 = (bf16[1,128,2048]{2,1,0:T(8,128)(2,1)S(1)}, bf16[1,128,2048]{2,1,0:T(8,128)(2,1)S(1)}, u32[]{:S(2)}, u32[]{:S(2)}) collective-permute-start(bf16[1,128,2048]{2,1,0:T(8,128)(2,1)S(1)} %copy-done.1), channel_id=1, source_target_pairs={{0,1},{1,2},{2,3},{3,0},{4,5},{5,6},{6,7},{7,4},{8,9},{9,10},{10,1... | collective-permute-start | bytes 1572872 | tf_op jit(solution)/shard_map/ppermute | solution.py:466
  9.1 2.1 %collective-permute-start.8 = (bf16[1,128,2048]{2,1,0:T(8,128)(2,1)S(1)}, bf16[1,128,2048]{2,1,0:T(8,128)(2,1)S(1)}, u32[]{:S(2)}, u32[]{:S(2)}) collective-permute-start(bf16[1,128,2048]{2,1,0:T(8,128)(2,1)S(1)} %copy-done.1), channel_id=1, source_target_pairs={{0,3},{1,0},{2,1},{3,2},{4,7},{5,4},{6,5},{7,6},{8,11},{9,8},{10,9... | collective-permute-start | bytes 1572872 | tf_op jit(solution)/shard_map/ppermute | solution.py:466
  11.2 2.7 %collective-permute-start.3 = (bf16[64,768]{1,0:T(8,128)(2,1)S(1)}, bf16[64,768]{1,0:T(8,128)(2,1)S(1)}, u32[]{:S(2)}, u32[]{:S(2)}) collective-permute-start(bf16[64,768]{1,0:T(8,128)(2,1)S(1)} %add_convert_fusion.refs_0_), channel_id=1, source_target_pairs={{0,24},{4,28},{8,16},{12,20},{16,8},{20,12},{24,0},{28,4},{1,25},{... | collective-permute-start | bytes 294920 | tf_op jit(solution)/shard_map/ppermute | solution.py:462
  14.8 2.3 %collective-permute-done.3.refs_3_ = bf16[64,768]{1,0:T(8,128)(2,1)S(1)} collective-permute-done((bf16[64,768]{1,0:T(8,128)(2,1)S(1)}, bf16[64,768]{1,0:T(8,128)(2,1)S(1)}, u32[]{:S(2)}, u32[]{:S(2)}) %collective-permute-start.3) | collective-permute-done | bytes 98336 | tf_op jit(solution)/shard_map/ppermute | solution.py:462
  17.1 2.0 %collective-permute-done.2.refs_2_ = bf16[64,768]{1,0:T(8,128)(2,1)S(1)} collective-permute-done((bf16[64,768]{1,0:T(8,128)(2,1)S(1)}, bf16[64,768]{1,0:T(8,128)(2,1)S(1)}, u32[]{:S(2)}, u32[]{:S(2)}) %collective-permute-start.2) | collective-permute-done | bytes 98336 | tf_op jit(solution)/shard_map/ppermute | solution.py:462
  19.1 4.8 %collective-permute-done.4.refs_5_ = bf16[1,128,2048]{2,1,0:T(8,128)(2,1)S(1)} collective-permute-done((bf16[1,128,2048]{2,1,0:T(8,128)(2,1)S(1)}, bf16[1,128,2048]{2,1,0:T(8,128)(2,1)S(1)}, u32[]{:S(2)}, u32[]{:S(2)}) %collective-permute-start.4) | collective-permute-done | bytes 524320 | tf_op jit(solution)/shard_map/ppermute | solution.py:466
  24.6 1.2 %collective-permute-done.5.got_ref = bf16[256,128]{1,0:T(8,128)(2,1)S(1)} collective-permute-done((bf16[256,128]{1,0:T(8,128)(2,1)S(1)}, bf16[256,128]{1,0:T(8,128)(2,1)S(1)}, u32[]{:S(2)}, u32[]{:S(2)}) %collective-permute-start.5) | collective-permute-done | bytes 65568 | tf_op jit(solution)/shard_map/ppermute | solution.py:462
  25.9 1.7 %collective-permute-start.6 = (bf16[128,128]{1,0:T(8,128)(2,1)S(1)}, bf16[128,128]{1,0:T(8,128)(2,1)S(1)}, u32[]{:S(2)}, u32[]{:S(2)}) collective-permute-start(bf16[128,128]{1,0:T(8,128)(2,1)S(1)} %get-tuple-element.49), channel_id=1, source_target_pairs={{0,8},{4,12},{8,0},{12,4},{16,24},{20,28},{24,16},{28,20},{1,9},{5... | collective-permute-start | bytes 98312 | tf_op jit(solution)/shard_map/ppermute | solution.py:462
  27.6 2.3 %collective-permute-done.6.got_ref = bf16[128,128]{1,0:T(8,128)(2,1)S(1)} collective-permute-done((bf16[128,128]{1,0:T(8,128)(2,1)S(1)}, bf16[128,128]{1,0:T(8,128)(2,1)S(1)}, u32[]{:S(2)}, u32[]{:S(2)}) %collective-permute-start.6) | collective-permute-done | bytes 32800 | tf_op jit(solution)/shard_map/ppermute | solution.py:462
  29.9 1.7 %collective-permute-start.7 = (bf16[64,128]{1,0:T(8,128)(2,1)S(1)}, bf16[64,128]{1,0:T(8,128)(2,1)S(1)}, u32[]{:S(2)}, u32[]{:S(2)}) collective-permute-start(bf16[64,128]{1,0:T(8,128)(2,1)S(1)} %get-tuple-element.51), channel_id=1, source_target_pairs={{0,16},{4,20},{8,24},{12,28},{16,0},{20,4},{24,8},{28,12},{1,17},{... | collective-permute-start | bytes 49160 | tf_op jit(solution)/shard_map/ppermute | solution.py:462
  31.6 2.7 %collective-permute-done.8.refs_7_ = bf16[1,128,2048]{2,1,0:T(8,128)(2,1)S(1)} collective-permute-done((bf16[1,128,2048]{2,1,0:T(8,128)(2,1)S(1)}, bf16[1,128,2048]{2,1,0:T(8,128)(2,1)S(1)}, u32[]{:S(2)}, u32[]{:S(2)}) %collective-permute-start.8) | collective-permute-done | bytes 524320 | tf_op jit(solution)/shard_map/ppermute | solution.py:466
  34.3 12.2 %collective-permute-start.11 = (bf16[160,128]{1,0:T(8,128)(2,1)S(1)}, bf16[160,128]{1,0:T(8,128)(2,1)S(1)}, u32[]{:S(2)}, u32[]{:S(2)}) collective-permute-start(bf16[160,128]{1,0:T(8,128)(2,1)S(1)} %line_load.1.refs_0_), channel_id=1, source_target_pairs={{0,3},{1,0},{2,1},{3,2},{4,7},{5,4},{6,5},{7,6},{8,11},{9,8},{10,9... | collective-permute-start | bytes 122888 | tf_op jit(solution)/shard_map/ppermute | solution.py:466
  46.5 1.0 %collective-permute-start.9 = (bf16[160,128]{1,0:T(8,128)(2,1)S(1)}, bf16[160,128]{1,0:T(8,128)(2,1)S(1)}, u32[]{:S(2)}, u32[]{:S(2)}) collective-permute-start(bf16[160,128]{1,0:T(8,128)(2,1)S(1)} %line_load.1.refs_0_), channel_id=1, source_target_pairs={{0,1},{1,2},{2,3},{3,0},{4,5},{5,6},{6,7},{7,4},{8,9},{9,10},{10,1... | collective-permute-start | bytes 122888 | tf_op jit(solution)/shard_map/ppermute | solution.py:466
  48.1 3.2 %collective-permute-done.10.refs_2_ = bf16[160,128]{1,0:T(8,128)(2,1)S(1)} collective-permute-done((bf16[160,128]{1,0:T(8,128)(2,1)S(1)}, bf16[160,128]{1,0:T(8,128)(2,1)S(1)}, u32[]{:S(2)}, u32[]{:S(2)}) %collective-permute-start.10) | collective-permute-done | bytes 40992 | tf_op jit(solution)/shard_map/ppermute | solution.py:466
  51.4 0.9 %collective-permute-done.9.refs_1_ = bf16[160,128]{1,0:T(8,128)(2,1)S(1)} collective-permute-done((bf16[160,128]{1,0:T(8,128)(2,1)S(1)}, bf16[160,128]{1,0:T(8,128)(2,1)S(1)}, u32[]{:S(2)}, u32[]{:S(2)}) %collective-permute-start.9) | collective-permute-done | bytes 40992 | tf_op jit(solution)/shard_map/ppermute | solution.py:466
  52.4 1.6 %collective-permute-start.12 = (bf16[64,128]{1,0:T(8,128)(2,1)S(1)}, bf16[64,128]{1,0:T(8,128)(2,1)S(1)}, u32[]{:S(2)}, u32[]{:S(2)}) collective-permute-start(bf16[64,128]{1,0:T(8,128)(2,1)S(1)} %line_sum.1.own_ref), channel_id=1, source_target_pairs={{0,16},{4,20},{8,24},{12,28},{16,0},{20,4},{24,8},{28,12},{1,17},{... | collective-permute-start | bytes 49160 | tf_op jit(solution)/shard_map/ppermute | solution.py:462
  53.9 2.2 %collective-permute-done.12.got_ref = bf16[64,128]{1,0:T(8,128)(2,1)S(1)} collective-permute-done((bf16[64,128]{1,0:T(8,128)(2,1)S(1)}, bf16[64,128]{1,0:T(8,128)(2,1)S(1)}, u32[]{:S(2)}, u32[]{:S(2)}) %collective-permute-start.12) | collective-permute-done | bytes 16416 | tf_op jit(solution)/shard_map/ppermute | solution.py:462
  56.2 1.5 %collective-permute-start.13 = (bf16[128,128]{1,0:T(8,128)(2,1)S(1)}, bf16[128,128]{1,0:T(8,128)(2,1)S(1)}, u32[]{:S(2)}, u32[]{:S(2)}) collective-permute-start(bf16[128,128]{1,0:T(8,128)(2,1)S(1)} %double.2.own_ref), channel_id=1, source_target_pairs={{0,8},{4,12},{8,0},{12,4},{16,24},{20,28},{24,16},{28,20},{1,9},{5... | collective-permute-start | bytes 98312 | tf_op jit(solution)/shard_map/ppermute | solution.py:462
  57.7 2.4 %collective-permute-done.13.got_ref = bf16[128,128]{1,0:T(8,128)(2,1)S(1)} collective-permute-done((bf16[128,128]{1,0:T(8,128)(2,1)S(1)}, bf16[128,128]{1,0:T(8,128)(2,1)S(1)}, u32[]{:S(2)}, u32[]{:S(2)}) %collective-permute-start.13) | collective-permute-done | bytes 32800 | tf_op jit(solution)/shard_map/ppermute | solution.py:462
  60.3 3.8 %collective-permute-start.17 = (bf16[192,128]{1,0:T(8,128)(2,1)S(1)}, bf16[192,128]{1,0:T(8,128)(2,1)S(1)}, u32[]{:S(2)}, u32[]{:S(2)}) collective-permute-start(bf16[192,128]{1,0:T(8,128)(2,1)S(1)} %get-tuple-element.67), channel_id=1, source_target_pairs={{0,3},{1,0},{2,1},{3,2},{4,7},{5,4},{6,5},{7,6},{8,11},{9,8},{10,9... | collective-permute-start | bytes 147464 | tf_op jit(solution)/shard_map/ppermute | solution.py:466
  64.8 3.6 %inverse_factor.1 = (f32[64,64]{1,0:T(8,128)S(1)}, bf16[768,64]{1,0:T(8,128)(2,1)S(1)}) custom-call(bf16[160,128]{1,0:T(8,128)(2,1)S(1)} %line_load.1.refs_0_, bf16[160,128]{1,0:T(8,128)(2,1)S(1)} %collective-permute-done.9.refs_1_, bf16[160,128]{1,0:T(8,128)(2,1)S(1)} %collective-permute-done.10.refs_2_, ...), custom_call_target="tpu_custom_call" | custom-call | flops 1000 | bytes 1000 | tf_op jit(solution)/shard_map/inverse_factor/pallas_call | solution.py:298
  68.4 1.6 %finish.1 = (f32[64,1024]{1,0:T(8,128)}, bf16[1,768,1024]{2,1,0:T(8,128)(2,1)}) custom-call(f32[64,64]{1,0:T(8,128)S(1)} %get-tuple-element.56.w_ref, bf16[256,128]{1,0:T(8,128)(2,1)S(1)} %double.3.own_ref, bf16[256,128]{1,0:T(8,128)(2,1)S(1)} %collective-permute-done.14.got_ref, bf16[768,64]{1,0:T(8,128)(2,1)S(1)} %get-tuple-element.57.basis_ref, ...), custom_call_target="tpu_custom_call" | custom-call | flops 1000 | bytes 1000 | tf_op jit(solution)/shard_map/finish/pallas_call | solution.py:349
  70.2 4.5 %expert_step.1 = (f32[1,192,2048]{2,1,0:T(8,128)}, f32[1,192,2048]{2,1,0:T(8,128)}, bf16[1,192,2048]{2,1,0:T(8,128)(2,1)}) custom-call(bf16[192,128]{1,0:T(8,128)(2,1)S(1)} %get-tuple-element.61.refs_0_, bf16[192,128]{1,0:T(8,128)(2,1)S(1)} %collective-permute-done.15.refs_1_, bf16[192,128]{1,0:T(8,128)(2,1)S(1)} %collective-permute-done.16.refs_2_, ...), custom_call_target="tpu_custom_call" | custom-call | flops 1000 | bytes 1000 | tf_op jit(solution)/shard_map/expert_step/pallas_call | solution.py:433
  (31 shorter events, 4.0 us)
Async XLA Ops:
  0.6 5.8 %copy-start.1 = (bf16[1,128,2048]{2,1,0:T(8,128)(2,1)S(1)}, bf16[1,128,2048]{2,1,0:T(8,128)(2,1)}, u32[]{:S(2)}) copy-start(bf16[1,128,2048]{2,1,0:T(8,128)(2,1)} %refs_4_) | copy-start | bytes 1572868
  5.9 5.3 %collective-permute-start = (f32[64,768]{1,0:T(8,128)S(1)}, f32[64,768]{1,0:T(8,128)S(1)}, u32[]{:S(2)}, u32[]{:S(2)}) collective-permute-start(f32[64,768]{1,0:T(8,128)S(1)} %get-tuple-element.40), channel_id=1, source_target_pairs={{0,4},{4,0},{8,12},{12,8},{16,20},{20,16},{24,28},{28,24},{1,5},{5... | collective-permute-start | bytes 589832 | tf_op jit(solution)/shard_map/ppermute | solution.py:462
  6.4 17.5 %collective-permute-start.4 = (bf16[1,128,2048]{2,1,0:T(8,128)(2,1)S(1)}, bf16[1,128,2048]{2,1,0:T(8,128)(2,1)S(1)}, u32[]{:S(2)}, u32[]{:S(2)}) collective-permute-start(bf16[1,128,2048]{2,1,0:T(8,128)(2,1)S(1)} %copy-done.1), channel_id=1, source_target_pairs={{0,1},{1,2},{2,3},{3,0},{4,5},{5,6},{6,7},{7,4},{8,9},{9,10},{10,1... | collective-permute-start | bytes 1572872 | tf_op jit(solution)/shard_map/ppermute | solution.py:466
  9.1 25.2 %collective-permute-start.8 = (bf16[1,128,2048]{2,1,0:T(8,128)(2,1)S(1)}, bf16[1,128,2048]{2,1,0:T(8,128)(2,1)S(1)}, u32[]{:S(2)}, u32[]{:S(2)}) collective-permute-start(bf16[1,128,2048]{2,1,0:T(8,128)(2,1)S(1)} %copy-done.1), channel_id=1, source_target_pairs={{0,3},{1,0},{2,1},{3,2},{4,7},{5,4},{6,5},{7,6},{8,11},{9,8},{10,9... | collective-permute-start | bytes 1572872 | tf_op jit(solution)/shard_map/ppermute | solution.py:466
  11.2 5.8 %collective-permute-start.3 = (bf16[64,768]{1,0:T(8,128)(2,1)S(1)}, bf16[64,768]{1,0:T(8,128)(2,1)S(1)}, u32[]{:S(2)}, u32[]{:S(2)}) collective-permute-start(bf16[64,768]{1,0:T(8,128)(2,1)S(1)} %add_convert_fusion.refs_0_), channel_id=1, source_target_pairs={{0,24},{4,28},{8,16},{12,20},{16,8},{20,12},{24,0},{28,4},{1,25},{... | collective-permute-start | bytes 294920 | tf_op jit(solution)/shard_map/ppermute | solution.py:462
  13.9 5.2 %collective-permute-start.2 = (bf16[64,768]{1,0:T(8,128)(2,1)S(1)}, bf16[64,768]{1,0:T(8,128)(2,1)S(1)}, u32[]{:S(2)}, u32[]{:S(2)}) collective-permute-start(bf16[64,768]{1,0:T(8,128)(2,1)S(1)} %add_convert_fusion.refs_0_), channel_id=1, source_target_pairs={{0,16},{4,20},{8,24},{12,28},{16,0},{20,4},{24,8},{28,12},{1,17},{... | collective-permute-start | bytes 294920 | tf_op jit(solution)/shard_map/ppermute | solution.py:462
  14.4 4.8 %collective-permute-start.1 = (bf16[64,768]{1,0:T(8,128)(2,1)S(1)}, bf16[64,768]{1,0:T(8,128)(2,1)S(1)}, u32[]{:S(2)}, u32[]{:S(2)}) collective-permute-start(bf16[64,768]{1,0:T(8,128)(2,1)S(1)} %add_convert_fusion.refs_0_), channel_id=1, source_target_pairs={{0,8},{4,12},{8,0},{12,4},{16,24},{20,28},{24,16},{28,20},{1,9},{5... | collective-permute-start | bytes 294920 | tf_op jit(solution)/shard_map/ppermute | solution.py:462
  23.9 36.3 %copy-start = (bf16[1,128,768]{2,1,0:T(8,128)(2,1)S(1)}, bf16[1,128,768]{2,1,0:T(8,128)(2,1)}, u32[]{:S(2)}) copy-start(bf16[1,128,768]{2,1,0:T(8,128)(2,1)} %hidden_ref) | copy-start | bytes 589828
  24.6 1.3 %collective-permute-start.5 = (bf16[256,128]{1,0:T(8,128)(2,1)S(1)}, bf16[256,128]{1,0:T(8,128)(2,1)S(1)}, u32[]{:S(2)}, u32[]{:S(2)}) collective-permute-start(bf16[256,128]{1,0:T(8,128)(2,1)S(1)} %get-tuple-element.47), channel_id=1, source_target_pairs={{0,4},{4,0},{8,12},{12,8},{16,20},{20,16},{24,28},{28,24},{1,5},{5... | collective-permute-start | bytes 196616 | tf_op jit(solution)/shard_map/ppermute | solution.py:462
  25.9 4.0 %collective-permute-start.6 = (bf16[128,128]{1,0:T(8,128)(2,1)S(1)}, bf16[128,128]{1,0:T(8,128)(2,1)S(1)}, u32[]{:S(2)}, u32[]{:S(2)}) collective-permute-start(bf16[128,128]{1,0:T(8,128)(2,1)S(1)} %get-tuple-element.49), channel_id=1, source_target_pairs={{0,8},{4,12},{8,0},{12,4},{16,24},{20,28},{24,16},{28,20},{1,9},{5... | collective-permute-start | bytes 98312 | tf_op jit(solution)/shard_map/ppermute | solution.py:462
  29.9 4.4 %collective-permute-start.7 = (bf16[64,128]{1,0:T(8,128)(2,1)S(1)}, bf16[64,128]{1,0:T(8,128)(2,1)S(1)}, u32[]{:S(2)}, u32[]{:S(2)}) collective-permute-start(bf16[64,128]{1,0:T(8,128)(2,1)S(1)} %get-tuple-element.51), channel_id=1, source_target_pairs={{0,16},{4,20},{8,24},{12,28},{16,0},{20,4},{24,8},{28,12},{1,17},{... | collective-permute-start | bytes 49160 | tf_op jit(solution)/shard_map/ppermute | solution.py:462
  34.3 13.8 %collective-permute-start.11 = (bf16[160,128]{1,0:T(8,128)(2,1)S(1)}, bf16[160,128]{1,0:T(8,128)(2,1)S(1)}, u32[]{:S(2)}, u32[]{:S(2)}) collective-permute-start(bf16[160,128]{1,0:T(8,128)(2,1)S(1)} %line_load.1.refs_0_), channel_id=1, source_target_pairs={{0,3},{1,0},{2,1},{3,2},{4,7},{5,4},{6,5},{7,6},{8,11},{9,8},{10,9... | collective-permute-start | bytes 122888 | tf_op jit(solution)/shard_map/ppermute | solution.py:466
  46.5 4.9 %collective-permute-start.10 = (bf16[160,128]{1,0:T(8,128)(2,1)S(1)}, bf16[160,128]{1,0:T(8,128)(2,1)S(1)}, u32[]{:S(2)}, u32[]{:S(2)}) collective-permute-start(bf16[160,128]{1,0:T(8,128)(2,1)S(1)} %line_load.1.refs_0_), channel_id=1, source_target_pairs={{0,2},{1,3},{2,0},{3,1},{4,6},{5,7},{6,4},{7,5},{8,10},{9,11},{10,... | collective-permute-start | bytes 122888 | tf_op jit(solution)/shard_map/ppermute | solution.py:466
  46.5 5.8 %collective-permute-start.9 = (bf16[160,128]{1,0:T(8,128)(2,1)S(1)}, bf16[160,128]{1,0:T(8,128)(2,1)S(1)}, u32[]{:S(2)}, u32[]{:S(2)}) collective-permute-start(bf16[160,128]{1,0:T(8,128)(2,1)S(1)} %line_load.1.refs_0_), channel_id=1, source_target_pairs={{0,1},{1,2},{2,3},{3,0},{4,5},{5,6},{6,7},{7,4},{8,9},{9,10},{10,1... | collective-permute-start | bytes 122888 | tf_op jit(solution)/shard_map/ppermute | solution.py:466
  52.3 17.9 %collective-permute-start.18 = (bf16[1,128,2048]{2,1,0:T(8,128)(2,1)S(1)}, bf16[1,128,2048]{2,1,0:T(8,128)(2,1)S(1)}, u32[]{:S(2)}, u32[]{:S(2)}) collective-permute-start(bf16[1,128,2048]{2,1,0:T(8,128)(2,1)S(1)} %collective-permute-done.4.refs_5_), channel_id=1, source_target_pairs={{0,1},{1,2},{2,3},{3,0},{4,5},{5,6},{6,7},{7,4},{8,9},{9,10},{10,1... | collective-permute-start | bytes 1572872 | tf_op jit(solution)/shard_map/ppermute | solution.py:466
  52.4 3.8 %collective-permute-start.12 = (bf16[64,128]{1,0:T(8,128)(2,1)S(1)}, bf16[64,128]{1,0:T(8,128)(2,1)S(1)}, u32[]{:S(2)}, u32[]{:S(2)}) collective-permute-start(bf16[64,128]{1,0:T(8,128)(2,1)S(1)} %line_sum.1.own_ref), channel_id=1, source_target_pairs={{0,16},{4,20},{8,24},{12,28},{16,0},{20,4},{24,8},{28,12},{1,17},{... | collective-permute-start | bytes 49160 | tf_op jit(solution)/shard_map/ppermute | solution.py:462
  56.2 3.9 %collective-permute-start.13 = (bf16[128,128]{1,0:T(8,128)(2,1)S(1)}, bf16[128,128]{1,0:T(8,128)(2,1)S(1)}, u32[]{:S(2)}, u32[]{:S(2)}) collective-permute-start(bf16[128,128]{1,0:T(8,128)(2,1)S(1)} %double.2.own_ref), channel_id=1, source_target_pairs={{0,8},{4,12},{8,0},{12,4},{16,24},{20,28},{24,16},{28,20},{1,9},{5... | collective-permute-start | bytes 98312 | tf_op jit(solution)/shard_map/ppermute | solution.py:462
  60.1 8.3 %collective-permute-start.14 = (bf16[256,128]{1,0:T(8,128)(2,1)S(1)}, bf16[256,128]{1,0:T(8,128)(2,1)S(1)}, u32[]{:S(2)}, u32[]{:S(2)}) collective-permute-start(bf16[256,128]{1,0:T(8,128)(2,1)S(1)} %double.3.own_ref), channel_id=1, source_target_pairs={{0,4},{4,0},{8,12},{12,8},{16,20},{20,16},{24,28},{28,24},{1,5},{5... | collective-permute-start | bytes 196616 | tf_op jit(solution)/shard_map/ppermute | solution.py:462
  60.3 9.7 %collective-permute-start.17 = (bf16[192,128]{1,0:T(8,128)(2,1)S(1)}, bf16[192,128]{1,0:T(8,128)(2,1)S(1)}, u32[]{:S(2)}, u32[]{:S(2)}) collective-permute-start(bf16[192,128]{1,0:T(8,128)(2,1)S(1)} %get-tuple-element.67), channel_id=1, source_target_pairs={{0,3},{1,0},{2,1},{3,2},{4,7},{5,4},{6,5},{7,6},{8,11},{9,8},{10,9... | collective-permute-start | bytes 147464 | tf_op jit(solution)/shard_map/ppermute | solution.py:466
  64.1 6.0 %collective-permute-start.16 = (bf16[192,128]{1,0:T(8,128)(2,1)S(1)}, bf16[192,128]{1,0:T(8,128)(2,1)S(1)}, u32[]{:S(2)}, u32[]{:S(2)}) collective-permute-start(bf16[192,128]{1,0:T(8,128)(2,1)S(1)} %get-tuple-element.65), channel_id=1, source_target_pairs={{0,2},{1,3},{2,0},{3,1},{4,6},{5,7},{6,4},{7,5},{8,10},{9,11},{10,... | collective-permute-start | bytes 147464 | tf_op jit(solution)/shard_map/ppermute | solution.py:466
  64.1 6.0 %collective-permute-start.15 = (bf16[192,128]{1,0:T(8,128)(2,1)S(1)}, bf16[192,128]{1,0:T(8,128)(2,1)S(1)}, u32[]{:S(2)}, u32[]{:S(2)}) collective-permute-start(bf16[192,128]{1,0:T(8,128)(2,1)S(1)} %get-tuple-element.63), channel_id=1, source_target_pairs={{0,1},{1,2},{2,3},{3,0},{4,5},{5,6},{6,7},{7,4},{8,9},{9,10},{10,1... | collective-permute-start | bytes 147464 | tf_op jit(solution)/shard_map/ppermute | solution.py:466

commit v7 on v5

--- a/solution.py
+++ b/solution.py
@@ -50,9 +50,9 @@
 
 def merge_kernel(acts_ref, kv_ref, err_ref, vt_ref, merged_ref, lt_ref):
     merged = lax.dot_general(acts_ref[...], kv_ref[...], ROWS_FIRST, preferred_element_type=F32)
-    merged = merged + err_ref[0].astype(F32)
+    merged = (merged + err_ref[0].astype(F32)).astype(BF16)
     merged_ref[...] = merged
-    lt_ref[...] = left_times(vt_ref[...], merged.astype(BF16), COLS_LAST)
+    lt_ref[...] = left_times(vt_ref[...], merged, COLS_LAST)
 
 
 def merge(acts, kv, err, vt):
@@ -74,7 +74,7 @@
             pl.BlockSpec((rank, block), lambda i: (0, i)),
         ],
         out_shape=[
-            jax.ShapeDtypeStruct((rows, cols), F32),
+            jax.ShapeDtypeStruct((rows, cols), BF16),
             jax.ShapeDtypeStruct((rank, rows), F32),
         ],
         compiler_params=params(24),
@@ -83,26 +83,29 @@
     )(*[pltpu.with_memory_space_constraint(x, pltpu.HBM) for x in (acts, kv, err, vt)])
 
 
-def slab_kernel(hidden_ref, own_ref, *refs):
-    send_refs, all_ref = refs[:-1], refs[-1]
-    n_exp = all_ref.shape[0]
+def pack_kernel(hidden_ref, gram_ref, *refs):
+    load_refs, all_ref = refs[:-1], refs[-1]
+    n_exp, units = all_ref.shape[:2]
+    terms = gram_ref.shape[0]
     all_ref[...] = hidden_ref[0].T.reshape(all_ref.shape)
     place = lax.axis_index("exp")
-    for k, ref in enumerate((own_ref,) + tuple(send_refs)):
-        ref[...] = all_ref[lax.rem(place + k, n_exp)]
-
-
-def unit_slabs(hidden, n_exp):
+    for k, ref in enumerate(load_refs):
+        ref[0:terms] = gram_ref[...]
+        ref[terms : terms + units] = all_ref[lax.rem(place + k, n_exp)]
+
+
+def pack(hidden, gram, n_exp):
     _, tokens, units = hidden.shape
     slab = (units // n_exp, tokens)
-    return pl.pallas_call(
-        slab_kernel,
-        out_shape=[jax.ShapeDtypeStruct(slab, BF16)] * n_exp,
+    load = (gram.shape[0] + slab[0], tokens)
+    return pl.pallas_call(
+        pack_kernel,
+        out_shape=[jax.ShapeDtypeStruct(load, BF16)] * n_exp,
         scratch_shapes=[pltpu.VMEM((n_exp,) + slab, BF16)],
         compiler_params=params(8),
         cost_estimate=SMALL,
-        name="unit_slabs",
-    )(hidden)
+        name="pack",
+    )(hidden, gram)
 
 
 def right_kernel(n_parts, *refs):
@@ -114,7 +117,7 @@
     lt = parts[0]
     rank = lt.shape[0]
     lt_ref[...] = lt
-    product = left_times(lt, merged_ref[...].astype(BF16), (((1,), (0,)), ((), ()))).astype(BF16)
+    product = left_times(lt, merged_ref[...], (((1,), (0,)), ((), ()))).astype(BF16)
     across = product.shape[1] // TILE_C
     for a in range(rank // TILE_R):
         for b in range(across):
@@ -175,7 +178,7 @@
     rank = lt_ref.shape[0]
     half = rank // 2
     copies = [
-        pltpu.make_async_copy(load_hbms[k], terms_ref.at[k], sems.at[k])
+        pltpu.make_async_copy(load_hbms[k].at[0 : 3 * half], terms_ref.at[k], sems.at[k])
         for k in range(n_exp)
     ]
     lt_copy = pltpu.make_async_copy(lt_hbm, lt_ref, sems.at[n_exp])
@@ -230,7 +233,7 @@
             pltpu.SemaphoreType.DMA((n_exp + 1,)),
         ],
         compiler_params=params(8),
-        cost_estimate=SMALL,
+        cost_estimate=pl.CostEstimate(flops=4_000_000_000, bytes_accessed=1000, transcendentals=0),
         name="inverse_factor",
     )(*loads, lt)
 
@@ -259,7 +262,7 @@
     for i in range(rows // block):
         here = slice(i * block, (i + 1) * block)
         approx = jnp.dot(basis_ref[here, :], rounded, preferred_element_type=F32)
-        err_ref[here, :] = (merged_ref[here, :] - approx).astype(BF16)
+        err_ref[here, :] = (merged_ref[here, :].astype(F32) - approx).astype(BF16)
         copies.append(
             pltpu.make_async_copy(err_ref.at[here, :], err_hbm.at[0, here, :], sems.at[i + 1])
         )
@@ -299,9 +302,10 @@
     units, width = one.shape
     tokens = grad_hbms[0].shape[1]
     count = width // chunk
+    terms = load_hbms[0].shape[0] - units
 
     slabs = [
-        pltpu.make_async_copy(load_hbms[k], hid.at[k], in_sems.at[count, k])
+        pltpu.make_async_copy(load_hbms[k].at[terms : terms + units], hid.at[k], in_sems.at[count, k])
         for k in range(n_exp)
     ]
 
@@ -403,7 +407,6 @@
     merged, lt = merge(activations, kv_grad, errors, right_factor.T)
 
     lt = (lt + swap(lt, "rep", n_rep, 1)).astype(BF16)
-    slabs = unit_slabs(after(hidden, lt), n_exp)
     bit = 2
     parts = [lt]
     while bit < n_rep:
@@ -415,19 +418,19 @@
         bit *= len(parts)
     lt, gram, chunks = right_product(parts, merged)
 
-    slabs = [slabs[0]] + [shift(after(slabs[k], gram), n_exp, k) for k in range(1, n_exp)]
-    grams = [gram] + [shift(gram, n_exp, k) for k in range(1, n_exp)]
+    loads = pack(hidden, gram, n_exp)
+    loads = [loads[0]] + [shift(loads[k], n_exp, k) for k in range(1, n_exp)]
 
     if chunks.shape[0] == n_rep * n_exp:
         both = ("rep", "exp")
         shares = lax.all_to_all(chunks, both, 0, 0, tiled=True)
-        shares, grams, grads = lax.optimization_barrier((shares, grams, grads))
+        shares, grads = lax.optimization_barrier((shares, grads))
         share = fold(shares)
         chunks = lax.all_to_all(share, both, 0, 0, tiled=True)
     else:
         share = chunks
         chunks = lax.psum(chunks.astype(F32), ("rep", "exp")).astype(BF16)
-    w, basis = inverse_factor(grams, lt)
+    w, basis = inverse_factor(loads, lt)
 
     left, right = 1, n_exp - 1
     while right - left > 1:
@@ -440,7 +443,7 @@
 
     new_right, new_error = finish(n_rep, w, chunks, basis, merged)
     first_new, second_new, step = expert_step(
-        slabs, [grads[k] for k in range(n_exp)], moment_one, moment_two
+        loads, [grads[k] for k in range(n_exp)], moment_one, moment_two
     )
     return new_error, new_right.T, first_new, second_new, step
 

time: 69.9 us -> 76.5 us (1.094)
  waiting for transfers between devices: 16.7 us -> 29.6 us
  starting transfers between devices: 27.6 us -> 19.9 us
  Pallas kernels: 17.3 us -> 18.3 us
    ppermute x9 -> x6, waiting for transfers between devices: 11.1 us -> 21 us  [shift(): return lax.ppermute(x, 'exp', [(i, (i + k) % size) for i in range(size)])]
    ppermute x9 -> x6, starting transfers between devices: 14.9 us -> 10.1 us  [shift(): return lax.ppermute(x, 'exp', [(i, (i + k) % size) for i in range(size)])]
    all_to_all x1, waiting for transfers between devices: 0.01 us -> 4.21 us  [body(): shares = lax.all_to_all(chunks, both, 0, 0, tiled=True)]
    all_to_all x1, starting transfers between devices: 5.35 us -> 2.58 us  [body(): chunks = lax.all_to_all(share, both, 0, 0, tiled=True)]
    all_to_all x1, waiting for transfers between devices: 1.22 us -> 0.01 us  [body(): chunks = lax.all_to_all(share, both, 0, 0, tiled=True)]
    unnamed x24 -> x26, local copies, waits for them, and re-layouts: 7.03 us -> 7.39 us
  transfers between devices with their start and end apart: 15 -> 12, of which waited for: 7 -> 7; matrix products, arithmetic and copies ran while one was open for 0% -> 0% of each run, Pallas kernels for 10% -> 10%
where the time goes in v7:
time: 76.5 us; the launch traced here: 76 us
  waiting for transfers between devices  29.6 us (39%)
  starting transfers between devices  19.9 us (26%)
  Pallas kernels  18.3 us (24%)
  local copies, waits for them, and re-layouts  7.39 us (10%)
    ppermute x6, waiting for transfers between devices, shift(): return lax.ppermute(x, 'exp', [(i, (i + k) % size) for i in range(size)])  21 us
    ppermute x6, starting transfers between devices, shift(): return lax.ppermute(x, 'exp', [(i, (i + k) % size) for i in range(size)])  10.1 us
    unnamed x26, local copies, waits for them, and re-layouts  7.39 us
    pallas_call x1, Pallas kernels, merge(): pl.pallas_call(merge_kernel, grid=(rows // block,), in_specs=[pl.BlockSpe...  5.22 us
    pallas_call x1, Pallas kernels, expert_step(): pl.pallas_call(functools.partial(expert_kernel, n_exp, chunk), in_specs=[...  4.43 us
    ppermute x4, waiting for transfers between devices, swap(): return lax.ppermute(x, axis, [(i, i ^ mask) for i in range(size)])  4.36 us
    all_to_all x1, waiting for transfers between devices, body(): shares = lax.all_to_all(chunks, both, 0, 0, tiled=True)  4.21 us
    ppermute x4, starting transfers between devices, swap(): return lax.ppermute(x, axis, [(i, i ^ mask) for i in range(size)])  4.07 us
  transfers between devices with their start and end apart: 12, of which 7 were waited for; matrix products, arithmetic and copies ran while one was open for 0% of the time, Pallas kernels for 10%

profile of v7, /device:TPU:0, one launch (start us, length us, event | category | flops | bytes accessed | tf_op | source)
XLA Modules:
  0.0 76.0 jit_solution(15111980210100409934)
XLA Ops:
  0.6 5.2 %merge.1 = (bf16[768,1024]{1,0:T(8,128)(2,1)S(1)}, f32[64,768]{1,0:T(8,128)S(1)}) custom-call(bf16[1024,768]{1,0:T(8,128)(2,1)} %acts_ref.1, bf16[1024,1024]{1,0:T(8,128)(2,1)} %kv_ref.1, bf16[1,768,1024]{2,1,0:T(8,128)(2,1)} %err_ref.1, f32[64,1024]{1,0:T(8,128)} %bitcast.2), custom_call_target="tpu_custom_call" | custom-call | flops 1000 | bytes 1000 | tf_op jit(solution)/shard_map/merge/pallas_call | solution.py:63
  6.4 2.6 %collective-permute-start.7 = (bf16[1,128,2048]{2,1,0:T(8,128)(2,1)}, bf16[1,128,2048]{2,1,0:T(8,128)(2,1)S(1)}, u32[]{:S(2)}, u32[]{:S(2)}) collective-permute-start(bf16[1,128,2048]{2,1,0:T(8,128)(2,1)} %refs_4_), channel_id=1, source_target_pairs={{0,1},{1,2},{2,3},{3,0},{4,5},{5,6},{6,7},{7,4},{8,9},{9,10},{10,1... | collective-permute-start | bytes 1572872 | tf_op jit(solution)/shard_map/ppermute | solution.py:396
  9.0 2.1 %collective-permute-start.8 = (bf16[1,128,2048]{2,1,0:T(8,128)(2,1)}, bf16[1,128,2048]{2,1,0:T(8,128)(2,1)S(1)}, u32[]{:S(2)}, u32[]{:S(2)}) collective-permute-start(bf16[1,128,2048]{2,1,0:T(8,128)(2,1)} %refs_4_), channel_id=1, source_target_pairs={{0,3},{1,0},{2,1},{3,2},{4,7},{5,4},{6,5},{7,6},{8,11},{9,8},{10,9... | collective-permute-start | bytes 1572872 | tf_op jit(solution)/shard_map/ppermute | solution.py:396
  11.2 2.6 %collective-permute-start.3 = (bf16[64,768]{1,0:T(8,128)(2,1)S(1)}, bf16[64,768]{1,0:T(8,128)(2,1)S(1)}, u32[]{:S(2)}, u32[]{:S(2)}) collective-permute-start(bf16[64,768]{1,0:T(8,128)(2,1)S(1)} %add_convert_fusion.refs_0_), channel_id=1, source_target_pairs={{0,24},{4,28},{8,16},{12,20},{16,8},{20,12},{24,0},{28,4},{1,25},{... | collective-permute-start | bytes 294920 | tf_op jit(solution)/shard_map/ppermute | solution.py:392
  14.7 2.3 %collective-permute-done.3.refs_3_ = bf16[64,768]{1,0:T(8,128)(2,1)S(1)} collective-permute-done((bf16[64,768]{1,0:T(8,128)(2,1)S(1)}, bf16[64,768]{1,0:T(8,128)(2,1)S(1)}, u32[]{:S(2)}, u32[]{:S(2)}) %collective-permute-start.3) | collective-permute-done | bytes 98336 | tf_op jit(solution)/shard_map/ppermute | solution.py:392
  17.0 2.0 %collective-permute-done.2.refs_2_ = bf16[64,768]{1,0:T(8,128)(2,1)S(1)} collective-permute-done((bf16[64,768]{1,0:T(8,128)(2,1)S(1)}, bf16[64,768]{1,0:T(8,128)(2,1)S(1)}, u32[]{:S(2)}, u32[]{:S(2)}) %collective-permute-start.2) | collective-permute-done | bytes 98336 | tf_op jit(solution)/shard_map/ppermute | solution.py:392
  19.1 1.2 %right_product.1 = (f32[64,768]{1,0:T(8,128)S(1)}, bf16[96,128]{1,0:T(8,128)(2,1)S(1)}, bf16[32,16,128]{2,1,0:T(8,128)(2,1)}) custom-call(bf16[64,768]{1,0:T(8,128)(2,1)S(1)} %add_convert_fusion.refs_0_, bf16[64,768]{1,0:T(8,128)(2,1)S(1)} %collective-permute-done.1.refs_1_, bf16[64,768]{1,0:T(8,128)(2,1)S(1)} %collective-permute-done.2.refs_2_, ...), custom_call_target="tpu_custom_call" | custom-call | flops 1000 | bytes 1000 | tf_op jit(solution)/shard_map/right_product/pallas_call | solution.py:143
  21.5 3.2 %all-to-all-start = ((bf16[32,16,128]{2,1,0:T(8,128)(2,1)}), bf16[32,16,128]{2,1,0:T(8,128)(2,1)S(1)}, u32[]{:S(2)}, u32[]{:S(2)}) async-start(bf16[32,16,128]{2,1,0:T(8,128)(2,1)} %get-tuple-element.35), calls=%async_computation | async-start | bytes 262144 | tf_op jit(solution)/shard_map/all_to_all | solution.py:426
  24.8 10.0 %collective-permute-done.8.refs_7_ = bf16[1,128,2048]{2,1,0:T(8,128)(2,1)S(1)} collective-permute-done((bf16[1,128,2048]{2,1,0:T(8,128)(2,1)}, bf16[1,128,2048]{2,1,0:T(8,128)(2,1)S(1)}, u32[]{:S(2)}, u32[]{:S(2)}) %collective-permute-start.8) | collective-permute-done | bytes 524320 | tf_op jit(solution)/shard_map/ppermute | solution.py:396
  34.8 4.2 %all-to-all-done.share_ref = bf16[32,16,128]{2,1,0:T(8,128)(2,1)S(1)} async-done(((bf16[32,16,128]{2,1,0:T(8,128)(2,1)}), bf16[32,16,128]{2,1,0:T(8,128)(2,1)S(1)}, u32[]{:S(2)}, u32[]{:S(2)}) %all-to-all-start) | async-done | bytes 131104 | tf_op jit(solution)/shard_map/all_to_all | solution.py:426
  39.7 1.2 %collective-permute-start.9 = (bf16[1,128,2048]{2,1,0:T(8,128)(2,1)S(1)}, bf16[1,128,2048]{2,1,0:T(8,128)(2,1)S(1)}, u32[]{:S(2)}, u32[]{:S(2)}) collective-permute-start(bf16[1,128,2048]{2,1,0:T(8,128)(2,1)S(1)} %collective-permute-done.7.refs_5_), channel_id=1, source_target_pairs={{0,1},{1,2},{2,3},{3,0},{4,5},{5,6},{6,7},{7,4},{8,9},{9,10},{10,1... | collective-permute-start | bytes 1572872 | tf_op jit(solution)/shard_map/ppermute | solution.py:396
  41.6 0.8 %pack.1 = (bf16[288,128]{1,0:T(8,128)(2,1)S(1)}, bf16[288,128]{1,0:T(8,128)(2,1)}, bf16[288,128]{1,0:T(8,128)(2,1)}, bf16[288,128]{1,0:T(8,128)(2,1)}) custom-call(bf16[1,128,768]{2,1,0:T(8,128)(2,1)S(1)} %copy-done, bf16[96,128]{1,0:T(8,128)(2,1)S(1)} %copy-done.10), custom_call_target="tpu_custom_call" | custom-call | flops 1000 | bytes 1000 | tf_op jit(solution)/shard_map/pack/pallas_call | solution.py:101
  43.0 2.7 %collective-permute-start.5 = (bf16[288,128]{1,0:T(8,128)(2,1)}, bf16[288,128]{1,0:T(8,128)(2,1)S(1)}, u32[]{:S(2)}, u32[]{:S(2)}) collective-permute-start(bf16[288,128]{1,0:T(8,128)(2,1)} %get-tuple-element.31), channel_id=1, source_target_pairs={{0,2},{1,3},{2,0},{3,1},{4,6},{5,7},{6,4},{7,5},{8,10},{9,11},{10,... | collective-permute-start | bytes 221192 | tf_op jit(solution)/shard_map/ppermute | solution.py:396
  45.7 0.9 %collective-permute-start.6 = (bf16[288,128]{1,0:T(8,128)(2,1)}, bf16[288,128]{1,0:T(8,128)(2,1)}, u32[]{:S(2)}, u32[]{:S(2)}) collective-permute-start(bf16[288,128]{1,0:T(8,128)(2,1)} %get-tuple-element.32), channel_id=1, source_target_pairs={{0,3},{1,0},{2,1},{3,2},{4,7},{5,4},{6,5},{7,6},{8,11},{9,8},{10,9... | collective-permute-start | bytes 221192 | tf_op jit(solution)/shard_map/ppermute | solution.py:396
  46.6 2.6 %all-to-all-start.1 = ((bf16[32,16,128]{2,1,0:T(8,128)(2,1)}), bf16[32,16,128]{2,1,0:T(8,128)(2,1)S(1)}, u32[]{:S(2)}, u32[]{:S(2)}) async-start(bf16[32,16,128]{2,1,0:T(8,128)(2,1)} %fold.1), calls=%async_computation.1 | async-start | bytes 262144 | tf_op jit(solution)/shard_map/all_to_all | solution.py:429
  49.2 8.8 %collective-permute-done.4.refs_1_ = bf16[288,128]{1,0:T(8,128)(2,1)S(1)} collective-permute-done((bf16[288,128]{1,0:T(8,128)(2,1)}, bf16[288,128]{1,0:T(8,128)(2,1)S(1)}, u32[]{:S(2)}, u32[]{:S(2)}) %collective-permute-start.4) | collective-permute-done | bytes 73760 | tf_op jit(solution)/shard_map/ppermute | solution.py:396
  58.6 2.2 %collective-permute-done.5.refs_2_ = bf16[288,128]{1,0:T(8,128)(2,1)S(1)} collective-permute-done((bf16[288,128]{1,0:T(8,128)(2,1)}, bf16[288,128]{1,0:T(8,128)(2,1)S(1)}, u32[]{:S(2)}, u32[]{:S(2)}) %collective-permute-start.5) | collective-permute-done | bytes 73760 | tf_op jit(solution)/shard_map/ppermute | solution.py:396
  61.5 0.9 %copy-done.2 = bf16[288,128]{1,0:T(8,128)(2,1)S(1)} copy-done((bf16[288,128]{1,0:T(8,128)(2,1)S(1)}, bf16[288,128]{1,0:T(8,128)(2,1)}, u32[]{:S(2)}) %copy-start.2) | copy-done | bytes 73752
  62.3 0.9 %copy-done.5 = bf16[288,128]{1,0:T(8,128)(2,1)S(1)} copy-done((bf16[288,128]{1,0:T(8,128)(2,1)S(1)}, bf16[288,128]{1,0:T(8,128)(2,1)}, u32[]{:S(2)}) %copy-start.5) | copy-done | bytes 73752
  63.2 0.9 %copy-done.12 = f32[64,768]{1,0:T(8,128)S(1)} copy-done((f32[64,768]{1,0:T(8,128)S(1)}, f32[64,768]{1,0:T(8,128)}, u32[]{:S(2)}) %copy-start.12) | copy-done | bytes 196632
  64.1 4.1 %inverse_factor.1 = (f32[64,64]{1,0:T(8,128)S(1)}, bf16[768,64]{1,0:T(8,128)(2,1)S(1)}) custom-call(bf16[288,128]{1,0:T(8,128)(2,1)S(1)} %get-tuple-element.29.refs_0_, bf16[288,128]{1,0:T(8,128)(2,1)S(1)} %copy-done.2, bf16[288,128]{1,0:T(8,128)(2,1)S(1)} %copy-done.5, bf16[288,128]{1,0:T(8,128)(2,1)} %collective-permute-done.6.refs_3_, ...), custom_call_target="tpu_custom_call" | custom-call | flops 4000000000 | bytes 1000 | tf_op jit(solution)/shard_map/inverse_factor/pallas_call | solution.py:222
  68.8 0.8 %copy-done.8 = f32[64,64]{1,0:T(8,128)S(1)} copy-done((f32[64,64]{1,0:T(8,128)S(1)}, f32[64,64]{1,0:T(8,128)}, u32[]{:S(2)}) %copy-start.8) | copy-done | bytes 16408
  69.6 1.9 %finish.1 = (f32[64,1024]{1,0:T(8,128)}, bf16[1,768,1024]{2,1,0:T(8,128)(2,1)}) custom-call(f32[64,64]{1,0:T(8,128)S(1)} %copy-done.8, bf16[32,16,128]{2,1,0:T(8,128)(2,1)S(1)} %all-to-all-done.1.chunk_ref, bf16[768,64]{1,0:T(8,128)(2,1)S(1)} %get-tuple-element.37.basis_any, bf16[768,1024]{1,0:T(8,128)(2,1)S(1)} %get-tuple-element.27.refs_4_.merged_ref), custom_call_target="tpu_custom_call" | custom-call | flops 1000 | bytes 1000 | tf_op jit(solution)/shard_map/finish/pallas_call | solution.py:277
  71.6 4.4 %expert_step.1 = (f32[1,192,2048]{2,1,0:T(8,128)}, f32[1,192,2048]{2,1,0:T(8,128)}, bf16[1,192,2048]{2,1,0:T(8,128)(2,1)}) custom-call(bf16[288,128]{1,0:T(8,128)(2,1)S(1)} %get-tuple-element.29.refs_0_, bf16[288,128]{1,0:T(8,128)(2,1)S(1)} %copy-done.3, bf16[288,128]{1,0:T(8,128)(2,1)S(1)} %copy-done.6, bf16[288,128]{1,0:T(8,128)(2,1)} %collective-permute-done.6.refs_3_, ...), custom_call_target="tpu_custom_call" | custom-call | flops 1000 | bytes 1000 | tf_op jit(solution)/shard_map/expert_step/pallas_call | solution.py:363
  (34 shorter events, 6.6 us)
Async XLA Ops:
  5.9 35.1 %copy-start = (bf16[1,128,768]{2,1,0:T(8,128)(2,1)S(1)}, bf16[1,128,768]{2,1,0:T(8,128)(2,1)}, u32[]{:S(2)}) copy-start(bf16[1,128,768]{2,1,0:T(8,128)(2,1)} %hidden_ref.1) | copy-start | bytes 589828
  5.9 5.3 %collective-permute-start = (f32[64,768]{1,0:T(8,128)S(1)}, f32[64,768]{1,0:T(8,128)S(1)}, u32[]{:S(2)}, u32[]{:S(2)}) collective-permute-start(f32[64,768]{1,0:T(8,128)S(1)} %get-tuple-element.26), channel_id=1, source_target_pairs={{0,4},{4,0},{8,12},{12,8},{16,20},{20,16},{24,28},{28,24},{1,5},{5... | collective-permute-start | bytes 589832 | tf_op jit(solution)/shard_map/ppermute | solution.py:392
  6.4 18.4 %collective-permute-start.7 = (bf16[1,128,2048]{2,1,0:T(8,128)(2,1)}, bf16[1,128,2048]{2,1,0:T(8,128)(2,1)S(1)}, u32[]{:S(2)}, u32[]{:S(2)}) collective-permute-start(bf16[1,128,2048]{2,1,0:T(8,128)(2,1)} %refs_4_), channel_id=1, source_target_pairs={{0,1},{1,2},{2,3},{3,0},{4,5},{5,6},{6,7},{7,4},{8,9},{9,10},{10,1... | collective-permute-start | bytes 1572872 | tf_op jit(solution)/shard_map/ppermute | solution.py:396
  9.0 25.8 %collective-permute-start.8 = (bf16[1,128,2048]{2,1,0:T(8,128)(2,1)}, bf16[1,128,2048]{2,1,0:T(8,128)(2,1)S(1)}, u32[]{:S(2)}, u32[]{:S(2)}) collective-permute-start(bf16[1,128,2048]{2,1,0:T(8,128)(2,1)} %refs_4_), channel_id=1, source_target_pairs={{0,3},{1,0},{2,1},{3,2},{4,7},{5,4},{6,5},{7,6},{8,11},{9,8},{10,9... | collective-permute-start | bytes 1572872 | tf_op jit(solution)/shard_map/ppermute | solution.py:396
  11.2 5.8 %collective-permute-start.3 = (bf16[64,768]{1,0:T(8,128)(2,1)S(1)}, bf16[64,768]{1,0:T(8,128)(2,1)S(1)}, u32[]{:S(2)}, u32[]{:S(2)}) collective-permute-start(bf16[64,768]{1,0:T(8,128)(2,1)S(1)} %add_convert_fusion.refs_0_), channel_id=1, source_target_pairs={{0,24},{4,28},{8,16},{12,20},{16,8},{20,12},{24,0},{28,4},{1,25},{... | collective-permute-start | bytes 294920 | tf_op jit(solution)/shard_map/ppermute | solution.py:392
  13.8 5.2 %collective-permute-start.2 = (bf16[64,768]{1,0:T(8,128)(2,1)S(1)}, bf16[64,768]{1,0:T(8,128)(2,1)S(1)}, u32[]{:S(2)}, u32[]{:S(2)}) collective-permute-start(bf16[64,768]{1,0:T(8,128)(2,1)S(1)} %add_convert_fusion.refs_0_), channel_id=1, source_target_pairs={{0,16},{4,20},{8,24},{12,28},{16,0},{20,4},{24,8},{28,12},{1,17},{... | collective-permute-start | bytes 294920 | tf_op jit(solution)/shard_map/ppermute | solution.py:392
  14.3 4.8 %collective-permute-start.1 = (bf16[64,768]{1,0:T(8,128)(2,1)S(1)}, bf16[64,768]{1,0:T(8,128)(2,1)S(1)}, u32[]{:S(2)}, u32[]{:S(2)}) collective-permute-start(bf16[64,768]{1,0:T(8,128)(2,1)S(1)} %add_convert_fusion.refs_0_), channel_id=1, source_target_pairs={{0,8},{4,12},{8,0},{12,4},{16,24},{20,28},{24,16},{28,20},{1,9},{5... | collective-permute-start | bytes 294920 | tf_op jit(solution)/shard_map/ppermute | solution.py:392
  20.9 0.7 copy-start.11
  21.5 17.5 %all-to-all-start = ((bf16[32,16,128]{2,1,0:T(8,128)(2,1)}), bf16[32,16,128]{2,1,0:T(8,128)(2,1)S(1)}, u32[]{:S(2)}, u32[]{:S(2)}) async-start(bf16[32,16,128]{2,1,0:T(8,128)(2,1)} %get-tuple-element.35), calls=%async_computation | async-start | bytes 262144 | tf_op jit(solution)/shard_map/all_to_all | solution.py:426
  39.7 31.8 %collective-permute-start.9 = (bf16[1,128,2048]{2,1,0:T(8,128)(2,1)S(1)}, bf16[1,128,2048]{2,1,0:T(8,128)(2,1)S(1)}, u32[]{:S(2)}, u32[]{:S(2)}) collective-permute-start(bf16[1,128,2048]{2,1,0:T(8,128)(2,1)S(1)} %collective-permute-done.7.refs_5_), channel_id=1, source_target_pairs={{0,1},{1,2},{2,3},{3,0},{4,5},{5,6},{6,7},{7,4},{8,9},{9,10},{10,1... | collective-permute-start | bytes 1572872 | tf_op jit(solution)/shard_map/ppermute | solution.py:396
  40.9 0.7 copy-start.10
  42.5 15.6 %collective-permute-start.4 = (bf16[288,128]{1,0:T(8,128)(2,1)}, bf16[288,128]{1,0:T(8,128)(2,1)S(1)}, u32[]{:S(2)}, u32[]{:S(2)}) collective-permute-start(bf16[288,128]{1,0:T(8,128)(2,1)} %get-tuple-element.30), channel_id=1, source_target_pairs={{0,1},{1,2},{2,3},{3,0},{4,5},{5,6},{6,7},{7,4},{8,9},{9,10},{10,1... | collective-permute-start | bytes 221192 | tf_op jit(solution)/shard_map/ppermute | solution.py:396
  43.0 17.8 %collective-permute-start.5 = (bf16[288,128]{1,0:T(8,128)(2,1)}, bf16[288,128]{1,0:T(8,128)(2,1)S(1)}, u32[]{:S(2)}, u32[]{:S(2)}) collective-permute-start(bf16[288,128]{1,0:T(8,128)(2,1)} %get-tuple-element.31), channel_id=1, source_target_pairs={{0,2},{1,3},{2,0},{3,1},{4,6},{5,7},{6,4},{7,5},{8,10},{9,11},{10,... | collective-permute-start | bytes 221192 | tf_op jit(solution)/shard_map/ppermute | solution.py:396
  45.7 15.8 %collective-permute-start.6 = (bf16[288,128]{1,0:T(8,128)(2,1)}, bf16[288,128]{1,0:T(8,128)(2,1)}, u32[]{:S(2)}, u32[]{:S(2)}) collective-permute-start(bf16[288,128]{1,0:T(8,128)(2,1)} %get-tuple-element.32), channel_id=1, source_target_pairs={{0,3},{1,0},{2,1},{3,2},{4,7},{5,4},{6,5},{7,6},{8,11},{9,8},{10,9... | collective-permute-start | bytes 221192 | tf_op jit(solution)/shard_map/ppermute | solution.py:396
  46.6 22.2 %all-to-all-start.1 = ((bf16[32,16,128]{2,1,0:T(8,128)(2,1)}), bf16[32,16,128]{2,1,0:T(8,128)(2,1)S(1)}, u32[]{:S(2)}, u32[]{:S(2)}) async-start(bf16[32,16,128]{2,1,0:T(8,128)(2,1)} %fold.1), calls=%async_computation.1 | async-start | bytes 262144 | tf_op jit(solution)/shard_map/all_to_all | solution.py:429
  58.0 0.6 copy-start.1
  60.8 0.6 copy-start.4
  61.5 0.9 %copy-start.2 = (bf16[288,128]{1,0:T(8,128)(2,1)S(1)}, bf16[288,128]{1,0:T(8,128)(2,1)}, u32[]{:S(2)}) copy-start(bf16[288,128]{1,0:T(8,128)(2,1)} %copy-done.1) | copy-start | bytes 221188
  62.3 0.9 %copy-start.5 = (bf16[288,128]{1,0:T(8,128)(2,1)S(1)}, bf16[288,128]{1,0:T(8,128)(2,1)}, u32[]{:S(2)}) copy-start(bf16[288,128]{1,0:T(8,128)(2,1)} %copy-done.4) | copy-start | bytes 221188
  63.2 0.9 %copy-start.12 = (f32[64,768]{1,0:T(8,128)S(1)}, f32[64,768]{1,0:T(8,128)}, u32[]{:S(2)}) copy-start(f32[64,768]{1,0:T(8,128)} %copy-done.11) | copy-start | bytes 589828
  68.2 0.6 copy-start.7
  68.8 2.7 %copy-start.3 = (bf16[288,128]{1,0:T(8,128)(2,1)S(1)}, bf16[288,128]{1,0:T(8,128)(2,1)}, u32[]{:S(2)}) copy-start(bf16[288,128]{1,0:T(8,128)(2,1)} %copy-done.1) | copy-start | bytes 221188
  68.8 2.7 %copy-start.6 = (bf16[288,128]{1,0:T(8,128)(2,1)S(1)}, bf16[288,128]{1,0:T(8,128)(2,1)}, u32[]{:S(2)}) copy-start(bf16[288,128]{1,0:T(8,128)(2,1)} %copy-done.4) | copy-start | bytes 221188
  68.8 0.8 %copy-start.8 = (f32[64,64]{1,0:T(8,128)S(1)}, f32[64,64]{1,0:T(8,128)}, u32[]{:S(2)}) copy-start(f32[64,64]{1,0:T(8,128)} %copy-done.7) | copy-start | bytes 49156
  (1 other events, 0.6 us)

commit v8 on v5

--- a/solution.py
+++ b/solution.py
@@ -50,9 +50,9 @@
 
 def merge_kernel(acts_ref, kv_ref, err_ref, vt_ref, merged_ref, lt_ref):
     merged = lax.dot_general(acts_ref[...], kv_ref[...], ROWS_FIRST, preferred_element_type=F32)
-    merged = merged + err_ref[0].astype(F32)
+    merged = (merged + err_ref[0].astype(F32)).astype(BF16)
     merged_ref[...] = merged
-    lt_ref[...] = left_times(vt_ref[...], merged.astype(BF16), COLS_LAST)
+    lt_ref[...] = left_times(vt_ref[...], merged, COLS_LAST)
 
 
 def merge(acts, kv, err, vt):
@@ -74,7 +74,7 @@
             pl.BlockSpec((rank, block), lambda i: (0, i)),
         ],
         out_shape=[
-            jax.ShapeDtypeStruct((rows, cols), F32),
+            jax.ShapeDtypeStruct((rows, cols), BF16),
             jax.ShapeDtypeStruct((rank, rows), F32),
         ],
         compiler_params=params(24),
@@ -105,44 +105,56 @@
     )(hidden)
 
 
+def as_terms(x, hold=lambda rounded: rounded):
+    high = hold(x.astype(BF16)).astype(F32)
+    rest = x - high
+    middle = hold(rest.astype(BF16)).astype(F32)
+    low = rest - middle
+    return jnp.concatenate([high, middle], axis=-1), jnp.concatenate([low, jnp.zeros_like(low)], axis=-1)
+
+
+def from_terms(first, second):
+    rank = first.shape[-1] // 2
+    return first[..., :rank] + first[..., rank:] + second[..., :rank]
+
+
 def right_kernel(n_parts, *refs):
     part_refs, merged_ref = refs[:n_parts], refs[n_parts]
-    lt_ref, gram_ref, chunk_ref = refs[n_parts + 1 :]
+    lt_ref, chunk_ref = refs[n_parts + 1 :]
     parts = [ref[...].astype(F32) for ref in part_refs]
     while len(parts) > 1:
         parts = [a + b for a, b in zip(parts[0::2], parts[1::2])]
     lt = parts[0]
     rank = lt.shape[0]
-    lt_ref[...] = lt
-    product = left_times(lt, merged_ref[...].astype(BF16), (((1,), (0,)), ((), ()))).astype(BF16)
+    lt_ref[...] = lt.astype(BF16)
+    product = left_times(lt, merged_ref[...], (((1,), (0,)), ((), ()))).astype(BF16)
     across = product.shape[1] // TILE_C
     for a in range(rank // TILE_R):
         for b in range(across):
-            chunk_ref[a * across + b] = product[
+            chunk_ref[a * across + b, 0:TILE_R] = product[
                 a * TILE_R : (a + 1) * TILE_R, b * TILE_C : (b + 1) * TILE_C
             ]
-    gram = lax.dot_general(lt, lt, COLS_LAST, precision=HIGHEST, preferred_element_type=F32)
-    half = rank // 2
-    packed = jnp.concatenate([gram[:half], gram[half:]], axis=1)
-    high = packed.astype(BF16)
-    rest = packed - high.astype(F32)
-    middle = rest.astype(BF16)
-    low = (rest - middle.astype(F32)).astype(BF16)
-    gram_ref[0:half] = high
-    gram_ref[half : 2 * half] = middle
-    gram_ref[2 * half : 3 * half] = low
+    first, second = as_terms(
+        lax.dot_general(lt, lt, COLS_LAST, precision=HIGHEST, preferred_element_type=F32)
+    )
+    chunks, pieces = chunk_ref.shape[0], rank // 8
+    for i in range(pieces):
+        here = slice(8 * i, 8 * i + 8)
+        piece = jnp.concatenate([first[here], second[here]], axis=0).astype(BF16)
+        for c in range(i * chunks // pieces, (i + 1) * chunks // pieces):
+            chunk_ref[c, TILE_R:] = piece
 
 
 def right_product(parts, merged):
     rank, rows = parts[0].shape
     cols = merged.shape[1]
+    assert 2 * rank == TILE_C
     chunks = rank * cols // (TILE_R * TILE_C)
     return pl.pallas_call(
         functools.partial(right_kernel, len(parts)),
         out_shape=[
-            jax.ShapeDtypeStruct((rank, rows), F32),
-            jax.ShapeDtypeStruct((3 * (rank // 2), 2 * rank), BF16),
-            jax.ShapeDtypeStruct((chunks, TILE_R, TILE_C), BF16),
+            jax.ShapeDtypeStruct((rank, rows), BF16),
+            jax.ShapeDtypeStruct((chunks, 2 * TILE_R, TILE_C), BF16),
         ],
         compiler_params=params(16),
         cost_estimate=SMALL,
@@ -150,18 +162,25 @@
     )(*parts, merged)
 
 
-def fold_kernel(share_ref, out_ref):
-    total = share_ref[0].astype(F32)
+def fold_kernel(n_exp, share_ref, out_ref):
+    total = share_ref[0, 0:TILE_R].astype(F32)
     for i in range(1, share_ref.shape[0]):
-        total = total + share_ref[i].astype(F32)
+        total = total + share_ref[i, 0:TILE_R].astype(F32)
     total = total.astype(BF16)
+    gram = None
+    for j in range(n_exp):
+        terms = share_ref[j, TILE_R:].astype(F32)
+        part = from_terms(terms[:8], terms[8:])
+        gram = part if gram is None else gram + part
+    piece = jnp.concatenate(as_terms(gram), axis=0).astype(BF16)
     for i in range(out_ref.shape[0]):
-        out_ref[i] = total
-
-
-def fold(shares):
-    return pl.pallas_call(
-        fold_kernel,
+        out_ref[i, 0:TILE_R] = total
+        out_ref[i, TILE_R:] = piece
+
+
+def fold(shares, n_exp):
+    return pl.pallas_call(
+        functools.partial(fold_kernel, n_exp),
         out_shape=jax.ShapeDtypeStruct(shares.shape, BF16),
         compiler_params=params(4),
         cost_estimate=SMALL,
@@ -169,28 +188,16 @@
     )(shares)
 
 
-def inverse_kernel(n_exp, *refs):
-    load_hbms, lt_hbm = refs[:n_exp], refs[n_exp]
-    w_ref, basis_ref, terms_ref, lt_ref, wide_ref, sems = refs[n_exp + 1 :]
-    rank = lt_ref.shape[0]
-    half = rank // 2
-    copies = [
-        pltpu.make_async_copy(load_hbms[k], terms_ref.at[k], sems.at[k])
-        for k in range(n_exp)
-    ]
-    lt_copy = pltpu.make_async_copy(lt_hbm, lt_ref, sems.at[n_exp])
-    for copy in copies:
-        copy.start()
-    lt_copy.start()
-    for copy in copies:
-        copy.wait()
-    place = lax.axis_index("exp")
-    packed = None
-    for j in range(n_exp):
-        terms = terms_ref[lax.rem(place + n_exp - j, n_exp)].astype(F32)
-        part = terms[:half] + terms[half : 2 * half] + terms[2 * half :]
-        packed = part if packed is None else packed + part
-    gram = jnp.concatenate([packed[:, :rank], packed[:, rank:]], axis=0)
+def fold_any(chunks):
+    wide = chunks.astype(F32)
+    total = lax.psum(wide[:, :TILE_R], ("rep", "exp"))
+    terms = lax.psum(wide[:, TILE_R:], "exp")
+    pieces = as_terms(from_terms(terms[:, :8], terms[:, 8:]), lax.optimization_barrier)
+    return jnp.concatenate([total, *pieces], axis=1).astype(BF16)
+
+
+def inverse_of_factor(gram, wide_ref):
+    rank = gram.shape[0]
     row = lax.broadcasted_iota(jnp.int32, (rank, rank), 0)
     col = lax.broadcasted_iota(jnp.int32, (rank, rank), 1)
     a = jnp.concatenate([gram, jnp.where(row == col, 1.0, 0.0).astype(F32)], axis=1)
@@ -206,60 +213,41 @@
                 cols[m] = cols[m] - factor * cols[m][k + j : k + j + 1, :]
                 rows[m] = rows[m] - factor[k + m : k + m + 1, :] * rows[j]
             a = a - factor * rows[j]
-    w = wide_ref[:, rank:]
-    w_ref[...] = w
-    lt_copy.wait()
-    basis = jnp.dot(w, lt_ref[...], precision=HIGHEST, preferred_element_type=F32)
-    basis_ref[...] = basis.T.astype(BF16)
-
-
-def inverse_factor(loads, lt):
-    rank, rows = lt.shape
-    n_exp = len(loads)
-    return pl.pallas_call(
-        functools.partial(inverse_kernel, n_exp),
-        in_specs=[ANY] * (n_exp + 1),
-        out_shape=[
-            jax.ShapeDtypeStruct((rank, rank), F32),
-            jax.ShapeDtypeStruct((rows, rank), BF16),
-        ],
-        scratch_shapes=[
-            pltpu.VMEM((n_exp, 3 * (rank // 2), 2 * rank), BF16),
-            pltpu.VMEM((rank, rows), F32),
-            pltpu.VMEM((rank, 2 * rank), F32),
-            pltpu.SemaphoreType.DMA((n_exp + 1,)),
-        ],
-        compiler_params=params(8),
-        cost_estimate=SMALL,
-        name="inverse_factor",
-    )(*loads, lt)
+    return wide_ref[:, rank:]
 
 
 def finish_kernel(
-    replicas, w_any, chunk_ref, basis_any, merged_ref, right_hbm, err_hbm, w_ref, basis_ref, right_ref, err_ref, sems
+    replicas, chunk_ref, lt_any, merged_ref, right_hbm, err_hbm, lt_ref, wide_ref, right_ref, err_ref, sems
 ):
     rank, cols = right_ref.shape
     rows, block = err_ref.shape[0], 128
-    w_copy = pltpu.make_async_copy(w_any, w_ref, sems.at[rows // block + 1])
-    w_copy.start()
-    basis_copy = pltpu.make_async_copy(basis_any, basis_ref, sems.at[rows // block + 2])
-    basis_copy.start()
+    lt_copy = pltpu.make_async_copy(lt_any, lt_ref, sems.at[rows // block + 1])
+    lt_copy.start()
+    chunks, count = chunk_ref.shape[0], rank // 8
+    gram = []
+    for i in range(count):
+        terms = chunk_ref[i * chunks // count, TILE_R:].astype(F32)
+        gram.append(from_terms(terms[:8], terms[8:]))
+    w = inverse_of_factor(jnp.concatenate(gram, axis=0), wide_ref)
     across = cols // TILE_C
     pieces = []
     for a in range(rank // TILE_R):
-        pieces.append(jnp.concatenate([chunk_ref[a * across + b] for b in range(across)], axis=1))
+        pieces.append(
+            jnp.concatenate([chunk_ref[a * across + b, 0:TILE_R] for b in range(across)], axis=1)
+        )
     product = jnp.concatenate(pieces, axis=0)
-    w_copy.wait()
-    new_right = left_times(w_ref[...], product, (((1,), (0,)), ((), ()))) * (1.0 / replicas)
+    inner = (((1,), (0,)), ((), ()))
+    new_right = left_times(w, product, inner) * (1.0 / replicas)
     right_ref[...] = new_right
     copies = [pltpu.make_async_copy(right_ref, right_hbm, sems.at[0])]
     copies[0].start()
     rounded = new_right.astype(BF16)
-    basis_copy.wait()
+    lt_copy.wait()
+    basis = left_times(w, lt_ref[...], inner).T.astype(BF16)
     for i in range(rows // block):
         here = slice(i * block, (i + 1) * block)
-        approx = jnp.dot(basis_ref[here, :], rounded, preferred_element_type=F32)
-        err_ref[here, :] = (merged_ref[here, :] - approx).astype(BF16)
+        approx = jnp.dot(basis[here, :], rounded, preferred_element_type=F32)
+        err_ref[here, :] = (merged_ref[here, :].astype(F32) - approx).astype(BF16)
         copies.append(
             pltpu.make_async_copy(err_ref.at[here, :], err_hbm.at[0, here, :], sems.at[i + 1])
         )
@@ -268,28 +256,28 @@
         copy.wait()
 
 
-def finish(replicas, w, chunks, basis, merged):
-    rows, rank = basis.shape
+def finish(replicas, chunks, lt, merged):
+    rank, rows = lt.shape
     cols = merged.shape[1]
     return pl.pallas_call(
         functools.partial(finish_kernel, replicas),
-        in_specs=[ANY, VMEM, ANY, VMEM],
+        in_specs=[VMEM, ANY, VMEM],
         out_specs=[HBM] * 2,
         out_shape=[
             jax.ShapeDtypeStruct((rank, cols), F32),
             jax.ShapeDtypeStruct((1, rows, cols), BF16),
         ],
         scratch_shapes=[
-            pltpu.VMEM((rank, rank), F32),
-            pltpu.VMEM((rows, rank), BF16),
+            pltpu.VMEM((rank, rows), BF16),
+            pltpu.VMEM((rank, 2 * rank), F32),
             pltpu.VMEM((rank, cols), F32),
             pltpu.VMEM((rows, cols), BF16),
-            pltpu.SemaphoreType.DMA((rows // 128 + 3,)),
+            pltpu.SemaphoreType.DMA((rows // 128 + 2,)),
         ],
         compiler_params=params(16),
         cost_estimate=SMALL,
         name="finish",
-    )(w, chunks, basis, merged)
+    )(chunks, lt, merged)
 
 
 def expert_kernel(n_exp, chunk, *refs):
@@ -413,22 +401,19 @@
         masks = [bit] if 2 * bit >= n_rep else [bit, 2 * bit, 3 * bit]
         parts = [own] + [swap(own, "rep", n_rep, m) for m in masks]
         bit *= len(parts)
-    lt, gram, chunks = right_product(parts, merged)
-
-    slabs = [slabs[0]] + [shift(after(slabs[k], gram), n_exp, k) for k in range(1, n_exp)]
-    grams = [gram] + [shift(gram, n_exp, k) for k in range(1, n_exp)]
-
-    if chunks.shape[0] == n_rep * n_exp:
+    lt, chunks = right_product(parts, merged)
+
+    if chunks.shape[0] == n_rep * n_exp and 8 * n_rep == lt.shape[0]:
         both = ("rep", "exp")
         shares = lax.all_to_all(chunks, both, 0, 0, tiled=True)
-        shares, grams, grads = lax.optimization_barrier((shares, grams, grads))
-        share = fold(shares)
+        shares, grads = lax.optimization_barrier((shares, grads))
+        share = fold(shares, n_exp)
         chunks = lax.all_to_all(share, both, 0, 0, tiled=True)
     else:
         share = chunks
-        chunks = lax.psum(chunks.astype(F32), ("rep", "exp")).astype(BF16)
-    w, basis = inverse_factor(grams, lt)
-
+        chunks = fold_any(chunks)
+
+    slabs = [slabs[0]] + [shift(after(slabs[k], share), n_exp, k) for k in range(1, n_exp)]
     left, right = 1, n_exp - 1
     while right - left > 1:
         if left <= n_exp - right:
@@ -438,7 +423,7 @@
             grads[right - 1] = shift(after(grads[right], share), n_exp, -1)
             right -= 1
 
-    new_right, new_error = finish(n_rep, w, chunks, basis, merged)
+    new_right, new_error = finish(n_rep, chunks, lt, merged)
     first_new, second_new, step = expert_step(
         slabs, [grads[k] for k in range(n_exp)], moment_one, moment_two
     )

time: 69.9 us -> 78.8 us (1.13)
  waiting for transfers between devices: 16.7 us -> 35.3 us
  local copies, waits for them, and re-layouts: 7.03 us -> 0.93 us
  starting transfers between devices: 27.6 us -> 24.1 us
    all_to_all x1, waiting for transfers between devices: 1.22 us -> 11.8 us  [body(): chunks = lax.all_to_all(share, both, 0, 0, tiled=True)]
    unnamed x24 -> x4, local copies, waits for them, and re-layouts: 7.03 us -> 0.93 us
    all_to_all x1, waiting for transfers between devices: 0.01 us -> 5.68 us  [body(): shares = lax.all_to_all(chunks, both, 0, 0, tiled=True)]
    ppermute x9 -> x6, waiting for transfers between devices: 11.1 us -> 15.9 us  [shift(): return lax.ppermute(x, 'exp', [(i, (i + k) % size) for i in range(size)])]
    ppermute x9 -> x6, starting transfers between devices: 14.9 us -> 10.5 us  [shift(): return lax.ppermute(x, 'exp', [(i, (i + k) % size) for i in range(size)])]
    ppermute x4, waiting for transfers between devices: 4.36 us -> 1.87 us  [swap(): return lax.ppermute(x, axis, [(i, i ^ mask) for i in range(size)])]
    all_to_all x1, starting transfers between devices: 5.35 us -> 3.45 us  [body(): chunks = lax.all_to_all(share, both, 0, 0, tiled=True)]
    all_to_all x1, starting transfers between devices: 3.24 us -> 5.09 us  [body(): shares = lax.all_to_all(chunks, both, 0, 0, tiled=True)]
  transfers between devices with their start and end apart: 15 -> 12, of which waited for: 7 -> 7; matrix products, arithmetic and copies ran while one was open for 0% -> 0% of each run, Pallas kernels for 10% -> 9%
where the time goes in v8:
time: 78.8 us; the launch traced here: 78.4 us
  waiting for transfers between devices  35.3 us (45%)
  starting transfers between devices  24.1 us (31%)
  Pallas kernels  17.4 us (22%)
  local copies, waits for them, and re-layouts  0.93 us (1%)
    ppermute x6, waiting for transfers between devices, shift(): return lax.ppermute(x, 'exp', [(i, (i + k) % size) for i in range(size)])  15.9 us
    all_to_all x1, waiting for transfers between devices, body(): chunks = lax.all_to_all(share, both, 0, 0, tiled=True)  11.8 us
    ppermute x6, starting transfers between devices, shift(): return lax.ppermute(x, 'exp', [(i, (i + k) % size) for i in range(size)])  10.5 us
    all_to_all x1, waiting for transfers between devices, body(): shares = lax.all_to_all(chunks, both, 0, 0, tiled=True)  5.68 us
    pallas_call x1, Pallas kernels, merge(): pl.pallas_call(merge_kernel, grid=(rows // block,), in_specs=[pl.BlockSpe...  5.26 us
    all_to_all x1, starting transfers between devices, body(): shares = lax.all_to_all(chunks, both, 0, 0, tiled=True)  5.09 us
    ppermute x4, starting transfers between devices, swap(): return lax.ppermute(x, axis, [(i, i ^ mask) for i in range(size)])  5.04 us
    pallas_call x1, Pallas kernels, finish(): pl.pallas_call(functools.partial(finish_kernel, replicas), in_specs=[VMEM...  4.78 us
  transfers between devices with their start and end apart: 12, of which 7 were waited for; matrix products, arithmetic and copies ran while one was open for 0% of the time, Pallas kernels for 9%

profile of v8, /device:TPU:0, one launch (start us, length us, event | category | flops | bytes accessed | tf_op | source)
XLA Modules:
  0.0 78.4 jit_solution(15126353776819781545)
XLA Ops:
  0.6 5.3 %merge.1 = (bf16[768,1024]{1,0:T(8,128)(2,1)S(1)}, f32[64,768]{1,0:T(8,128)S(1)}) custom-call(bf16[1024,768]{1,0:T(8,128)(2,1)} %acts_ref.1, bf16[1024,1024]{1,0:T(8,128)(2,1)} %kv_ref.1, bf16[1,768,1024]{2,1,0:T(8,128)(2,1)} %err_ref.1, f32[64,1024]{1,0:T(8,128)} %bitcast.2), custom_call_target="tpu_custom_call" | custom-call | flops 1000 | bytes 1000 | tf_op jit(solution)/shard_map/merge/pallas_call | solution.py:63
  5.9 0.5 collective-permute-start
  6.4 1.1 %collective-permute-done = f32[64,768]{1,0:T(8,128)S(1)} collective-permute-done((f32[64,768]{1,0:T(8,128)S(1)}, f32[64,768]{1,0:T(8,128)S(1)}, u32[]{:S(2)}, u32[]{:S(2)}) %collective-permute-start) | collective-permute-done | bytes 196640 | tf_op jit(solution)/shard_map/ppermute | solution.py:376
  7.5 3.9 %collective-permute-start.3 = (bf16[64,768]{1,0:T(8,128)(2,1)S(1)}, bf16[64,768]{1,0:T(8,128)(2,1)S(1)}, u32[]{:S(2)}, u32[]{:S(2)}) collective-permute-start(bf16[64,768]{1,0:T(8,128)(2,1)S(1)} %add_convert_fusion.refs_0_), channel_id=1, source_target_pairs={{0,24},{4,28},{8,16},{12,20},{16,8},{20,12},{24,0},{28,4},{1,25},{... | collective-permute-start | bytes 294920 | tf_op jit(solution)/shard_map/ppermute | solution.py:376
  11.4 0.5 collective-permute-start.2
  12.0 2.0 %collective-permute-start.4 = (bf16[1,128,2048]{2,1,0:T(8,128)(2,1)S(1)}, bf16[1,128,2048]{2,1,0:T(8,128)(2,1)S(1)}, u32[]{:S(2)}, u32[]{:S(2)}) collective-permute-start(bf16[1,128,2048]{2,1,0:T(8,128)(2,1)S(1)} %copy-done.1), channel_id=1, source_target_pairs={{0,1},{1,2},{2,3},{3,0},{4,5},{5,6},{6,7},{7,4},{8,9},{9,10},{10,1... | collective-permute-start | bytes 1572872 | tf_op jit(solution)/shard_map/ppermute | solution.py:380
  14.0 2.0 %collective-permute-start.5 = (bf16[1,128,2048]{2,1,0:T(8,128)(2,1)S(1)}, bf16[1,128,2048]{2,1,0:T(8,128)(2,1)S(1)}, u32[]{:S(2)}, u32[]{:S(2)}) collective-permute-start(bf16[1,128,2048]{2,1,0:T(8,128)(2,1)S(1)} %copy-done.1), channel_id=1, source_target_pairs={{0,3},{1,0},{2,1},{3,2},{4,7},{5,4},{6,5},{7,6},{8,11},{9,8},{10,9... | collective-permute-start | bytes 1572872 | tf_op jit(solution)/shard_map/ppermute | solution.py:380
  16.1 0.6 collective-permute-done.2.refs_2_
  16.6 0.2 collective-permute-done.1.refs_1_
  16.9 1.3 %right_product.1 = (bf16[64,768]{1,0:T(8,128)(2,1)S(1)}, bf16[32,32,128]{2,1,0:T(8,128)(2,1)}) custom-call(bf16[64,768]{1,0:T(8,128)(2,1)S(1)} %add_convert_fusion.refs_0_, bf16[64,768]{1,0:T(8,128)(2,1)S(1)} %collective-permute-done.1.refs_1_, bf16[64,768]{1,0:T(8,128)(2,1)S(1)} %collective-permute-done.2.refs_2_, ...), custom_call_target="tpu_custom_call" | custom-call | flops 1000 | bytes 1000 | tf_op jit(solution)/shard_map/right_product/pallas_call | solution.py:153
  18.2 5.1 %all-to-all-start = ((bf16[32,32,128]{2,1,0:T(8,128)(2,1)}), bf16[32,32,128]{2,1,0:T(8,128)(2,1)S(1)}, u32[]{:S(2)}, u32[]{:S(2)}) async-start(bf16[32,32,128]{2,1,0:T(8,128)(2,1)} %get-tuple-element.29), calls=%async_computation | async-start | bytes 524288 | tf_op jit(solution)/shard_map/all_to_all | solution.py:408
  23.3 5.6 %collective-permute-done.4.refs_5_ = bf16[1,128,2048]{2,1,0:T(8,128)(2,1)S(1)} collective-permute-done((bf16[1,128,2048]{2,1,0:T(8,128)(2,1)S(1)}, bf16[1,128,2048]{2,1,0:T(8,128)(2,1)S(1)}, u32[]{:S(2)}, u32[]{:S(2)}) %collective-permute-start.4) | collective-permute-done | bytes 524320 | tf_op jit(solution)/shard_map/ppermute | solution.py:380
  28.9 10.2 %collective-permute-done.5.refs_7_ = bf16[1,128,2048]{2,1,0:T(8,128)(2,1)S(1)} collective-permute-done((bf16[1,128,2048]{2,1,0:T(8,128)(2,1)S(1)}, bf16[1,128,2048]{2,1,0:T(8,128)(2,1)S(1)}, u32[]{:S(2)}, u32[]{:S(2)}) %collective-permute-start.5) | collective-permute-done | bytes 524320 | tf_op jit(solution)/shard_map/ppermute | solution.py:380
  39.2 5.7 %all-to-all-done.share_ref = bf16[32,32,128]{2,1,0:T(8,128)(2,1)S(1)} async-done(((bf16[32,32,128]{2,1,0:T(8,128)(2,1)}), bf16[32,32,128]{2,1,0:T(8,128)(2,1)S(1)}, u32[]{:S(2)}, u32[]{:S(2)}) %all-to-all-start) | async-done | bytes 262176 | tf_op jit(solution)/shard_map/all_to_all | solution.py:408
  44.8 0.9 %fold.1 = bf16[32,32,128]{2,1,0:T(8,128)(2,1)} custom-call(bf16[32,32,128]{2,1,0:T(8,128)(2,1)S(1)} %all-to-all-done.share_ref), custom_call_target="tpu_custom_call" | custom-call | flops 1000 | bytes 1000 | tf_op jit(solution)/shard_map/fold/pallas_call | solution.py:182
  45.7 1.8 %collective-permute-start.9 = (bf16[1,128,2048]{2,1,0:T(8,128)(2,1)S(1)}, bf16[1,128,2048]{2,1,0:T(8,128)(2,1)S(1)}, u32[]{:S(2)}, u32[]{:S(2)}) collective-permute-start(bf16[1,128,2048]{2,1,0:T(8,128)(2,1)S(1)} %collective-permute-done.4.refs_5_), channel_id=1, source_target_pairs={{0,1},{1,2},{2,3},{3,0},{4,5},{5,6},{6,7},{7,4},{8,9},{9,10},{10,1... | collective-permute-start | bytes 1572872 | tf_op jit(solution)/shard_map/ppermute | solution.py:380
  47.5 3.4 %all-to-all-start.1 = ((bf16[32,32,128]{2,1,0:T(8,128)(2,1)}), bf16[32,32,128]{2,1,0:T(8,128)(2,1)S(1)}, u32[]{:S(2)}, u32[]{:S(2)}) async-start(bf16[32,32,128]{2,1,0:T(8,128)(2,1)} %fold.1), calls=%async_computation.1 | async-start | bytes 524288 | tf_op jit(solution)/shard_map/all_to_all | solution.py:411
  51.0 0.9 %copy-done = bf16[1,128,768]{2,1,0:T(8,128)(2,1)S(1)} copy-done((bf16[1,128,768]{2,1,0:T(8,128)(2,1)S(1)}, bf16[1,128,768]{2,1,0:T(8,128)(2,1)}, u32[]{:S(2)}) %copy-start) | copy-done | bytes 196632
  51.9 0.8 unit_slabs.1
  52.7 3.6 %collective-permute-start.8 = (bf16[192,128]{1,0:T(8,128)(2,1)}, bf16[192,128]{1,0:T(8,128)(2,1)}, u32[]{:S(2)}, u32[]{:S(2)}) collective-permute-start(bf16[192,128]{1,0:T(8,128)(2,1)} %get-tuple-element.41), channel_id=1, source_target_pairs={{0,3},{1,0},{2,1},{3,2},{4,7},{5,4},{6,5},{7,6},{8,11},{9,8},{10,9... | collective-permute-start | bytes 147464 | tf_op jit(solution)/shard_map/ppermute | solution.py:380
  56.3 1.1 %collective-permute-start.6 = (bf16[192,128]{1,0:T(8,128)(2,1)}, bf16[192,128]{1,0:T(8,128)(2,1)}, u32[]{:S(2)}, u32[]{:S(2)}) collective-permute-start(bf16[192,128]{1,0:T(8,128)(2,1)} %get-tuple-element.37), channel_id=1, source_target_pairs={{0,1},{1,2},{2,3},{3,0},{4,5},{5,6},{6,7},{7,4},{8,9},{9,10},{10,1... | collective-permute-start | bytes 147464 | tf_op jit(solution)/shard_map/ppermute | solution.py:380
  57.4 11.8 %all-to-all-done.1.chunk_ref = bf16[32,32,128]{2,1,0:T(8,128)(2,1)S(1)} async-done(((bf16[32,32,128]{2,1,0:T(8,128)(2,1)}), bf16[32,32,128]{2,1,0:T(8,128)(2,1)S(1)}, u32[]{:S(2)}, u32[]{:S(2)}) %all-to-all-start.1) | async-done | bytes 262176 | tf_op jit(solution)/shard_map/all_to_all | solution.py:411
  69.2 4.8 %finish.1 = (f32[64,1024]{1,0:T(8,128)}, bf16[1,768,1024]{2,1,0:T(8,128)(2,1)}) custom-call(bf16[32,32,128]{2,1,0:T(8,128)(2,1)S(1)} %all-to-all-done.1.chunk_ref, bf16[64,768]{1,0:T(8,128)(2,1)S(1)} %get-tuple-element.31.lt_any, bf16[768,1024]{1,0:T(8,128)(2,1)S(1)} %get-tuple-element.28.refs_4_.merged_ref), custom_call_target="tpu_custom_call" | custom-call | flops 1000 | bytes 1000 | tf_op jit(solution)/shard_map/finish/pallas_call | solution.py:262
  74.0 4.4 %expert_step.1 = (f32[1,192,2048]{2,1,0:T(8,128)}, f32[1,192,2048]{2,1,0:T(8,128)}, bf16[1,192,2048]{2,1,0:T(8,128)(2,1)}) custom-call(bf16[192,128]{1,0:T(8,128)(2,1)S(1)} %get-tuple-element.35.refs_0_, bf16[192,128]{1,0:T(8,128)(2,1)} %collective-permute-done.6.refs_1_, bf16[192,128]{1,0:T(8,128)(2,1)} %collective-permute-done.7.refs_2_, ...), custom_call_target="tpu_custom_call" | custom-call | flops 1000 | bytes 1000 | tf_op jit(solution)/shard_map/expert_step/pallas_call | solution.py:347
  (11 shorter events, 0.2 us)
Async XLA Ops:
  0.6 11.4 %copy-start.1 = (bf16[1,128,2048]{2,1,0:T(8,128)(2,1)S(1)}, bf16[1,128,2048]{2,1,0:T(8,128)(2,1)}, u32[]{:S(2)}) copy-start(bf16[1,128,2048]{2,1,0:T(8,128)(2,1)} %refs_4_) | copy-start | bytes 1572868
  5.9 1.6 %collective-permute-start = (f32[64,768]{1,0:T(8,128)S(1)}, f32[64,768]{1,0:T(8,128)S(1)}, u32[]{:S(2)}, u32[]{:S(2)}) collective-permute-start(f32[64,768]{1,0:T(8,128)S(1)} %get-tuple-element.27), channel_id=1, source_target_pairs={{0,4},{4,0},{8,12},{12,8},{16,20},{20,16},{24,28},{28,24},{1,5},{5... | collective-permute-start | bytes 589832 | tf_op jit(solution)/shard_map/ppermute | solution.py:376
  7.5 8.5 %collective-permute-start.3 = (bf16[64,768]{1,0:T(8,128)(2,1)S(1)}, bf16[64,768]{1,0:T(8,128)(2,1)S(1)}, u32[]{:S(2)}, u32[]{:S(2)}) collective-permute-start(bf16[64,768]{1,0:T(8,128)(2,1)S(1)} %add_convert_fusion.refs_0_), channel_id=1, source_target_pairs={{0,24},{4,28},{8,16},{12,20},{16,8},{20,12},{24,0},{28,4},{1,25},{... | collective-permute-start | bytes 294920 | tf_op jit(solution)/shard_map/ppermute | solution.py:376
  11.4 5.2 %collective-permute-start.2 = (bf16[64,768]{1,0:T(8,128)(2,1)S(1)}, bf16[64,768]{1,0:T(8,128)(2,1)S(1)}, u32[]{:S(2)}, u32[]{:S(2)}) collective-permute-start(bf16[64,768]{1,0:T(8,128)(2,1)S(1)} %add_convert_fusion.refs_0_), channel_id=1, source_target_pairs={{0,16},{4,20},{8,24},{12,28},{16,0},{20,4},{24,8},{28,12},{1,17},{... | collective-permute-start | bytes 294920 | tf_op jit(solution)/shard_map/ppermute | solution.py:376
  11.9 4.9 %collective-permute-start.1 = (bf16[64,768]{1,0:T(8,128)(2,1)S(1)}, bf16[64,768]{1,0:T(8,128)(2,1)S(1)}, u32[]{:S(2)}, u32[]{:S(2)}) collective-permute-start(bf16[64,768]{1,0:T(8,128)(2,1)S(1)} %add_convert_fusion.refs_0_), channel_id=1, source_target_pairs={{0,8},{4,12},{8,0},{12,4},{16,24},{20,28},{24,16},{28,20},{1,9},{5... | collective-permute-start | bytes 294920 | tf_op jit(solution)/shard_map/ppermute | solution.py:376
  12.0 16.9 %collective-permute-start.4 = (bf16[1,128,2048]{2,1,0:T(8,128)(2,1)S(1)}, bf16[1,128,2048]{2,1,0:T(8,128)(2,1)S(1)}, u32[]{:S(2)}, u32[]{:S(2)}) collective-permute-start(bf16[1,128,2048]{2,1,0:T(8,128)(2,1)S(1)} %copy-done.1), channel_id=1, source_target_pairs={{0,1},{1,2},{2,3},{3,0},{4,5},{5,6},{6,7},{7,4},{8,9},{9,10},{10,1... | collective-permute-start | bytes 1572872 | tf_op jit(solution)/shard_map/ppermute | solution.py:380
  14.0 25.1 %collective-permute-start.5 = (bf16[1,128,2048]{2,1,0:T(8,128)(2,1)S(1)}, bf16[1,128,2048]{2,1,0:T(8,128)(2,1)S(1)}, u32[]{:S(2)}, u32[]{:S(2)}) collective-permute-start(bf16[1,128,2048]{2,1,0:T(8,128)(2,1)S(1)} %copy-done.1), channel_id=1, source_target_pairs={{0,3},{1,0},{2,1},{3,2},{4,7},{5,4},{6,5},{7,6},{8,11},{9,8},{10,9... | collective-permute-start | bytes 1572872 | tf_op jit(solution)/shard_map/ppermute | solution.py:380
  18.2 26.7 %all-to-all-start = ((bf16[32,32,128]{2,1,0:T(8,128)(2,1)}), bf16[32,32,128]{2,1,0:T(8,128)(2,1)S(1)}, u32[]{:S(2)}, u32[]{:S(2)}) async-start(bf16[32,32,128]{2,1,0:T(8,128)(2,1)} %get-tuple-element.29), calls=%async_computation | async-start | bytes 524288 | tf_op jit(solution)/shard_map/all_to_all | solution.py:408
  45.7 28.3 %collective-permute-start.9 = (bf16[1,128,2048]{2,1,0:T(8,128)(2,1)S(1)}, bf16[1,128,2048]{2,1,0:T(8,128)(2,1)S(1)}, u32[]{:S(2)}, u32[]{:S(2)}) collective-permute-start(bf16[1,128,2048]{2,1,0:T(8,128)(2,1)S(1)} %collective-permute-done.4.refs_5_), channel_id=1, source_target_pairs={{0,1},{1,2},{2,3},{3,0},{4,5},{5,6},{6,7},{7,4},{8,9},{9,10},{10,1... | collective-permute-start | bytes 1572872 | tf_op jit(solution)/shard_map/ppermute | solution.py:380
  47.5 21.7 %all-to-all-start.1 = ((bf16[32,32,128]{2,1,0:T(8,128)(2,1)}), bf16[32,32,128]{2,1,0:T(8,128)(2,1)S(1)}, u32[]{:S(2)}, u32[]{:S(2)}) async-start(bf16[32,32,128]{2,1,0:T(8,128)(2,1)} %fold.1), calls=%async_computation.1 | async-start | bytes 524288 | tf_op jit(solution)/shard_map/all_to_all | solution.py:411
  51.0 0.9 %copy-start = (bf16[1,128,768]{2,1,0:T(8,128)(2,1)S(1)}, bf16[1,128,768]{2,1,0:T(8,128)(2,1)}, u32[]{:S(2)}) copy-start(bf16[1,128,768]{2,1,0:T(8,128)(2,1)} %hidden_ref) | copy-start | bytes 589828
  52.7 21.3 %collective-permute-start.8 = (bf16[192,128]{1,0:T(8,128)(2,1)}, bf16[192,128]{1,0:T(8,128)(2,1)}, u32[]{:S(2)}, u32[]{:S(2)}) collective-permute-start(bf16[192,128]{1,0:T(8,128)(2,1)} %get-tuple-element.41), channel_id=1, source_target_pairs={{0,3},{1,0},{2,1},{3,2},{4,7},{5,4},{6,5},{7,6},{8,11},{9,8},{10,9... | collective-permute-start | bytes 147464 | tf_op jit(solution)/shard_map/ppermute | solution.py:380
  56.3 17.7 %collective-permute-start.7 = (bf16[192,128]{1,0:T(8,128)(2,1)}, bf16[192,128]{1,0:T(8,128)(2,1)}, u32[]{:S(2)}, u32[]{:S(2)}) collective-permute-start(bf16[192,128]{1,0:T(8,128)(2,1)} %get-tuple-element.39), channel_id=1, source_target_pairs={{0,2},{1,3},{2,0},{3,1},{4,6},{5,7},{6,4},{7,5},{8,10},{9,11},{10,... | collective-permute-start | bytes 147464 | tf_op jit(solution)/shard_map/ppermute | solution.py:380
  56.3 17.7 %collective-permute-start.6 = (bf16[192,128]{1,0:T(8,128)(2,1)}, bf16[192,128]{1,0:T(8,128)(2,1)}, u32[]{:S(2)}, u32[]{:S(2)}) collective-permute-start(bf16[192,128]{1,0:T(8,128)(2,1)} %get-tuple-element.37), channel_id=1, source_target_pairs={{0,1},{1,2},{2,3},{3,0},{4,5},{5,6},{6,7},{7,4},{8,9},{9,10},{10,1... | collective-permute-start | bytes 147464 | tf_op jit(solution)/shard_map/ppermute | solution.py:380

commit v9 on v8

--- a/solution.py
+++ b/solution.py
@@ -78,7 +78,7 @@
             jax.ShapeDtypeStruct((rank, rows), F32),
         ],
         compiler_params=params(24),
-        cost_estimate=SMALL,
+        cost_estimate=pl.CostEstimate(flops=4_000_000_000, bytes_accessed=8_000_000, transcendentals=0),
         name="merge",
     )(*[pltpu.with_memory_space_constraint(x, pltpu.HBM) for x in (acts, kv, err, vt)])
 
@@ -120,7 +120,7 @@
 
 def right_kernel(n_parts, *refs):
     part_refs, merged_ref = refs[:n_parts], refs[n_parts]
-    lt_ref, chunk_ref = refs[n_parts + 1 :]
+    lt_ref, chunk_ref, terms_ref = refs[n_parts + 1 :]
     parts = [ref[...].astype(F32) for ref in part_refs]
     while len(parts) > 1:
         parts = [a + b for a, b in zip(parts[0::2], parts[1::2])]
@@ -137,12 +137,13 @@
     first, second = as_terms(
         lax.dot_general(lt, lt, COLS_LAST, precision=HIGHEST, preferred_element_type=F32)
     )
-    chunks, pieces = chunk_ref.shape[0], rank // 8
-    for i in range(pieces):
-        here = slice(8 * i, 8 * i + 8)
-        piece = jnp.concatenate([first[here], second[here]], axis=0).astype(BF16)
-        for c in range(i * chunks // pieces, (i + 1) * chunks // pieces):
-            chunk_ref[c, TILE_R:] = piece
+    terms_ref[0] = first
+    terms_ref[1] = second
+    piece = lax.rem(lax.axis_index("rep"), rank // 8)
+    here = pl.ds(pl.multiple_of(piece * 8, 8), 8)
+    piece = jnp.concatenate([terms_ref[0, here, :], terms_ref[1, here, :]], axis=0).astype(BF16)
+    for c in range(chunk_ref.shape[0]):
+        chunk_ref[c, TILE_R:] = piece
 
 
 def right_product(parts, merged):
@@ -156,44 +157,48 @@
             jax.ShapeDtypeStruct((rank, rows), BF16),
             jax.ShapeDtypeStruct((chunks, 2 * TILE_R, TILE_C), BF16),
         ],
+        scratch_shapes=[pltpu.VMEM((2, rank, TILE_C), F32)],
         compiler_params=params(16),
         cost_estimate=SMALL,
         name="right_product",
     )(*parts, merged)
 
 
-def fold_kernel(n_exp, share_ref, out_ref):
+def fold_kernel(n_exp, share_ref, out_ref, gram_ref):
     total = share_ref[0, 0:TILE_R].astype(F32)
     for i in range(1, share_ref.shape[0]):
         total = total + share_ref[i, 0:TILE_R].astype(F32)
     total = total.astype(BF16)
-    gram = None
-    for j in range(n_exp):
-        terms = share_ref[j, TILE_R:].astype(F32)
-        part = from_terms(terms[:8], terms[8:])
-        gram = part if gram is None else gram + part
-    piece = jnp.concatenate(as_terms(gram), axis=0).astype(BF16)
     for i in range(out_ref.shape[0]):
-        out_ref[i, 0:TILE_R] = total
-        out_ref[i, TILE_R:] = piece
+        out_ref[i] = total
+    for r in range(share_ref.shape[0] // n_exp):
+        rows = None
+        for j in range(n_exp):
+            terms = share_ref[r * n_exp + j, TILE_R:].astype(F32)
+            part = from_terms(terms[:8], terms[8:])
+            rows = part if rows is None else rows + part
+        gram_ref[8 * r : 8 * r + 8, :] = rows
 
 
 def fold(shares, n_exp):
+    count = shares.shape[0]
+    rank = 8 * (count // n_exp)
     return pl.pallas_call(
         functools.partial(fold_kernel, n_exp),
-        out_shape=jax.ShapeDtypeStruct(shares.shape, BF16),
+        out_shape=[
+            jax.ShapeDtypeStruct((count, TILE_R, TILE_C), BF16),
+            jax.ShapeDtypeStruct((rank, rank), F32),
+        ],
         compiler_params=params(4),
         cost_estimate=SMALL,
         name="fold",
     )(shares)
 
 
-def fold_any(chunks):
-    wide = chunks.astype(F32)
-    total = lax.psum(wide[:, :TILE_R], ("rep", "exp"))
-    terms = lax.psum(wide[:, TILE_R:], "exp")
-    pieces = as_terms(from_terms(terms[:, :8], terms[:, 8:]), lax.optimization_barrier)
-    return jnp.concatenate([total, *pieces], axis=1).astype(BF16)
+def fold_any(chunks, lt):
+    total = lax.psum(chunks[:, :TILE_R].astype(F32), ("rep", "exp")).astype(BF16)
+    wide = lt.astype(F32)
+    return total, lax.psum(jnp.dot(wide, wide.T, precision=HIGHEST), "exp")
 
 
 def inverse_of_factor(gram, wide_ref):
@@ -216,37 +221,60 @@
     return wide_ref[:, rank:]
 
 
+def inverse_kernel(gram_any, lt_any, w_ref, basis_ref, gram_ref, lt_ref, wide_ref, sems):
+    gram_copy = pltpu.make_async_copy(gram_any, gram_ref, sems.at[0])
+    gram_copy.start()
+    lt_copy = pltpu.make_async_copy(lt_any, lt_ref, sems.at[1])
+    lt_copy.start()
+    gram_copy.wait()
+    w = inverse_of_factor(gram_ref[...], wide_ref)
+    w_ref[...] = w
+    lt_copy.wait()
+    basis_ref[...] = left_times(w, lt_ref[...], (((1,), (0,)), ((), ()))).T.astype(BF16)
+
+
+def inverse_factor(gram, lt):
+    rank, rows = lt.shape
+    return pl.pallas_call(
+        inverse_kernel,
+        in_specs=[ANY] * 2,
+        out_shape=[pltpu.HBM((rank, rank), F32), pltpu.HBM((rows, rank), BF16)],
+        scratch_shapes=[
+            pltpu.VMEM((rank, rank), F32),
+            pltpu.VMEM((rank, rows), BF16),
+            pltpu.VMEM((rank, 2 * rank), F32),
+            pltpu.SemaphoreType.DMA((2,)),
+        ],
+        compiler_params=params(8),
+        cost_estimate=pl.CostEstimate(flops=4_000_000_000, bytes_accessed=1000, transcendentals=0),
+        name="inverse_factor",
+    )(gram, lt)
+
+
 def finish_kernel(
-    replicas, chunk_ref, lt_any, merged_ref, right_hbm, err_hbm, lt_ref, wide_ref, right_ref, err_ref, sems
+    replicas, w_any, chunk_ref, basis_any, merged_ref, right_hbm, err_hbm, w_ref, basis_ref, right_ref, err_ref, sems
 ):
     rank, cols = right_ref.shape
     rows, block = err_ref.shape[0], 128
-    lt_copy = pltpu.make_async_copy(lt_any, lt_ref, sems.at[rows // block + 1])
-    lt_copy.start()
-    chunks, count = chunk_ref.shape[0], rank // 8
-    gram = []
-    for i in range(count):
-        terms = chunk_ref[i * chunks // count, TILE_R:].astype(F32)
-        gram.append(from_terms(terms[:8], terms[8:]))
-    w = inverse_of_factor(jnp.concatenate(gram, axis=0), wide_ref)
+    w_copy = pltpu.make_async_copy(w_any, w_ref, sems.at[rows // block + 1])
+    w_copy.start()
+    basis_copy = pltpu.make_async_copy(basis_any, basis_ref, sems.at[rows // block + 2])
+    basis_copy.start()
     across = cols // TILE_C
     pieces = []
     for a in range(rank // TILE_R):
-        pieces.append(
-            jnp.concatenate([chunk_ref[a * across + b, 0:TILE_R] for b in range(across)], axis=1)
-        )
+        pieces.append(jnp.concatenate([chunk_ref[a * across + b] for b in range(across)], axis=1))
     product = jnp.concatenate(pieces, axis=0)
-    inner = (((1,), (0,)), ((), ()))
-    new_right = left_times(w, product, inner) * (1.0 / replicas)
+    w_copy.wait()
+    new_right = left_times(w_ref[...], product, (((1,), (0,)), ((), ()))) * (1.0 / replicas)
     right_ref[...] = new_right
     copies = [pltpu.make_async_copy(right_ref, right_hbm, sems.at[0])]
     copies[0].start()
     rounded = new_right.astype(BF16)
-    lt_copy.wait()
-    basis = left_times(w, lt_ref[...], inner).T.astype(BF16)
+    basis_copy.wait()
     for i in range(rows // block):
         here = slice(i * block, (i + 1) * block)
-        approx = jnp.dot(basis[here, :], rounded, preferred_element_type=F32)
+        approx = jnp.dot(basis_ref[here, :], rounded, preferred_element_type=F32)
         err_ref[here, :] = (merged_ref[here, :].astype(F32) - approx).astype(BF16)
         copies.append(
             pltpu.make_async_copy(err_ref.at[here, :], err_hbm.at[0, here, :], sems.at[i + 1])
@@ -256,36 +284,35 @@
         copy.wait()
 
 
-def finish(replicas, chunks, lt, merged):
-    rank, rows = lt.shape
+def finish(replicas, w, chunks, basis, merged):
+    rows, rank = basis.shape
     cols = merged.shape[1]
     return pl.pallas_call(
         functools.partial(finish_kernel, replicas),
-        in_specs=[VMEM, ANY, VMEM],
+        in_specs=[HBM, VMEM, HBM, VMEM],
         out_specs=[HBM] * 2,
         out_shape=[
             jax.ShapeDtypeStruct((rank, cols), F32),
             jax.ShapeDtypeStruct((1, rows, cols), BF16),
         ],
         scratch_shapes=[
-            pltpu.VMEM((rank, rows), BF16),
-            pltpu.VMEM((rank, 2 * rank), F32),
+            pltpu.VMEM((rank, rank), F32),
+            pltpu.VMEM((rows, rank), BF16),
             pltpu.VMEM((rank, cols), F32),
             pltpu.VMEM((rows, cols), BF16),
-            pltpu.SemaphoreType.DMA((rows // 128 + 2,)),
+            pltpu.SemaphoreType.DMA((rows // 128 + 3,)),
         ],
         compiler_params=params(16),
         cost_estimate=SMALL,
         name="finish",
-    )(chunks, lt, merged)
-
-
-def expert_kernel(n_exp, chunk, *refs):
-    load_hbms, grad_hbms = refs[:n_exp], refs[n_exp : 2 * n_exp]
-    one_hbm, two_hbm, first_hbm, second_hbm, step_hbm = refs[2 * n_exp : 2 * n_exp + 5]
-    hid, rows, one, two, first, second, step, in_sems, out_sems = refs[2 * n_exp + 5 :]
+    )(*in_hbm(w), chunks, *in_hbm(basis), merged)
+
+
+def expert_kernel(n_exp, n_grad, chunk, *refs):
+    load_hbms, grad_hbms = refs[:n_exp], refs[n_exp : n_exp + n_grad]
+    one_hbm, two_hbm, first_hbm, second_hbm, step_hbm = refs[n_exp + n_grad : n_exp + n_grad + 5]
+    hid, rows, one, two, first, second, step, in_sems, out_sems = refs[n_exp + n_grad + 5 :]
     units, width = one.shape
-    tokens = grad_hbms[0].shape[1]
     count = width // chunk
 
     slabs = [
@@ -295,10 +322,11 @@
 
     def loads(c):
         here = slice(c * chunk, (c + 1) * chunk)
-        pairs = [
-            (grad_hbms[k].at[0, :, here], rows.at[k * tokens : (k + 1) * tokens, here])
-            for k in range(n_exp)
-        ]
+        pairs, at = [], 0
+        for grad_hbm in grad_hbms:
+            end = at + grad_hbm.shape[1]
+            pairs.append((grad_hbm.at[0, :, here], rows.at[at:end, here]))
+            at = end
         pairs += [(one_hbm.at[0, :, here], one.at[:, here]), (two_hbm.at[0, :, here], two.at[:, here])]
         return [pltpu.make_async_copy(a, b, in_sems.at[c, i]) for i, (a, b) in enumerate(pairs)]
 
@@ -342,11 +370,11 @@
 def expert_step(slabs, grads, moment_one, moment_two):
     _, units, width = moment_one.shape
     chunk = 512
-    n_exp = len(grads)
-    tokens = grads[0].shape[1]
-    return pl.pallas_call(
-        functools.partial(expert_kernel, n_exp, chunk),
-        in_specs=[ANY] * n_exp + [HBM] + [ANY] * (n_exp - 1) + [HBM] * 2,
+    n_exp, n_grad = len(slabs), len(grads)
+    tokens = slabs[0].shape[1]
+    return pl.pallas_call(
+        functools.partial(expert_kernel, n_exp, n_grad, chunk),
+        in_specs=[ANY] * n_exp + [HBM] + [ANY] * (n_grad - 1) + [HBM] * 2,
         out_specs=[HBM] * 3,
         out_shape=[
             jax.ShapeDtypeStruct((1, units, width), F32),
@@ -361,7 +389,7 @@
             pltpu.VMEM((units, width), F32),
             pltpu.VMEM((units, width), F32),
             pltpu.VMEM((units, width), BF16),
-            pltpu.SemaphoreType.DMA((width // chunk + 1, n_exp + 2)),
+            pltpu.SemaphoreType.DMA((width // chunk + 1, n_grad + 2)),
             pltpu.SemaphoreType.DMA((width // chunk, 3)),
         ],
         compiler_params=params(24),
@@ -385,10 +413,13 @@
 
 
 def body(n_rep, n_exp, activations, kv_grad, errors, right_factor, hidden, out_grad, moment_one, moment_two):
-    grads = {0: out_grad, 1: shift(out_grad, n_exp, 1)}
-    if n_exp > 2:
-        grads[n_exp - 1] = shift(out_grad, n_exp, -1)
+    half = out_grad.shape[1] // 2
+    left_first = shift(out_grad[:, :half], n_exp, -1)
     merged, lt = merge(activations, kv_grad, errors, right_factor.T)
+
+    lt, left_first = lax.optimization_barrier((lt, left_first))
+    grads = {0: [out_grad], 1: [shift(out_grad, n_exp, 1)]}
+    grads[n_exp - 1] = [left_first, shift(out_grad[:, half:], n_exp, -1)]
 
     lt = (lt + swap(lt, "rep", n_rep, 1)).astype(BF16)
     slabs = unit_slabs(after(hidden, lt), n_exp)
@@ -403,29 +434,31 @@
         bit *= len(parts)
     lt, chunks = right_product(parts, merged)
 
-    if chunks.shape[0] == n_rep * n_exp and 8 * n_rep == lt.shape[0]:
-        both = ("rep", "exp")
+    fits = chunks.shape[0] == n_rep * n_exp and 8 * n_rep == lt.shape[0]
+    both = ("rep", "exp")
+    if fits:
         shares = lax.all_to_all(chunks, both, 0, 0, tiled=True)
         shares, grads = lax.optimization_barrier((shares, grads))
-        share = fold(shares, n_exp)
+        share, gram = fold(shares, n_exp)
         chunks = lax.all_to_all(share, both, 0, 0, tiled=True)
     else:
-        share = chunks
-        chunks = fold_any(chunks)
+        share, gram = fold_any(chunks, lt)
+        chunks = share
+    w, basis = inverse_factor(gram, lt)
 
     slabs = [slabs[0]] + [shift(after(slabs[k], share), n_exp, k) for k in range(1, n_exp)]
     left, right = 1, n_exp - 1
     while right - left > 1:
         if left <= n_exp - right:
-            grads[left + 1] = shift(after(grads[left], share), n_exp, 1)
+            grads[left + 1] = [shift(after(g, share), n_exp, 1) for g in grads[left]]
             left += 1
         else:
-            grads[right - 1] = shift(after(grads[right], share), n_exp, -1)
+            grads[right - 1] = [shift(after(g, share), n_exp, -1) for g in grads[right]]
             right -= 1
 
-    new_right, new_error = finish(n_rep, chunks, lt, merged)
+    new_right, new_error = finish(n_rep, w, chunks, basis, merged)
     first_new, second_new, step = expert_step(
-        slabs, [grads[k] for k in range(n_exp)], moment_one, moment_two
+        slabs, [g for k in range(n_exp) for g in grads[k]], moment_one, moment_two
     )
     return new_error, new_right.T, first_new, second_new, step
 

time: 78.8 us -> 72.7 us (0.923)
  waiting for transfers between devices: 35.3 us -> 17.7 us
  starting transfers between devices: 24.1 us -> 29.3 us
  local copies, waits for them, and re-layouts: 0.93 us -> 5.61 us
  Pallas kernels: 17.4 us -> 18.9 us
    all_to_all x1, waiting for transfers between devices: 11.8 us -> 1.92 us  [body(): chunks = lax.all_to_all(share, both, 0, 0, tiled=True)]
    ppermute x6 -> x7, starting transfers between devices: 10.5 us -> 16.2 us  [shift(): return lax.ppermute(x, 'exp', [(i, (i + k) % size) for i in range(size)])]
    all_to_all x1, waiting for transfers between devices: 5.68 us -> 0.01 us  [body(): shares = lax.all_to_all(chunks, both, 0, 0, tiled=True)]
    ppermute x6 -> x7, waiting for transfers between devices: 15.9 us -> 10.4 us  [shift(): return lax.ppermute(x, 'exp', [(i, (i + k) % size) for i in range(size)])]
    ppermute x4, waiting for transfers between devices: 1.87 us -> 5.39 us  [swap(): return lax.ppermute(x, axis, [(i, i ^ mask) for i in range(size)])]
    unnamed x4 -> x12, local copies, waits for them, and re-layouts: 0.93 us -> 3.83 us
    slice x0 -> x1, local copies, waits for them, and re-layouts: none -> 1.78 us  [body(): grads[n_exp - 1] = [left_first, shift(out_grad[:, half:], n_exp, -1)]]
    pallas_call x3 -> x4, Pallas kernels: 9.99 us -> 11.6 us  [the longest x1 4.51 us: expert_step(): pl.pallas_call(functools.partial(expert_kernel, n_exp, n_grad, chunk), in...]
  transfers between devices with their start and end apart: 12 -> 13, of which waited for: 7 -> 8; matrix products, arithmetic and copies ran while one was open for 0% -> 0% of each run, Pallas kernels for 9% -> 19%
where the time goes in v9:
time: 72.7 us; the launch traced here: 72.3 us
  starting transfers between devices  29.3 us (40%)
  Pallas kernels  18.9 us (26%)
  waiting for transfers between devices  17.7 us (24%)
  local copies, waits for them, and re-layouts  5.61 us (8%)
    ppermute x7, starting transfers between devices, shift(): return lax.ppermute(x, 'exp', [(i, (i + k) % size) for i in range(size)])  16.2 us
    ppermute x7, waiting for transfers between devices, shift(): return lax.ppermute(x, 'exp', [(i, (i + k) % size) for i in range(size)])  10.4 us
    all_to_all x1, starting transfers between devices, body(): shares = lax.all_to_all(chunks, both, 0, 0, tiled=True)  5.78 us
    ppermute x4, waiting for transfers between devices, swap(): return lax.ppermute(x, axis, [(i, i ^ mask) for i in range(size)])  5.39 us
    pallas_call x1, Pallas kernels, merge(): pl.pallas_call(merge_kernel, grid=(rows // block,), in_specs=[pl.BlockSpe...  5.24 us
    pallas_call x1, Pallas kernels, expert_step(): pl.pallas_call(functools.partial(expert_kernel, n_exp, n_grad, chunk), in...  4.51 us
    pallas_call x1, Pallas kernels, inverse_factor(): pl.pallas_call(inverse_kernel, in_specs=[ANY] * 2, out_shape=[pltpu.HBM((...  3.98 us
    unnamed x12, local copies, waits for them, and re-layouts  3.83 us
  transfers between devices with their start and end apart: 13, of which 8 were waited for; matrix products, arithmetic and copies ran while one was open for 0% of the time, Pallas kernels for 19%

profile of v9, /device:TPU:0, one launch (start us, length us, event | category | flops | bytes accessed | tf_op | source)
XLA Modules:
  0.0 72.3 jit_solution(203556528172584644)
XLA Ops:
  0.6 1.8 %fusion = (bf16[1,64,2048]{2,1,0:T(8,128)(2,1)}, bf16[1,64,2048]{2,1,0:T(8,128)(2,1)S(1)}) fusion(bf16[1,128,2048]{2,1,0:T(8,128)(2,1)} %refs_4_), kind=kLoop, calls=%fused_computation.1 | loop fusion | bytes 1048576 | tf_op jit(solution)/shard_map/slice | solution.py:422
  2.4 5.0 %collective-permute-start = (bf16[1,64,2048]{2,1,0:T(8,128)(2,1)S(1)}, bf16[1,64,2048]{2,1,0:T(8,128)(2,1)S(1)}, u32[]{:S(2)}, u32[]{:S(2)}) collective-permute-start(bf16[1,64,2048]{2,1,0:T(8,128)(2,1)S(1)} %get-tuple-element.64), channel_id=1, source_target_pairs={{0,3},{1,0},{2,1},{3,2},{4,7},{5,4},{6,5},{7,6},{8,11},{9,8},{10,9... | collective-permute-start | bytes 786440 | tf_op jit(solution)/shard_map/ppermute | solution.py:408
  7.5 5.2 %merge.1 = (bf16[768,1024]{1,0:T(8,128)(2,1)S(1)}, f32[64,768]{1,0:T(8,128)S(1)}) custom-call(bf16[1024,768]{1,0:T(8,128)(2,1)} %acts_ref.1, bf16[1024,1024]{1,0:T(8,128)(2,1)} %kv_ref.1, bf16[1,768,1024]{2,1,0:T(8,128)(2,1)} %err_ref.1, f32[64,1024]{1,0:T(8,128)} %bitcast.2), custom_call_target="tpu_custom_call" | custom-call | flops 4000000000 | bytes 8000000 | tf_op jit(solution)/shard_map/merge/pallas_call | solution.py:63
  13.0 1.4 %collective-permute-done.1 = f32[64,768]{1,0:T(8,128)S(1)} collective-permute-done((f32[64,768]{1,0:T(8,128)S(1)}, f32[64,768]{1,0:T(8,128)S(1)}, u32[]{:S(2)}, u32[]{:S(2)}) %collective-permute-start.1) | collective-permute-done | bytes 196640 | tf_op jit(solution)/shard_map/ppermute | solution.py:404
  14.5 2.5 %collective-permute-start.4 = (bf16[64,768]{1,0:T(8,128)(2,1)S(1)}, bf16[64,768]{1,0:T(8,128)(2,1)S(1)}, u32[]{:S(2)}, u32[]{:S(2)}) collective-permute-start(bf16[64,768]{1,0:T(8,128)(2,1)S(1)} %add_convert_fusion.refs_0_), channel_id=1, source_target_pairs={{0,24},{4,28},{8,16},{12,20},{16,8},{20,12},{24,0},{28,4},{1,25},{... | collective-permute-start | bytes 294920 | tf_op jit(solution)/shard_map/ppermute | solution.py:404
  18.5 1.9 %collective-permute-done.4.refs_3_ = bf16[64,768]{1,0:T(8,128)(2,1)S(1)} collective-permute-done((bf16[64,768]{1,0:T(8,128)(2,1)S(1)}, bf16[64,768]{1,0:T(8,128)(2,1)S(1)}, u32[]{:S(2)}, u32[]{:S(2)}) %collective-permute-start.4) | collective-permute-done | bytes 98336 | tf_op jit(solution)/shard_map/ppermute | solution.py:404
  20.4 2.0 %collective-permute-done.3.refs_2_ = bf16[64,768]{1,0:T(8,128)(2,1)S(1)} collective-permute-done((bf16[64,768]{1,0:T(8,128)(2,1)S(1)}, bf16[64,768]{1,0:T(8,128)(2,1)S(1)}, u32[]{:S(2)}, u32[]{:S(2)}) %collective-permute-start.3) | collective-permute-done | bytes 98336 | tf_op jit(solution)/shard_map/ppermute | solution.py:404
  22.5 1.3 %right_product.1 = (bf16[64,768]{1,0:T(8,128)(2,1)S(1)}, bf16[32,32,128]{2,1,0:T(8,128)(2,1)}) custom-call(bf16[64,768]{1,0:T(8,128)(2,1)S(1)} %add_convert_fusion.refs_0_, bf16[64,768]{1,0:T(8,128)(2,1)S(1)} %collective-permute-done.2.refs_1_, bf16[64,768]{1,0:T(8,128)(2,1)S(1)} %collective-permute-done.3.refs_2_, ...), custom_call_target="tpu_custom_call" | custom-call | flops 1000 | bytes 1000 | tf_op jit(solution)/shard_map/right_product/pallas_call | solution.py:154
  24.4 5.8 %all-to-all-start = ((bf16[32,32,128]{2,1,0:T(8,128)(2,1)}), bf16[32,32,128]{2,1,0:T(8,128)(2,1)S(1)}, u32[]{:S(2)}, u32[]{:S(2)}) async-start(bf16[32,32,128]{2,1,0:T(8,128)(2,1)} %get-tuple-element.37), calls=%async_computation | async-start | bytes 524288 | tf_op jit(solution)/shard_map/all_to_all | solution.py:440
  30.2 3.7 %collective-permute-start.6 = (bf16[1,64,2048]{2,1,0:T(8,128)(2,1)}, bf16[1,64,2048]{2,1,0:T(8,128)(2,1)S(1)}, u32[]{:S(2)}, u32[]{:S(2)}) collective-permute-start(bf16[1,64,2048]{2,1,0:T(8,128)(2,1)} %get-tuple-element.63), channel_id=1, source_target_pairs={{0,3},{1,0},{2,1},{3,2},{4,7},{5,4},{6,5},{7,6},{8,11},{9,8},{10,9... | collective-permute-start | bytes 786440 | tf_op jit(solution)/shard_map/ppermute | solution.py:408
  33.9 9.6 %collective-permute-done.6.refs_8_ = bf16[1,64,2048]{2,1,0:T(8,128)(2,1)S(1)} collective-permute-done((bf16[1,64,2048]{2,1,0:T(8,128)(2,1)}, bf16[1,64,2048]{2,1,0:T(8,128)(2,1)S(1)}, u32[]{:S(2)}, u32[]{:S(2)}) %collective-permute-start.6) | collective-permute-done | bytes 262176 | tf_op jit(solution)/shard_map/ppermute | solution.py:408
  43.6 0.7 fold.1
  44.9 2.2 %collective-permute-start.10 = (bf16[1,128,2048]{2,1,0:T(8,128)(2,1)S(1)}, bf16[1,128,2048]{2,1,0:T(8,128)(2,1)S(1)}, u32[]{:S(2)}, u32[]{:S(2)}) collective-permute-start(bf16[1,128,2048]{2,1,0:T(8,128)(2,1)S(1)} %collective-permute-done.5.refs_5_), channel_id=1, source_target_pairs={{0,1},{1,2},{2,3},{3,0},{4,5},{5,6},{6,7},{7,4},{8,9},{9,10},{10,1... | collective-permute-start | bytes 1572872 | tf_op jit(solution)/shard_map/ppermute | solution.py:408
  47.1 0.9 %copy-done = bf16[1,128,768]{2,1,0:T(8,128)(2,1)S(1)} copy-done((bf16[1,128,768]{2,1,0:T(8,128)(2,1)S(1)}, bf16[1,128,768]{2,1,0:T(8,128)(2,1)}, u32[]{:S(2)}) %copy-start) | copy-done | bytes 196632
  48.0 0.8 %unit_slabs.1 = (bf16[192,128]{1,0:T(8,128)(2,1)S(1)}, bf16[192,128]{1,0:T(8,128)(2,1)S(1)}, bf16[192,128]{1,0:T(8,128)(2,1)}, bf16[192,128]{1,0:T(8,128)(2,1)}) custom-call(bf16[1,128,768]{2,1,0:T(8,128)(2,1)S(1)} %copy-done), custom_call_target="tpu_custom_call" | custom-call | flops 1000 | bytes 1000 | tf_op jit(solution)/shard_map/unit_slabs/pallas_call | solution.py:98
  48.8 3.8 %all-to-all-start.1 = ((bf16[32,16,128]{2,1,0:T(8,128)(2,1)}), bf16[32,16,128]{2,1,0:T(8,128)(2,1)S(1)}, u32[]{:S(2)}, u32[]{:S(2)}) async-start(bf16[32,16,128]{2,1,0:T(8,128)(2,1)} %get-tuple-element.43), calls=%async_computation.1 | async-start | bytes 262144 | tf_op jit(solution)/shard_map/all_to_all | solution.py:443
  52.6 3.7 %collective-permute-start.9 = (bf16[192,128]{1,0:T(8,128)(2,1)}, bf16[192,128]{1,0:T(8,128)(2,1)S(1)}, u32[]{:S(2)}, u32[]{:S(2)}) collective-permute-start(bf16[192,128]{1,0:T(8,128)(2,1)} %get-tuple-element.54), channel_id=1, source_target_pairs={{0,3},{1,0},{2,1},{3,2},{4,7},{5,4},{6,5},{7,6},{8,11},{9,8},{10,9... | collective-permute-start | bytes 147464 | tf_op jit(solution)/shard_map/ppermute | solution.py:408
  56.3 1.1 %collective-permute-start.7 = (bf16[192,128]{1,0:T(8,128)(2,1)S(1)}, bf16[192,128]{1,0:T(8,128)(2,1)S(1)}, u32[]{:S(2)}, u32[]{:S(2)}) collective-permute-start(bf16[192,128]{1,0:T(8,128)(2,1)S(1)} %get-tuple-element.50), channel_id=1, source_target_pairs={{0,1},{1,2},{2,3},{3,0},{4,5},{5,6},{6,7},{7,4},{8,9},{9,10},{10,1... | collective-permute-start | bytes 147464 | tf_op jit(solution)/shard_map/ppermute | solution.py:408
  57.4 0.9 %copy-done.2 = bf16[64,768]{1,0:T(8,128)(2,1)S(1)} copy-done((bf16[64,768]{1,0:T(8,128)(2,1)S(1)}, bf16[64,768]{1,0:T(8,128)(2,1)}, u32[]{:S(2)}) %copy-start.2) | copy-done | bytes 98328
  58.3 0.8 %copy-done.4 = f32[64,64]{1,0:T(8,128)S(1)} copy-done((f32[64,64]{1,0:T(8,128)S(1)}, f32[64,64]{1,0:T(8,128)}, u32[]{:S(2)}) %copy-start.4) | copy-done | bytes 16408
  59.0 4.0 %inverse_factor.1 = (f32[64,64]{1,0:T(8,128)}, bf16[768,64]{1,0:T(8,128)(2,1)}) custom-call(f32[64,64]{1,0:T(8,128)S(1)} %copy-done.4, bf16[64,768]{1,0:T(8,128)(2,1)S(1)} %copy-done.2), custom_call_target="tpu_custom_call" | custom-call | flops 4000000000 | bytes 1000 | tf_op jit(solution)/shard_map/inverse_factor/pallas_call | solution.py:238
  63.0 1.9 %all-to-all-done.1.chunk_ref = bf16[32,16,128]{2,1,0:T(8,128)(2,1)S(1)} async-done(((bf16[32,16,128]{2,1,0:T(8,128)(2,1)}), bf16[32,16,128]{2,1,0:T(8,128)(2,1)S(1)}, u32[]{:S(2)}, u32[]{:S(2)}) %all-to-all-start.1) | async-done | bytes 131104 | tf_op jit(solution)/shard_map/all_to_all | solution.py:443
  65.0 2.4 %finish.1 = (f32[64,1024]{1,0:T(8,128)}, bf16[1,768,1024]{2,1,0:T(8,128)(2,1)}) custom-call(f32[64,64]{1,0:T(8,128)} %get-tuple-element.42.w_any, bf16[32,16,128]{2,1,0:T(8,128)(2,1)S(1)} %all-to-all-done.1.chunk_ref, bf16[768,64]{1,0:T(8,128)(2,1)} %get-tuple-element.44.basis_any, bf16[768,1024]{1,0:T(8,128)(2,1)S(1)} %get-tuple-element.36.refs_4_.merged_ref), custom_call_target="tpu_custom_call" | custom-call | flops 1000 | bytes 1000 | tf_op jit(solution)/shard_map/finish/pallas_call | solution.py:290
  67.8 4.5 %expert_step.1 = (f32[1,192,2048]{2,1,0:T(8,128)}, f32[1,192,2048]{2,1,0:T(8,128)}, bf16[1,192,2048]{2,1,0:T(8,128)(2,1)}) custom-call(bf16[192,128]{1,0:T(8,128)(2,1)S(1)} %get-tuple-element.48.refs_0_, bf16[192,128]{1,0:T(8,128)(2,1)S(1)} %collective-permute-done.7.refs_1_, bf16[192,128]{1,0:T(8,128)(2,1)S(1)} %collective-permute-done.8.refs_2_, ...), custom_call_target="tpu_custom_call" | custom-call | flops 1000 | bytes 1000 | tf_op jit(solution)/shard_map/expert_step/pallas_call | solution.py:375
  (23 shorter events, 3.6 us)
Async XLA Ops:
  2.4 10.6 %collective-permute-start = (bf16[1,64,2048]{2,1,0:T(8,128)(2,1)S(1)}, bf16[1,64,2048]{2,1,0:T(8,128)(2,1)S(1)}, u32[]{:S(2)}, u32[]{:S(2)}) collective-permute-start(bf16[1,64,2048]{2,1,0:T(8,128)(2,1)S(1)} %get-tuple-element.64), channel_id=1, source_target_pairs={{0,3},{1,0},{2,1},{3,2},{4,7},{5,4},{6,5},{7,6},{8,11},{9,8},{10,9... | collective-permute-start | bytes 786440 | tf_op jit(solution)/shard_map/ppermute | solution.py:408
  7.5 10.6 %copy-start.5 = (bf16[1,128,2048]{2,1,0:T(8,128)(2,1)S(1)}, bf16[1,128,2048]{2,1,0:T(8,128)(2,1)}, u32[]{:S(2)}) copy-start(bf16[1,128,2048]{2,1,0:T(8,128)(2,1)} %refs_4_) | copy-start | bytes 1572868
  13.0 1.4 %collective-permute-start.1 = (f32[64,768]{1,0:T(8,128)S(1)}, f32[64,768]{1,0:T(8,128)S(1)}, u32[]{:S(2)}, u32[]{:S(2)}) collective-permute-start(f32[64,768]{1,0:T(8,128)S(1)} %get-tuple-element.35), channel_id=1, source_target_pairs={{0,4},{4,0},{8,12},{12,8},{16,20},{20,16},{24,28},{28,24},{1,5},{5... | collective-permute-start | bytes 589832 | tf_op jit(solution)/shard_map/ppermute | solution.py:404
  14.5 5.9 %collective-permute-start.4 = (bf16[64,768]{1,0:T(8,128)(2,1)S(1)}, bf16[64,768]{1,0:T(8,128)(2,1)S(1)}, u32[]{:S(2)}, u32[]{:S(2)}) collective-permute-start(bf16[64,768]{1,0:T(8,128)(2,1)S(1)} %add_convert_fusion.refs_0_), channel_id=1, source_target_pairs={{0,24},{4,28},{8,16},{12,20},{16,8},{20,12},{24,0},{28,4},{1,25},{... | collective-permute-start | bytes 294920 | tf_op jit(solution)/shard_map/ppermute | solution.py:404
  17.0 5.4 %collective-permute-start.3 = (bf16[64,768]{1,0:T(8,128)(2,1)S(1)}, bf16[64,768]{1,0:T(8,128)(2,1)S(1)}, u32[]{:S(2)}, u32[]{:S(2)}) collective-permute-start(bf16[64,768]{1,0:T(8,128)(2,1)S(1)} %add_convert_fusion.refs_0_), channel_id=1, source_target_pairs={{0,16},{4,20},{8,24},{12,28},{16,0},{20,4},{24,8},{28,12},{1,17},{... | collective-permute-start | bytes 294920 | tf_op jit(solution)/shard_map/ppermute | solution.py:404
  17.5 4.9 %collective-permute-start.2 = (bf16[64,768]{1,0:T(8,128)(2,1)S(1)}, bf16[64,768]{1,0:T(8,128)(2,1)S(1)}, u32[]{:S(2)}, u32[]{:S(2)}) collective-permute-start(bf16[64,768]{1,0:T(8,128)(2,1)S(1)} %add_convert_fusion.refs_0_), channel_id=1, source_target_pairs={{0,8},{4,12},{8,0},{12,4},{16,24},{20,28},{24,16},{28,20},{1,9},{5... | collective-permute-start | bytes 294920 | tf_op jit(solution)/shard_map/ppermute | solution.py:404
  18.1 25.5 %collective-permute-start.5 = (bf16[1,128,2048]{2,1,0:T(8,128)(2,1)S(1)}, bf16[1,128,2048]{2,1,0:T(8,128)(2,1)S(1)}, u32[]{:S(2)}, u32[]{:S(2)}) collective-permute-start(bf16[1,128,2048]{2,1,0:T(8,128)(2,1)S(1)} %copy-done.5), channel_id=1, source_target_pairs={{0,1},{1,2},{2,3},{3,0},{4,5},{5,6},{6,7},{7,4},{8,9},{9,10},{10,1... | collective-permute-start | bytes 1572872 | tf_op jit(solution)/shard_map/ppermute | solution.py:408
  23.8 0.6 copy-start.1
  24.4 19.1 %all-to-all-start = ((bf16[32,32,128]{2,1,0:T(8,128)(2,1)}), bf16[32,32,128]{2,1,0:T(8,128)(2,1)S(1)}, u32[]{:S(2)}, u32[]{:S(2)}) async-start(bf16[32,32,128]{2,1,0:T(8,128)(2,1)} %get-tuple-element.37), calls=%async_computation | async-start | bytes 524288 | tf_op jit(solution)/shard_map/all_to_all | solution.py:440
  30.2 13.3 %collective-permute-start.6 = (bf16[1,64,2048]{2,1,0:T(8,128)(2,1)}, bf16[1,64,2048]{2,1,0:T(8,128)(2,1)S(1)}, u32[]{:S(2)}, u32[]{:S(2)}) collective-permute-start(bf16[1,64,2048]{2,1,0:T(8,128)(2,1)} %get-tuple-element.63), channel_id=1, source_target_pairs={{0,3},{1,0},{2,1},{3,2},{4,7},{5,4},{6,5},{7,6},{8,11},{9,8},{10,9... | collective-permute-start | bytes 786440 | tf_op jit(solution)/shard_map/ppermute | solution.py:408
  44.3 0.6 copy-start.3
  44.9 22.9 %collective-permute-start.10 = (bf16[1,128,2048]{2,1,0:T(8,128)(2,1)S(1)}, bf16[1,128,2048]{2,1,0:T(8,128)(2,1)S(1)}, u32[]{:S(2)}, u32[]{:S(2)}) collective-permute-start(bf16[1,128,2048]{2,1,0:T(8,128)(2,1)S(1)} %collective-permute-done.5.refs_5_), channel_id=1, source_target_pairs={{0,1},{1,2},{2,3},{3,0},{4,5},{5,6},{6,7},{7,4},{8,9},{9,10},{10,1... | collective-permute-start | bytes 1572872 | tf_op jit(solution)/shard_map/ppermute | solution.py:408
  47.1 0.9 %copy-start = (bf16[1,128,768]{2,1,0:T(8,128)(2,1)S(1)}, bf16[1,128,768]{2,1,0:T(8,128)(2,1)}, u32[]{:S(2)}) copy-start(bf16[1,128,768]{2,1,0:T(8,128)(2,1)} %hidden_ref) | copy-start | bytes 589828
  48.8 16.1 %all-to-all-start.1 = ((bf16[32,16,128]{2,1,0:T(8,128)(2,1)}), bf16[32,16,128]{2,1,0:T(8,128)(2,1)S(1)}, u32[]{:S(2)}, u32[]{:S(2)}) async-start(bf16[32,16,128]{2,1,0:T(8,128)(2,1)} %get-tuple-element.43), calls=%async_computation.1 | async-start | bytes 262144 | tf_op jit(solution)/shard_map/all_to_all | solution.py:443
  52.6 14.7 %collective-permute-start.9 = (bf16[192,128]{1,0:T(8,128)(2,1)}, bf16[192,128]{1,0:T(8,128)(2,1)S(1)}, u32[]{:S(2)}, u32[]{:S(2)}) collective-permute-start(bf16[192,128]{1,0:T(8,128)(2,1)} %get-tuple-element.54), channel_id=1, source_target_pairs={{0,3},{1,0},{2,1},{3,2},{4,7},{5,4},{6,5},{7,6},{8,11},{9,8},{10,9... | collective-permute-start | bytes 147464 | tf_op jit(solution)/shard_map/ppermute | solution.py:408
  56.3 11.4 %collective-permute-start.8 = (bf16[192,128]{1,0:T(8,128)(2,1)}, bf16[192,128]{1,0:T(8,128)(2,1)S(1)}, u32[]{:S(2)}, u32[]{:S(2)}) collective-permute-start(bf16[192,128]{1,0:T(8,128)(2,1)} %get-tuple-element.52), channel_id=1, source_target_pairs={{0,2},{1,3},{2,0},{3,1},{4,6},{5,7},{6,4},{7,5},{8,10},{9,11},{10,... | collective-permute-start | bytes 147464 | tf_op jit(solution)/shard_map/ppermute | solution.py:408
  56.3 11.4 %collective-permute-start.7 = (bf16[192,128]{1,0:T(8,128)(2,1)S(1)}, bf16[192,128]{1,0:T(8,128)(2,1)S(1)}, u32[]{:S(2)}, u32[]{:S(2)}) collective-permute-start(bf16[192,128]{1,0:T(8,128)(2,1)S(1)} %get-tuple-element.50), channel_id=1, source_target_pairs={{0,1},{1,2},{2,3},{3,0},{4,5},{5,6},{6,7},{7,4},{8,9},{9,10},{10,1... | collective-permute-start | bytes 147464 | tf_op jit(solution)/shard_map/ppermute | solution.py:408
  57.4 0.9 %copy-start.2 = (bf16[64,768]{1,0:T(8,128)(2,1)S(1)}, bf16[64,768]{1,0:T(8,128)(2,1)}, u32[]{:S(2)}) copy-start(bf16[64,768]{1,0:T(8,128)(2,1)} %copy-done.1) | copy-start | bytes 294916
  58.3 0.8 %copy-start.4 = (f32[64,64]{1,0:T(8,128)S(1)}, f32[64,64]{1,0:T(8,128)}, u32[]{:S(2)}) copy-start(f32[64,64]{1,0:T(8,128)} %copy-done.3) | copy-start | bytes 49156

commit v10 on v9

--- a/solution.py
+++ b/solution.py
@@ -97,7 +97,7 @@
     slab = (units // n_exp, tokens)
     return pl.pallas_call(
         slab_kernel,
-        out_shape=[jax.ShapeDtypeStruct(slab, BF16)] * n_exp,
+        out_shape=[pltpu.HBM(slab, BF16)] * n_exp,
         scratch_shapes=[pltpu.VMEM((n_exp,) + slab, BF16)],
         compiler_params=params(8),
         cost_estimate=SMALL,
@@ -248,7 +248,7 @@
         compiler_params=params(8),
         cost_estimate=pl.CostEstimate(flops=4_000_000_000, bytes_accessed=1000, transcendentals=0),
         name="inverse_factor",
-    )(gram, lt)
+    )(*in_hbm(gram, lt))
 
 
 def finish_kernel(
@@ -413,15 +413,14 @@
 
 
 def body(n_rep, n_exp, activations, kv_grad, errors, right_factor, hidden, out_grad, moment_one, moment_two):
-    half = out_grad.shape[1] // 2
-    left_first = shift(out_grad[:, :half], n_exp, -1)
+    grads = {0: out_grad, n_exp - 1: shift(out_grad, n_exp, -1)}
     merged, lt = merge(activations, kv_grad, errors, right_factor.T)
 
-    lt, left_first = lax.optimization_barrier((lt, left_first))
-    grads = {0: [out_grad], 1: [shift(out_grad, n_exp, 1)]}
-    grads[n_exp - 1] = [left_first, shift(out_grad[:, half:], n_exp, -1)]
-
-    lt = (lt + swap(lt, "rep", n_rep, 1)).astype(BF16)
+    lt = lt + swap(lt, "rep", n_rep, 1)
+    lt, grads[n_exp - 1] = lax.optimization_barrier((lt, grads[n_exp - 1]))
+    lt = lt.astype(BF16)
+    if n_exp > 2:
+        grads[1] = shift(after(out_grad, lt), n_exp, 1)
     slabs = unit_slabs(after(hidden, lt), n_exp)
     bit = 2
     parts = [lt]
@@ -436,29 +435,30 @@
 
     fits = chunks.shape[0] == n_rep * n_exp and 8 * n_rep == lt.shape[0]
     both = ("rep", "exp")
+    slabs = [slabs[0]] + [shift(after(slabs[k], chunks), n_exp, k) for k in range(1, n_exp)]
     if fits:
         shares = lax.all_to_all(chunks, both, 0, 0, tiled=True)
         shares, grads = lax.optimization_barrier((shares, grads))
         share, gram = fold(shares, n_exp)
+        share, slabs = lax.optimization_barrier((share, slabs))
         chunks = lax.all_to_all(share, both, 0, 0, tiled=True)
     else:
         share, gram = fold_any(chunks, lt)
         chunks = share
     w, basis = inverse_factor(gram, lt)
 
-    slabs = [slabs[0]] + [shift(after(slabs[k], share), n_exp, k) for k in range(1, n_exp)]
     left, right = 1, n_exp - 1
     while right - left > 1:
         if left <= n_exp - right:
-            grads[left + 1] = [shift(after(g, share), n_exp, 1) for g in grads[left]]
+            grads[left + 1] = shift(after(grads[left], share), n_exp, 1)
             left += 1
         else:
-            grads[right - 1] = [shift(after(g, share), n_exp, -1) for g in grads[right]]
+            grads[right - 1] = shift(after(grads[right], share), n_exp, -1)
             right -= 1
 
     new_right, new_error = finish(n_rep, w, chunks, basis, merged)
     first_new, second_new, step = expert_step(
-        slabs, [g for k in range(n_exp) for g in grads[k]], moment_one, moment_two
+        slabs, [grads[k] for k in range(n_exp)], moment_one, moment_two
     )
     return new_error, new_right.T, first_new, second_new, step
 

time: 72.7 us -> 72.3 us (level)
  waiting for transfers between devices: 17.7 us -> 25.3 us
  local copies, waits for them, and re-layouts: 5.61 us -> 1.25 us
  starting transfers between devices: 29.3 us -> 25.2 us
    all_to_all x1, waiting for transfers between devices: 1.92 us -> 8.59 us  [body(): chunks = lax.all_to_all(share, both, 0, 0, tiled=True)]
    ppermute x7 -> x6, starting transfers between devices: 16.2 us -> 10.2 us  [shift(): return lax.ppermute(x, 'exp', [(i, (i + k) % size) for i in range(size)])]
    all_to_all x1, waiting for transfers between devices: 0.01 us -> 4.68 us  [body(): shares = lax.all_to_all(chunks, both, 0, 0, tiled=True)]
    ppermute x7 -> x6, waiting for transfers between devices: 10.4 us -> 6.85 us  [shift(): return lax.ppermute(x, 'exp', [(i, (i + k) % size) for i in range(size)])]
    unnamed x12 -> x8, local copies, waits for them, and re-layouts: 3.83 us -> 1.25 us
    all_to_all x1, starting transfers between devices: 3.83 us -> 6.01 us  [body(): chunks = lax.all_to_all(share, both, 0, 0, tiled=True)]
    slice x1 -> x0, local copies, waits for them, and re-layouts: 1.78 us -> none  [body(): grads[n_exp - 1] = [left_first, shift(out_grad[:, half:], n_exp, -1)]]
  transfers between devices with their start and end apart: 13 -> 12, of which waited for: 8 -> 8; matrix products, arithmetic and copies ran while one was open for 0% -> 0% of each run, Pallas kernels for 19% -> 21%
where the time goes in v10:
time: 72.3 us; the launch traced here: 72 us
  waiting for transfers between devices  25.3 us (35%)
  starting transfers between devices  25.2 us (35%)
  Pallas kernels  19.5 us (27%)
  local copies, waits for them, and re-layouts  1.25 us (2%)
  between operations  0.74 us (1%)
    ppermute x6, starting transfers between devices, shift(): return lax.ppermute(x, 'exp', [(i, (i + k) % size) for i in range(size)])  10.2 us
    all_to_all x1, waiting for transfers between devices, body(): chunks = lax.all_to_all(share, both, 0, 0, tiled=True)  8.59 us
    ppermute x6, waiting for transfers between devices, shift(): return lax.ppermute(x, 'exp', [(i, (i + k) % size) for i in range(size)])  6.85 us
    all_to_all x1, starting transfers between devices, body(): chunks = lax.all_to_all(share, both, 0, 0, tiled=True)  6.01 us
    all_to_all x1, starting transfers between devices, body(): shares = lax.all_to_all(chunks, both, 0, 0, tiled=True)  5.5 us
    pallas_call x1, Pallas kernels, merge(): pl.pallas_call(merge_kernel, grid=(rows // block,), in_specs=[pl.BlockSpe...  5.19 us
    ppermute x4, waiting for transfers between devices, swap(): return lax.ppermute(x, axis, [(i, i ^ mask) for i in range(size)])  5.16 us
    all_to_all x1, waiting for transfers between devices, body(): shares = lax.all_to_all(chunks, both, 0, 0, tiled=True)  4.68 us
  transfers between devices with their start and end apart: 12, of which 8 were waited for; matrix products, arithmetic and copies ran while one was open for 0% of the time, Pallas kernels for 21%

profile of v10, /device:TPU:0, one launch (start us, length us, event | category | flops | bytes accessed | tf_op | source)
XLA Modules:
  0.0 72.0 jit_solution(15760402284296352923)
XLA Ops:
  0.6 5.1 %collective-permute-start.1 = (bf16[1,128,2048]{2,1,0:T(8,128)(2,1)}, bf16[1,128,2048]{2,1,0:T(8,128)(2,1)S(1)}, u32[]{:S(2)}, u32[]{:S(2)}) collective-permute-start(bf16[1,128,2048]{2,1,0:T(8,128)(2,1)} %refs_4_), channel_id=1, source_target_pairs={{0,3},{1,0},{2,1},{3,2},{4,7},{5,4},{6,5},{7,6},{8,11},{9,8},{10,9... | collective-permute-start | bytes 1572872 | tf_op jit(solution)/shard_map/ppermute | solution.py:408
  5.7 5.2 %merge.1 = (bf16[768,1024]{1,0:T(8,128)(2,1)S(1)}, f32[64,768]{1,0:T(8,128)S(1)}) custom-call(bf16[1024,768]{1,0:T(8,128)(2,1)} %acts_ref.1, bf16[1024,1024]{1,0:T(8,128)(2,1)} %kv_ref.1, bf16[1,768,1024]{2,1,0:T(8,128)(2,1)} %err_ref.1, f32[64,1024]{1,0:T(8,128)} %bitcast.2), custom_call_target="tpu_custom_call" | custom-call | flops 4000000000 | bytes 8000000 | tf_op jit(solution)/shard_map/merge/pallas_call | solution.py:63
  11.0 1.4 %collective-permute-done = f32[64,768]{1,0:T(8,128)S(1)} collective-permute-done((f32[64,768]{1,0:T(8,128)S(1)}, f32[64,768]{1,0:T(8,128)S(1)}, u32[]{:S(2)}, u32[]{:S(2)}) %collective-permute-start) | collective-permute-done | bytes 196640 | tf_op jit(solution)/shard_map/ppermute | solution.py:404
  12.5 4.8 %collective-permute-done.1.refs_7_ = bf16[1,128,2048]{2,1,0:T(8,128)(2,1)S(1)} collective-permute-done((bf16[1,128,2048]{2,1,0:T(8,128)(2,1)}, bf16[1,128,2048]{2,1,0:T(8,128)(2,1)S(1)}, u32[]{:S(2)}, u32[]{:S(2)}) %collective-permute-start.1) | collective-permute-done | bytes 524320 | tf_op jit(solution)/shard_map/ppermute | solution.py:408
  17.2 2.4 %collective-permute-start.4 = (bf16[64,768]{1,0:T(8,128)(2,1)S(1)}, bf16[64,768]{1,0:T(8,128)(2,1)S(1)}, u32[]{:S(2)}, u32[]{:S(2)}) collective-permute-start(bf16[64,768]{1,0:T(8,128)(2,1)S(1)} %add.3.refs_0_), channel_id=1, source_target_pairs={{0,24},{4,28},{8,16},{12,20},{16,8},{20,12},{24,0},{28,4},{1,25},{... | collective-permute-start | bytes 294920 | tf_op jit(solution)/shard_map/ppermute | solution.py:404
  19.7 0.5 collective-permute-start.3
  20.2 0.5 collective-permute-start.2
  21.1 2.4 %collective-permute-done.4.refs_3_ = bf16[64,768]{1,0:T(8,128)(2,1)S(1)} collective-permute-done((bf16[64,768]{1,0:T(8,128)(2,1)S(1)}, bf16[64,768]{1,0:T(8,128)(2,1)S(1)}, u32[]{:S(2)}, u32[]{:S(2)}) %collective-permute-start.4) | collective-permute-done | bytes 98336 | tf_op jit(solution)/shard_map/ppermute | solution.py:404
  23.4 1.0 %collective-permute-done.3.refs_2_ = bf16[64,768]{1,0:T(8,128)(2,1)S(1)} collective-permute-done((bf16[64,768]{1,0:T(8,128)(2,1)S(1)}, bf16[64,768]{1,0:T(8,128)(2,1)S(1)}, u32[]{:S(2)}, u32[]{:S(2)}) %collective-permute-start.3) | collective-permute-done | bytes 98336 | tf_op jit(solution)/shard_map/ppermute | solution.py:404
  24.8 1.3 %right_product.1 = (bf16[64,768]{1,0:T(8,128)(2,1)S(1)}, bf16[32,32,128]{2,1,0:T(8,128)(2,1)}) custom-call(bf16[64,768]{1,0:T(8,128)(2,1)S(1)} %add.3.refs_0_, bf16[64,768]{1,0:T(8,128)(2,1)S(1)} %collective-permute-done.2.refs_1_, bf16[64,768]{1,0:T(8,128)(2,1)S(1)} %collective-permute-done.3.refs_2_, bf16[64,768]{1,0:T(8,128)(2,1)S(1)} %collective-permute-done.4.refs_3_, ...), custom_call_target="tpu_custom_call" | custom-call | flops 1000 | bytes 1000 | tf_op jit(solution)/shard_map/right_product/pallas_call | solution.py:154
  26.1 0.6 copy-done.2
  26.8 5.5 %all-to-all-start = ((bf16[32,32,128]{2,1,0:T(8,128)(2,1)}), bf16[32,32,128]{2,1,0:T(8,128)(2,1)S(1)}, u32[]{:S(2)}, u32[]{:S(2)}) async-start(bf16[32,32,128]{2,1,0:T(8,128)(2,1)} %get-tuple-element.42), calls=%async_computation | async-start | bytes 524288 | tf_op jit(solution)/shard_map/all_to_all | solution.py:440
  32.3 0.8 %unit_slabs.1 = (bf16[192,128]{1,0:T(8,128)(2,1)}, bf16[192,128]{1,0:T(8,128)(2,1)}, bf16[192,128]{1,0:T(8,128)(2,1)}, bf16[192,128]{1,0:T(8,128)(2,1)}) custom-call(bf16[1,128,768]{2,1,0:T(8,128)(2,1)S(1)} %copy-done), custom_call_target="tpu_custom_call" | custom-call | flops 1000 | bytes 1000 | tf_op jit(solution)/shard_map/unit_slabs/pallas_call | solution.py:98
  33.1 3.6 %collective-permute-start.8 = (bf16[192,128]{1,0:T(8,128)(2,1)}, bf16[192,128]{1,0:T(8,128)(2,1)S(1)}, u32[]{:S(2)}, u32[]{:S(2)}) collective-permute-start(bf16[192,128]{1,0:T(8,128)(2,1)} %get-tuple-element.57), channel_id=1, source_target_pairs={{0,3},{1,0},{2,1},{3,2},{4,7},{5,4},{6,5},{7,6},{8,11},{9,8},{10,9... | collective-permute-start | bytes 147464 | tf_op jit(solution)/shard_map/ppermute | solution.py:408
  36.7 1.1 %collective-permute-start.6 = (bf16[192,128]{1,0:T(8,128)(2,1)}, bf16[192,128]{1,0:T(8,128)(2,1)S(1)}, u32[]{:S(2)}, u32[]{:S(2)}) collective-permute-start(bf16[192,128]{1,0:T(8,128)(2,1)} %get-tuple-element.53), channel_id=1, source_target_pairs={{0,1},{1,2},{2,3},{3,0},{4,5},{5,6},{6,7},{7,4},{8,9},{9,10},{10,1... | collective-permute-start | bytes 147464 | tf_op jit(solution)/shard_map/ppermute | solution.py:408
  37.8 4.7 %all-to-all-done.share_ref = bf16[32,32,128]{2,1,0:T(8,128)(2,1)S(1)} async-done(((bf16[32,32,128]{2,1,0:T(8,128)(2,1)}), bf16[32,32,128]{2,1,0:T(8,128)(2,1)S(1)}, u32[]{:S(2)}, u32[]{:S(2)}) %all-to-all-start) | async-done | bytes 262176 | tf_op jit(solution)/shard_map/all_to_all | solution.py:440
  42.5 0.7 fold.1
  43.2 0.6 copy-done.3
  43.8 2.1 %collective-permute-done.7.refs_2_ = bf16[192,128]{1,0:T(8,128)(2,1)S(1)} collective-permute-done((bf16[192,128]{1,0:T(8,128)(2,1)}, bf16[192,128]{1,0:T(8,128)(2,1)S(1)}, u32[]{:S(2)}, u32[]{:S(2)}) %collective-permute-start.7) | collective-permute-done | bytes 49184 | tf_op jit(solution)/shard_map/ppermute | solution.py:408
  45.9 6.0 %all-to-all-start.1 = ((bf16[32,16,128]{2,1,0:T(8,128)(2,1)}), bf16[32,16,128]{2,1,0:T(8,128)(2,1)S(1)}, u32[]{:S(2)}, u32[]{:S(2)}) async-start(bf16[32,16,128]{2,1,0:T(8,128)(2,1)} %get-tuple-element.58), calls=%async_computation.1 | async-start | bytes 262144 | tf_op jit(solution)/shard_map/all_to_all | solution.py:444
  51.9 4.6 %inverse_factor.1 = (f32[64,64]{1,0:T(8,128)}, bf16[768,64]{1,0:T(8,128)(2,1)}) custom-call(f32[64,64]{1,0:T(8,128)} %copy-done.3, bf16[64,768]{1,0:T(8,128)(2,1)} %copy-done.2), custom_call_target="tpu_custom_call" | custom-call | flops 4000000000 | bytes 1000 | tf_op jit(solution)/shard_map/inverse_factor/pallas_call | solution.py:238
  56.5 8.6 %all-to-all-done.1.chunk_ref = bf16[32,16,128]{2,1,0:T(8,128)(2,1)S(1)} async-done(((bf16[32,16,128]{2,1,0:T(8,128)(2,1)}), bf16[32,16,128]{2,1,0:T(8,128)(2,1)S(1)}, u32[]{:S(2)}, u32[]{:S(2)}) %all-to-all-start.1) | async-done | bytes 131104 | tf_op jit(solution)/shard_map/all_to_all | solution.py:444
  65.1 2.4 %finish.1 = (f32[64,1024]{1,0:T(8,128)}, bf16[1,768,1024]{2,1,0:T(8,128)(2,1)}) custom-call(f32[64,64]{1,0:T(8,128)} %get-tuple-element.48.w_any, bf16[32,16,128]{2,1,0:T(8,128)(2,1)S(1)} %all-to-all-done.1.chunk_ref, bf16[768,64]{1,0:T(8,128)(2,1)} %get-tuple-element.59.basis_any, bf16[768,1024]{1,0:T(8,128)(2,1)S(1)} %get-tuple-element.41.refs_4_.merged_ref), custom_call_target="tpu_custom_call" | custom-call | flops 1000 | bytes 1000 | tf_op jit(solution)/shard_map/finish/pallas_call | solution.py:290
  67.5 4.5 %expert_step.1 = (f32[1,192,2048]{2,1,0:T(8,128)}, f32[1,192,2048]{2,1,0:T(8,128)}, bf16[1,192,2048]{2,1,0:T(8,128)(2,1)}) custom-call(bf16[192,128]{1,0:T(8,128)(2,1)S(1)} %copy-done.1, bf16[192,128]{1,0:T(8,128)(2,1)S(1)} %collective-permute-done.6.refs_1_, bf16[192,128]{1,0:T(8,128)(2,1)S(1)} %collective-permute-done.7.refs_2_, ...), custom_call_target="tpu_custom_call" | custom-call | flops 1000 | bytes 1000 | tf_op jit(solution)/shard_map/expert_step/pallas_call | solution.py:375
  (16 shorter events, 0.9 us)
Async XLA Ops:
  0.6 16.6 %collective-permute-start.1 = (bf16[1,128,2048]{2,1,0:T(8,128)(2,1)}, bf16[1,128,2048]{2,1,0:T(8,128)(2,1)S(1)}, u32[]{:S(2)}, u32[]{:S(2)}) collective-permute-start(bf16[1,128,2048]{2,1,0:T(8,128)(2,1)} %refs_4_), channel_id=1, source_target_pairs={{0,3},{1,0},{2,1},{3,2},{4,7},{5,4},{6,5},{7,6},{8,11},{9,8},{10,9... | collective-permute-start | bytes 1572872 | tf_op jit(solution)/shard_map/ppermute | solution.py:408
  10.9 21.4 %copy-start = (bf16[1,128,768]{2,1,0:T(8,128)(2,1)S(1)}, bf16[1,128,768]{2,1,0:T(8,128)(2,1)}, u32[]{:S(2)}) copy-start(bf16[1,128,768]{2,1,0:T(8,128)(2,1)} %hidden_ref) | copy-start | bytes 589828
  10.9 1.5 %collective-permute-start = (f32[64,768]{1,0:T(8,128)S(1)}, f32[64,768]{1,0:T(8,128)S(1)}, u32[]{:S(2)}, u32[]{:S(2)}) collective-permute-start(f32[64,768]{1,0:T(8,128)S(1)} %get-tuple-element.39), channel_id=1, source_target_pairs={{0,4},{4,0},{8,12},{12,8},{16,20},{20,16},{24,28},{28,24},{1,5},{5... | collective-permute-start | bytes 589832 | tf_op jit(solution)/shard_map/ppermute | solution.py:404
  17.2 6.2 %collective-permute-start.4 = (bf16[64,768]{1,0:T(8,128)(2,1)S(1)}, bf16[64,768]{1,0:T(8,128)(2,1)S(1)}, u32[]{:S(2)}, u32[]{:S(2)}) collective-permute-start(bf16[64,768]{1,0:T(8,128)(2,1)S(1)} %add.3.refs_0_), channel_id=1, source_target_pairs={{0,24},{4,28},{8,16},{12,20},{16,8},{20,12},{24,0},{28,4},{1,25},{... | collective-permute-start | bytes 294920 | tf_op jit(solution)/shard_map/ppermute | solution.py:404
  19.7 4.7 %collective-permute-start.3 = (bf16[64,768]{1,0:T(8,128)(2,1)S(1)}, bf16[64,768]{1,0:T(8,128)(2,1)S(1)}, u32[]{:S(2)}, u32[]{:S(2)}) collective-permute-start(bf16[64,768]{1,0:T(8,128)(2,1)S(1)} %add.3.refs_0_), channel_id=1, source_target_pairs={{0,16},{4,20},{8,24},{12,28},{16,0},{20,4},{24,8},{28,12},{1,17},{... | collective-permute-start | bytes 294920 | tf_op jit(solution)/shard_map/ppermute | solution.py:404
  20.2 4.6 %collective-permute-start.2 = (bf16[64,768]{1,0:T(8,128)(2,1)S(1)}, bf16[64,768]{1,0:T(8,128)(2,1)S(1)}, u32[]{:S(2)}, u32[]{:S(2)}) collective-permute-start(bf16[64,768]{1,0:T(8,128)(2,1)S(1)} %add.3.refs_0_), channel_id=1, source_target_pairs={{0,8},{4,12},{8,0},{12,4},{16,24},{20,28},{24,16},{28,20},{1,9},{5... | collective-permute-start | bytes 294920 | tf_op jit(solution)/shard_map/ppermute | solution.py:404
  20.7 17.1 %collective-permute-start.5 = (bf16[1,128,2048]{2,1,0:T(8,128)(2,1)}, bf16[1,128,2048]{2,1,0:T(8,128)(2,1)S(1)}, u32[]{:S(2)}, u32[]{:S(2)}) collective-permute-start(bf16[1,128,2048]{2,1,0:T(8,128)(2,1)} %refs_4_), channel_id=1, source_target_pairs={{0,1},{1,2},{2,3},{3,0},{4,5},{5,6},{6,7},{7,4},{8,9},{9,10},{10,1... | collective-permute-start | bytes 1572872 | tf_op jit(solution)/shard_map/ppermute | solution.py:408
  26.1 0.6 copy-start.2
  26.8 15.7 %all-to-all-start = ((bf16[32,32,128]{2,1,0:T(8,128)(2,1)}), bf16[32,32,128]{2,1,0:T(8,128)(2,1)S(1)}, u32[]{:S(2)}, u32[]{:S(2)}) async-start(bf16[32,32,128]{2,1,0:T(8,128)(2,1)} %get-tuple-element.42), calls=%async_computation | async-start | bytes 524288 | tf_op jit(solution)/shard_map/all_to_all | solution.py:440
  33.1 10.7 %collective-permute-start.8 = (bf16[192,128]{1,0:T(8,128)(2,1)}, bf16[192,128]{1,0:T(8,128)(2,1)S(1)}, u32[]{:S(2)}, u32[]{:S(2)}) collective-permute-start(bf16[192,128]{1,0:T(8,128)(2,1)} %get-tuple-element.57), channel_id=1, source_target_pairs={{0,3},{1,0},{2,1},{3,2},{4,7},{5,4},{6,5},{7,6},{8,11},{9,8},{10,9... | collective-permute-start | bytes 147464 | tf_op jit(solution)/shard_map/ppermute | solution.py:408
  36.7 9.2 %collective-permute-start.7 = (bf16[192,128]{1,0:T(8,128)(2,1)}, bf16[192,128]{1,0:T(8,128)(2,1)S(1)}, u32[]{:S(2)}, u32[]{:S(2)}) collective-permute-start(bf16[192,128]{1,0:T(8,128)(2,1)} %get-tuple-element.55), channel_id=1, source_target_pairs={{0,2},{1,3},{2,0},{3,1},{4,6},{5,7},{6,4},{7,5},{8,10},{9,11},{10,... | collective-permute-start | bytes 147464 | tf_op jit(solution)/shard_map/ppermute | solution.py:408
  36.7 9.2 %collective-permute-start.6 = (bf16[192,128]{1,0:T(8,128)(2,1)}, bf16[192,128]{1,0:T(8,128)(2,1)S(1)}, u32[]{:S(2)}, u32[]{:S(2)}) collective-permute-start(bf16[192,128]{1,0:T(8,128)(2,1)} %get-tuple-element.53), channel_id=1, source_target_pairs={{0,1},{1,2},{2,3},{3,0},{4,5},{5,6},{6,7},{7,4},{8,9},{9,10},{10,1... | collective-permute-start | bytes 147464 | tf_op jit(solution)/shard_map/ppermute | solution.py:408
  43.2 0.6 copy-start.3
  45.9 21.6 %collective-permute-start.9 = (bf16[1,128,2048]{2,1,0:T(8,128)(2,1)S(1)}, bf16[1,128,2048]{2,1,0:T(8,128)(2,1)S(1)}, u32[]{:S(2)}, u32[]{:S(2)}) collective-permute-start(bf16[1,128,2048]{2,1,0:T(8,128)(2,1)S(1)} %collective-permute-done.5.refs_5_), channel_id=1, source_target_pairs={{0,1},{1,2},{2,3},{3,0},{4,5},{5,6},{6,7},{7,4},{8,9},{9,10},{10,1... | collective-permute-start | bytes 1572872 | tf_op jit(solution)/shard_map/ppermute | solution.py:408
  45.9 19.2 %all-to-all-start.1 = ((bf16[32,16,128]{2,1,0:T(8,128)(2,1)}), bf16[32,16,128]{2,1,0:T(8,128)(2,1)S(1)}, u32[]{:S(2)}, u32[]{:S(2)}) async-start(bf16[32,16,128]{2,1,0:T(8,128)(2,1)} %get-tuple-element.58), calls=%async_computation.1 | async-start | bytes 262144 | tf_op jit(solution)/shard_map/all_to_all | solution.py:444
  56.5 11.0 %copy-start.1 = (bf16[192,128]{1,0:T(8,128)(2,1)S(1)}, bf16[192,128]{1,0:T(8,128)(2,1)}, u32[]{:S(2)}) copy-start(bf16[192,128]{1,0:T(8,128)(2,1)} %get-tuple-element.62.refs_0_) | copy-start | bytes 147460

commit v11 on v10

--- a/solution.py
+++ b/solution.py
@@ -105,100 +105,100 @@
     )(hidden)
 
 
-def as_terms(x, hold=lambda rounded: rounded):
-    high = hold(x.astype(BF16)).astype(F32)
-    rest = x - high
-    middle = hold(rest.astype(BF16)).astype(F32)
-    low = rest - middle
-    return jnp.concatenate([high, middle], axis=-1), jnp.concatenate([low, jnp.zeros_like(low)], axis=-1)
-
-
-def from_terms(first, second):
-    rank = first.shape[-1] // 2
-    return first[..., :rank] + first[..., rank:] + second[..., :rank]
-
-
 def right_kernel(n_parts, *refs):
     part_refs, merged_ref = refs[:n_parts], refs[n_parts]
-    lt_ref, chunk_ref, terms_ref = refs[n_parts + 1 :]
+    lt_ref, gram_ref, chunk_ref = refs[n_parts + 1 :]
     parts = [ref[...].astype(F32) for ref in part_refs]
     while len(parts) > 1:
         parts = [a + b for a, b in zip(parts[0::2], parts[1::2])]
     lt = parts[0]
     rank = lt.shape[0]
     lt_ref[...] = lt.astype(BF16)
+    gram = lax.dot_general(lt, lt, COLS_LAST, precision=HIGHEST, preferred_element_type=F32)
+    half = rank // 2
+    packed = jnp.concatenate([gram[:half], gram[half:]], axis=1)
+    high = packed.astype(BF16)
+    rest = packed - high.astype(F32)
+    middle = rest.astype(BF16)
+    low = (rest - middle.astype(F32)).astype(BF16)
+    gram_ref[0:half] = high
+    gram_ref[half : 2 * half] = middle
+    gram_ref[2 * half : 3 * half] = low
     product = left_times(lt, merged_ref[...], (((1,), (0,)), ((), ()))).astype(BF16)
     across = product.shape[1] // TILE_C
     for a in range(rank // TILE_R):
         for b in range(across):
-            chunk_ref[a * across + b, 0:TILE_R] = product[
+            chunk_ref[a * across + b] = product[
                 a * TILE_R : (a + 1) * TILE_R, b * TILE_C : (b + 1) * TILE_C
             ]
-    first, second = as_terms(
-        lax.dot_general(lt, lt, COLS_LAST, precision=HIGHEST, preferred_element_type=F32)
-    )
-    terms_ref[0] = first
-    terms_ref[1] = second
-    piece = lax.rem(lax.axis_index("rep"), rank // 8)
-    here = pl.ds(pl.multiple_of(piece * 8, 8), 8)
-    piece = jnp.concatenate([terms_ref[0, here, :], terms_ref[1, here, :]], axis=0).astype(BF16)
-    for c in range(chunk_ref.shape[0]):
-        chunk_ref[c, TILE_R:] = piece
 
 
 def right_product(parts, merged):
     rank, rows = parts[0].shape
     cols = merged.shape[1]
-    assert 2 * rank == TILE_C
     chunks = rank * cols // (TILE_R * TILE_C)
     return pl.pallas_call(
         functools.partial(right_kernel, len(parts)),
         out_shape=[
             jax.ShapeDtypeStruct((rank, rows), BF16),
-            jax.ShapeDtypeStruct((chunks, 2 * TILE_R, TILE_C), BF16),
-        ],
-        scratch_shapes=[pltpu.VMEM((2, rank, TILE_C), F32)],
+            pltpu.HBM((3 * (rank // 2), 2 * rank), BF16),
+            jax.ShapeDtypeStruct((chunks, TILE_R, TILE_C), BF16),
+        ],
         compiler_params=params(16),
         cost_estimate=SMALL,
         name="right_product",
     )(*parts, merged)
 
 
-def fold_kernel(n_exp, share_ref, out_ref, gram_ref):
-    total = share_ref[0, 0:TILE_R].astype(F32)
+def load_kernel(share_ref, gram_hbm, load_ref, gram_ref, sem):
+    terms = gram_ref.shape[0]
+    copy = pltpu.make_async_copy(gram_hbm, gram_ref, sem)
+    copy.start()
+    total = share_ref[0].astype(F32)
     for i in range(1, share_ref.shape[0]):
-        total = total + share_ref[i, 0:TILE_R].astype(F32)
+        total = total + share_ref[i].astype(F32)
+    load_ref[terms:] = total.astype(BF16)
+    copy.wait()
+    load_ref[0:terms] = gram_ref[...]
+
+
+def line_load(shares, gram):
+    return pl.pallas_call(
+        load_kernel,
+        in_specs=[VMEM, HBM],
+        out_shape=jax.ShapeDtypeStruct((gram.shape[0] + shares.shape[1], TILE_C), BF16),
+        scratch_shapes=[pltpu.VMEM(gram.shape, BF16), pltpu.SemaphoreType.DMA],
+        compiler_params=params(4),
+        cost_estimate=SMALL,
+        name="line_load",
+    )(shares, *in_hbm(gram))
+
+
+def line_kernel(terms, *refs):
+    load_refs, out_ref, parts_ref = refs[:-2], refs[-2], refs[-1]
+    n_exp = len(load_refs)
+    for k in range(n_exp):
+        parts_ref[k] = load_refs[k][terms:].astype(F32)
+    place = lax.axis_index("exp")
+    total = None
+    for j in range(n_exp):
+        part = parts_ref[lax.rem(place + n_exp - j, n_exp)]
+        total = part if total is None else total + part
     total = total.astype(BF16)
     for i in range(out_ref.shape[0]):
         out_ref[i] = total
-    for r in range(share_ref.shape[0] // n_exp):
-        rows = None
-        for j in range(n_exp):
-            terms = share_ref[r * n_exp + j, TILE_R:].astype(F32)
-            part = from_terms(terms[:8], terms[8:])
-            rows = part if rows is None else rows + part
-        gram_ref[8 * r : 8 * r + 8, :] = rows
-
-
-def fold(shares, n_exp):
-    count = shares.shape[0]
-    rank = 8 * (count // n_exp)
-    return pl.pallas_call(
-        functools.partial(fold_kernel, n_exp),
-        out_shape=[
-            jax.ShapeDtypeStruct((count, TILE_R, TILE_C), BF16),
-            jax.ShapeDtypeStruct((rank, rank), F32),
-        ],
+
+
+def line_sum(loads, terms, n_rep):
+    rows = loads[0].shape[0] - terms
+    return pl.pallas_call(
+        functools.partial(line_kernel, terms),
+        out_shape=jax.ShapeDtypeStruct((n_rep, rows, TILE_C), BF16),
+        scratch_shapes=[pltpu.VMEM((len(loads), rows, TILE_C), F32)],
         compiler_params=params(4),
         cost_estimate=SMALL,
-        name="fold",
-    )(shares)
-
-
-def fold_any(chunks, lt):
-    total = lax.psum(chunks[:, :TILE_R].astype(F32), ("rep", "exp")).astype(BF16)
-    wide = lt.astype(F32)
-    return total, lax.psum(jnp.dot(wide, wide.T, precision=HIGHEST), "exp")
+        name="line_sum",
+    )(*loads)
 
 
 def inverse_of_factor(gram, wide_ref):
@@ -221,34 +221,50 @@
     return wide_ref[:, rank:]
 
 
-def inverse_kernel(gram_any, lt_any, w_ref, basis_ref, gram_ref, lt_ref, wide_ref, sems):
-    gram_copy = pltpu.make_async_copy(gram_any, gram_ref, sems.at[0])
-    gram_copy.start()
-    lt_copy = pltpu.make_async_copy(lt_any, lt_ref, sems.at[1])
+def inverse_kernel(n_exp, *refs):
+    load_hbms, lt_hbm = refs[:n_exp], refs[n_exp]
+    w_ref, basis_ref, terms_ref, lt_ref, wide_ref, sems = refs[n_exp + 1 :]
+    rank = lt_ref.shape[0]
+    half = rank // 2
+    copies = [
+        pltpu.make_async_copy(load_hbms[k].at[0 : 3 * half], terms_ref.at[k], sems.at[k])
+        for k in range(n_exp)
+    ]
+    lt_copy = pltpu.make_async_copy(lt_hbm, lt_ref, sems.at[n_exp])
+    for copy in copies:
+        copy.start()
     lt_copy.start()
-    gram_copy.wait()
-    w = inverse_of_factor(gram_ref[...], wide_ref)
+    for copy in copies:
+        copy.wait()
+    place = lax.axis_index("exp")
+    packed = None
+    for j in range(n_exp):
+        terms = terms_ref[lax.rem(place + n_exp - j, n_exp)].astype(F32)
+        part = terms[:half] + terms[half : 2 * half] + terms[2 * half :]
+        packed = part if packed is None else packed + part
+    w = inverse_of_factor(jnp.concatenate([packed[:, :rank], packed[:, rank:]], axis=0), wide_ref)
     w_ref[...] = w
     lt_copy.wait()
     basis_ref[...] = left_times(w, lt_ref[...], (((1,), (0,)), ((), ()))).T.astype(BF16)
 
 
-def inverse_factor(gram, lt):
+def inverse_factor(loads, lt):
     rank, rows = lt.shape
-    return pl.pallas_call(
-        inverse_kernel,
-        in_specs=[ANY] * 2,
+    n_exp = len(loads)
+    return pl.pallas_call(
+        functools.partial(inverse_kernel, n_exp),
+        in_specs=[ANY] * n_exp + [HBM],
         out_shape=[pltpu.HBM((rank, rank), F32), pltpu.HBM((rows, rank), BF16)],
         scratch_shapes=[
-            pltpu.VMEM((rank, rank), F32),
+            pltpu.VMEM((n_exp, 3 * (rank // 2), 2 * rank), BF16),
             pltpu.VMEM((rank, rows), BF16),
             pltpu.VMEM((rank, 2 * rank), F32),
-            pltpu.SemaphoreType.DMA((2,)),
+            pltpu.SemaphoreType.DMA((n_exp + 1,)),
         ],
         compiler_params=params(8),
         cost_estimate=pl.CostEstimate(flops=4_000_000_000, bytes_accessed=1000, transcendentals=0),
         name="inverse_factor",
-    )(*in_hbm(gram, lt))
+    )(*loads, *in_hbm(lt))
 
 
 def finish_kernel(
@@ -413,14 +429,12 @@
 
 
 def body(n_rep, n_exp, activations, kv_grad, errors, right_factor, hidden, out_grad, moment_one, moment_two):
-    grads = {0: out_grad, n_exp - 1: shift(out_grad, n_exp, -1)}
+    grads = {0: out_grad, 1: shift(out_grad, n_exp, 1)}
+    if n_exp > 2:
+        grads[n_exp - 1] = shift(out_grad, n_exp, -1)
     merged, lt = merge(activations, kv_grad, errors, right_factor.T)
 
-    lt = lt + swap(lt, "rep", n_rep, 1)
-    lt, grads[n_exp - 1] = lax.optimization_barrier((lt, grads[n_exp - 1]))
-    lt = lt.astype(BF16)
-    if n_exp > 2:
-        grads[1] = shift(after(out_grad, lt), n_exp, 1)
+    lt = (lt + swap(lt, "rep", n_rep, 1)).astype(BF16)
     slabs = unit_slabs(after(hidden, lt), n_exp)
     bit = 2
     parts = [lt]
@@ -431,21 +445,19 @@
         masks = [bit] if 2 * bit >= n_rep else [bit, 2 * bit, 3 * bit]
         parts = [own] + [swap(own, "rep", n_rep, m) for m in masks]
         bit *= len(parts)
-    lt, chunks = right_product(parts, merged)
-
-    fits = chunks.shape[0] == n_rep * n_exp and 8 * n_rep == lt.shape[0]
-    both = ("rep", "exp")
-    slabs = [slabs[0]] + [shift(after(slabs[k], chunks), n_exp, k) for k in range(1, n_exp)]
-    if fits:
-        shares = lax.all_to_all(chunks, both, 0, 0, tiled=True)
-        shares, grads = lax.optimization_barrier((shares, grads))
-        share, gram = fold(shares, n_exp)
-        share, slabs = lax.optimization_barrier((share, slabs))
-        chunks = lax.all_to_all(share, both, 0, 0, tiled=True)
-    else:
-        share, gram = fold_any(chunks, lt)
-        chunks = share
-    w, basis = inverse_factor(gram, lt)
+    lt, gram, chunks = right_product(parts, merged)
+
+    slabs = [slabs[0]] + [shift(after(slabs[k], lt), n_exp, k) for k in range(1, n_exp)]
+    rows = chunks.shape[0] * TILE_R // n_rep
+    shares = lax.all_to_all(chunks.reshape(n_rep, rows, TILE_C), "rep", 0, 0, tiled=True)
+    shares, grads = lax.optimization_barrier((shares, grads))
+
+    load = line_load(shares, gram)
+    loads = [load] + [shift(load, n_exp, k) for k in range(1, n_exp)]
+    loads, slabs = lax.optimization_barrier((loads, slabs))
+    share = line_sum(loads, gram.shape[0], n_rep)
+    w, basis = inverse_factor(loads, lt)
+    chunks = lax.all_to_all(share, "rep", 0, 0, tiled=True).reshape(chunks.shape)
 
     left, right = 1, n_exp - 1
     while right - left > 1:

time: 72.3 us -> 64.3 us (0.89)
  waiting for transfers between devices: 25.3 us -> 18.1 us
  starting transfers between devices: 25.2 us -> 23.4 us
  local copies, waits for them, and re-layouts: 1.25 us -> 2.04 us
    all_to_all x2, waiting for transfers between devices: 13.3 us -> 2.61 us  [the longest x1 1.87 us: body(): lax.all_to_all(chunks.reshape(n_rep, rows, TILE_C), 'rep', 0, 0, tiled=True)]
    all_to_all x2, starting transfers between devices: 11.5 us -> 7.1 us  [the longest x1 3.73 us: body(): lax.all_to_all(share, 'rep', 0, 0, tiled=True).reshape(chunks.shape)]
    ppermute x6 -> x9, waiting for transfers between devices: 6.85 us -> 11.2 us  [shift(): return lax.ppermute(x, 'exp', [(i, (i + k) % size) for i in range(size)])]
    ppermute x6 -> x9, starting transfers between devices: 10.2 us -> 12.2 us  [shift(): return lax.ppermute(x, 'exp', [(i, (i + k) % size) for i in range(size)])]
    ppermute x4, waiting for transfers between devices: 5.16 us -> 4.36 us  [swap(): return lax.ppermute(x, axis, [(i, i ^ mask) for i in range(size)])]
    unnamed x8 -> x10, local copies, waits for them, and re-layouts: 1.25 us -> 2.04 us
    pallas_call x2 -> x3, Pallas kernels: 5.31 us -> 5.42 us  [the longest x1 3.99 us: inverse_factor(): pl.pallas_call(functools.partial(inverse_kernel, n_exp), in_specs=[ANY] *...]
  transfers between devices with their start and end apart: 12 -> 15, of which waited for: 8 -> 9; matrix products, arithmetic and copies ran while one was open for 0% -> 0% of each run, Pallas kernels for 21% -> 14%
where the time goes in v11:
time: 64.3 us; the launch traced here: 63.8 us
  starting transfers between devices  23.4 us (36%)
  Pallas kernels  19.4 us (30%)
  waiting for transfers between devices  18.1 us (28%)
  local copies, waits for them, and re-layouts  2.04 us (3%)
  between operations  0.72 us (1%)
    ppermute x9, starting transfers between devices, shift(): return lax.ppermute(x, 'exp', [(i, (i + k) % size) for i in range(size)])  12.2 us
    ppermute x9, waiting for transfers between devices, shift(): return lax.ppermute(x, 'exp', [(i, (i + k) % size) for i in range(size)])  11.2 us
    pallas_call x1, Pallas kernels, merge(): pl.pallas_call(merge_kernel, grid=(rows // block,), in_specs=[pl.BlockSpe...  5.22 us
    pallas_call x1, Pallas kernels, expert_step(): pl.pallas_call(functools.partial(expert_kernel, n_exp, n_grad, chunk), in...  4.44 us
    ppermute x4, waiting for transfers between devices, swap(): return lax.ppermute(x, axis, [(i, i ^ mask) for i in range(size)])  4.36 us
    ppermute x4, starting transfers between devices, swap(): return lax.ppermute(x, axis, [(i, i ^ mask) for i in range(size)])  4.07 us
    pallas_call x1, Pallas kernels, inverse_factor(): pl.pallas_call(functools.partial(inverse_kernel, n_exp), in_specs=[ANY] *...  3.99 us
    all_to_all x1, starting transfers between devices, body(): lax.all_to_all(share, 'rep', 0, 0, tiled=True).reshape(chunks.shape)  3.73 us
  transfers between devices with their start and end apart: 15, of which 9 were waited for; matrix products, arithmetic and copies ran while one was open for 0% of the time, Pallas kernels for 14%

profile of v11, /device:TPU:0, one launch (start us, length us, event | category | flops | bytes accessed | tf_op | source)
XLA Modules:
  0.0 63.8 jit_solution(769226022128294258)
XLA Ops:
  0.6 5.2 %merge.1 = (bf16[768,1024]{1,0:T(8,128)(2,1)S(1)}, f32[64,768]{1,0:T(8,128)S(1)}) custom-call(bf16[1024,768]{1,0:T(8,128)(2,1)} %acts_ref.1, bf16[1024,1024]{1,0:T(8,128)(2,1)} %kv_ref.1, bf16[1,768,1024]{2,1,0:T(8,128)(2,1)} %err_ref.1, f32[64,1024]{1,0:T(8,128)} %bitcast.5), custom_call_target="tpu_custom_call" | custom-call | flops 4000000000 | bytes 8000000 | tf_op jit(solution)/shard_map/merge/pallas_call | solution.py:63
  6.4 2.6 %collective-permute-start.4 = (bf16[1,128,2048]{2,1,0:T(8,128)(2,1)}, bf16[1,128,2048]{2,1,0:T(8,128)(2,1)S(1)}, u32[]{:S(2)}, u32[]{:S(2)}) collective-permute-start(bf16[1,128,2048]{2,1,0:T(8,128)(2,1)} %refs_4_), channel_id=1, source_target_pairs={{0,1},{1,2},{2,3},{3,0},{4,5},{5,6},{6,7},{7,4},{8,9},{9,10},{10,1... | collective-permute-start | bytes 1572872 | tf_op jit(solution)/shard_map/ppermute | solution.py:424
  9.0 2.1 %collective-permute-start.5 = (bf16[1,128,2048]{2,1,0:T(8,128)(2,1)}, bf16[1,128,2048]{2,1,0:T(8,128)(2,1)S(1)}, u32[]{:S(2)}, u32[]{:S(2)}) collective-permute-start(bf16[1,128,2048]{2,1,0:T(8,128)(2,1)} %refs_4_), channel_id=1, source_target_pairs={{0,3},{1,0},{2,1},{3,2},{4,7},{5,4},{6,5},{7,6},{8,11},{9,8},{10,9... | collective-permute-start | bytes 1572872 | tf_op jit(solution)/shard_map/ppermute | solution.py:424
  11.2 2.6 %collective-permute-start.3 = (bf16[64,768]{1,0:T(8,128)(2,1)S(1)}, bf16[64,768]{1,0:T(8,128)(2,1)S(1)}, u32[]{:S(2)}, u32[]{:S(2)}) collective-permute-start(bf16[64,768]{1,0:T(8,128)(2,1)S(1)} %add_convert_fusion.refs_0_), channel_id=1, source_target_pairs={{0,24},{4,28},{8,16},{12,20},{16,8},{20,12},{24,0},{28,4},{1,25},{... | collective-permute-start | bytes 294920 | tf_op jit(solution)/shard_map/ppermute | solution.py:420
  14.7 2.3 %collective-permute-done.3.refs_3_ = bf16[64,768]{1,0:T(8,128)(2,1)S(1)} collective-permute-done((bf16[64,768]{1,0:T(8,128)(2,1)S(1)}, bf16[64,768]{1,0:T(8,128)(2,1)S(1)}, u32[]{:S(2)}, u32[]{:S(2)}) %collective-permute-start.3) | collective-permute-done | bytes 98336 | tf_op jit(solution)/shard_map/ppermute | solution.py:420
  17.0 2.0 %collective-permute-done.2.refs_2_ = bf16[64,768]{1,0:T(8,128)(2,1)S(1)} collective-permute-done((bf16[64,768]{1,0:T(8,128)(2,1)S(1)}, bf16[64,768]{1,0:T(8,128)(2,1)S(1)}, u32[]{:S(2)}, u32[]{:S(2)}) %collective-permute-start.2) | collective-permute-done | bytes 98336 | tf_op jit(solution)/shard_map/ppermute | solution.py:420
  19.1 1.2 %right_product.1 = (bf16[64,768]{1,0:T(8,128)(2,1)S(1)}, bf16[96,128]{1,0:T(8,128)(2,1)}, bf16[32,16,128]{2,1,0:T(8,128)(2,1)}) custom-call(bf16[64,768]{1,0:T(8,128)(2,1)S(1)} %add_convert_fusion.refs_0_, bf16[64,768]{1,0:T(8,128)(2,1)S(1)} %collective-permute-done.1.refs_1_, bf16[64,768]{1,0:T(8,128)(2,1)S(1)} %collective-permute-done.2.refs_2_, ...), custom_call_target="tpu_custom_call" | custom-call | flops 1000 | bytes 1000 | tf_op jit(solution)/shard_map/right_product/pallas_call | solution.py:140
  20.9 3.4 %all-to-all-start = ((bf16[8,64,128]{2,1,0:T(8,128)(2,1)}), bf16[8,64,128]{2,1,0:T(8,128)(2,1)S(1)}, u32[]{:S(2)}, u32[]{:S(2)}) async-start(bf16[8,64,128]{2,1,0:T(8,128)(2,1)} %bitcast.1), calls=%async_computation | async-start | bytes 262144 | tf_op jit(solution)/shard_map/all_to_all | solution.py:452
  24.3 0.8 %unit_slabs.1 = (bf16[192,128]{1,0:T(8,128)(2,1)}, bf16[192,128]{1,0:T(8,128)(2,1)}, bf16[192,128]{1,0:T(8,128)(2,1)}, bf16[192,128]{1,0:T(8,128)(2,1)}) custom-call(bf16[1,128,768]{2,1,0:T(8,128)(2,1)S(1)} %copy-done), custom_call_target="tpu_custom_call" | custom-call | flops 1000 | bytes 1000 | tf_op jit(solution)/shard_map/unit_slabs/pallas_call | solution.py:98
  25.1 1.8 %collective-permute-start.11 = (bf16[192,128]{1,0:T(8,128)(2,1)}, bf16[192,128]{1,0:T(8,128)(2,1)S(1)}, u32[]{:S(2)}, u32[]{:S(2)}) collective-permute-start(bf16[192,128]{1,0:T(8,128)(2,1)} %get-tuple-element.51), channel_id=1, source_target_pairs={{0,3},{1,0},{2,1},{3,2},{4,7},{5,4},{6,5},{7,6},{8,11},{9,8},{10,9... | collective-permute-start | bytes 147464 | tf_op jit(solution)/shard_map/ppermute | solution.py:424
  26.9 1.0 %collective-permute-start.9 = (bf16[192,128]{1,0:T(8,128)(2,1)}, bf16[192,128]{1,0:T(8,128)(2,1)S(1)}, u32[]{:S(2)}, u32[]{:S(2)}) collective-permute-start(bf16[192,128]{1,0:T(8,128)(2,1)} %get-tuple-element.47), channel_id=1, source_target_pairs={{0,1},{1,2},{2,3},{3,0},{4,5},{5,6},{6,7},{7,4},{8,9},{9,10},{10,1... | collective-permute-start | bytes 147464 | tf_op jit(solution)/shard_map/ppermute | solution.py:424
  27.9 1.9 %all-to-all-done.share_ref = bf16[8,64,128]{2,1,0:T(8,128)(2,1)S(1)} async-done(((bf16[8,64,128]{2,1,0:T(8,128)(2,1)}), bf16[8,64,128]{2,1,0:T(8,128)(2,1)S(1)}, u32[]{:S(2)}, u32[]{:S(2)}) %all-to-all-start) | async-done | bytes 131104 | tf_op jit(solution)/shard_map/all_to_all | solution.py:452
  29.8 5.2 %collective-permute-done.5.refs_7_ = bf16[1,128,2048]{2,1,0:T(8,128)(2,1)S(1)} collective-permute-done((bf16[1,128,2048]{2,1,0:T(8,128)(2,1)}, bf16[1,128,2048]{2,1,0:T(8,128)(2,1)S(1)}, u32[]{:S(2)}, u32[]{:S(2)}) %collective-permute-start.5) | collective-permute-done | bytes 524320 | tf_op jit(solution)/shard_map/ppermute | solution.py:424
  35.0 0.7 %line_load.1.refs_0_ = bf16[160,128]{1,0:T(8,128)(2,1)S(1)} custom-call(bf16[8,64,128]{2,1,0:T(8,128)(2,1)S(1)} %all-to-all-done.share_ref, bf16[96,128]{1,0:T(8,128)(2,1)} %get-tuple-element.42.gram_hbm), custom_call_target="tpu_custom_call" | custom-call | flops 1000 | bytes 1000 | tf_op jit(solution)/shard_map/line_load/pallas_call | solution.py:166
  35.7 2.5 %collective-permute-start.8 = (bf16[160,128]{1,0:T(8,128)(2,1)S(1)}, bf16[160,128]{1,0:T(8,128)(2,1)S(1)}, u32[]{:S(2)}, u32[]{:S(2)}) collective-permute-start(bf16[160,128]{1,0:T(8,128)(2,1)S(1)} %line_load.1.refs_0_), channel_id=1, source_target_pairs={{0,3},{1,0},{2,1},{3,2},{4,7},{5,4},{6,5},{7,6},{8,11},{9,8},{10,9... | collective-permute-start | bytes 122888 | tf_op jit(solution)/shard_map/ppermute | solution.py:424
  38.4 1.9 %collective-permute-start.6 = (bf16[160,128]{1,0:T(8,128)(2,1)S(1)}, bf16[160,128]{1,0:T(8,128)(2,1)S(1)}, u32[]{:S(2)}, u32[]{:S(2)}) collective-permute-start(bf16[160,128]{1,0:T(8,128)(2,1)S(1)} %line_load.1.refs_0_), channel_id=1, source_target_pairs={{0,1},{1,2},{2,3},{3,0},{4,5},{5,6},{6,7},{7,4},{8,9},{9,10},{10,1... | collective-permute-start | bytes 122888 | tf_op jit(solution)/shard_map/ppermute | solution.py:424
  40.3 2.9 %collective-permute-done.7.refs_2_ = bf16[160,128]{1,0:T(8,128)(2,1)S(1)} collective-permute-done((bf16[160,128]{1,0:T(8,128)(2,1)S(1)}, bf16[160,128]{1,0:T(8,128)(2,1)S(1)}, u32[]{:S(2)}, u32[]{:S(2)}) %collective-permute-start.7) | collective-permute-done | bytes 40992 | tf_op jit(solution)/shard_map/ppermute | solution.py:424
  43.2 1.0 %collective-permute-done.6.refs_1_ = bf16[160,128]{1,0:T(8,128)(2,1)S(1)} collective-permute-done((bf16[160,128]{1,0:T(8,128)(2,1)S(1)}, bf16[160,128]{1,0:T(8,128)(2,1)S(1)}, u32[]{:S(2)}, u32[]{:S(2)}) %collective-permute-start.6) | collective-permute-done | bytes 40992 | tf_op jit(solution)/shard_map/ppermute | solution.py:424
  45.6 3.7 %all-to-all-start.1 = ((bf16[8,64,128]{2,1,0:T(8,128)(2,1)}), bf16[8,64,128]{2,1,0:T(8,128)(2,1)S(1)}, u32[]{:S(2)}, u32[]{:S(2)}) async-start(bf16[8,64,128]{2,1,0:T(8,128)(2,1)} %line_sum.1), calls=%async_computation.1 | async-start | bytes 262144 | tf_op jit(solution)/shard_map/all_to_all | solution.py:460
  49.3 0.8 %copy-done.3 = bf16[160,128]{1,0:T(8,128)(2,1)S(1)} copy-done((bf16[160,128]{1,0:T(8,128)(2,1)S(1)}, bf16[160,128]{1,0:T(8,128)(2,1)}, u32[]{:S(2)}) %copy-start.3) | copy-done | bytes 40984
  50.1 4.0 %inverse_factor.1 = (f32[64,64]{1,0:T(8,128)}, bf16[768,64]{1,0:T(8,128)(2,1)}) custom-call(bf16[160,128]{1,0:T(8,128)(2,1)S(1)} %line_load.1.refs_0_, bf16[160,128]{1,0:T(8,128)(2,1)S(1)} %copy-done.3, bf16[160,128]{1,0:T(8,128)(2,1)S(1)} %collective-permute-done.7.refs_2_, bf16[160,128]{1,0:T(8,128)(2,1)S(1)} %collective-permute-done.8.refs_3_, ...), custom_call_target="tpu_custom_call" | custom-call | flops 4000000000 | bytes 1000 | tf_op jit(solution)/shard_map/inverse_factor/pallas_call | solution.py:254
  54.9 2.4 %finish.1 = (f32[64,1024]{1,0:T(8,128)}, bf16[1,768,1024]{2,1,0:T(8,128)(2,1)}) custom-call(f32[64,64]{1,0:T(8,128)} %get-tuple-element.56.w_any, bf16[32,16,128]{2,1,0:T(8,128)(2,1)S(1)} %bitcast.4, bf16[768,64]{1,0:T(8,128)(2,1)} %get-tuple-element.57.basis_any, bf16[768,1024]{1,0:T(8,128)(2,1)S(1)} %get-tuple-element.39.refs_4_.merged_ref), custom_call_target="tpu_custom_call" | custom-call | flops 1000 | bytes 1000 | tf_op jit(solution)/shard_map/finish/pallas_call | solution.py:306
  57.3 2.1 %collective-permute-done.12.refs_6_ = bf16[1,128,2048]{2,1,0:T(8,128)(2,1)S(1)} collective-permute-done((bf16[1,128,2048]{2,1,0:T(8,128)(2,1)S(1)}, bf16[1,128,2048]{2,1,0:T(8,128)(2,1)S(1)}, u32[]{:S(2)}, u32[]{:S(2)}) %collective-permute-start.12) | collective-permute-done | bytes 524320 | tf_op jit(solution)/shard_map/ppermute | solution.py:424
  59.4 4.4 %expert_step.1 = (f32[1,192,2048]{2,1,0:T(8,128)}, f32[1,192,2048]{2,1,0:T(8,128)}, bf16[1,192,2048]{2,1,0:T(8,128)(2,1)}) custom-call(bf16[192,128]{1,0:T(8,128)(2,1)S(1)} %copy-done.1, bf16[192,128]{1,0:T(8,128)(2,1)S(1)} %collective-permute-done.9.refs_1_, bf16[192,128]{1,0:T(8,128)(2,1)S(1)} %collective-permute-done.10.refs_2_, ...), custom_call_target="tpu_custom_call" | custom-call | flops 1000 | bytes 1000 | tf_op jit(solution)/shard_map/expert_step/pallas_call | solution.py:391
  (25 shorter events, 4.4 us)
Async XLA Ops:
  5.9 18.4 %copy-start = (bf16[1,128,768]{2,1,0:T(8,128)(2,1)S(1)}, bf16[1,128,768]{2,1,0:T(8,128)(2,1)}, u32[]{:S(2)}) copy-start(bf16[1,128,768]{2,1,0:T(8,128)(2,1)} %hidden_ref) | copy-start | bytes 589828
  5.9 5.3 %collective-permute-start = (f32[64,768]{1,0:T(8,128)S(1)}, f32[64,768]{1,0:T(8,128)S(1)}, u32[]{:S(2)}, u32[]{:S(2)}) collective-permute-start(f32[64,768]{1,0:T(8,128)S(1)} %get-tuple-element.38), channel_id=1, source_target_pairs={{0,4},{4,0},{8,12},{12,8},{16,20},{20,16},{24,28},{28,24},{1,5},{5... | collective-permute-start | bytes 589832 | tf_op jit(solution)/shard_map/ppermute | solution.py:420
  6.4 23.4 %collective-permute-start.4 = (bf16[1,128,2048]{2,1,0:T(8,128)(2,1)}, bf16[1,128,2048]{2,1,0:T(8,128)(2,1)S(1)}, u32[]{:S(2)}, u32[]{:S(2)}) collective-permute-start(bf16[1,128,2048]{2,1,0:T(8,128)(2,1)} %refs_4_), channel_id=1, source_target_pairs={{0,1},{1,2},{2,3},{3,0},{4,5},{5,6},{6,7},{7,4},{8,9},{9,10},{10,1... | collective-permute-start | bytes 1572872 | tf_op jit(solution)/shard_map/ppermute | solution.py:424
  9.0 26.0 %collective-permute-start.5 = (bf16[1,128,2048]{2,1,0:T(8,128)(2,1)}, bf16[1,128,2048]{2,1,0:T(8,128)(2,1)S(1)}, u32[]{:S(2)}, u32[]{:S(2)}) collective-permute-start(bf16[1,128,2048]{2,1,0:T(8,128)(2,1)} %refs_4_), channel_id=1, source_target_pairs={{0,3},{1,0},{2,1},{3,2},{4,7},{5,4},{6,5},{7,6},{8,11},{9,8},{10,9... | collective-permute-start | bytes 1572872 | tf_op jit(solution)/shard_map/ppermute | solution.py:424
  11.2 5.8 %collective-permute-start.3 = (bf16[64,768]{1,0:T(8,128)(2,1)S(1)}, bf16[64,768]{1,0:T(8,128)(2,1)S(1)}, u32[]{:S(2)}, u32[]{:S(2)}) collective-permute-start(bf16[64,768]{1,0:T(8,128)(2,1)S(1)} %add_convert_fusion.refs_0_), channel_id=1, source_target_pairs={{0,24},{4,28},{8,16},{12,20},{16,8},{20,12},{24,0},{28,4},{1,25},{... | collective-permute-start | bytes 294920 | tf_op jit(solution)/shard_map/ppermute | solution.py:420
  13.8 5.2 %collective-permute-start.2 = (bf16[64,768]{1,0:T(8,128)(2,1)S(1)}, bf16[64,768]{1,0:T(8,128)(2,1)S(1)}, u32[]{:S(2)}, u32[]{:S(2)}) collective-permute-start(bf16[64,768]{1,0:T(8,128)(2,1)S(1)} %add_convert_fusion.refs_0_), channel_id=1, source_target_pairs={{0,16},{4,20},{8,24},{12,28},{16,0},{20,4},{24,8},{28,12},{1,17},{... | collective-permute-start | bytes 294920 | tf_op jit(solution)/shard_map/ppermute | solution.py:420
  14.3 4.8 %collective-permute-start.1 = (bf16[64,768]{1,0:T(8,128)(2,1)S(1)}, bf16[64,768]{1,0:T(8,128)(2,1)S(1)}, u32[]{:S(2)}, u32[]{:S(2)}) collective-permute-start(bf16[64,768]{1,0:T(8,128)(2,1)S(1)} %add_convert_fusion.refs_0_), channel_id=1, source_target_pairs={{0,8},{4,12},{8,0},{12,4},{16,24},{20,28},{24,16},{28,20},{1,9},{5... | collective-permute-start | bytes 294920 | tf_op jit(solution)/shard_map/ppermute | solution.py:420
  20.3 0.6 %copy-start.4 = (bf16[64,768]{1,0:T(8,128)(2,1)}, bf16[64,768]{1,0:T(8,128)(2,1)S(1)}, u32[]{:S(2)}) copy-start(bf16[64,768]{1,0:T(8,128)(2,1)S(1)} %get-tuple-element.46.refs_4_) | copy-start | bytes 294916
  20.9 8.8 %all-to-all-start = ((bf16[8,64,128]{2,1,0:T(8,128)(2,1)}), bf16[8,64,128]{2,1,0:T(8,128)(2,1)S(1)}, u32[]{:S(2)}, u32[]{:S(2)}) async-start(bf16[8,64,128]{2,1,0:T(8,128)(2,1)} %bitcast.1), calls=%async_computation | async-start | bytes 262144 | tf_op jit(solution)/shard_map/all_to_all | solution.py:452
  25.1 13.3 %collective-permute-start.11 = (bf16[192,128]{1,0:T(8,128)(2,1)}, bf16[192,128]{1,0:T(8,128)(2,1)S(1)}, u32[]{:S(2)}, u32[]{:S(2)}) collective-permute-start(bf16[192,128]{1,0:T(8,128)(2,1)} %get-tuple-element.51), channel_id=1, source_target_pairs={{0,3},{1,0},{2,1},{3,2},{4,7},{5,4},{6,5},{7,6},{8,11},{9,8},{10,9... | collective-permute-start | bytes 147464 | tf_op jit(solution)/shard_map/ppermute | solution.py:424
  26.9 13.4 %collective-permute-start.10 = (bf16[192,128]{1,0:T(8,128)(2,1)}, bf16[192,128]{1,0:T(8,128)(2,1)S(1)}, u32[]{:S(2)}, u32[]{:S(2)}) collective-permute-start(bf16[192,128]{1,0:T(8,128)(2,1)} %get-tuple-element.49), channel_id=1, source_target_pairs={{0,2},{1,3},{2,0},{3,1},{4,6},{5,7},{6,4},{7,5},{8,10},{9,11},{10,... | collective-permute-start | bytes 147464 | tf_op jit(solution)/shard_map/ppermute | solution.py:424
  26.9 13.4 %collective-permute-start.9 = (bf16[192,128]{1,0:T(8,128)(2,1)}, bf16[192,128]{1,0:T(8,128)(2,1)S(1)}, u32[]{:S(2)}, u32[]{:S(2)}) collective-permute-start(bf16[192,128]{1,0:T(8,128)(2,1)} %get-tuple-element.47), channel_id=1, source_target_pairs={{0,1},{1,2},{2,3},{3,0},{4,5},{5,6},{6,7},{7,4},{8,9},{9,10},{10,1... | collective-permute-start | bytes 147464 | tf_op jit(solution)/shard_map/ppermute | solution.py:424
  35.7 4.6 %collective-permute-start.8 = (bf16[160,128]{1,0:T(8,128)(2,1)S(1)}, bf16[160,128]{1,0:T(8,128)(2,1)S(1)}, u32[]{:S(2)}, u32[]{:S(2)}) collective-permute-start(bf16[160,128]{1,0:T(8,128)(2,1)S(1)} %line_load.1.refs_0_), channel_id=1, source_target_pairs={{0,3},{1,0},{2,1},{3,2},{4,7},{5,4},{6,5},{7,6},{8,11},{9,8},{10,9... | collective-permute-start | bytes 122888 | tf_op jit(solution)/shard_map/ppermute | solution.py:424
  38.3 4.9 %collective-permute-start.7 = (bf16[160,128]{1,0:T(8,128)(2,1)S(1)}, bf16[160,128]{1,0:T(8,128)(2,1)S(1)}, u32[]{:S(2)}, u32[]{:S(2)}) collective-permute-start(bf16[160,128]{1,0:T(8,128)(2,1)S(1)} %line_load.1.refs_0_), channel_id=1, source_target_pairs={{0,2},{1,3},{2,0},{3,1},{4,6},{5,7},{6,4},{7,5},{8,10},{9,11},{10,... | collective-permute-start | bytes 122888 | tf_op jit(solution)/shard_map/ppermute | solution.py:424
  38.4 5.8 %collective-permute-start.6 = (bf16[160,128]{1,0:T(8,128)(2,1)S(1)}, bf16[160,128]{1,0:T(8,128)(2,1)S(1)}, u32[]{:S(2)}, u32[]{:S(2)}) collective-permute-start(bf16[160,128]{1,0:T(8,128)(2,1)S(1)} %line_load.1.refs_0_), channel_id=1, source_target_pairs={{0,1},{1,2},{2,3},{3,0},{4,5},{5,6},{6,7},{7,4},{8,9},{9,10},{10,1... | collective-permute-start | bytes 122888 | tf_op jit(solution)/shard_map/ppermute | solution.py:424
  44.8 0.6 copy-start.2
  45.5 13.9 %collective-permute-start.12 = (bf16[1,128,2048]{2,1,0:T(8,128)(2,1)S(1)}, bf16[1,128,2048]{2,1,0:T(8,128)(2,1)S(1)}, u32[]{:S(2)}, u32[]{:S(2)}) collective-permute-start(bf16[1,128,2048]{2,1,0:T(8,128)(2,1)S(1)} %collective-permute-done.4.refs_5_), channel_id=1, source_target_pairs={{0,1},{1,2},{2,3},{3,0},{4,5},{5,6},{6,7},{7,4},{8,9},{9,10},{10,1... | collective-permute-start | bytes 1572872 | tf_op jit(solution)/shard_map/ppermute | solution.py:424
  45.6 9.3 %all-to-all-start.1 = ((bf16[8,64,128]{2,1,0:T(8,128)(2,1)}), bf16[8,64,128]{2,1,0:T(8,128)(2,1)S(1)}, u32[]{:S(2)}, u32[]{:S(2)}) async-start(bf16[8,64,128]{2,1,0:T(8,128)(2,1)} %line_sum.1), calls=%async_computation.1 | async-start | bytes 262144 | tf_op jit(solution)/shard_map/all_to_all | solution.py:460
  49.3 0.8 %copy-start.3 = (bf16[160,128]{1,0:T(8,128)(2,1)S(1)}, bf16[160,128]{1,0:T(8,128)(2,1)}, u32[]{:S(2)}) copy-start(bf16[160,128]{1,0:T(8,128)(2,1)} %copy-done.2) | copy-start | bytes 122884
  54.1 5.2 %copy-start.1 = (bf16[192,128]{1,0:T(8,128)(2,1)S(1)}, bf16[192,128]{1,0:T(8,128)(2,1)}, u32[]{:S(2)}) copy-start(bf16[192,128]{1,0:T(8,128)(2,1)} %get-tuple-element.60.refs_0_) | copy-start | bytes 147460

commit v12 on v11

--- a/solution.py
+++ b/solution.py
@@ -83,26 +83,43 @@
     )(*[pltpu.with_memory_space_constraint(x, pltpu.HBM) for x in (acts, kv, err, vt)])
 
 
-def slab_kernel(hidden_ref, own_ref, *refs):
-    send_refs, all_ref = refs[:-1], refs[-1]
-    n_exp = all_ref.shape[0]
+def pack_kernel(hidden_hbm, gram_hbm, *refs):
+    load_refs, (hidden_ref, gram_ref, all_ref, sems) = refs[:-4], refs[-4:]
+    n_exp, units = all_ref.shape[:2]
+    terms = gram_ref.shape[0]
+    copies = [
+        pltpu.make_async_copy(hidden_hbm, hidden_ref, sems.at[0]),
+        pltpu.make_async_copy(gram_hbm, gram_ref, sems.at[1]),
+    ]
+    for copy in copies:
+        copy.start()
+    for copy in copies:
+        copy.wait()
     all_ref[...] = hidden_ref[0].T.reshape(all_ref.shape)
     place = lax.axis_index("exp")
-    for k, ref in enumerate((own_ref,) + tuple(send_refs)):
-        ref[...] = all_ref[lax.rem(place + k, n_exp)]
-
-
-def unit_slabs(hidden, n_exp):
+    for k, ref in enumerate(load_refs):
+        ref[0:terms] = gram_ref[...]
+        ref[terms : terms + units] = all_ref[lax.rem(place + k, n_exp)]
+
+
+def pack(hidden, gram, n_exp):
     _, tokens, units = hidden.shape
     slab = (units // n_exp, tokens)
-    return pl.pallas_call(
-        slab_kernel,
-        out_shape=[pltpu.HBM(slab, BF16)] * n_exp,
-        scratch_shapes=[pltpu.VMEM((n_exp,) + slab, BF16)],
+    load = (gram.shape[0] + slab[0], tokens)
+    return pl.pallas_call(
+        pack_kernel,
+        in_specs=[HBM] * 2,
+        out_shape=[pltpu.HBM(load, BF16)] + [jax.ShapeDtypeStruct(load, BF16)] * (n_exp - 1),
+        scratch_shapes=[
+            pltpu.VMEM(hidden.shape, BF16),
+            pltpu.VMEM(gram.shape, BF16),
+            pltpu.VMEM((n_exp,) + slab, BF16),
+            pltpu.SemaphoreType.DMA((2,)),
+        ],
         compiler_params=params(8),
         cost_estimate=SMALL,
-        name="unit_slabs",
-    )(hidden)
+        name="pack",
+    )(*in_hbm(hidden, gram))
 
 
 def right_kernel(n_parts, *refs):
@@ -140,7 +157,7 @@
     return pl.pallas_call(
         functools.partial(right_kernel, len(parts)),
         out_shape=[
-            jax.ShapeDtypeStruct((rank, rows), BF16),
+            pltpu.HBM((rank, rows), BF16),
             pltpu.HBM((3 * (rank // 2), 2 * rank), BF16),
             jax.ShapeDtypeStruct((chunks, TILE_R, TILE_C), BF16),
         ],
@@ -150,35 +167,28 @@
     )(*parts, merged)
 
 
-def load_kernel(share_ref, gram_hbm, load_ref, gram_ref, sem):
-    terms = gram_ref.shape[0]
-    copy = pltpu.make_async_copy(gram_hbm, gram_ref, sem)
-    copy.start()
+def sum_kernel(share_ref, out_ref):
     total = share_ref[0].astype(F32)
     for i in range(1, share_ref.shape[0]):
         total = total + share_ref[i].astype(F32)
-    load_ref[terms:] = total.astype(BF16)
-    copy.wait()
-    load_ref[0:terms] = gram_ref[...]
-
-
-def line_load(shares, gram):
-    return pl.pallas_call(
-        load_kernel,
-        in_specs=[VMEM, HBM],
-        out_shape=jax.ShapeDtypeStruct((gram.shape[0] + shares.shape[1], TILE_C), BF16),
-        scratch_shapes=[pltpu.VMEM(gram.shape, BF16), pltpu.SemaphoreType.DMA],
+    out_ref[...] = total.astype(BF16)
+
+
+def replica_sum(shares):
+    return pl.pallas_call(
+        sum_kernel,
+        out_shape=jax.ShapeDtypeStruct(shares.shape[1:], BF16),
         compiler_params=params(4),
         cost_estimate=SMALL,
-        name="line_load",
-    )(shares, *in_hbm(gram))
-
-
-def line_kernel(terms, *refs):
+        name="replica_sum",
+    )(shares)
+
+
+def line_kernel(*refs):
     load_refs, out_ref, parts_ref = refs[:-2], refs[-2], refs[-1]
     n_exp = len(load_refs)
     for k in range(n_exp):
-        parts_ref[k] = load_refs[k][terms:].astype(F32)
+        parts_ref[k] = load_refs[k][...].astype(F32)
     place = lax.axis_index("exp")
     total = None
     for j in range(n_exp):
@@ -189,12 +199,11 @@
         out_ref[i] = total
 
 
-def line_sum(loads, terms, n_rep):
-    rows = loads[0].shape[0] - terms
-    return pl.pallas_call(
-        functools.partial(line_kernel, terms),
-        out_shape=jax.ShapeDtypeStruct((n_rep, rows, TILE_C), BF16),
-        scratch_shapes=[pltpu.VMEM((len(loads), rows, TILE_C), F32)],
+def line_sum(loads, n_rep):
+    return pl.pallas_call(
+        line_kernel,
+        out_shape=jax.ShapeDtypeStruct((n_rep,) + loads[0].shape, BF16),
+        scratch_shapes=[pltpu.VMEM((len(loads),) + loads[0].shape, F32)],
         compiler_params=params(4),
         cost_estimate=SMALL,
         name="line_sum",
@@ -253,7 +262,7 @@
     n_exp = len(loads)
     return pl.pallas_call(
         functools.partial(inverse_kernel, n_exp),
-        in_specs=[ANY] * n_exp + [HBM],
+        in_specs=[HBM] + [ANY] * (n_exp - 1) + [HBM],
         out_shape=[pltpu.HBM((rank, rank), F32), pltpu.HBM((rows, rank), BF16)],
         scratch_shapes=[
             pltpu.VMEM((n_exp, 3 * (rank // 2), 2 * rank), BF16),
@@ -264,7 +273,7 @@
         compiler_params=params(8),
         cost_estimate=pl.CostEstimate(flops=4_000_000_000, bytes_accessed=1000, transcendentals=0),
         name="inverse_factor",
-    )(*loads, *in_hbm(lt))
+    )(*in_hbm(loads[0]), *loads[1:], *in_hbm(lt))
 
 
 def finish_kernel(
@@ -330,9 +339,10 @@
     hid, rows, one, two, first, second, step, in_sems, out_sems = refs[n_exp + n_grad + 5 :]
     units, width = one.shape
     count = width // chunk
+    terms = load_hbms[0].shape[0] - units
 
     slabs = [
-        pltpu.make_async_copy(load_hbms[k], hid.at[k], in_sems.at[count, k])
+        pltpu.make_async_copy(load_hbms[k].at[terms : terms + units], hid.at[k], in_sems.at[count, k])
         for k in range(n_exp)
     ]
 
@@ -390,7 +400,7 @@
     tokens = slabs[0].shape[1]
     return pl.pallas_call(
         functools.partial(expert_kernel, n_exp, n_grad, chunk),
-        in_specs=[ANY] * n_exp + [HBM] + [ANY] * (n_grad - 1) + [HBM] * 2,
+        in_specs=[HBM] + [ANY] * (n_exp - 1) + [HBM] + [ANY] * (n_grad - 1) + [HBM] * 2,
         out_specs=[HBM] * 3,
         out_shape=[
             jax.ShapeDtypeStruct((1, units, width), F32),
@@ -412,7 +422,7 @@
         cost_estimate=SMALL,
         name="expert_step",
     )(
-        *slabs, *in_hbm(grads[0]), *grads[1:], *in_hbm(moment_one, moment_two)
+        *in_hbm(slabs[0]), *slabs[1:], *in_hbm(grads[0]), *grads[1:], *in_hbm(moment_one, moment_two)
     )
 
 
@@ -435,7 +445,6 @@
     merged, lt = merge(activations, kv_grad, errors, right_factor.T)
 
     lt = (lt + swap(lt, "rep", n_rep, 1)).astype(BF16)
-    slabs = unit_slabs(after(hidden, lt), n_exp)
     bit = 2
     parts = [lt]
     while bit < n_rep:
@@ -447,16 +456,16 @@
         bit *= len(parts)
     lt, gram, chunks = right_product(parts, merged)
 
-    slabs = [slabs[0]] + [shift(after(slabs[k], lt), n_exp, k) for k in range(1, n_exp)]
+    slabs = pack(hidden, gram, n_exp)
+    slabs = [slabs[0]] + [shift(slabs[k], n_exp, k) for k in range(1, n_exp)]
+
     rows = chunks.shape[0] * TILE_R // n_rep
-    shares = lax.all_to_all(chunks.reshape(n_rep, rows, TILE_C), "rep", 0, 0, tiled=True)
-    shares, grads = lax.optimization_barrier((shares, grads))
-
-    load = line_load(shares, gram)
+    load = replica_sum(lax.all_to_all(chunks.reshape(n_rep, rows, TILE_C), "rep", 0, 0, tiled=True))
     loads = [load] + [shift(load, n_exp, k) for k in range(1, n_exp)]
-    loads, slabs = lax.optimization_barrier((loads, slabs))
-    share = line_sum(loads, gram.shape[0], n_rep)
-    w, basis = inverse_factor(loads, lt)
+    w, basis = inverse_factor(slabs, lt)
+    loads, grads = lax.optimization_barrier((loads, grads))
+    share = line_sum(loads, n_rep)
+    share, w, basis = lax.optimization_barrier((share, w, basis))
     chunks = lax.all_to_all(share, "rep", 0, 0, tiled=True).reshape(chunks.shape)
 
     left, right = 1, n_exp - 1

time: 64.3 us -> 71.6 us (1.11)
  blocking collectives: 0 us -> 9.05 us
  local copies, waits for them, and re-layouts: 2.04 us -> 0 us
  waiting for transfers between devices: 18.1 us -> 19.4 us
  starting transfers between devices: 23.4 us -> 22.4 us
    all_to_all x0 -> x1, blocking collectives: none -> 9.05 us  [body(): lax.all_to_all(share, 'rep', 0, 0, tiled=True).reshape(chunks.shape)]
    ppermute x9, waiting for transfers between devices: 11.2 us -> 17.5 us  [shift(): return lax.ppermute(x, 'exp', [(i, (i + k) % size) for i in range(size)])]
    all_to_all x1 -> x0, starting transfers between devices: 3.73 us -> none  [body(): lax.all_to_all(share, 'rep', 0, 0, tiled=True).reshape(chunks.shape)]
    ppermute x4, waiting for transfers between devices: 4.36 us -> 1.88 us  [swap(): return lax.ppermute(x, axis, [(i, i ^ mask) for i in range(size)])]
    unnamed x10 -> x0, local copies, waits for them, and re-layouts: 2.04 us -> none
    all_to_all x1, waiting for transfers between devices: 1.87 us -> 0.01 us  [body(): lax.all_to_all(chunks.reshape(n_rep, rows, TILE_C), 'rep', 0, 0, tiled=True)]
    ppermute x9, starting transfers between devices: 12.2 us -> 14 us  [shift(): return lax.ppermute(x, 'exp', [(i, (i + k) % size) for i in range(size)])]
    ppermute x4, starting transfers between devices: 4.07 us -> 5.04 us  [swap(): return lax.ppermute(x, axis, [(i, i ^ mask) for i in range(size)])]
  transfers between devices with their start and end apart: 15 -> 14, of which waited for: 9 -> 6; matrix products, arithmetic and copies ran while one was open for 0% -> 0% of each run, Pallas kernels for 14% -> 14%
where the time goes in v12:
time: 71.6 us; the launch traced here: 71.2 us
  starting transfers between devices  22.4 us (31%)
  Pallas kernels  19.5 us (27%)
  waiting for transfers between devices  19.4 us (27%)
  blocking collectives  9.05 us (13%)
  between operations  0.74 us (1%)
    ppermute x9, waiting for transfers between devices, shift(): return lax.ppermute(x, 'exp', [(i, (i + k) % size) for i in range(size)])  17.5 us
    ppermute x9, starting transfers between devices, shift(): return lax.ppermute(x, 'exp', [(i, (i + k) % size) for i in range(size)])  14 us
    all_to_all x1, blocking collectives, body(): lax.all_to_all(share, 'rep', 0, 0, tiled=True).reshape(chunks.shape)  9.05 us
    pallas_call x1, Pallas kernels, merge(): pl.pallas_call(merge_kernel, grid=(rows // block,), in_specs=[pl.BlockSpe...  5.22 us
    ppermute x4, starting transfers between devices, swap(): return lax.ppermute(x, axis, [(i, i ^ mask) for i in range(size)])  5.04 us
    pallas_call x1, Pallas kernels, inverse_factor(): pl.pallas_call(functools.partial(inverse_kernel, n_exp), in_specs=[HBM] +...  4.62 us
    pallas_call x1, Pallas kernels, expert_step(): pl.pallas_call(functools.partial(expert_kernel, n_exp, n_grad, chunk), in...  4.38 us
    all_to_all x1, starting transfers between devices, body(): lax.all_to_all(chunks.reshape(n_rep, rows, TILE_C), 'rep', 0, 0, tiled=True)  3.37 us
  transfers between devices with their start and end apart: 14, of which 6 were waited for; matrix products, arithmetic and copies ran while one was open for 0% of the time, Pallas kernels for 14%

profile of v12, /device:TPU:0, one launch (start us, length us, event | category | flops | bytes accessed | tf_op | source)
XLA Modules:
  0.0 71.2 jit_solution(14671943785438673985)
XLA Ops:
  0.6 5.2 %merge.1 = (bf16[768,1024]{1,0:T(8,128)(2,1)S(1)}, f32[64,768]{1,0:T(8,128)S(1)}) custom-call(bf16[1024,768]{1,0:T(8,128)(2,1)} %acts_ref.1, bf16[1024,1024]{1,0:T(8,128)(2,1)} %kv_ref.1, bf16[1,768,1024]{2,1,0:T(8,128)(2,1)} %err_ref.1, f32[64,1024]{1,0:T(8,128)} %bitcast.5), custom_call_target="tpu_custom_call" | custom-call | flops 4000000000 | bytes 8000000 | tf_op jit(solution)/shard_map/merge/pallas_call | solution.py:63
  5.9 0.5 collective-permute-start
  6.4 1.1 %collective-permute-done = f32[64,768]{1,0:T(8,128)S(1)} collective-permute-done((f32[64,768]{1,0:T(8,128)S(1)}, f32[64,768]{1,0:T(8,128)S(1)}, u32[]{:S(2)}, u32[]{:S(2)}) %collective-permute-start) | collective-permute-done | bytes 196640 | tf_op jit(solution)/shard_map/ppermute | solution.py:430
  7.5 3.9 %collective-permute-start.3 = (bf16[64,768]{1,0:T(8,128)(2,1)S(1)}, bf16[64,768]{1,0:T(8,128)(2,1)S(1)}, u32[]{:S(2)}, u32[]{:S(2)}) collective-permute-start(bf16[64,768]{1,0:T(8,128)(2,1)S(1)} %add_convert_fusion.refs_0_), channel_id=1, source_target_pairs={{0,24},{4,28},{8,16},{12,20},{16,8},{20,12},{24,0},{28,4},{1,25},{... | collective-permute-start | bytes 294920 | tf_op jit(solution)/shard_map/ppermute | solution.py:430
  11.3 0.5 collective-permute-start.2
  12.0 2.0 %collective-permute-start.7 = (bf16[1,128,2048]{2,1,0:T(8,128)(2,1)}, bf16[1,128,2048]{2,1,0:T(8,128)(2,1)S(1)}, u32[]{:S(2)}, u32[]{:S(2)}) collective-permute-start(bf16[1,128,2048]{2,1,0:T(8,128)(2,1)} %refs_4_), channel_id=1, source_target_pairs={{0,1},{1,2},{2,3},{3,0},{4,5},{5,6},{6,7},{7,4},{8,9},{9,10},{10,1... | collective-permute-start | bytes 1572872 | tf_op jit(solution)/shard_map/ppermute | solution.py:434
  14.0 2.0 %collective-permute-start.8 = (bf16[1,128,2048]{2,1,0:T(8,128)(2,1)}, bf16[1,128,2048]{2,1,0:T(8,128)(2,1)S(1)}, u32[]{:S(2)}, u32[]{:S(2)}) collective-permute-start(bf16[1,128,2048]{2,1,0:T(8,128)(2,1)} %refs_4_), channel_id=1, source_target_pairs={{0,3},{1,0},{2,1},{3,2},{4,7},{5,4},{6,5},{7,6},{8,11},{9,8},{10,9... | collective-permute-start | bytes 1572872 | tf_op jit(solution)/shard_map/ppermute | solution.py:434
  16.0 0.6 collective-permute-done.2.refs_2_
  16.8 1.2 %right_product.1 = (bf16[64,768]{1,0:T(8,128)(2,1)}, bf16[96,128]{1,0:T(8,128)(2,1)}, bf16[32,16,128]{2,1,0:T(8,128)(2,1)}) custom-call(bf16[64,768]{1,0:T(8,128)(2,1)S(1)} %add_convert_fusion.refs_0_, bf16[64,768]{1,0:T(8,128)(2,1)S(1)} %collective-permute-done.1.refs_1_, bf16[64,768]{1,0:T(8,128)(2,1)S(1)} %collective-permute-done.2.refs_2_, ...), custom_call_target="tpu_custom_call" | custom-call | flops 1000 | bytes 1000 | tf_op jit(solution)/shard_map/right_product/pallas_call | solution.py:157
  18.0 3.4 %all-to-all-start = ((bf16[8,64,128]{2,1,0:T(8,128)(2,1)}), bf16[8,64,128]{2,1,0:T(8,128)(2,1)S(1)}, u32[]{:S(2)}, u32[]{:S(2)}) async-start(bf16[8,64,128]{2,1,0:T(8,128)(2,1)} %bitcast.1), calls=%async_computation | async-start | bytes 262144 | tf_op jit(solution)/shard_map/all_to_all | solution.py:463
  21.4 1.7 %pack.1 = (bf16[288,128]{1,0:T(8,128)(2,1)}, bf16[288,128]{1,0:T(8,128)(2,1)S(1)}, bf16[288,128]{1,0:T(8,128)(2,1)S(1)}, bf16[288,128]{1,0:T(8,128)(2,1)S(1)}) custom-call(bf16[1,128,768]{2,1,0:T(8,128)(2,1)} %hidden_hbm.1, bf16[96,128]{1,0:T(8,128)(2,1)} %get-tuple-element.39.gram_hbm), custom_call_target="tpu_custom_call" | custom-call | flops 1000 | bytes 1000 | tf_op jit(solution)/shard_map/pack/pallas_call | solution.py:109
  23.1 1.6 %collective-permute-start.9 = (bf16[288,128]{1,0:T(8,128)(2,1)S(1)}, bf16[288,128]{1,0:T(8,128)(2,1)S(1)}, u32[]{:S(2)}, u32[]{:S(2)}) collective-permute-start(bf16[288,128]{1,0:T(8,128)(2,1)S(1)} %get-tuple-element.41), channel_id=1, source_target_pairs={{0,1},{1,2},{2,3},{3,0},{4,5},{5,6},{6,7},{7,4},{8,9},{9,10},{10,1... | collective-permute-start | bytes 221192 | tf_op jit(solution)/shard_map/ppermute | solution.py:434
  24.7 2.6 %collective-permute-start.10 = (bf16[288,128]{1,0:T(8,128)(2,1)S(1)}, bf16[288,128]{1,0:T(8,128)(2,1)S(1)}, u32[]{:S(2)}, u32[]{:S(2)}) collective-permute-start(bf16[288,128]{1,0:T(8,128)(2,1)S(1)} %get-tuple-element.42), channel_id=1, source_target_pairs={{0,2},{1,3},{2,0},{3,1},{4,6},{5,7},{6,4},{7,5},{8,10},{9,11},{10,... | collective-permute-start | bytes 221192 | tf_op jit(solution)/shard_map/ppermute | solution.py:434
  27.3 1.4 %collective-permute-start.11 = (bf16[288,128]{1,0:T(8,128)(2,1)S(1)}, bf16[288,128]{1,0:T(8,128)(2,1)S(1)}, u32[]{:S(2)}, u32[]{:S(2)}) collective-permute-start(bf16[288,128]{1,0:T(8,128)(2,1)S(1)} %get-tuple-element.43), channel_id=1, source_target_pairs={{0,3},{1,0},{2,1},{3,2},{4,7},{5,4},{6,5},{7,6},{8,11},{9,8},{10,9... | collective-permute-start | bytes 221192 | tf_op jit(solution)/shard_map/ppermute | solution.py:434
  28.7 13.2 %collective-permute-done.9.refs_1_ = bf16[288,128]{1,0:T(8,128)(2,1)S(1)} collective-permute-done((bf16[288,128]{1,0:T(8,128)(2,1)S(1)}, bf16[288,128]{1,0:T(8,128)(2,1)S(1)}, u32[]{:S(2)}, u32[]{:S(2)}) %collective-permute-start.9) | collective-permute-done | bytes 73760 | tf_op jit(solution)/shard_map/ppermute | solution.py:434
  41.9 0.5 collective-permute-start.6
  42.5 1.2 %collective-permute-done.10.refs_2_ = bf16[288,128]{1,0:T(8,128)(2,1)S(1)} collective-permute-done((bf16[288,128]{1,0:T(8,128)(2,1)S(1)}, bf16[288,128]{1,0:T(8,128)(2,1)S(1)}, u32[]{:S(2)}, u32[]{:S(2)}) %collective-permute-start.10) | collective-permute-done | bytes 73760 | tf_op jit(solution)/shard_map/ppermute | solution.py:434
  43.7 1.5 %collective-permute-start.5 = (bf16[64,128]{1,0:T(8,128)(2,1)S(1)}, bf16[64,128]{1,0:T(8,128)(2,1)S(1)}, u32[]{:S(2)}, u32[]{:S(2)}) collective-permute-start(bf16[64,128]{1,0:T(8,128)(2,1)S(1)} %replica_sum.1.refs_0_), channel_id=1, source_target_pairs={{0,2},{1,3},{2,0},{3,1},{4,6},{5,7},{6,4},{7,5},{8,10},{9,11},{10,... | collective-permute-start | bytes 49160 | tf_op jit(solution)/shard_map/ppermute | solution.py:434
  45.1 2.4 %collective-permute-start.4 = (bf16[64,128]{1,0:T(8,128)(2,1)S(1)}, bf16[64,128]{1,0:T(8,128)(2,1)S(1)}, u32[]{:S(2)}, u32[]{:S(2)}) collective-permute-start(bf16[64,128]{1,0:T(8,128)(2,1)S(1)} %replica_sum.1.refs_0_), channel_id=1, source_target_pairs={{0,1},{1,2},{2,3},{3,0},{4,5},{5,6},{6,7},{7,4},{8,9},{9,10},{10,1... | collective-permute-start | bytes 49160 | tf_op jit(solution)/shard_map/ppermute | solution.py:434
  47.5 4.6 %inverse_factor.1 = (f32[64,64]{1,0:T(8,128)}, bf16[768,64]{1,0:T(8,128)(2,1)}) custom-call(bf16[288,128]{1,0:T(8,128)(2,1)} %get-tuple-element.40.refs_0_, bf16[288,128]{1,0:T(8,128)(2,1)S(1)} %collective-permute-done.9.refs_1_, bf16[288,128]{1,0:T(8,128)(2,1)S(1)} %collective-permute-done.10.refs_2_, bf16[288,128]{1,0:T(8,128)(2,1)S(1)} %collective-permute-done.11.refs_3_, ...), custom_call_target="tpu_custom_call" | custom-call | flops 4000000000 | bytes 1000 | tf_op jit(solution)/shard_map/inverse_factor/pallas_call | solution.py:263
  52.3 9.1 %all_to_all.10 = bf16[8,64,128]{2,1,0:T(8,128)(2,1)S(1)} all-to-all(bf16[8,64,128]{2,1,0:T(8,128)(2,1)S(1)} %line_sum.1), channel_id=1, replica_groups=mesh['rep'=8,'exp'=4] {'rep'}, dimensions={0} | all-to-all | bytes 262144 | tf_op jit(solution)/shard_map/all_to_all | solution.py:469
  61.4 2.4 %finish.1 = (f32[64,1024]{1,0:T(8,128)}, bf16[1,768,1024]{2,1,0:T(8,128)(2,1)}) custom-call(f32[64,64]{1,0:T(8,128)} %get-tuple-element.47.w_any, bf16[32,16,128]{2,1,0:T(8,128)(2,1)S(1)} %bitcast.4, bf16[768,64]{1,0:T(8,128)(2,1)} %get-tuple-element.49.basis_any, bf16[768,1024]{1,0:T(8,128)(2,1)S(1)} %get-tuple-element.33.refs_4_.merged_ref), custom_call_target="tpu_custom_call" | custom-call | flops 1000 | bytes 1000 | tf_op jit(solution)/shard_map/finish/pallas_call | solution.py:315
  63.7 3.1 %collective-permute-done.12.refs_6_ = bf16[1,128,2048]{2,1,0:T(8,128)(2,1)S(1)} collective-permute-done((bf16[1,128,2048]{2,1,0:T(8,128)(2,1)S(1)}, bf16[1,128,2048]{2,1,0:T(8,128)(2,1)S(1)}, u32[]{:S(2)}, u32[]{:S(2)}) %collective-permute-start.12) | collective-permute-done | bytes 524320 | tf_op jit(solution)/shard_map/ppermute | solution.py:434
  66.8 4.4 %expert_step.1 = (f32[1,192,2048]{2,1,0:T(8,128)}, f32[1,192,2048]{2,1,0:T(8,128)}, bf16[1,192,2048]{2,1,0:T(8,128)(2,1)}) custom-call(bf16[288,128]{1,0:T(8,128)(2,1)} %get-tuple-element.40.refs_0_, bf16[288,128]{1,0:T(8,128)(2,1)S(1)} %collective-permute-done.9.refs_1_, bf16[288,128]{1,0:T(8,128)(2,1)S(1)} %collective-permute-done.10.refs_2_, ...), custom_call_target="tpu_custom_call" | custom-call | flops 1000 | bytes 1000 | tf_op jit(solution)/shard_map/expert_step/pallas_call | solution.py:401
  (14 shorter events, 0.5 us)
Async XLA Ops:
  5.9 1.6 %collective-permute-start = (f32[64,768]{1,0:T(8,128)S(1)}, f32[64,768]{1,0:T(8,128)S(1)}, u32[]{:S(2)}, u32[]{:S(2)}) collective-permute-start(f32[64,768]{1,0:T(8,128)S(1)} %get-tuple-element.32), channel_id=1, source_target_pairs={{0,4},{4,0},{8,12},{12,8},{16,20},{20,16},{24,28},{28,24},{1,5},{5... | collective-permute-start | bytes 589832 | tf_op jit(solution)/shard_map/ppermute | solution.py:430
  7.5 8.5 %collective-permute-start.3 = (bf16[64,768]{1,0:T(8,128)(2,1)S(1)}, bf16[64,768]{1,0:T(8,128)(2,1)S(1)}, u32[]{:S(2)}, u32[]{:S(2)}) collective-permute-start(bf16[64,768]{1,0:T(8,128)(2,1)S(1)} %add_convert_fusion.refs_0_), channel_id=1, source_target_pairs={{0,24},{4,28},{8,16},{12,20},{16,8},{20,12},{24,0},{28,4},{1,25},{... | collective-permute-start | bytes 294920 | tf_op jit(solution)/shard_map/ppermute | solution.py:430
  11.3 5.2 %collective-permute-start.2 = (bf16[64,768]{1,0:T(8,128)(2,1)S(1)}, bf16[64,768]{1,0:T(8,128)(2,1)S(1)}, u32[]{:S(2)}, u32[]{:S(2)}) collective-permute-start(bf16[64,768]{1,0:T(8,128)(2,1)S(1)} %add_convert_fusion.refs_0_), channel_id=1, source_target_pairs={{0,16},{4,20},{8,24},{12,28},{16,0},{20,4},{24,8},{28,12},{1,17},{... | collective-permute-start | bytes 294920 | tf_op jit(solution)/shard_map/ppermute | solution.py:430
  11.9 4.9 %collective-permute-start.1 = (bf16[64,768]{1,0:T(8,128)(2,1)S(1)}, bf16[64,768]{1,0:T(8,128)(2,1)S(1)}, u32[]{:S(2)}, u32[]{:S(2)}) collective-permute-start(bf16[64,768]{1,0:T(8,128)(2,1)S(1)} %add_convert_fusion.refs_0_), channel_id=1, source_target_pairs={{0,8},{4,12},{8,0},{12,4},{16,24},{20,28},{24,16},{28,20},{1,9},{5... | collective-permute-start | bytes 294920 | tf_op jit(solution)/shard_map/ppermute | solution.py:430
  12.0 40.2 %collective-permute-start.7 = (bf16[1,128,2048]{2,1,0:T(8,128)(2,1)}, bf16[1,128,2048]{2,1,0:T(8,128)(2,1)S(1)}, u32[]{:S(2)}, u32[]{:S(2)}) collective-permute-start(bf16[1,128,2048]{2,1,0:T(8,128)(2,1)} %refs_4_), channel_id=1, source_target_pairs={{0,1},{1,2},{2,3},{3,0},{4,5},{5,6},{6,7},{7,4},{8,9},{9,10},{10,1... | collective-permute-start | bytes 1572872 | tf_op jit(solution)/shard_map/ppermute | solution.py:434
  14.0 38.2 %collective-permute-start.8 = (bf16[1,128,2048]{2,1,0:T(8,128)(2,1)}, bf16[1,128,2048]{2,1,0:T(8,128)(2,1)S(1)}, u32[]{:S(2)}, u32[]{:S(2)}) collective-permute-start(bf16[1,128,2048]{2,1,0:T(8,128)(2,1)} %refs_4_), channel_id=1, source_target_pairs={{0,3},{1,0},{2,1},{3,2},{4,7},{5,4},{6,5},{7,6},{8,11},{9,8},{10,9... | collective-permute-start | bytes 1572872 | tf_op jit(solution)/shard_map/ppermute | solution.py:434
  18.0 10.7 %all-to-all-start = ((bf16[8,64,128]{2,1,0:T(8,128)(2,1)}), bf16[8,64,128]{2,1,0:T(8,128)(2,1)S(1)}, u32[]{:S(2)}, u32[]{:S(2)}) async-start(bf16[8,64,128]{2,1,0:T(8,128)(2,1)} %bitcast.1), calls=%async_computation | async-start | bytes 262144 | tf_op jit(solution)/shard_map/all_to_all | solution.py:463
  23.1 18.8 %collective-permute-start.9 = (bf16[288,128]{1,0:T(8,128)(2,1)S(1)}, bf16[288,128]{1,0:T(8,128)(2,1)S(1)}, u32[]{:S(2)}, u32[]{:S(2)}) collective-permute-start(bf16[288,128]{1,0:T(8,128)(2,1)S(1)} %get-tuple-element.41), channel_id=1, source_target_pairs={{0,1},{1,2},{2,3},{3,0},{4,5},{5,6},{6,7},{7,4},{8,9},{9,10},{10,1... | collective-permute-start | bytes 221192 | tf_op jit(solution)/shard_map/ppermute | solution.py:434
  24.7 18.9 %collective-permute-start.10 = (bf16[288,128]{1,0:T(8,128)(2,1)S(1)}, bf16[288,128]{1,0:T(8,128)(2,1)S(1)}, u32[]{:S(2)}, u32[]{:S(2)}) collective-permute-start(bf16[288,128]{1,0:T(8,128)(2,1)S(1)} %get-tuple-element.42), channel_id=1, source_target_pairs={{0,2},{1,3},{2,0},{3,1},{4,6},{5,7},{6,4},{7,5},{8,10},{9,11},{10,... | collective-permute-start | bytes 221192 | tf_op jit(solution)/shard_map/ppermute | solution.py:434
  27.3 17.8 %collective-permute-start.11 = (bf16[288,128]{1,0:T(8,128)(2,1)S(1)}, bf16[288,128]{1,0:T(8,128)(2,1)S(1)}, u32[]{:S(2)}, u32[]{:S(2)}) collective-permute-start(bf16[288,128]{1,0:T(8,128)(2,1)S(1)} %get-tuple-element.43), channel_id=1, source_target_pairs={{0,3},{1,0},{2,1},{3,2},{4,7},{5,4},{6,5},{7,6},{8,11},{9,8},{10,9... | collective-permute-start | bytes 221192 | tf_op jit(solution)/shard_map/ppermute | solution.py:434
  41.9 10.2 %collective-permute-start.6 = (bf16[64,128]{1,0:T(8,128)(2,1)S(1)}, bf16[64,128]{1,0:T(8,128)(2,1)S(1)}, u32[]{:S(2)}, u32[]{:S(2)}) collective-permute-start(bf16[64,128]{1,0:T(8,128)(2,1)S(1)} %replica_sum.1.refs_0_), channel_id=1, source_target_pairs={{0,3},{1,0},{2,1},{3,2},{4,7},{5,4},{6,5},{7,6},{8,11},{9,8},{10,9... | collective-permute-start | bytes 49160 | tf_op jit(solution)/shard_map/ppermute | solution.py:434
  43.7 8.5 %collective-permute-start.5 = (bf16[64,128]{1,0:T(8,128)(2,1)S(1)}, bf16[64,128]{1,0:T(8,128)(2,1)S(1)}, u32[]{:S(2)}, u32[]{:S(2)}) collective-permute-start(bf16[64,128]{1,0:T(8,128)(2,1)S(1)} %replica_sum.1.refs_0_), channel_id=1, source_target_pairs={{0,2},{1,3},{2,0},{3,1},{4,6},{5,7},{6,4},{7,5},{8,10},{9,11},{10,... | collective-permute-start | bytes 49160 | tf_op jit(solution)/shard_map/ppermute | solution.py:434
  45.1 7.1 %collective-permute-start.4 = (bf16[64,128]{1,0:T(8,128)(2,1)S(1)}, bf16[64,128]{1,0:T(8,128)(2,1)S(1)}, u32[]{:S(2)}, u32[]{:S(2)}) collective-permute-start(bf16[64,128]{1,0:T(8,128)(2,1)S(1)} %replica_sum.1.refs_0_), channel_id=1, source_target_pairs={{0,1},{1,2},{2,3},{3,0},{4,5},{5,6},{6,7},{7,4},{8,9},{9,10},{10,1... | collective-permute-start | bytes 49160 | tf_op jit(solution)/shard_map/ppermute | solution.py:434
  52.2 14.6 %collective-permute-start.12 = (bf16[1,128,2048]{2,1,0:T(8,128)(2,1)S(1)}, bf16[1,128,2048]{2,1,0:T(8,128)(2,1)S(1)}, u32[]{:S(2)}, u32[]{:S(2)}) collective-permute-start(bf16[1,128,2048]{2,1,0:T(8,128)(2,1)S(1)} %collective-permute-done.7.refs_5_), channel_id=1, source_target_pairs={{0,1},{1,2},{2,3},{3,0},{4,5},{5,6},{6,7},{7,4},{8,9},{9,10},{10,1... | collective-permute-start | bytes 1572872 | tf_op jit(solution)/shard_map/ppermute | solution.py:434

commit v13 on v11

--- a/solution.py
+++ b/solution.py
@@ -140,7 +140,7 @@
     return pl.pallas_call(
         functools.partial(right_kernel, len(parts)),
         out_shape=[
-            jax.ShapeDtypeStruct((rank, rows), BF16),
+            pltpu.HBM((rank, rows), BF16),
             pltpu.HBM((3 * (rank // 2), 2 * rank), BF16),
             jax.ShapeDtypeStruct((chunks, TILE_R, TILE_C), BF16),
         ],
@@ -175,26 +175,37 @@
 
 
 def line_kernel(terms, *refs):
-    load_refs, out_ref, parts_ref = refs[:-2], refs[-2], refs[-1]
+    load_refs, (out_ref, gram_ref, parts_ref) = refs[:-3], refs[-3:]
     n_exp = len(load_refs)
     for k in range(n_exp):
-        parts_ref[k] = load_refs[k][terms:].astype(F32)
+        parts_ref[k] = load_refs[k][...].astype(F32)
     place = lax.axis_index("exp")
-    total = None
+    half = terms // 3
+    total = packed = None
     for j in range(n_exp):
-        part = parts_ref[lax.rem(place + n_exp - j, n_exp)]
+        which = lax.rem(place + n_exp - j, n_exp)
+        part = parts_ref[which, terms:]
         total = part if total is None else total + part
+        gram = parts_ref[which, 0:half] + parts_ref[which, half : 2 * half]
+        gram = gram + parts_ref[which, 2 * half : terms]
+        packed = gram if packed is None else packed + gram
     total = total.astype(BF16)
     for i in range(out_ref.shape[0]):
         out_ref[i] = total
+    gram_ref[0:half] = packed[:, : gram_ref.shape[1]]
+    gram_ref[half:] = packed[:, gram_ref.shape[1] :]
 
 
 def line_sum(loads, terms, n_rep):
     rows = loads[0].shape[0] - terms
+    rank = 2 * (terms // 3)
     return pl.pallas_call(
         functools.partial(line_kernel, terms),
-        out_shape=jax.ShapeDtypeStruct((n_rep, rows, TILE_C), BF16),
-        scratch_shapes=[pltpu.VMEM((len(loads), rows, TILE_C), F32)],
+        out_shape=[
+            jax.ShapeDtypeStruct((n_rep, rows, TILE_C), BF16),
+            pltpu.HBM((rank, rank), F32),
+        ],
+        scratch_shapes=[pltpu.VMEM((len(loads),) + loads[0].shape, F32)],
         compiler_params=params(4),
         cost_estimate=SMALL,
         name="line_sum",
@@ -221,50 +232,34 @@
     return wide_ref[:, rank:]
 
 
-def inverse_kernel(n_exp, *refs):
-    load_hbms, lt_hbm = refs[:n_exp], refs[n_exp]
-    w_ref, basis_ref, terms_ref, lt_ref, wide_ref, sems = refs[n_exp + 1 :]
-    rank = lt_ref.shape[0]
-    half = rank // 2
-    copies = [
-        pltpu.make_async_copy(load_hbms[k].at[0 : 3 * half], terms_ref.at[k], sems.at[k])
-        for k in range(n_exp)
-    ]
-    lt_copy = pltpu.make_async_copy(lt_hbm, lt_ref, sems.at[n_exp])
-    for copy in copies:
-        copy.start()
+def inverse_kernel(gram_any, lt_any, w_ref, basis_ref, gram_ref, lt_ref, wide_ref, sems):
+    gram_copy = pltpu.make_async_copy(gram_any, gram_ref, sems.at[0])
+    gram_copy.start()
+    lt_copy = pltpu.make_async_copy(lt_any, lt_ref, sems.at[1])
     lt_copy.start()
-    for copy in copies:
-        copy.wait()
-    place = lax.axis_index("exp")
-    packed = None
-    for j in range(n_exp):
-        terms = terms_ref[lax.rem(place + n_exp - j, n_exp)].astype(F32)
-        part = terms[:half] + terms[half : 2 * half] + terms[2 * half :]
-        packed = part if packed is None else packed + part
-    w = inverse_of_factor(jnp.concatenate([packed[:, :rank], packed[:, rank:]], axis=0), wide_ref)
+    gram_copy.wait()
+    w = inverse_of_factor(gram_ref[...], wide_ref)
     w_ref[...] = w
     lt_copy.wait()
     basis_ref[...] = left_times(w, lt_ref[...], (((1,), (0,)), ((), ()))).T.astype(BF16)
 
 
-def inverse_factor(loads, lt):
+def inverse_factor(gram, lt):
     rank, rows = lt.shape
-    n_exp = len(loads)
-    return pl.pallas_call(
-        functools.partial(inverse_kernel, n_exp),
-        in_specs=[ANY] * n_exp + [HBM],
+    return pl.pallas_call(
+        inverse_kernel,
+        in_specs=[ANY] * 2,
         out_shape=[pltpu.HBM((rank, rank), F32), pltpu.HBM((rows, rank), BF16)],
         scratch_shapes=[
-            pltpu.VMEM((n_exp, 3 * (rank // 2), 2 * rank), BF16),
+            pltpu.VMEM((rank, rank), F32),
             pltpu.VMEM((rank, rows), BF16),
             pltpu.VMEM((rank, 2 * rank), F32),
-            pltpu.SemaphoreType.DMA((n_exp + 1,)),
+            pltpu.SemaphoreType.DMA((2,)),
         ],
         compiler_params=params(8),
         cost_estimate=pl.CostEstimate(flops=4_000_000_000, bytes_accessed=1000, transcendentals=0),
         name="inverse_factor",
-    )(*loads, *in_hbm(lt))
+    )(*in_hbm(gram, lt))
 
 
 def finish_kernel(
@@ -450,13 +445,12 @@
     slabs = [slabs[0]] + [shift(after(slabs[k], lt), n_exp, k) for k in range(1, n_exp)]
     rows = chunks.shape[0] * TILE_R // n_rep
     shares = lax.all_to_all(chunks.reshape(n_rep, rows, TILE_C), "rep", 0, 0, tiled=True)
-    shares, grads = lax.optimization_barrier((shares, grads))
 
     load = line_load(shares, gram)
     loads = [load] + [shift(load, n_exp, k) for k in range(1, n_exp)]
-    loads, slabs = lax.optimization_barrier((loads, slabs))
-    share = line_sum(loads, gram.shape[0], n_rep)
-    w, basis = inverse_factor(loads, lt)
+    loads, slabs, grads = lax.optimization_barrier((loads, slabs, grads))
+    share, gram = line_sum(loads, gram.shape[0], n_rep)
+    w, basis = inverse_factor(gram, lt)
     chunks = lax.all_to_all(share, "rep", 0, 0, tiled=True).reshape(chunks.shape)
 
     left, right = 1, n_exp - 1

time: 64.3 us -> 65.2 us (1.014)
  waiting for transfers between devices: 18.1 us -> 21.5 us
  local copies, waits for them, and re-layouts: 2.04 us -> 0.01 us
  starting transfers between devices: 23.4 us -> 22.4 us
  Pallas kernels: 19.4 us -> 20.1 us
    ppermute x9, waiting for transfers between devices: 11.2 us -> 14.4 us  [shift(): return lax.ppermute(x, 'exp', [(i, (i + k) % size) for i in range(size)])]
    unnamed x10 -> x4, local copies, waits for them, and re-layouts: 2.04 us -> 0.01 us
    ppermute x9, starting transfers between devices: 12.2 us -> 11.2 us  [shift(): return lax.ppermute(x, 'exp', [(i, (i + k) % size) for i in range(size)])]
    pallas_call x3, Pallas kernels: 5.87 us -> 6.53 us  [the longest x1 4.6 us: inverse_factor(): pl.pallas_call(inverse_kernel, in_specs=[ANY] * 2, out_shape=[pltpu.HBM((...]
  transfers between devices with their start and end apart: 15 -> 15, of which waited for: 9 -> 10; matrix products, arithmetic and copies ran while one was open for 0% -> 0% of each run, Pallas kernels for 14% -> 15%
where the time goes in v13:
time: 65.2 us; the launch traced here: 64.8 us
  starting transfers between devices  22.4 us (34%)
  waiting for transfers between devices  21.5 us (33%)
  Pallas kernels  20.1 us (31%)
  between operations  0.72 us (1%)
    ppermute x9, waiting for transfers between devices, shift(): return lax.ppermute(x, 'exp', [(i, (i + k) % size) for i in range(size)])  14.4 us
    ppermute x9, starting transfers between devices, shift(): return lax.ppermute(x, 'exp', [(i, (i + k) % size) for i in range(size)])  11.2 us
    pallas_call x1, Pallas kernels, merge(): pl.pallas_call(merge_kernel, grid=(rows // block,), in_specs=[pl.BlockSpe...  5.22 us
    pallas_call x1, Pallas kernels, inverse_factor(): pl.pallas_call(inverse_kernel, in_specs=[ANY] * 2, out_shape=[pltpu.HBM((...  4.6 us
    pallas_call x1, Pallas kernels, expert_step(): pl.pallas_call(functools.partial(expert_kernel, n_exp, n_grad, chunk), in...  4.44 us
    ppermute x4, waiting for transfers between devices, swap(): return lax.ppermute(x, axis, [(i, i ^ mask) for i in range(size)])  4.36 us
    ppermute x4, starting transfers between devices, swap(): return lax.ppermute(x, axis, [(i, i ^ mask) for i in range(size)])  4.07 us
    all_to_all x1, starting transfers between devices, body(): lax.all_to_all(share, 'rep', 0, 0, tiled=True).reshape(chunks.shape)  3.73 us
  transfers between devices with their start and end apart: 15, of which 10 were waited for; matrix products, arithmetic and copies ran while one was open for 0% of the time, Pallas kernels for 15%

profile of v13, /device:TPU:0, one launch (start us, length us, event | category | flops | bytes accessed | tf_op | source)
XLA Modules:
  0.0 64.8 jit_solution(14330392526168091102)
XLA Ops:
  0.6 5.2 %merge.1 = (bf16[768,1024]{1,0:T(8,128)(2,1)S(1)}, f32[64,768]{1,0:T(8,128)S(1)}) custom-call(bf16[1024,768]{1,0:T(8,128)(2,1)} %acts_ref.1, bf16[1024,1024]{1,0:T(8,128)(2,1)} %kv_ref.1, bf16[1,768,1024]{2,1,0:T(8,128)(2,1)} %err_ref.1, f32[64,1024]{1,0:T(8,128)} %bitcast.5), custom_call_target="tpu_custom_call" | custom-call | flops 4000000000 | bytes 8000000 | tf_op jit(solution)/shard_map/merge/pallas_call | solution.py:63
  6.4 2.6 %collective-permute-start.10 = (bf16[1,128,2048]{2,1,0:T(8,128)(2,1)}, bf16[1,128,2048]{2,1,0:T(8,128)(2,1)S(1)}, u32[]{:S(2)}, u32[]{:S(2)}) collective-permute-start(bf16[1,128,2048]{2,1,0:T(8,128)(2,1)} %refs_4_), channel_id=1, source_target_pairs={{0,1},{1,2},{2,3},{3,0},{4,5},{5,6},{6,7},{7,4},{8,9},{9,10},{10,1... | collective-permute-start | bytes 1572872 | tf_op jit(solution)/shard_map/ppermute | solution.py:419
  9.0 2.1 %collective-permute-start.11 = (bf16[1,128,2048]{2,1,0:T(8,128)(2,1)}, bf16[1,128,2048]{2,1,0:T(8,128)(2,1)S(1)}, u32[]{:S(2)}, u32[]{:S(2)}) collective-permute-start(bf16[1,128,2048]{2,1,0:T(8,128)(2,1)} %refs_4_), channel_id=1, source_target_pairs={{0,3},{1,0},{2,1},{3,2},{4,7},{5,4},{6,5},{7,6},{8,11},{9,8},{10,9... | collective-permute-start | bytes 1572872 | tf_op jit(solution)/shard_map/ppermute | solution.py:419
  11.2 2.6 %collective-permute-start.3 = (bf16[64,768]{1,0:T(8,128)(2,1)S(1)}, bf16[64,768]{1,0:T(8,128)(2,1)S(1)}, u32[]{:S(2)}, u32[]{:S(2)}) collective-permute-start(bf16[64,768]{1,0:T(8,128)(2,1)S(1)} %add_convert_fusion.refs_0_), channel_id=1, source_target_pairs={{0,24},{4,28},{8,16},{12,20},{16,8},{20,12},{24,0},{28,4},{1,25},{... | collective-permute-start | bytes 294920 | tf_op jit(solution)/shard_map/ppermute | solution.py:415
  14.7 2.3 %collective-permute-done.3.refs_3_ = bf16[64,768]{1,0:T(8,128)(2,1)S(1)} collective-permute-done((bf16[64,768]{1,0:T(8,128)(2,1)S(1)}, bf16[64,768]{1,0:T(8,128)(2,1)S(1)}, u32[]{:S(2)}, u32[]{:S(2)}) %collective-permute-start.3) | collective-permute-done | bytes 98336 | tf_op jit(solution)/shard_map/ppermute | solution.py:415
  17.0 2.0 %collective-permute-done.2.refs_2_ = bf16[64,768]{1,0:T(8,128)(2,1)S(1)} collective-permute-done((bf16[64,768]{1,0:T(8,128)(2,1)S(1)}, bf16[64,768]{1,0:T(8,128)(2,1)S(1)}, u32[]{:S(2)}, u32[]{:S(2)}) %collective-permute-start.2) | collective-permute-done | bytes 98336 | tf_op jit(solution)/shard_map/ppermute | solution.py:415
  19.1 1.2 %right_product.1 = (bf16[64,768]{1,0:T(8,128)(2,1)}, bf16[96,128]{1,0:T(8,128)(2,1)}, bf16[32,16,128]{2,1,0:T(8,128)(2,1)}) custom-call(bf16[64,768]{1,0:T(8,128)(2,1)S(1)} %add_convert_fusion.refs_0_, bf16[64,768]{1,0:T(8,128)(2,1)S(1)} %collective-permute-done.1.refs_1_, bf16[64,768]{1,0:T(8,128)(2,1)S(1)} %collective-permute-done.2.refs_2_, ...), custom_call_target="tpu_custom_call" | custom-call | flops 1000 | bytes 1000 | tf_op jit(solution)/shard_map/right_product/pallas_call | solution.py:140
  20.3 3.4 %all-to-all-start = ((bf16[8,64,128]{2,1,0:T(8,128)(2,1)}), bf16[8,64,128]{2,1,0:T(8,128)(2,1)S(1)}, u32[]{:S(2)}, u32[]{:S(2)}) async-start(bf16[8,64,128]{2,1,0:T(8,128)(2,1)} %bitcast.1), calls=%async_computation | async-start | bytes 262144 | tf_op jit(solution)/shard_map/all_to_all | solution.py:447
  23.7 0.8 %unit_slabs.1 = (bf16[192,128]{1,0:T(8,128)(2,1)}, bf16[192,128]{1,0:T(8,128)(2,1)}, bf16[192,128]{1,0:T(8,128)(2,1)}, bf16[192,128]{1,0:T(8,128)(2,1)}) custom-call(bf16[1,128,768]{2,1,0:T(8,128)(2,1)S(1)} %copy-done), custom_call_target="tpu_custom_call" | custom-call | flops 1000 | bytes 1000 | tf_op jit(solution)/shard_map/unit_slabs/pallas_call | solution.py:98
  24.5 1.8 %collective-permute-start.9 = (bf16[192,128]{1,0:T(8,128)(2,1)}, bf16[192,128]{1,0:T(8,128)(2,1)S(1)}, u32[]{:S(2)}, u32[]{:S(2)}) collective-permute-start(bf16[192,128]{1,0:T(8,128)(2,1)} %get-tuple-element.51), channel_id=1, source_target_pairs={{0,3},{1,0},{2,1},{3,2},{4,7},{5,4},{6,5},{7,6},{8,11},{9,8},{10,9... | collective-permute-start | bytes 147464 | tf_op jit(solution)/shard_map/ppermute | solution.py:419
  26.2 1.0 %collective-permute-start.7 = (bf16[192,128]{1,0:T(8,128)(2,1)}, bf16[192,128]{1,0:T(8,128)(2,1)S(1)}, u32[]{:S(2)}, u32[]{:S(2)}) collective-permute-start(bf16[192,128]{1,0:T(8,128)(2,1)} %get-tuple-element.47), channel_id=1, source_target_pairs={{0,1},{1,2},{2,3},{3,0},{4,5},{5,6},{6,7},{7,4},{8,9},{9,10},{10,1... | collective-permute-start | bytes 147464 | tf_op jit(solution)/shard_map/ppermute | solution.py:419
  27.3 1.9 %all-to-all-done.share_ref = bf16[8,64,128]{2,1,0:T(8,128)(2,1)S(1)} async-done(((bf16[8,64,128]{2,1,0:T(8,128)(2,1)}), bf16[8,64,128]{2,1,0:T(8,128)(2,1)S(1)}, u32[]{:S(2)}, u32[]{:S(2)}) %all-to-all-start) | async-done | bytes 131104 | tf_op jit(solution)/shard_map/all_to_all | solution.py:447
  29.1 0.7 %line_load.1.refs_0_ = bf16[160,128]{1,0:T(8,128)(2,1)S(1)} custom-call(bf16[8,64,128]{2,1,0:T(8,128)(2,1)S(1)} %all-to-all-done.share_ref, bf16[96,128]{1,0:T(8,128)(2,1)} %get-tuple-element.42.gram_hbm), custom_call_target="tpu_custom_call" | custom-call | flops 1000 | bytes 1000 | tf_op jit(solution)/shard_map/line_load/pallas_call | solution.py:166
  29.9 5.6 %collective-permute-done.9.refs_3_ = bf16[192,128]{1,0:T(8,128)(2,1)S(1)} collective-permute-done((bf16[192,128]{1,0:T(8,128)(2,1)}, bf16[192,128]{1,0:T(8,128)(2,1)S(1)}, u32[]{:S(2)}, u32[]{:S(2)}) %collective-permute-start.9) | collective-permute-done | bytes 49184 | tf_op jit(solution)/shard_map/ppermute | solution.py:419
  35.5 2.6 %collective-permute-start.6 = (bf16[160,128]{1,0:T(8,128)(2,1)S(1)}, bf16[160,128]{1,0:T(8,128)(2,1)S(1)}, u32[]{:S(2)}, u32[]{:S(2)}) collective-permute-start(bf16[160,128]{1,0:T(8,128)(2,1)S(1)} %line_load.1.refs_0_), channel_id=1, source_target_pairs={{0,3},{1,0},{2,1},{3,2},{4,7},{5,4},{6,5},{7,6},{8,11},{9,8},{10,9... | collective-permute-start | bytes 122888 | tf_op jit(solution)/shard_map/ppermute | solution.py:419
  38.2 1.2 %collective-permute-done.8.refs_2_ = bf16[192,128]{1,0:T(8,128)(2,1)S(1)} collective-permute-done((bf16[192,128]{1,0:T(8,128)(2,1)}, bf16[192,128]{1,0:T(8,128)(2,1)S(1)}, u32[]{:S(2)}, u32[]{:S(2)}) %collective-permute-start.8) | collective-permute-done | bytes 49184 | tf_op jit(solution)/shard_map/ppermute | solution.py:419
  39.3 1.0 %collective-permute-start.4 = (bf16[160,128]{1,0:T(8,128)(2,1)S(1)}, bf16[160,128]{1,0:T(8,128)(2,1)S(1)}, u32[]{:S(2)}, u32[]{:S(2)}) collective-permute-start(bf16[160,128]{1,0:T(8,128)(2,1)S(1)} %line_load.1.refs_0_), channel_id=1, source_target_pairs={{0,1},{1,2},{2,3},{3,0},{4,5},{5,6},{6,7},{7,4},{8,9},{9,10},{10,1... | collective-permute-start | bytes 122888 | tf_op jit(solution)/shard_map/ppermute | solution.py:419
  40.4 4.2 %collective-permute-done.5.refs_2_ = bf16[160,128]{1,0:T(8,128)(2,1)S(1)} collective-permute-done((bf16[160,128]{1,0:T(8,128)(2,1)S(1)}, bf16[160,128]{1,0:T(8,128)(2,1)S(1)}, u32[]{:S(2)}, u32[]{:S(2)}) %collective-permute-start.5) | collective-permute-done | bytes 40992 | tf_op jit(solution)/shard_map/ppermute | solution.py:419
  45.9 3.7 %all-to-all-start.1 = ((bf16[8,64,128]{2,1,0:T(8,128)(2,1)}), bf16[8,64,128]{2,1,0:T(8,128)(2,1)S(1)}, u32[]{:S(2)}, u32[]{:S(2)}) async-start(bf16[8,64,128]{2,1,0:T(8,128)(2,1)} %get-tuple-element.58), calls=%async_computation.1 | async-start | bytes 262144 | tf_op jit(solution)/shard_map/all_to_all | solution.py:454
  49.6 4.6 %inverse_factor.1 = (f32[64,64]{1,0:T(8,128)}, bf16[768,64]{1,0:T(8,128)(2,1)}) custom-call(f32[64,64]{1,0:T(8,128)} %get-tuple-element.56.gram_any, bf16[64,768]{1,0:T(8,128)(2,1)} %get-tuple-element.46.lt_any), custom_call_target="tpu_custom_call" | custom-call | flops 4000000000 | bytes 1000 | tf_op jit(solution)/shard_map/inverse_factor/pallas_call | solution.py:249
  54.2 0.9 %all-to-all-done.1 = bf16[8,64,128]{2,1,0:T(8,128)(2,1)S(1)} async-done(((bf16[8,64,128]{2,1,0:T(8,128)(2,1)}), bf16[8,64,128]{2,1,0:T(8,128)(2,1)S(1)}, u32[]{:S(2)}, u32[]{:S(2)}) %all-to-all-start.1) | async-done | bytes 131104 | tf_op jit(solution)/shard_map/all_to_all | solution.py:454
  55.1 2.4 %finish.1 = (f32[64,1024]{1,0:T(8,128)}, bf16[1,768,1024]{2,1,0:T(8,128)(2,1)}) custom-call(f32[64,64]{1,0:T(8,128)} %get-tuple-element.57.w_any, bf16[32,16,128]{2,1,0:T(8,128)(2,1)S(1)} %bitcast.4, bf16[768,64]{1,0:T(8,128)(2,1)} %get-tuple-element.59.basis_any, bf16[768,1024]{1,0:T(8,128)(2,1)S(1)} %get-tuple-element.40.refs_4_.merged_ref), custom_call_target="tpu_custom_call" | custom-call | flops 1000 | bytes 1000 | tf_op jit(solution)/shard_map/finish/pallas_call | solution.py:301
  57.5 2.8 %collective-permute-done.12.refs_6_ = bf16[1,128,2048]{2,1,0:T(8,128)(2,1)S(1)} collective-permute-done((bf16[1,128,2048]{2,1,0:T(8,128)(2,1)S(1)}, bf16[1,128,2048]{2,1,0:T(8,128)(2,1)S(1)}, u32[]{:S(2)}, u32[]{:S(2)}) %collective-permute-start.12) | collective-permute-done | bytes 524320 | tf_op jit(solution)/shard_map/ppermute | solution.py:419
  60.3 4.4 %expert_step.1 = (f32[1,192,2048]{2,1,0:T(8,128)}, f32[1,192,2048]{2,1,0:T(8,128)}, bf16[1,192,2048]{2,1,0:T(8,128)(2,1)}) custom-call(bf16[192,128]{1,0:T(8,128)(2,1)S(1)} %copy-done.1, bf16[192,128]{1,0:T(8,128)(2,1)S(1)} %collective-permute-done.7.refs_1_, bf16[192,128]{1,0:T(8,128)(2,1)S(1)} %collective-permute-done.8.refs_2_, ...), custom_call_target="tpu_custom_call" | custom-call | flops 1000 | bytes 1000 | tf_op jit(solution)/shard_map/expert_step/pallas_call | solution.py:386
  (19 shorter events, 2.9 us)
Async XLA Ops:
  5.9 17.8 %copy-start = (bf16[1,128,768]{2,1,0:T(8,128)(2,1)S(1)}, bf16[1,128,768]{2,1,0:T(8,128)(2,1)}, u32[]{:S(2)}) copy-start(bf16[1,128,768]{2,1,0:T(8,128)(2,1)} %hidden_ref) | copy-start | bytes 589828
  5.9 5.3 %collective-permute-start = (f32[64,768]{1,0:T(8,128)S(1)}, f32[64,768]{1,0:T(8,128)S(1)}, u32[]{:S(2)}, u32[]{:S(2)}) collective-permute-start(f32[64,768]{1,0:T(8,128)S(1)} %get-tuple-element.39), channel_id=1, source_target_pairs={{0,4},{4,0},{8,12},{12,8},{16,20},{20,16},{24,28},{28,24},{1,5},{5... | collective-permute-start | bytes 589832 | tf_op jit(solution)/shard_map/ppermute | solution.py:415
  6.4 38.8 %collective-permute-start.10 = (bf16[1,128,2048]{2,1,0:T(8,128)(2,1)}, bf16[1,128,2048]{2,1,0:T(8,128)(2,1)S(1)}, u32[]{:S(2)}, u32[]{:S(2)}) collective-permute-start(bf16[1,128,2048]{2,1,0:T(8,128)(2,1)} %refs_4_), channel_id=1, source_target_pairs={{0,1},{1,2},{2,3},{3,0},{4,5},{5,6},{6,7},{7,4},{8,9},{9,10},{10,1... | collective-permute-start | bytes 1572872 | tf_op jit(solution)/shard_map/ppermute | solution.py:419
  9.0 36.1 %collective-permute-start.11 = (bf16[1,128,2048]{2,1,0:T(8,128)(2,1)}, bf16[1,128,2048]{2,1,0:T(8,128)(2,1)S(1)}, u32[]{:S(2)}, u32[]{:S(2)}) collective-permute-start(bf16[1,128,2048]{2,1,0:T(8,128)(2,1)} %refs_4_), channel_id=1, source_target_pairs={{0,3},{1,0},{2,1},{3,2},{4,7},{5,4},{6,5},{7,6},{8,11},{9,8},{10,9... | collective-permute-start | bytes 1572872 | tf_op jit(solution)/shard_map/ppermute | solution.py:419
  11.2 5.8 %collective-permute-start.3 = (bf16[64,768]{1,0:T(8,128)(2,1)S(1)}, bf16[64,768]{1,0:T(8,128)(2,1)S(1)}, u32[]{:S(2)}, u32[]{:S(2)}) collective-permute-start(bf16[64,768]{1,0:T(8,128)(2,1)S(1)} %add_convert_fusion.refs_0_), channel_id=1, source_target_pairs={{0,24},{4,28},{8,16},{12,20},{16,8},{20,12},{24,0},{28,4},{1,25},{... | collective-permute-start | bytes 294920 | tf_op jit(solution)/shard_map/ppermute | solution.py:415
  13.8 5.2 %collective-permute-start.2 = (bf16[64,768]{1,0:T(8,128)(2,1)S(1)}, bf16[64,768]{1,0:T(8,128)(2,1)S(1)}, u32[]{:S(2)}, u32[]{:S(2)}) collective-permute-start(bf16[64,768]{1,0:T(8,128)(2,1)S(1)} %add_convert_fusion.refs_0_), channel_id=1, source_target_pairs={{0,16},{4,20},{8,24},{12,28},{16,0},{20,4},{24,8},{28,12},{1,17},{... | collective-permute-start | bytes 294920 | tf_op jit(solution)/shard_map/ppermute | solution.py:415
  14.3 4.8 %collective-permute-start.1 = (bf16[64,768]{1,0:T(8,128)(2,1)S(1)}, bf16[64,768]{1,0:T(8,128)(2,1)S(1)}, u32[]{:S(2)}, u32[]{:S(2)}) collective-permute-start(bf16[64,768]{1,0:T(8,128)(2,1)S(1)} %add_convert_fusion.refs_0_), channel_id=1, source_target_pairs={{0,8},{4,12},{8,0},{12,4},{16,24},{20,28},{24,16},{28,20},{1,9},{5... | collective-permute-start | bytes 294920 | tf_op jit(solution)/shard_map/ppermute | solution.py:415
  20.3 8.8 %all-to-all-start = ((bf16[8,64,128]{2,1,0:T(8,128)(2,1)}), bf16[8,64,128]{2,1,0:T(8,128)(2,1)S(1)}, u32[]{:S(2)}, u32[]{:S(2)}) async-start(bf16[8,64,128]{2,1,0:T(8,128)(2,1)} %bitcast.1), calls=%async_computation | async-start | bytes 262144 | tf_op jit(solution)/shard_map/all_to_all | solution.py:447
  24.5 11.1 %collective-permute-start.9 = (bf16[192,128]{1,0:T(8,128)(2,1)}, bf16[192,128]{1,0:T(8,128)(2,1)S(1)}, u32[]{:S(2)}, u32[]{:S(2)}) collective-permute-start(bf16[192,128]{1,0:T(8,128)(2,1)} %get-tuple-element.51), channel_id=1, source_target_pairs={{0,3},{1,0},{2,1},{3,2},{4,7},{5,4},{6,5},{7,6},{8,11},{9,8},{10,9... | collective-permute-start | bytes 147464 | tf_op jit(solution)/shard_map/ppermute | solution.py:419
  26.2 13.1 %collective-permute-start.8 = (bf16[192,128]{1,0:T(8,128)(2,1)}, bf16[192,128]{1,0:T(8,128)(2,1)S(1)}, u32[]{:S(2)}, u32[]{:S(2)}) collective-permute-start(bf16[192,128]{1,0:T(8,128)(2,1)} %get-tuple-element.49), channel_id=1, source_target_pairs={{0,2},{1,3},{2,0},{3,1},{4,6},{5,7},{6,4},{7,5},{8,10},{9,11},{10,... | collective-permute-start | bytes 147464 | tf_op jit(solution)/shard_map/ppermute | solution.py:419
  26.2 13.1 %collective-permute-start.7 = (bf16[192,128]{1,0:T(8,128)(2,1)}, bf16[192,128]{1,0:T(8,128)(2,1)S(1)}, u32[]{:S(2)}, u32[]{:S(2)}) collective-permute-start(bf16[192,128]{1,0:T(8,128)(2,1)} %get-tuple-element.47), channel_id=1, source_target_pairs={{0,1},{1,2},{2,3},{3,0},{4,5},{5,6},{6,7},{7,4},{8,9},{9,10},{10,1... | collective-permute-start | bytes 147464 | tf_op jit(solution)/shard_map/ppermute | solution.py:419
  35.5 4.9 %collective-permute-start.6 = (bf16[160,128]{1,0:T(8,128)(2,1)S(1)}, bf16[160,128]{1,0:T(8,128)(2,1)S(1)}, u32[]{:S(2)}, u32[]{:S(2)}) collective-permute-start(bf16[160,128]{1,0:T(8,128)(2,1)S(1)} %line_load.1.refs_0_), channel_id=1, source_target_pairs={{0,3},{1,0},{2,1},{3,2},{4,7},{5,4},{6,5},{7,6},{8,11},{9,8},{10,9... | collective-permute-start | bytes 122888 | tf_op jit(solution)/shard_map/ppermute | solution.py:419
  39.3 5.2 %collective-permute-start.5 = (bf16[160,128]{1,0:T(8,128)(2,1)S(1)}, bf16[160,128]{1,0:T(8,128)(2,1)S(1)}, u32[]{:S(2)}, u32[]{:S(2)}) collective-permute-start(bf16[160,128]{1,0:T(8,128)(2,1)S(1)} %line_load.1.refs_0_), channel_id=1, source_target_pairs={{0,2},{1,3},{2,0},{3,1},{4,6},{5,7},{6,4},{7,5},{8,10},{9,11},{10,... | collective-permute-start | bytes 122888 | tf_op jit(solution)/shard_map/ppermute | solution.py:419
  39.3 5.8 %collective-permute-start.4 = (bf16[160,128]{1,0:T(8,128)(2,1)S(1)}, bf16[160,128]{1,0:T(8,128)(2,1)S(1)}, u32[]{:S(2)}, u32[]{:S(2)}) collective-permute-start(bf16[160,128]{1,0:T(8,128)(2,1)S(1)} %line_load.1.refs_0_), channel_id=1, source_target_pairs={{0,1},{1,2},{2,3},{3,0},{4,5},{5,6},{6,7},{7,4},{8,9},{9,10},{10,1... | collective-permute-start | bytes 122888 | tf_op jit(solution)/shard_map/ppermute | solution.py:419
  45.9 14.4 %collective-permute-start.12 = (bf16[1,128,2048]{2,1,0:T(8,128)(2,1)S(1)}, bf16[1,128,2048]{2,1,0:T(8,128)(2,1)S(1)}, u32[]{:S(2)}, u32[]{:S(2)}) collective-permute-start(bf16[1,128,2048]{2,1,0:T(8,128)(2,1)S(1)} %collective-permute-done.10.refs_5_), channel_id=1, source_target_pairs={{0,1},{1,2},{2,3},{3,0},{4,5},{5,6},{6,7},{7,4},{8,9},{9,10},{10,1... | collective-permute-start | bytes 1572872 | tf_op jit(solution)/shard_map/ppermute | solution.py:419
  45.9 9.3 %all-to-all-start.1 = ((bf16[8,64,128]{2,1,0:T(8,128)(2,1)}), bf16[8,64,128]{2,1,0:T(8,128)(2,1)S(1)}, u32[]{:S(2)}, u32[]{:S(2)}) async-start(bf16[8,64,128]{2,1,0:T(8,128)(2,1)} %get-tuple-element.58), calls=%async_computation.1 | async-start | bytes 262144 | tf_op jit(solution)/shard_map/all_to_all | solution.py:454
  54.2 6.1 %copy-start.1 = (bf16[192,128]{1,0:T(8,128)(2,1)S(1)}, bf16[192,128]{1,0:T(8,128)(2,1)}, u32[]{:S(2)}) copy-start(bf16[192,128]{1,0:T(8,128)(2,1)} %get-tuple-element.62.refs_0_) | copy-start | bytes 147460

commit v14 on v13

--- a/solution.py
+++ b/solution.py
@@ -448,8 +448,9 @@
 
     load = line_load(shares, gram)
     loads = [load] + [shift(load, n_exp, k) for k in range(1, n_exp)]
-    loads, slabs, grads = lax.optimization_barrier((loads, slabs, grads))
+    loads, grads = lax.optimization_barrier((loads, grads))
     share, gram = line_sum(loads, gram.shape[0], n_rep)
+    share, slabs = lax.optimization_barrier((share, slabs))
     w, basis = inverse_factor(gram, lt)
     chunks = lax.all_to_all(share, "rep", 0, 0, tiled=True).reshape(chunks.shape)
 

time: 65.2 us -> 63.9 us (0.980)
  blocking collectives: 0 us -> 8.28 us
  waiting for transfers between devices: 21.5 us -> 15.1 us
  starting transfers between devices: 22.4 us -> 19.2 us
    all_to_all x0 -> x1, blocking collectives: none -> 8.28 us  [body(): lax.all_to_all(chunks.reshape(n_rep, rows, TILE_C), 'rep', 0, 0, tiled=True)]
    ppermute x9, waiting for transfers between devices: 14.4 us -> 9.87 us  [shift(): return lax.ppermute(x, 'exp', [(i, (i + k) % size) for i in range(size)])]
    all_to_all x1 -> x0, starting transfers between devices: 3.37 us -> none  [body(): lax.all_to_all(chunks.reshape(n_rep, rows, TILE_C), 'rep', 0, 0, tiled=True)]
    all_to_all x1 -> x0, waiting for transfers between devices: 1.86 us -> none  [body(): lax.all_to_all(chunks.reshape(n_rep, rows, TILE_C), 'rep', 0, 0, tiled=True)]
  transfers between devices with their start and end apart: 15 -> 14, of which waited for: 10 -> 9; matrix products, arithmetic and copies ran while one was open for 0% -> 0% of each run, Pallas kernels for 15% -> 16%
where the time goes in v14:
time: 63.9 us; the launch traced here: 63.5 us
  Pallas kernels  20.1 us (31%)
  starting transfers between devices  19.2 us (30%)
  waiting for transfers between devices  15.1 us (24%)
  blocking collectives  8.28 us (13%)
  between operations  0.71 us (1%)
    ppermute x9, starting transfers between devices, shift(): return lax.ppermute(x, 'exp', [(i, (i + k) % size) for i in range(size)])  11.4 us
    ppermute x9, waiting for transfers between devices, shift(): return lax.ppermute(x, 'exp', [(i, (i + k) % size) for i in range(size)])  9.87 us
    all_to_all x1, blocking collectives, body(): lax.all_to_all(chunks.reshape(n_rep, rows, TILE_C), 'rep', 0, 0, tiled=True)  8.28 us
    pallas_call x1, Pallas kernels, merge(): pl.pallas_call(merge_kernel, grid=(rows // block,), in_specs=[pl.BlockSpe...  5.26 us
    pallas_call x1, Pallas kernels, inverse_factor(): pl.pallas_call(inverse_kernel, in_specs=[ANY] * 2, out_shape=[pltpu.HBM((...  4.6 us
    pallas_call x1, Pallas kernels, expert_step(): pl.pallas_call(functools.partial(expert_kernel, n_exp, n_grad, chunk), in...  4.44 us
    ppermute x4, waiting for transfers between devices, swap(): return lax.ppermute(x, axis, [(i, i ^ mask) for i in range(size)])  4.36 us
    ppermute x4, starting transfers between devices, swap(): return lax.ppermute(x, axis, [(i, i ^ mask) for i in range(size)])  4.07 us
  transfers between devices with their start and end apart: 14, of which 9 were waited for; matrix products, arithmetic and copies ran while one was open for 0% of the time, Pallas kernels for 16%

profile of v14, /device:TPU:0, one launch (start us, length us, event | category | flops | bytes accessed | tf_op | source)
XLA Modules:
  0.0 63.5 jit_solution(11249444238192121080)
XLA Ops:
  0.6 5.3 %merge.1 = (bf16[768,1024]{1,0:T(8,128)(2,1)S(1)}, f32[64,768]{1,0:T(8,128)S(1)}) custom-call(bf16[1024,768]{1,0:T(8,128)(2,1)} %acts_ref.1, bf16[1024,1024]{1,0:T(8,128)(2,1)} %kv_ref.1, bf16[1,768,1024]{2,1,0:T(8,128)(2,1)} %err_ref.1, f32[64,1024]{1,0:T(8,128)} %bitcast.6), custom_call_target="tpu_custom_call" | custom-call | flops 4000000000 | bytes 8000000 | tf_op jit(solution)/shard_map/merge/pallas_call | solution.py:63
  6.4 2.6 %collective-permute-start.7 = (bf16[1,128,2048]{2,1,0:T(8,128)(2,1)S(1)}, bf16[1,128,2048]{2,1,0:T(8,128)(2,1)S(1)}, u32[]{:S(2)}, u32[]{:S(2)}) collective-permute-start(bf16[1,128,2048]{2,1,0:T(8,128)(2,1)S(1)} %copy-done.2), channel_id=1, source_target_pairs={{0,1},{1,2},{2,3},{3,0},{4,5},{5,6},{6,7},{7,4},{8,9},{9,10},{10,1... | collective-permute-start | bytes 1572872 | tf_op jit(solution)/shard_map/ppermute | solution.py:419
  9.1 2.1 %collective-permute-start.8 = (bf16[1,128,2048]{2,1,0:T(8,128)(2,1)S(1)}, bf16[1,128,2048]{2,1,0:T(8,128)(2,1)S(1)}, u32[]{:S(2)}, u32[]{:S(2)}) collective-permute-start(bf16[1,128,2048]{2,1,0:T(8,128)(2,1)S(1)} %copy-done.2), channel_id=1, source_target_pairs={{0,3},{1,0},{2,1},{3,2},{4,7},{5,4},{6,5},{7,6},{8,11},{9,8},{10,9... | collective-permute-start | bytes 1572872 | tf_op jit(solution)/shard_map/ppermute | solution.py:419
  11.2 2.7 %collective-permute-start.3 = (bf16[64,768]{1,0:T(8,128)(2,1)S(1)}, bf16[64,768]{1,0:T(8,128)(2,1)S(1)}, u32[]{:S(2)}, u32[]{:S(2)}) collective-permute-start(bf16[64,768]{1,0:T(8,128)(2,1)S(1)} %add_convert_fusion.refs_0_), channel_id=1, source_target_pairs={{0,24},{4,28},{8,16},{12,20},{16,8},{20,12},{24,0},{28,4},{1,25},{... | collective-permute-start | bytes 294920 | tf_op jit(solution)/shard_map/ppermute | solution.py:415
  14.8 2.3 %collective-permute-done.3.refs_3_ = bf16[64,768]{1,0:T(8,128)(2,1)S(1)} collective-permute-done((bf16[64,768]{1,0:T(8,128)(2,1)S(1)}, bf16[64,768]{1,0:T(8,128)(2,1)S(1)}, u32[]{:S(2)}, u32[]{:S(2)}) %collective-permute-start.3) | collective-permute-done | bytes 98336 | tf_op jit(solution)/shard_map/ppermute | solution.py:415
  17.1 2.0 %collective-permute-done.2.refs_2_ = bf16[64,768]{1,0:T(8,128)(2,1)S(1)} collective-permute-done((bf16[64,768]{1,0:T(8,128)(2,1)S(1)}, bf16[64,768]{1,0:T(8,128)(2,1)S(1)}, u32[]{:S(2)}, u32[]{:S(2)}) %collective-permute-start.2) | collective-permute-done | bytes 98336 | tf_op jit(solution)/shard_map/ppermute | solution.py:415
  19.1 1.1 %right_product.1 = (bf16[64,768]{1,0:T(8,128)(2,1)}, bf16[96,128]{1,0:T(8,128)(2,1)}, bf16[32,16,128]{2,1,0:T(8,128)(2,1)S(1)}) custom-call(bf16[64,768]{1,0:T(8,128)(2,1)S(1)} %add_convert_fusion.refs_0_, bf16[64,768]{1,0:T(8,128)(2,1)S(1)} %collective-permute-done.1.refs_1_, bf16[64,768]{1,0:T(8,128)(2,1)S(1)} %collective-permute-done.2.refs_2_, ...), custom_call_target="tpu_custom_call" | custom-call | flops 1000 | bytes 1000 | tf_op jit(solution)/shard_map/right_product/pallas_call | solution.py:140
  20.3 8.3 %all_to_all.10.share_ref = bf16[8,64,128]{2,1,0:T(8,128)(2,1)S(1)} all-to-all(bf16[8,64,128]{2,1,0:T(8,128)(2,1)S(1)} %bitcast.5), channel_id=1, replica_groups=mesh['rep'=8,'exp'=4] {'rep'}, dimensions={0} | all-to-all | bytes 262144 | tf_op jit(solution)/shard_map/all_to_all | solution.py:447
  28.6 0.7 %line_load.1.refs_0_ = bf16[160,128]{1,0:T(8,128)(2,1)S(1)} custom-call(bf16[8,64,128]{2,1,0:T(8,128)(2,1)S(1)} %all_to_all.10.share_ref, bf16[96,128]{1,0:T(8,128)(2,1)} %get-tuple-element.43.gram_hbm), custom_call_target="tpu_custom_call" | custom-call | flops 1000 | bytes 1000 | tf_op jit(solution)/shard_map/line_load/pallas_call | solution.py:166
  29.3 1.8 %collective-permute-start.6 = (bf16[160,128]{1,0:T(8,128)(2,1)S(1)}, bf16[160,128]{1,0:T(8,128)(2,1)S(1)}, u32[]{:S(2)}, u32[]{:S(2)}) collective-permute-start(bf16[160,128]{1,0:T(8,128)(2,1)S(1)} %line_load.1.refs_0_), channel_id=1, source_target_pairs={{0,3},{1,0},{2,1},{3,2},{4,7},{5,4},{6,5},{7,6},{8,11},{9,8},{10,9... | collective-permute-start | bytes 122888 | tf_op jit(solution)/shard_map/ppermute | solution.py:419
  31.1 1.0 %collective-permute-start.4 = (bf16[160,128]{1,0:T(8,128)(2,1)S(1)}, bf16[160,128]{1,0:T(8,128)(2,1)S(1)}, u32[]{:S(2)}, u32[]{:S(2)}) collective-permute-start(bf16[160,128]{1,0:T(8,128)(2,1)S(1)} %line_load.1.refs_0_), channel_id=1, source_target_pairs={{0,1},{1,2},{2,3},{3,0},{4,5},{5,6},{6,7},{7,4},{8,9},{9,10},{10,1... | collective-permute-start | bytes 122888 | tf_op jit(solution)/shard_map/ppermute | solution.py:419
  32.1 0.8 %unit_slabs.1 = (bf16[192,128]{1,0:T(8,128)(2,1)}, bf16[192,128]{1,0:T(8,128)(2,1)}, bf16[192,128]{1,0:T(8,128)(2,1)}, bf16[192,128]{1,0:T(8,128)(2,1)}) custom-call(bf16[1,128,768]{2,1,0:T(8,128)(2,1)S(1)} %copy-done), custom_call_target="tpu_custom_call" | custom-call | flops 1000 | bytes 1000 | tf_op jit(solution)/shard_map/unit_slabs/pallas_call | solution.py:98
  32.9 2.2 %collective-permute-done.6.refs_3_ = bf16[160,128]{1,0:T(8,128)(2,1)S(1)} collective-permute-done((bf16[160,128]{1,0:T(8,128)(2,1)S(1)}, bf16[160,128]{1,0:T(8,128)(2,1)S(1)}, u32[]{:S(2)}, u32[]{:S(2)}) %collective-permute-start.6) | collective-permute-done | bytes 40992 | tf_op jit(solution)/shard_map/ppermute | solution.py:419
  35.2 2.6 %collective-permute-start.11 = (bf16[192,128]{1,0:T(8,128)(2,1)}, bf16[192,128]{1,0:T(8,128)(2,1)S(1)}, u32[]{:S(2)}, u32[]{:S(2)}) collective-permute-start(bf16[192,128]{1,0:T(8,128)(2,1)} %get-tuple-element.59), channel_id=1, source_target_pairs={{0,3},{1,0},{2,1},{3,2},{4,7},{5,4},{6,5},{7,6},{8,11},{9,8},{10,9... | collective-permute-start | bytes 147464 | tf_op jit(solution)/shard_map/ppermute | solution.py:419
  37.8 0.7 %collective-permute-done.5.refs_2_ = bf16[160,128]{1,0:T(8,128)(2,1)S(1)} collective-permute-done((bf16[160,128]{1,0:T(8,128)(2,1)S(1)}, bf16[160,128]{1,0:T(8,128)(2,1)S(1)}, u32[]{:S(2)}, u32[]{:S(2)}) %collective-permute-start.5) | collective-permute-done | bytes 40992 | tf_op jit(solution)/shard_map/ppermute | solution.py:419
  38.5 1.2 %collective-permute-start.9 = (bf16[192,128]{1,0:T(8,128)(2,1)}, bf16[192,128]{1,0:T(8,128)(2,1)S(1)}, u32[]{:S(2)}, u32[]{:S(2)}) collective-permute-start(bf16[192,128]{1,0:T(8,128)(2,1)} %get-tuple-element.55), channel_id=1, source_target_pairs={{0,1},{1,2},{2,3},{3,0},{4,5},{5,6},{6,7},{7,4},{8,9},{9,10},{10,1... | collective-permute-start | bytes 147464 | tf_op jit(solution)/shard_map/ppermute | solution.py:419
  39.7 0.7 %line_sum.1 = (bf16[8,64,128]{2,1,0:T(8,128)(2,1)}, f32[64,64]{1,0:T(8,128)}) custom-call(bf16[160,128]{1,0:T(8,128)(2,1)S(1)} %line_load.1.refs_0_, bf16[160,128]{1,0:T(8,128)(2,1)S(1)} %collective-permute-done.4.refs_1_, bf16[160,128]{1,0:T(8,128)(2,1)S(1)} %collective-permute-done.5.refs_2_, bf16[160,128]{1,0:T(8,128)(2,1)S(1)} %collective-permute-done.6.refs_3_), custom_call_target="tpu_custom_call" | custom-call | flops 1000 | bytes 1000 | tf_op jit(solution)/shard_map/line_sum/pallas_call | solution.py:202
  40.4 3.7 %collective-permute-done.10.refs_2_ = bf16[192,128]{1,0:T(8,128)(2,1)S(1)} collective-permute-done((bf16[192,128]{1,0:T(8,128)(2,1)}, bf16[192,128]{1,0:T(8,128)(2,1)S(1)}, u32[]{:S(2)}, u32[]{:S(2)}) %collective-permute-start.10) | collective-permute-done | bytes 49184 | tf_op jit(solution)/shard_map/ppermute | solution.py:419
  44.6 3.7 %all-to-all-start.1 = ((bf16[8,64,128]{2,1,0:T(8,128)(2,1)}), bf16[8,64,128]{2,1,0:T(8,128)(2,1)S(1)}, u32[]{:S(2)}, u32[]{:S(2)}) async-start(bf16[8,64,128]{2,1,0:T(8,128)(2,1)} %get-tuple-element.60), calls=%async_computation.1 | async-start | bytes 262144 | tf_op jit(solution)/shard_map/all_to_all | solution.py:455
  48.3 4.6 %inverse_factor.1 = (f32[64,64]{1,0:T(8,128)}, bf16[768,64]{1,0:T(8,128)(2,1)}) custom-call(f32[64,64]{1,0:T(8,128)} %get-tuple-element.48.gram_any, bf16[64,768]{1,0:T(8,128)(2,1)} %get-tuple-element.49.lt_any), custom_call_target="tpu_custom_call" | custom-call | flops 4000000000 | bytes 1000 | tf_op jit(solution)/shard_map/inverse_factor/pallas_call | solution.py:249
  53.0 0.9 %all-to-all-done.1 = bf16[8,64,128]{2,1,0:T(8,128)(2,1)S(1)} async-done(((bf16[8,64,128]{2,1,0:T(8,128)(2,1)}), bf16[8,64,128]{2,1,0:T(8,128)(2,1)S(1)}, u32[]{:S(2)}, u32[]{:S(2)}) %all-to-all-start.1) | async-done | bytes 131104 | tf_op jit(solution)/shard_map/all_to_all | solution.py:455
  53.9 2.4 %finish.1 = (f32[64,1024]{1,0:T(8,128)}, bf16[1,768,1024]{2,1,0:T(8,128)(2,1)}) custom-call(f32[64,64]{1,0:T(8,128)} %get-tuple-element.50.w_any, bf16[32,16,128]{2,1,0:T(8,128)(2,1)S(1)} %bitcast.4, bf16[768,64]{1,0:T(8,128)(2,1)} %get-tuple-element.61.basis_any, bf16[768,1024]{1,0:T(8,128)(2,1)S(1)} %get-tuple-element.41.refs_4_.merged_ref), custom_call_target="tpu_custom_call" | custom-call | flops 1000 | bytes 1000 | tf_op jit(solution)/shard_map/finish/pallas_call | solution.py:301
  56.3 2.8 %collective-permute-done.12.refs_6_ = bf16[1,128,2048]{2,1,0:T(8,128)(2,1)S(1)} collective-permute-done((bf16[1,128,2048]{2,1,0:T(8,128)(2,1)S(1)}, bf16[1,128,2048]{2,1,0:T(8,128)(2,1)S(1)}, u32[]{:S(2)}, u32[]{:S(2)}) %collective-permute-start.12) | collective-permute-done | bytes 524320 | tf_op jit(solution)/shard_map/ppermute | solution.py:419
  59.0 4.4 %expert_step.1 = (f32[1,192,2048]{2,1,0:T(8,128)}, f32[1,192,2048]{2,1,0:T(8,128)}, bf16[1,192,2048]{2,1,0:T(8,128)(2,1)}) custom-call(bf16[192,128]{1,0:T(8,128)(2,1)S(1)} %copy-done.1, bf16[192,128]{1,0:T(8,128)(2,1)S(1)} %collective-permute-done.9.refs_1_, bf16[192,128]{1,0:T(8,128)(2,1)S(1)} %collective-permute-done.10.refs_2_, ...), custom_call_target="tpu_custom_call" | custom-call | flops 1000 | bytes 1000 | tf_op jit(solution)/shard_map/expert_step/pallas_call | solution.py:386
  (20 shorter events, 2.1 us)
Async XLA Ops:
  0.6 5.8 %copy-start.2 = (bf16[1,128,2048]{2,1,0:T(8,128)(2,1)S(1)}, bf16[1,128,2048]{2,1,0:T(8,128)(2,1)}, u32[]{:S(2)}) copy-start(bf16[1,128,2048]{2,1,0:T(8,128)(2,1)} %refs_4_) | copy-start | bytes 1572868
  5.9 26.2 %copy-start = (bf16[1,128,768]{2,1,0:T(8,128)(2,1)S(1)}, bf16[1,128,768]{2,1,0:T(8,128)(2,1)}, u32[]{:S(2)}) copy-start(bf16[1,128,768]{2,1,0:T(8,128)(2,1)} %hidden_ref) | copy-start | bytes 589828
  5.9 5.3 %collective-permute-start = (f32[64,768]{1,0:T(8,128)S(1)}, f32[64,768]{1,0:T(8,128)S(1)}, u32[]{:S(2)}, u32[]{:S(2)}) collective-permute-start(f32[64,768]{1,0:T(8,128)S(1)} %get-tuple-element.40), channel_id=1, source_target_pairs={{0,4},{4,0},{8,12},{12,8},{16,20},{20,16},{24,28},{28,24},{1,5},{5... | collective-permute-start | bytes 589832 | tf_op jit(solution)/shard_map/ppermute | solution.py:415
  6.4 33.3 %collective-permute-start.7 = (bf16[1,128,2048]{2,1,0:T(8,128)(2,1)S(1)}, bf16[1,128,2048]{2,1,0:T(8,128)(2,1)S(1)}, u32[]{:S(2)}, u32[]{:S(2)}) collective-permute-start(bf16[1,128,2048]{2,1,0:T(8,128)(2,1)S(1)} %copy-done.2), channel_id=1, source_target_pairs={{0,1},{1,2},{2,3},{3,0},{4,5},{5,6},{6,7},{7,4},{8,9},{9,10},{10,1... | collective-permute-start | bytes 1572872 | tf_op jit(solution)/shard_map/ppermute | solution.py:419
  9.1 30.6 %collective-permute-start.8 = (bf16[1,128,2048]{2,1,0:T(8,128)(2,1)S(1)}, bf16[1,128,2048]{2,1,0:T(8,128)(2,1)S(1)}, u32[]{:S(2)}, u32[]{:S(2)}) collective-permute-start(bf16[1,128,2048]{2,1,0:T(8,128)(2,1)S(1)} %copy-done.2), channel_id=1, source_target_pairs={{0,3},{1,0},{2,1},{3,2},{4,7},{5,4},{6,5},{7,6},{8,11},{9,8},{10,9... | collective-permute-start | bytes 1572872 | tf_op jit(solution)/shard_map/ppermute | solution.py:419
  11.2 5.8 %collective-permute-start.3 = (bf16[64,768]{1,0:T(8,128)(2,1)S(1)}, bf16[64,768]{1,0:T(8,128)(2,1)S(1)}, u32[]{:S(2)}, u32[]{:S(2)}) collective-permute-start(bf16[64,768]{1,0:T(8,128)(2,1)S(1)} %add_convert_fusion.refs_0_), channel_id=1, source_target_pairs={{0,24},{4,28},{8,16},{12,20},{16,8},{20,12},{24,0},{28,4},{1,25},{... | collective-permute-start | bytes 294920 | tf_op jit(solution)/shard_map/ppermute | solution.py:415
  13.9 5.2 %collective-permute-start.2 = (bf16[64,768]{1,0:T(8,128)(2,1)S(1)}, bf16[64,768]{1,0:T(8,128)(2,1)S(1)}, u32[]{:S(2)}, u32[]{:S(2)}) collective-permute-start(bf16[64,768]{1,0:T(8,128)(2,1)S(1)} %add_convert_fusion.refs_0_), channel_id=1, source_target_pairs={{0,16},{4,20},{8,24},{12,28},{16,0},{20,4},{24,8},{28,12},{1,17},{... | collective-permute-start | bytes 294920 | tf_op jit(solution)/shard_map/ppermute | solution.py:415
  14.4 4.8 %collective-permute-start.1 = (bf16[64,768]{1,0:T(8,128)(2,1)S(1)}, bf16[64,768]{1,0:T(8,128)(2,1)S(1)}, u32[]{:S(2)}, u32[]{:S(2)}) collective-permute-start(bf16[64,768]{1,0:T(8,128)(2,1)S(1)} %add_convert_fusion.refs_0_), channel_id=1, source_target_pairs={{0,8},{4,12},{8,0},{12,4},{16,24},{20,28},{24,16},{28,20},{1,9},{5... | collective-permute-start | bytes 294920 | tf_op jit(solution)/shard_map/ppermute | solution.py:415
  29.3 5.9 %collective-permute-start.6 = (bf16[160,128]{1,0:T(8,128)(2,1)S(1)}, bf16[160,128]{1,0:T(8,128)(2,1)S(1)}, u32[]{:S(2)}, u32[]{:S(2)}) collective-permute-start(bf16[160,128]{1,0:T(8,128)(2,1)S(1)} %line_load.1.refs_0_), channel_id=1, source_target_pairs={{0,3},{1,0},{2,1},{3,2},{4,7},{5,4},{6,5},{7,6},{8,11},{9,8},{10,9... | collective-permute-start | bytes 122888 | tf_op jit(solution)/shard_map/ppermute | solution.py:419
  31.1 7.4 %collective-permute-start.5 = (bf16[160,128]{1,0:T(8,128)(2,1)S(1)}, bf16[160,128]{1,0:T(8,128)(2,1)S(1)}, u32[]{:S(2)}, u32[]{:S(2)}) collective-permute-start(bf16[160,128]{1,0:T(8,128)(2,1)S(1)} %line_load.1.refs_0_), channel_id=1, source_target_pairs={{0,2},{1,3},{2,0},{3,1},{4,6},{5,7},{6,4},{7,5},{8,10},{9,11},{10,... | collective-permute-start | bytes 122888 | tf_op jit(solution)/shard_map/ppermute | solution.py:419
  31.1 7.4 %collective-permute-start.4 = (bf16[160,128]{1,0:T(8,128)(2,1)S(1)}, bf16[160,128]{1,0:T(8,128)(2,1)S(1)}, u32[]{:S(2)}, u32[]{:S(2)}) collective-permute-start(bf16[160,128]{1,0:T(8,128)(2,1)S(1)} %line_load.1.refs_0_), channel_id=1, source_target_pairs={{0,1},{1,2},{2,3},{3,0},{4,5},{5,6},{6,7},{7,4},{8,9},{9,10},{10,1... | collective-permute-start | bytes 122888 | tf_op jit(solution)/shard_map/ppermute | solution.py:419
  35.2 5.2 %collective-permute-start.11 = (bf16[192,128]{1,0:T(8,128)(2,1)}, bf16[192,128]{1,0:T(8,128)(2,1)S(1)}, u32[]{:S(2)}, u32[]{:S(2)}) collective-permute-start(bf16[192,128]{1,0:T(8,128)(2,1)} %get-tuple-element.59), channel_id=1, source_target_pairs={{0,3},{1,0},{2,1},{3,2},{4,7},{5,4},{6,5},{7,6},{8,11},{9,8},{10,9... | collective-permute-start | bytes 147464 | tf_op jit(solution)/shard_map/ppermute | solution.py:419
  38.5 5.6 %collective-permute-start.10 = (bf16[192,128]{1,0:T(8,128)(2,1)}, bf16[192,128]{1,0:T(8,128)(2,1)S(1)}, u32[]{:S(2)}, u32[]{:S(2)}) collective-permute-start(bf16[192,128]{1,0:T(8,128)(2,1)} %get-tuple-element.57), channel_id=1, source_target_pairs={{0,2},{1,3},{2,0},{3,1},{4,6},{5,7},{6,4},{7,5},{8,10},{9,11},{10,... | collective-permute-start | bytes 147464 | tf_op jit(solution)/shard_map/ppermute | solution.py:419
  38.5 6.1 %collective-permute-start.9 = (bf16[192,128]{1,0:T(8,128)(2,1)}, bf16[192,128]{1,0:T(8,128)(2,1)S(1)}, u32[]{:S(2)}, u32[]{:S(2)}) collective-permute-start(bf16[192,128]{1,0:T(8,128)(2,1)} %get-tuple-element.55), channel_id=1, source_target_pairs={{0,1},{1,2},{2,3},{3,0},{4,5},{5,6},{6,7},{7,4},{8,9},{9,10},{10,1... | collective-permute-start | bytes 147464 | tf_op jit(solution)/shard_map/ppermute | solution.py:419
  44.6 14.4 %collective-permute-start.12 = (bf16[1,128,2048]{2,1,0:T(8,128)(2,1)S(1)}, bf16[1,128,2048]{2,1,0:T(8,128)(2,1)S(1)}, u32[]{:S(2)}, u32[]{:S(2)}) collective-permute-start(bf16[1,128,2048]{2,1,0:T(8,128)(2,1)S(1)} %collective-permute-done.7.refs_5_), channel_id=1, source_target_pairs={{0,1},{1,2},{2,3},{3,0},{4,5},{5,6},{6,7},{7,4},{8,9},{9,10},{10,1... | collective-permute-start | bytes 1572872 | tf_op jit(solution)/shard_map/ppermute | solution.py:419
  44.6 9.3 %all-to-all-start.1 = ((bf16[8,64,128]{2,1,0:T(8,128)(2,1)}), bf16[8,64,128]{2,1,0:T(8,128)(2,1)S(1)}, u32[]{:S(2)}, u32[]{:S(2)}) async-start(bf16[8,64,128]{2,1,0:T(8,128)(2,1)} %get-tuple-element.60), calls=%async_computation.1 | async-start | bytes 262144 | tf_op jit(solution)/shard_map/all_to_all | solution.py:455
  53.0 6.1 %copy-start.1 = (bf16[192,128]{1,0:T(8,128)(2,1)S(1)}, bf16[192,128]{1,0:T(8,128)(2,1)}, u32[]{:S(2)}) copy-start(bf16[192,128]{1,0:T(8,128)(2,1)} %get-tuple-element.64.refs_0_) | copy-start | bytes 147460

commit v15 on v14

--- a/solution.py
+++ b/solution.py
@@ -442,7 +442,6 @@
         bit *= len(parts)
     lt, gram, chunks = right_product(parts, merged)
 
-    slabs = [slabs[0]] + [shift(after(slabs[k], lt), n_exp, k) for k in range(1, n_exp)]
     rows = chunks.shape[0] * TILE_R // n_rep
     shares = lax.all_to_all(chunks.reshape(n_rep, rows, TILE_C), "rep", 0, 0, tiled=True)
 
@@ -450,7 +449,7 @@
     loads = [load] + [shift(load, n_exp, k) for k in range(1, n_exp)]
     loads, grads = lax.optimization_barrier((loads, grads))
     share, gram = line_sum(loads, gram.shape[0], n_rep)
-    share, slabs = lax.optimization_barrier((share, slabs))
+    slabs = [slabs[0]] + [shift(after(slabs[k], share), n_exp, k) for k in range(1, n_exp)]
     w, basis = inverse_factor(gram, lt)
     chunks = lax.all_to_all(share, "rep", 0, 0, tiled=True).reshape(chunks.shape)
 

time: 63.9 us -> 63.9 us (level)
    all_to_all x1, waiting for transfers between devices: 0.91 us -> 0.01 us  [body(): lax.all_to_all(share, 'rep', 0, 0, tiled=True).reshape(chunks.shape)]
  transfers between devices with their start and end apart: 14 -> 14, of which waited for: 9 -> 7; matrix products, arithmetic and copies ran while one was open for 0% -> 0% of each run, Pallas kernels for 16% -> 15%
where the time goes in v15:
time: 63.9 us; the launch traced here: 63.5 us
  Pallas kernels  20.1 us (31%)
  starting transfers between devices  19.8 us (31%)
  waiting for transfers between devices  14.5 us (23%)
  blocking collectives  8.28 us (13%)
  between operations  0.72 us (1%)
    ppermute x9, starting transfers between devices, shift(): return lax.ppermute(x, 'exp', [(i, (i + k) % size) for i in range(size)])  12 us
    ppermute x9, waiting for transfers between devices, shift(): return lax.ppermute(x, 'exp', [(i, (i + k) % size) for i in range(size)])  10.1 us
    all_to_all x1, blocking collectives, body(): lax.all_to_all(chunks.reshape(n_rep, rows, TILE_C), 'rep', 0, 0, tiled=True)  8.28 us
    pallas_call x1, Pallas kernels, merge(): pl.pallas_call(merge_kernel, grid=(rows // block,), in_specs=[pl.BlockSpe...  5.26 us
    pallas_call x1, Pallas kernels, inverse_factor(): pl.pallas_call(inverse_kernel, in_specs=[ANY] * 2, out_shape=[pltpu.HBM((...  4.6 us
    pallas_call x1, Pallas kernels, expert_step(): pl.pallas_call(functools.partial(expert_kernel, n_exp, n_grad, chunk), in...  4.47 us
    ppermute x4, waiting for transfers between devices, swap(): return lax.ppermute(x, axis, [(i, i ^ mask) for i in range(size)])  4.36 us
    ppermute x4, starting transfers between devices, swap(): return lax.ppermute(x, axis, [(i, i ^ mask) for i in range(size)])  4.07 us
  transfers between devices with their start and end apart: 14, of which 7 were waited for; matrix products, arithmetic and copies ran while one was open for 0% of the time, Pallas kernels for 15%

profile of v15, /device:TPU:0, one launch (start us, length us, event | category | flops | bytes accessed | tf_op | source)
XLA Modules:
  0.0 63.5 jit_solution(3149049762732867466)
XLA Ops:
  0.6 5.3 %merge.1 = (bf16[768,1024]{1,0:T(8,128)(2,1)S(1)}, f32[64,768]{1,0:T(8,128)S(1)}) custom-call(bf16[1024,768]{1,0:T(8,128)(2,1)} %acts_ref.1, bf16[1024,1024]{1,0:T(8,128)(2,1)} %kv_ref.1, bf16[1,768,1024]{2,1,0:T(8,128)(2,1)} %err_ref.1, f32[64,1024]{1,0:T(8,128)} %bitcast.6), custom_call_target="tpu_custom_call" | custom-call | flops 4000000000 | bytes 8000000 | tf_op jit(solution)/shard_map/merge/pallas_call | solution.py:63
  5.9 0.5 collective-permute-start
  6.4 2.6 %collective-permute-start.7 = (bf16[1,128,2048]{2,1,0:T(8,128)(2,1)S(1)}, bf16[1,128,2048]{2,1,0:T(8,128)(2,1)S(1)}, u32[]{:S(2)}, u32[]{:S(2)}) collective-permute-start(bf16[1,128,2048]{2,1,0:T(8,128)(2,1)S(1)} %copy-done.2), channel_id=1, source_target_pairs={{0,1},{1,2},{2,3},{3,0},{4,5},{5,6},{6,7},{7,4},{8,9},{9,10},{10,1... | collective-permute-start | bytes 1572872 | tf_op jit(solution)/shard_map/ppermute | solution.py:419
  9.1 2.1 %collective-permute-start.8 = (bf16[1,128,2048]{2,1,0:T(8,128)(2,1)S(1)}, bf16[1,128,2048]{2,1,0:T(8,128)(2,1)S(1)}, u32[]{:S(2)}, u32[]{:S(2)}) collective-permute-start(bf16[1,128,2048]{2,1,0:T(8,128)(2,1)S(1)} %copy-done.2), channel_id=1, source_target_pairs={{0,3},{1,0},{2,1},{3,2},{4,7},{5,4},{6,5},{7,6},{8,11},{9,8},{10,9... | collective-permute-start | bytes 1572872 | tf_op jit(solution)/shard_map/ppermute | solution.py:419
  11.2 2.7 %collective-permute-start.3 = (bf16[64,768]{1,0:T(8,128)(2,1)S(1)}, bf16[64,768]{1,0:T(8,128)(2,1)S(1)}, u32[]{:S(2)}, u32[]{:S(2)}) collective-permute-start(bf16[64,768]{1,0:T(8,128)(2,1)S(1)} %add_convert_fusion.refs_0_), channel_id=1, source_target_pairs={{0,24},{4,28},{8,16},{12,20},{16,8},{20,12},{24,0},{28,4},{1,25},{... | collective-permute-start | bytes 294920 | tf_op jit(solution)/shard_map/ppermute | solution.py:415
  14.8 2.3 %collective-permute-done.3.refs_3_ = bf16[64,768]{1,0:T(8,128)(2,1)S(1)} collective-permute-done((bf16[64,768]{1,0:T(8,128)(2,1)S(1)}, bf16[64,768]{1,0:T(8,128)(2,1)S(1)}, u32[]{:S(2)}, u32[]{:S(2)}) %collective-permute-start.3) | collective-permute-done | bytes 98336 | tf_op jit(solution)/shard_map/ppermute | solution.py:415
  17.1 2.0 %collective-permute-done.2.refs_2_ = bf16[64,768]{1,0:T(8,128)(2,1)S(1)} collective-permute-done((bf16[64,768]{1,0:T(8,128)(2,1)S(1)}, bf16[64,768]{1,0:T(8,128)(2,1)S(1)}, u32[]{:S(2)}, u32[]{:S(2)}) %collective-permute-start.2) | collective-permute-done | bytes 98336 | tf_op jit(solution)/shard_map/ppermute | solution.py:415
  19.1 1.1 %right_product.1 = (bf16[64,768]{1,0:T(8,128)(2,1)}, bf16[96,128]{1,0:T(8,128)(2,1)}, bf16[32,16,128]{2,1,0:T(8,128)(2,1)S(1)}) custom-call(bf16[64,768]{1,0:T(8,128)(2,1)S(1)} %add_convert_fusion.refs_0_, bf16[64,768]{1,0:T(8,128)(2,1)S(1)} %collective-permute-done.1.refs_1_, bf16[64,768]{1,0:T(8,128)(2,1)S(1)} %collective-permute-done.2.refs_2_, ...), custom_call_target="tpu_custom_call" | custom-call | flops 1000 | bytes 1000 | tf_op jit(solution)/shard_map/right_product/pallas_call | solution.py:140
  20.3 8.3 %all_to_all.10.share_ref = bf16[8,64,128]{2,1,0:T(8,128)(2,1)S(1)} all-to-all(bf16[8,64,128]{2,1,0:T(8,128)(2,1)S(1)} %bitcast.5), channel_id=1, replica_groups=mesh['rep'=8,'exp'=4] {'rep'}, dimensions={0} | all-to-all | bytes 262144 | tf_op jit(solution)/shard_map/all_to_all | solution.py:446
  28.6 0.7 %line_load.1.refs_0_ = bf16[160,128]{1,0:T(8,128)(2,1)S(1)} custom-call(bf16[8,64,128]{2,1,0:T(8,128)(2,1)S(1)} %all_to_all.10.share_ref, bf16[96,128]{1,0:T(8,128)(2,1)} %get-tuple-element.38.gram_hbm), custom_call_target="tpu_custom_call" | custom-call | flops 1000 | bytes 1000 | tf_op jit(solution)/shard_map/line_load/pallas_call | solution.py:166
  29.3 1.8 %collective-permute-start.6 = (bf16[160,128]{1,0:T(8,128)(2,1)S(1)}, bf16[160,128]{1,0:T(8,128)(2,1)S(1)}, u32[]{:S(2)}, u32[]{:S(2)}) collective-permute-start(bf16[160,128]{1,0:T(8,128)(2,1)S(1)} %line_load.1.refs_0_), channel_id=1, source_target_pairs={{0,3},{1,0},{2,1},{3,2},{4,7},{5,4},{6,5},{7,6},{8,11},{9,8},{10,9... | collective-permute-start | bytes 122888 | tf_op jit(solution)/shard_map/ppermute | solution.py:419
  31.1 1.0 %collective-permute-start.4 = (bf16[160,128]{1,0:T(8,128)(2,1)S(1)}, bf16[160,128]{1,0:T(8,128)(2,1)S(1)}, u32[]{:S(2)}, u32[]{:S(2)}) collective-permute-start(bf16[160,128]{1,0:T(8,128)(2,1)S(1)} %line_load.1.refs_0_), channel_id=1, source_target_pairs={{0,1},{1,2},{2,3},{3,0},{4,5},{5,6},{6,7},{7,4},{8,9},{9,10},{10,1... | collective-permute-start | bytes 122888 | tf_op jit(solution)/shard_map/ppermute | solution.py:419
  32.1 3.1 %collective-permute-done.6.refs_3_ = bf16[160,128]{1,0:T(8,128)(2,1)S(1)} collective-permute-done((bf16[160,128]{1,0:T(8,128)(2,1)S(1)}, bf16[160,128]{1,0:T(8,128)(2,1)S(1)}, u32[]{:S(2)}, u32[]{:S(2)}) %collective-permute-start.6) | collective-permute-done | bytes 40992 | tf_op jit(solution)/shard_map/ppermute | solution.py:419
  35.2 3.2 %collective-permute-done.5.refs_2_ = bf16[160,128]{1,0:T(8,128)(2,1)S(1)} collective-permute-done((bf16[160,128]{1,0:T(8,128)(2,1)S(1)}, bf16[160,128]{1,0:T(8,128)(2,1)S(1)}, u32[]{:S(2)}, u32[]{:S(2)}) %collective-permute-start.5) | collective-permute-done | bytes 40992 | tf_op jit(solution)/shard_map/ppermute | solution.py:419
  38.4 0.7 %line_sum.1 = (bf16[8,64,128]{2,1,0:T(8,128)(2,1)}, f32[64,64]{1,0:T(8,128)}) custom-call(bf16[160,128]{1,0:T(8,128)(2,1)S(1)} %line_load.1.refs_0_, bf16[160,128]{1,0:T(8,128)(2,1)S(1)} %collective-permute-done.4.refs_1_, bf16[160,128]{1,0:T(8,128)(2,1)S(1)} %collective-permute-done.5.refs_2_, bf16[160,128]{1,0:T(8,128)(2,1)S(1)} %collective-permute-done.6.refs_3_), custom_call_target="tpu_custom_call" | custom-call | flops 1000 | bytes 1000 | tf_op jit(solution)/shard_map/line_sum/pallas_call | solution.py:202
  39.1 0.8 %unit_slabs.1 = (bf16[192,128]{1,0:T(8,128)(2,1)}, bf16[192,128]{1,0:T(8,128)(2,1)}, bf16[192,128]{1,0:T(8,128)(2,1)}, bf16[192,128]{1,0:T(8,128)(2,1)}) custom-call(bf16[1,128,768]{2,1,0:T(8,128)(2,1)S(1)} %copy-done), custom_call_target="tpu_custom_call" | custom-call | flops 1000 | bytes 1000 | tf_op jit(solution)/shard_map/unit_slabs/pallas_call | solution.py:98
  39.9 3.7 %all-to-all-start.1 = ((bf16[8,64,128]{2,1,0:T(8,128)(2,1)}), bf16[8,64,128]{2,1,0:T(8,128)(2,1)S(1)}, u32[]{:S(2)}, u32[]{:S(2)}) async-start(bf16[8,64,128]{2,1,0:T(8,128)(2,1)} %get-tuple-element.46), calls=%async_computation.1 | async-start | bytes 262144 | tf_op jit(solution)/shard_map/all_to_all | solution.py:454
  43.6 3.8 %collective-permute-start.11 = (bf16[192,128]{1,0:T(8,128)(2,1)}, bf16[192,128]{1,0:T(8,128)(2,1)S(1)}, u32[]{:S(2)}, u32[]{:S(2)}) collective-permute-start(bf16[192,128]{1,0:T(8,128)(2,1)} %get-tuple-element.57), channel_id=1, source_target_pairs={{0,3},{1,0},{2,1},{3,2},{4,7},{5,4},{6,5},{7,6},{8,11},{9,8},{10,9... | collective-permute-start | bytes 147464 | tf_op jit(solution)/shard_map/ppermute | solution.py:419
  47.5 0.6 collective-permute-start.9
  48.1 4.6 %inverse_factor.1 = (f32[64,64]{1,0:T(8,128)}, bf16[768,64]{1,0:T(8,128)(2,1)}) custom-call(f32[64,64]{1,0:T(8,128)} %get-tuple-element.43.gram_any, bf16[64,768]{1,0:T(8,128)(2,1)} %get-tuple-element.44.lt_any), custom_call_target="tpu_custom_call" | custom-call | flops 4000000000 | bytes 1000 | tf_op jit(solution)/shard_map/inverse_factor/pallas_call | solution.py:249
  52.7 2.4 %finish.1 = (f32[64,1024]{1,0:T(8,128)}, bf16[1,768,1024]{2,1,0:T(8,128)(2,1)}) custom-call(f32[64,64]{1,0:T(8,128)} %get-tuple-element.45.w_any, bf16[32,16,128]{2,1,0:T(8,128)(2,1)S(1)} %bitcast.4, bf16[768,64]{1,0:T(8,128)(2,1)} %get-tuple-element.47.basis_any, bf16[768,1024]{1,0:T(8,128)(2,1)S(1)} %get-tuple-element.36.refs_4_.merged_ref), custom_call_target="tpu_custom_call" | custom-call | flops 1000 | bytes 1000 | tf_op jit(solution)/shard_map/finish/pallas_call | solution.py:301
  55.1 0.7 %collective-permute-done.11.refs_3_ = bf16[192,128]{1,0:T(8,128)(2,1)S(1)} collective-permute-done((bf16[192,128]{1,0:T(8,128)(2,1)}, bf16[192,128]{1,0:T(8,128)(2,1)S(1)}, u32[]{:S(2)}, u32[]{:S(2)}) %collective-permute-start.11) | collective-permute-done | bytes 49184 | tf_op jit(solution)/shard_map/ppermute | solution.py:419
  55.8 3.2 %collective-permute-done.10.refs_2_ = bf16[192,128]{1,0:T(8,128)(2,1)S(1)} collective-permute-done((bf16[192,128]{1,0:T(8,128)(2,1)}, bf16[192,128]{1,0:T(8,128)(2,1)S(1)}, u32[]{:S(2)}, u32[]{:S(2)}) %collective-permute-start.10) | collective-permute-done | bytes 49184 | tf_op jit(solution)/shard_map/ppermute | solution.py:419
  59.0 4.5 %expert_step.1 = (f32[1,192,2048]{2,1,0:T(8,128)}, f32[1,192,2048]{2,1,0:T(8,128)}, bf16[1,192,2048]{2,1,0:T(8,128)(2,1)}) custom-call(bf16[192,128]{1,0:T(8,128)(2,1)S(1)} %copy-done.1, bf16[192,128]{1,0:T(8,128)(2,1)S(1)} %collective-permute-done.9.refs_1_, bf16[192,128]{1,0:T(8,128)(2,1)S(1)} %collective-permute-done.10.refs_2_, ...), custom_call_target="tpu_custom_call" | custom-call | flops 1000 | bytes 1000 | tf_op jit(solution)/shard_map/expert_step/pallas_call | solution.py:386
  (20 shorter events, 1.0 us)
Async XLA Ops:
  0.6 5.8 %copy-start.2 = (bf16[1,128,2048]{2,1,0:T(8,128)(2,1)S(1)}, bf16[1,128,2048]{2,1,0:T(8,128)(2,1)}, u32[]{:S(2)}) copy-start(bf16[1,128,2048]{2,1,0:T(8,128)(2,1)} %refs_4_) | copy-start | bytes 1572868
  5.9 33.2 %copy-start = (bf16[1,128,768]{2,1,0:T(8,128)(2,1)S(1)}, bf16[1,128,768]{2,1,0:T(8,128)(2,1)}, u32[]{:S(2)}) copy-start(bf16[1,128,768]{2,1,0:T(8,128)(2,1)} %hidden_ref) | copy-start | bytes 589828
  5.9 5.3 %collective-permute-start = (f32[64,768]{1,0:T(8,128)S(1)}, f32[64,768]{1,0:T(8,128)S(1)}, u32[]{:S(2)}, u32[]{:S(2)}) collective-permute-start(f32[64,768]{1,0:T(8,128)S(1)} %get-tuple-element.35), channel_id=1, source_target_pairs={{0,4},{4,0},{8,12},{12,8},{16,20},{20,16},{24,28},{28,24},{1,5},{5... | collective-permute-start | bytes 589832 | tf_op jit(solution)/shard_map/ppermute | solution.py:415
  6.4 31.9 %collective-permute-start.7 = (bf16[1,128,2048]{2,1,0:T(8,128)(2,1)S(1)}, bf16[1,128,2048]{2,1,0:T(8,128)(2,1)S(1)}, u32[]{:S(2)}, u32[]{:S(2)}) collective-permute-start(bf16[1,128,2048]{2,1,0:T(8,128)(2,1)S(1)} %copy-done.2), channel_id=1, source_target_pairs={{0,1},{1,2},{2,3},{3,0},{4,5},{5,6},{6,7},{7,4},{8,9},{9,10},{10,1... | collective-permute-start | bytes 1572872 | tf_op jit(solution)/shard_map/ppermute | solution.py:419
  9.1 29.3 %collective-permute-start.8 = (bf16[1,128,2048]{2,1,0:T(8,128)(2,1)S(1)}, bf16[1,128,2048]{2,1,0:T(8,128)(2,1)S(1)}, u32[]{:S(2)}, u32[]{:S(2)}) collective-permute-start(bf16[1,128,2048]{2,1,0:T(8,128)(2,1)S(1)} %copy-done.2), channel_id=1, source_target_pairs={{0,3},{1,0},{2,1},{3,2},{4,7},{5,4},{6,5},{7,6},{8,11},{9,8},{10,9... | collective-permute-start | bytes 1572872 | tf_op jit(solution)/shard_map/ppermute | solution.py:419
  11.2 5.8 %collective-permute-start.3 = (bf16[64,768]{1,0:T(8,128)(2,1)S(1)}, bf16[64,768]{1,0:T(8,128)(2,1)S(1)}, u32[]{:S(2)}, u32[]{:S(2)}) collective-permute-start(bf16[64,768]{1,0:T(8,128)(2,1)S(1)} %add_convert_fusion.refs_0_), channel_id=1, source_target_pairs={{0,24},{4,28},{8,16},{12,20},{16,8},{20,12},{24,0},{28,4},{1,25},{... | collective-permute-start | bytes 294920 | tf_op jit(solution)/shard_map/ppermute | solution.py:415
  13.9 5.2 %collective-permute-start.2 = (bf16[64,768]{1,0:T(8,128)(2,1)S(1)}, bf16[64,768]{1,0:T(8,128)(2,1)S(1)}, u32[]{:S(2)}, u32[]{:S(2)}) collective-permute-start(bf16[64,768]{1,0:T(8,128)(2,1)S(1)} %add_convert_fusion.refs_0_), channel_id=1, source_target_pairs={{0,16},{4,20},{8,24},{12,28},{16,0},{20,4},{24,8},{28,12},{1,17},{... | collective-permute-start | bytes 294920 | tf_op jit(solution)/shard_map/ppermute | solution.py:415
  14.4 4.8 %collective-permute-start.1 = (bf16[64,768]{1,0:T(8,128)(2,1)S(1)}, bf16[64,768]{1,0:T(8,128)(2,1)S(1)}, u32[]{:S(2)}, u32[]{:S(2)}) collective-permute-start(bf16[64,768]{1,0:T(8,128)(2,1)S(1)} %add_convert_fusion.refs_0_), channel_id=1, source_target_pairs={{0,8},{4,12},{8,0},{12,4},{16,24},{20,28},{24,16},{28,20},{1,9},{5... | collective-permute-start | bytes 294920 | tf_op jit(solution)/shard_map/ppermute | solution.py:415
  29.3 5.9 %collective-permute-start.6 = (bf16[160,128]{1,0:T(8,128)(2,1)S(1)}, bf16[160,128]{1,0:T(8,128)(2,1)S(1)}, u32[]{:S(2)}, u32[]{:S(2)}) collective-permute-start(bf16[160,128]{1,0:T(8,128)(2,1)S(1)} %line_load.1.refs_0_), channel_id=1, source_target_pairs={{0,3},{1,0},{2,1},{3,2},{4,7},{5,4},{6,5},{7,6},{8,11},{9,8},{10,9... | collective-permute-start | bytes 122888 | tf_op jit(solution)/shard_map/ppermute | solution.py:419
  31.1 7.3 %collective-permute-start.5 = (bf16[160,128]{1,0:T(8,128)(2,1)S(1)}, bf16[160,128]{1,0:T(8,128)(2,1)S(1)}, u32[]{:S(2)}, u32[]{:S(2)}) collective-permute-start(bf16[160,128]{1,0:T(8,128)(2,1)S(1)} %line_load.1.refs_0_), channel_id=1, source_target_pairs={{0,2},{1,3},{2,0},{3,1},{4,6},{5,7},{6,4},{7,5},{8,10},{9,11},{10,... | collective-permute-start | bytes 122888 | tf_op jit(solution)/shard_map/ppermute | solution.py:419
  31.1 7.3 %collective-permute-start.4 = (bf16[160,128]{1,0:T(8,128)(2,1)S(1)}, bf16[160,128]{1,0:T(8,128)(2,1)S(1)}, u32[]{:S(2)}, u32[]{:S(2)}) collective-permute-start(bf16[160,128]{1,0:T(8,128)(2,1)S(1)} %line_load.1.refs_0_), channel_id=1, source_target_pairs={{0,1},{1,2},{2,3},{3,0},{4,5},{5,6},{6,7},{7,4},{8,9},{9,10},{10,1... | collective-permute-start | bytes 122888 | tf_op jit(solution)/shard_map/ppermute | solution.py:419
  39.1 19.9 %collective-permute-start.12 = (bf16[1,128,2048]{2,1,0:T(8,128)(2,1)S(1)}, bf16[1,128,2048]{2,1,0:T(8,128)(2,1)S(1)}, u32[]{:S(2)}, u32[]{:S(2)}) collective-permute-start(bf16[1,128,2048]{2,1,0:T(8,128)(2,1)S(1)} %collective-permute-done.7.refs_5_), channel_id=1, source_target_pairs={{0,1},{1,2},{2,3},{3,0},{4,5},{5,6},{6,7},{7,4},{8,9},{9,10},{10,1... | collective-permute-start | bytes 1572872 | tf_op jit(solution)/shard_map/ppermute | solution.py:419
  39.9 12.8 %all-to-all-start.1 = ((bf16[8,64,128]{2,1,0:T(8,128)(2,1)}), bf16[8,64,128]{2,1,0:T(8,128)(2,1)S(1)}, u32[]{:S(2)}, u32[]{:S(2)}) async-start(bf16[8,64,128]{2,1,0:T(8,128)(2,1)} %get-tuple-element.46), calls=%async_computation.1 | async-start | bytes 262144 | tf_op jit(solution)/shard_map/all_to_all | solution.py:454
  43.6 12.2 %collective-permute-start.11 = (bf16[192,128]{1,0:T(8,128)(2,1)}, bf16[192,128]{1,0:T(8,128)(2,1)S(1)}, u32[]{:S(2)}, u32[]{:S(2)}) collective-permute-start(bf16[192,128]{1,0:T(8,128)(2,1)} %get-tuple-element.57), channel_id=1, source_target_pairs={{0,3},{1,0},{2,1},{3,2},{4,7},{5,4},{6,5},{7,6},{8,11},{9,8},{10,9... | collective-permute-start | bytes 147464 | tf_op jit(solution)/shard_map/ppermute | solution.py:419
  47.5 11.5 %collective-permute-start.10 = (bf16[192,128]{1,0:T(8,128)(2,1)}, bf16[192,128]{1,0:T(8,128)(2,1)S(1)}, u32[]{:S(2)}, u32[]{:S(2)}) collective-permute-start(bf16[192,128]{1,0:T(8,128)(2,1)} %get-tuple-element.55), channel_id=1, source_target_pairs={{0,2},{1,3},{2,0},{3,1},{4,6},{5,7},{6,4},{7,5},{8,10},{9,11},{10,... | collective-permute-start | bytes 147464 | tf_op jit(solution)/shard_map/ppermute | solution.py:419
  47.5 11.5 %collective-permute-start.9 = (bf16[192,128]{1,0:T(8,128)(2,1)}, bf16[192,128]{1,0:T(8,128)(2,1)S(1)}, u32[]{:S(2)}, u32[]{:S(2)}) collective-permute-start(bf16[192,128]{1,0:T(8,128)(2,1)} %get-tuple-element.53), channel_id=1, source_target_pairs={{0,1},{1,2},{2,3},{3,0},{4,5},{5,6},{6,7},{7,4},{8,9},{9,10},{10,1... | collective-permute-start | bytes 147464 | tf_op jit(solution)/shard_map/ppermute | solution.py:419
  52.7 6.3 %copy-start.1 = (bf16[192,128]{1,0:T(8,128)(2,1)S(1)}, bf16[192,128]{1,0:T(8,128)(2,1)}, u32[]{:S(2)}) copy-start(bf16[192,128]{1,0:T(8,128)(2,1)} %get-tuple-element.51.refs_0_) | copy-start | bytes 147460
